TPU v7x, 256 devices: a whole 4x4x8 slice. The times are simulated.
256 devices in a mesh: row: 4 (over y), col: 16 (over z, core), head: 4 (over x).
Axes of the slice: x: 4, y: 4, z: 8, core: 2. Of those that a mesh axis runs over, the one named last changes fastest.
Arguments:
- queries: bfloat16 [192, 512, 1024], P('row', 'col', 'head'), may hold values from -16 to 16
- keys: bfloat16 [192, 512, 1024], P('row', 'col', 'head'), may hold values from -16 to 16
- values: bfloat16 [192, 512, 1024], P('row', 'col', 'head'), may hold values from -16 to 16
- positions: int32 [2, 192, 512], P(None, 'row', 'col'), may hold values from 0 to 512, as said below
- conv_weight: float32 [9, 1024], P(None, 'head'), may hold values from -2 to 2
- norm_gain: float32 [1024], P('head'), may hold values from 0.5 to 1.5
- norm_bias: float32 [1024], P('head'), may hold values from -3 to 3
Outputs:
- normed: bfloat16 [192, 512, 1024], P('row', 'col', 'head')
Inputs may be any that keep to these rules, and one draw needn't show every extreme that they name: positions[0] depends only on the grid row and positions[1] only on the grid column; each starts at 0 on the first grid line, rises by 0, 1 or 2 from one line to the next, and ends at 192 (rows) or 512 (columns).
All inputs are finite; a program needn't handle non-finite values.
Results may differ from a plain program's by a relative error of at most 0.0055.
Values may be sent and summed in bfloat16 or wider, within the bound.
No kernel may reach another device: no remote copies, remote signals or barrier semaphores. Data moves between devices by JAX's collectives and lax.ppermute only.
A program may use at most 128 MiB of HBM per device.

v0:
```python
import math

import jax
import jax.numpy as jnp
from jax import lax
from jax.sharding import PartitionSpec as P

HD = 64
D = 1024
AGR = 4
AGC = 1


epsilon = 1e-05


def merged_2(part, axis, combine):
    gathered = jax.tree.map(lambda a: lax.all_gather(a, axis), part)

    def take(source):
        return jax.tree.map(lambda a: lax.dynamic_index_in_dim(a, source, 0, False), gathered)

    return lax.fori_loop(
        1, lax.axis_size(axis), lambda source, state: combine(state, take(source)), take(0)
    )


def extended(cells, sides, width):
    for axis, dim in sides:
        count = lax.axis_size(axis)
        ends = count - 1
        head = lax.slice_in_dim(cells, 0, width, axis=dim)
        tail = lax.slice_in_dim(cells, cells.shape[dim] - width, cells.shape[dim], axis=dim)
        cells = jnp.concatenate(
            [
                lax.ppermute(tail, axis, [(i, (i + 1) % count) for i in range(ends)]),
                cells,
                lax.ppermute(head, axis, [((i + 1) % count, i) for i in range(ends)]),
            ],
            axis=dim,
        )
    return cells


def rotate_pairs(segment, angles):
    quarter = segment.shape[-1] // 2
    cosine = jnp.cos(angles)[..., None, :]
    sines = jnp.sin(angles)[..., None, :]
    lower = segment[..., :quarter]
    upper = segment[..., quarter:]
    return jnp.concatenate([lower * cosine - upper * sines, lower * sines + upper * cosine], -1)


def rotary(inputs, positions, head_size):
    full_shape = inputs.shape
    head_count = full_shape[-1] // head_size
    quarter = head_size // 4
    half_size = head_size // 2
    frequency = jnp.power(jnp.float32(100.0), -jnp.arange(quarter, dtype=jnp.float32) / quarter)
    row_angles = positions[0].astype(jnp.float32)[..., None] * frequency
    col_angles = positions[1].astype(jnp.float32)[..., None] * frequency
    unpacked = inputs.astype(jnp.float32).reshape(full_shape[:-1] + (head_count, head_size))
    turned = jnp.concatenate(
        [
            rotate_pairs(unpacked[..., :half_size], row_angles),
            rotate_pairs(unpacked[..., half_size:], col_angles),
        ],
        -1,
    )
    return turned.reshape(full_shape).astype(jnp.bfloat16)


def join_partials(earlier, second):
    highest = jnp.maximum(earlier[0], second[0])
    weight_first = jnp.exp(earlier[0] - highest)
    weight_second = jnp.exp(second[0] - highest)
    return (
        highest,
        earlier[1] * weight_first + second[1] * weight_second,
        earlier[2] * weight_first[..., None] + second[2] * weight_second[..., None],
    )


def shards(queries, keys, values, positions, conv_weight, norm_gain, norm_bias):
    tile_rows, tile_cols, channels = queries.shape
    head_count = channels // HD
    patch_count = tile_rows * tile_cols
    score_scale = 1.0 / math.sqrt(HD)
    turned_queries = rotary(queries, positions, HD)
    pooled = turned_queries.astype(jnp.float32).reshape(
        AGR, tile_rows // AGR, AGC, tile_cols // AGC, channels
    )
    pooled = pooled.mean(axis=(1, 3)).reshape(AGR * AGC, channels).astype(jnp.bfloat16)
    agents = lax.all_gather(pooled, ("row", "col"), axis=0, tiled=True)
    agent_heads = agents.reshape(-1, head_count, HD)
    turned_keys = rotary(keys, positions, HD).reshape(patch_count, head_count, HD)
    value_heads = values.reshape(patch_count, head_count, HD)
    scores = (
        jnp.einsum("ahd,thd->hat", agent_heads, turned_keys, preferred_element_type=jnp.float32)
        * score_scale
    )
    highest = scores.max(-1)
    exponent = jnp.exp(scores - highest[..., None])
    totals = exponent.sum(-1)
    numerator = jnp.einsum(
        "hat,thd->had",
        exponent.astype(jnp.bfloat16),
        value_heads,
        preferred_element_type=jnp.float32,
    )
    merged = merged_2((highest, totals, numerator), ("row", "col"), join_partials)
    agent_values = (merged[2] / merged[1][..., None]).astype(jnp.bfloat16)
    query_scores = (
        jnp.einsum(
            "thd,ahd->hta",
            turned_queries.reshape(patch_count, head_count, HD),
            agent_heads,
            preferred_element_type=jnp.float32,
        )
        * score_scale
    )
    probabilities = jax.nn.softmax(query_scores, -1).astype(jnp.bfloat16)
    attended = jnp.einsum(
        "hta,had->thd", probabilities, agent_values, preferred_element_type=jnp.float32
    )
    attended = attended.reshape(tile_rows, tile_cols, channels)
    padded = extended(values, (("row", 0), ("col", 1)), 1)
    convolved = jnp.zeros((tile_rows, tile_cols, channels), jnp.float32)
    for step_row in range(3):
        for step_col in range(3):
            convolved = (
                convolved
                + padded[step_row : step_row + tile_rows, step_col : step_col + tile_cols].astype(
                    jnp.float32
                )
                * conv_weight[3 * step_row + step_col]
            )
    summed = attended + convolved
    average = lax.psum(summed.sum(-1), "head") / D
    centered = summed - average[..., None]
    variance = lax.psum((centered * centered).sum(-1), "head") / D
    normed = centered * lax.rsqrt(variance + epsilon)[..., None] * norm_gain + norm_bias
    return normed.astype(jnp.bfloat16)


def solution(mesh):
    in_specs = (
        P("row", "col", "head"),
        P("row", "col", "head"),
        P("row", "col", "head"),
        P(None, "row", "col"),
        P(None, "head"),
        P("head"),
        P("head"),
    )
    out_specs = P("row", "col", "head")
    return jax.shard_map(shards, mesh=mesh, in_specs=in_specs, out_specs=out_specs, check_vma=False)
```

profile of v0, /device:TPU:8, one launch (start us, length us, event | category | flops | bytes accessed | tf_op | source)
XLA Modules:
  0.0 377.2 jit_solution(12326600888701350629)
XLA Ops:
  7.4 2.8 reshape.91
  10.2 7.7 %fusion.29 = (f32[48,32,4,16]{3,2,1,0:T(4,128)}, f32[48,32,4,16]{3,2,1,0:T(4,128)}, f32[48,32,4,16]{3,2,1,0:T(4,128)}, f32[48,32,4,16]{3,2,1,0:T(4,128)}) fusion(f32[48,32,4,64]{3,2,1,0:T(4,128)S(1)} %reshape.91), kind=kLoop, calls=%fused_computation.77 | loop fusion | bytes 3145728 | tf_op jit(solution)/shard_map/slice | solution.py:49
  18.0 2.8 reshape.89
  20.7 5.2 %fusion.30 = (f32[48,32,4,16]{3,2,1,0:T(4,128)S(1)}, f32[48,32,4,16]{3,2,1,0:T(4,128)S(1)}, f32[48,32,4,16]{3,2,1,0:T(4,128)S(1)}, f32[48,32,4,16]{3,2,1,0:T(4,128)S(1)}) fusion(f32[48,32,4,64]{3,2,1,0:T(4,128)S(1)} %reshape.89), kind=kLoop, calls=%fused_computation.78 | loop fusion | bytes 3145728 | tf_op jit(solution)/shard_map/slice | solution.py:49
  25.9 5.5 %multiply_cosine_fusion.1 = (f32[48,32,16]{2,1,0:T(8,128)S(1)}, f32[48,32,16]{2,1,0:T(8,128)S(1)}, f32[48,32,16]{2,1,0:T(8,128)S(1)}, f32[48,32,16]{2,1,0:T(8,128)S(1)}) fusion(f32[16]{0:T(128)S(1)} %multiply_power_fusion, f32[48,32]{1,0:T(8,128)S(1)} %copy.45, f32[48,32]{1,0:T(8,128)S(1)} %copy.48), kind=kLoop, calls=%fused_computation.46 | loop fusion | flops 49152 | bytes 405568 | tf_op jit(solution)/shard_map/cos | solution.py:47
  31.5 2.1 multiply_subtract_fusion
  33.6 3.5 convert_reduce_fusion
  37.3 52.4 %all-gather.3 = bf16[64,4,256]{2,1,0:T(4,128)(2,1)S(1)} all-gather(bf16[1,4,256]{2,1,0:T(4,128)(2,1)S(1)} %fusion.24), channel_id=1, replica_groups=mesh['row'=4,'col'=16,'head'=4] {'row','col'}, dimensions={0}, use_global_device_ids=true | all-gather | bytes 133120 | tf_op jit(solution)/shard_map/all_gather | solution.py:94
  90.1 3.7 reshape.86
  93.8 5.9 %subtract_convert_fusion = (bf16[48,32,4,16]{3,1,0,2:T(8,128)(2,1)S(1)}, bf16[48,32,4,16]{3,1,0,2:T(8,128)(2,1)S(1)}, bf16[48,32,4,16]{3,1,0,2:T(8,128)(2,1)S(1)}, bf16[48,32,4,16]{3,1,0,2:T(8,128)(2,1)S(1)}) fusion(f32[48,32,4,16]{3,2,1,0:T(4,128)} %get-tuple-element.238, f32[48,32,4,16]{3,2,1,0:T(4,128)} %get-tuple-element.236, ...), kind=kLoop, calls=%fused_computation.24 | loop fusion | flops 1572864 | bytes 2752512 | tf_op jit(solution)/shard_map/convert.4
  99.8 2.0 pad_maximum_fusion
  101.8 1.1 multiply_reduce_fusion
  102.9 2.7 copy-done
  105.6 2.1 fusion.9
  107.7 3.3 collective-permute-start
  111.0 3.0 collective-permute-start.1
  114.0 4.0 %fusion.8 = f32[4,256]{1,0:T(4,128)S(1)} fusion(f32[4,256,1536]{2,1,0:T(8,128)} %copy-done, f32[4,256]{1,0:T(4,128)S(1)} %get-tuple-element.266), kind=kLoop, calls=%fused_computation.17 | loop fusion | flops 4717568 | bytes 6299648 | tf_op jit(solution)/shard_map/reduce_sum | solution.py:104
  117.9 41.9 %all-gather.5 = f32[64,4,256]{2,1,0:T(4,128)S(1)} all-gather(f32[1,4,256]{2,1,0:T(4,128)S(1)} %bitcast.55), channel_id=3, replica_groups=mesh['row'=4,'col'=16,'head'=4] {'row','col'}, dimensions={0}, use_global_device_ids=true | all-gather | bytes 266240 | tf_op jit(solution)/shard_map/all_gather | solution.py:18
  159.8 43.2 %all-gather.4 = f32[64,4,256]{2,1,0:T(4,128)S(1)} all-gather(f32[1,4,256]{2,1,0:T(4,128)S(1)} %bitcast.54), channel_id=2, replica_groups=mesh['row'=4,'col'=16,'head'=4] {'row','col'}, dimensions={0}, use_global_device_ids=true | all-gather | bytes 266240 | tf_op jit(solution)/shard_map/all_gather | solution.py:18
  203.6 4.6 %fusion.34 = (f32[4,1536]{1,0:T(4,128)S(1)}, f32[4,1536,256]{1,2,0:T(8,128)}) fusion(bf16[1536,4,64]{2,0,1:T(8,128)(2,1)S(1)} %bitcast.52, bf16[256,4,64]{0,2,1:T(8,128)(2,1)S(1)} %copy.55), kind=kOutput, calls=%fused_computation.82 | convolution fusion | flops 206045440 | bytes 7233536 | tf_op jit(solution)/shard_map/sub | solution.py:122
  209.4 2.2 collective-permute-start.2
  211.6 1.3 collective-permute-start.3
  214.1 107.0 %while.19 = (s32[]{:T(128)}, f32[4,256]{1,0:T(4,128)S(1)}, f32[4,256]{1,0:T(4,128)S(1)}, f32[4,256,64]{2,1,0:T(8,128)S(1)}, f32[64,4,256]{2,1,0:T(4,128)S(1)}, /...) while((s32[]{:T(128)}, f32[4,256]{1,0:T(4,128)S(1)}, ...), condition=%wide.region_5.6_spmd, body=%wide.region_4.5_spmd.sunk | while | flops 202757 | bytes 1876119 | solution.py:23
  214.2 1.0 constant_dynamic-slice_fusion.2
  215.9 1.0 constant_dynamic-slice_fusion.2
  221.0 1.0 constant_dynamic-slice_fusion.2
  222.7 1.0 constant_dynamic-slice_fusion.2
  226.1 1.0 constant_dynamic-slice_fusion.2
  227.8 1.0 constant_dynamic-slice_fusion.2
  232.9 1.0 constant_dynamic-slice_fusion.2
  234.6 1.0 constant_dynamic-slice_fusion.2
  239.7 1.0 constant_dynamic-slice_fusion.2
  241.4 1.0 constant_dynamic-slice_fusion.2
  246.5 1.0 constant_dynamic-slice_fusion.2
  248.2 1.0 constant_dynamic-slice_fusion.2
  253.2 1.0 constant_dynamic-slice_fusion.2
  254.9 1.0 constant_dynamic-slice_fusion.2
  258.3 1.0 constant_dynamic-slice_fusion.2
  260.0 1.0 constant_dynamic-slice_fusion.2
  265.1 1.0 constant_dynamic-slice_fusion.2
  266.8 1.0 constant_dynamic-slice_fusion.2
  271.9 1.0 constant_dynamic-slice_fusion.2
  273.6 1.0 constant_dynamic-slice_fusion.2
  278.7 1.0 constant_dynamic-slice_fusion.2
  280.4 1.0 constant_dynamic-slice_fusion.2
  285.5 1.0 constant_dynamic-slice_fusion.2
  287.2 1.0 constant_dynamic-slice_fusion.2
  290.6 1.0 constant_dynamic-slice_fusion.2
  292.3 1.0 constant_dynamic-slice_fusion.2
  297.4 1.0 constant_dynamic-slice_fusion.2
  299.1 1.0 constant_dynamic-slice_fusion.2
  304.2 1.0 constant_dynamic-slice_fusion.2
  305.9 1.0 constant_dynamic-slice_fusion.2
  311.0 1.0 constant_dynamic-slice_fusion.2
  312.7 1.0 constant_dynamic-slice_fusion.2
  317.8 1.0 constant_dynamic-slice_fusion.2
  319.5 1.0 constant_dynamic-slice_fusion.2
  321.1 4.7 %fusion.15 = f32[1536,4,64]{0,2,1:T(8,128)} fusion(f32[4,1536,256]{1,2,0:T(8,128)} %get-tuple-element.265, f32[4,1536]{1,0:T(4,128)S(1)} %get-tuple-element.264, f32[4,256,64]{2,1,0:T(8,128)S(1)} %get-tuple-element.182, f32[4,256]{1,0:T(4,128)S(1)} %get-tuple-element.183), kind=kOutput, calls=%fused_computation.33 | convolution fusion | flops 204603392 | bytes 8155136 | tf_op jit(solution)/shard_map/hta,had->thd/dot_general | solution.py:123
  325.9 2.9 copy.64
  328.8 2.6 reshape.87
  331.4 5.6 %fusion.28 = (f32[48,32]{1,0:T(8,128)S(1)}, f32[48,32,256]{2,1,0:T(8,128)S(1)}) fusion(f32[48,32,256]{2,1,0:T(8,128)} %reshape.87, f32[256]{0:T(256)S(1)} %bitcast.63, bf16[50,1,256]{2,1,0:T(2,128)(2,1)S(1)} %collective-permute-done.3, bf16[50,32,256]{2,1,0:T(8,128)(2,1)} %copy-done.9, f32[256]{0:T(256)S(1)} %bitcast.64, ...), kind=kLoop, calls=%fused_computation.76 | loop fusion | flops 20445696 | bytes 4850688 | tf_op jit(solution)/shard_map/reduce_sum | solution.py:139
  337.0 17.0 %psum.14 = f32[48,32]{1,0:T(8,128)S(1)} all-reduce(f32[48,32]{1,0:T(8,128)S(1)} %get-tuple-element.223), channel_id=1, replica_groups=mesh['row'=4,'col'=16,'head'=4] {'head'}, use_global_device_ids=true, to_apply=%region_9.10 | all-reduce | flops 1536 | bytes 12288 | tf_op jit(solution)/shard_map/psum | solution.py:139
  354.6 14.4 %psum.15 = f32[48,32]{1,0:T(8,128)S(1)} all-reduce(f32[48,32]{1,0:T(8,128)S(1)} %multiply_reduce_fusion.2), channel_id=1, replica_groups=mesh['row'=4,'col'=16,'head'=4] {'head'}, use_global_device_ids=true, to_apply=%region_11.12 | all-reduce | flops 1536 | bytes 12288 | tf_op jit(solution)/shard_map/psum | solution.py:141
  369.0 1.4 add_convert_fusion.2
  (275 shorter events, 76.4 us)
Async XLA Ops:
  6.5 206.4 %all-gather.8.cloned.1.call-start = ((), (), s32[]{:S(2)}) async-start(), calls=%async_computation | async-start | bytes 17039360 | tf_op jit(solution)/shard_map/all_gather | solution.py:18
  31.4 2.1 copy-start.3
  31.4 2.1 copy-start.4
  31.5 2.1 copy-start.5
  31.5 2.1 copy-start.6
  89.8 4.1 %copy-start.1 = (f32[48,32,4,16]{3,2,1,0:T(4,128)S(1)}, f32[48,32,4,16]{3,2,1,0:T(4,128)}, u32[]{:S(2)}) copy-start(f32[48,32,4,16]{3,2,1,0:T(4,128)} %get-tuple-element.235) | copy-start | bytes 1179652
  101.8 3.8 %copy-start.7 = (bf16[1536,4,64]{2,1,0:T(4,128)(2,1)S(1)}, bf16[1536,4,64]{2,1,0:T(4,128)(2,1)}, u32[]{:S(2)}) copy-start(bf16[1536,4,64]{2,1,0:T(4,128)(2,1)} %reshape.86) | copy-start | bytes 2359300
  102.9 2.7 copy-start
  105.6 2.1 copy-start.2
  107.7 100.6 %collective-permute-start = (bf16[1,32,256]{2,1,0:T(8,128)(2,1)S(1)}, bf16[1,32,256]{2,1,0:T(8,128)(2,1)S(1)}, u32[]{:S(2)}, u32[]{:S(2)}) collective-permute-start(bf16[1,32,256]{2,1,0:T(8,128)(2,1)S(1)} %get-tuple-element.246), channel_id=1, source_target_pairs={{0,64},{64,128},{128,192},{1,65},{65,129},{129,193},{2,66},{66,130... | collective-permute-start | bytes 49160 | tf_op jit(solution)/shard_map/ppermute | solution.py:36
  111.0 92.1 %copy-start.10 = (f32[9,256]{1,0:T(8,128)S(1)}, f32[9,256]{1,0:T(8,128)}, u32[]{:S(2)}) copy-start(f32[9,256]{1,0:T(8,128)} %param.13) | copy-start | bytes 27652
  111.0 92.6 %copy-start.8 = (bf16[48,32,4,64]{3,1,0,2:T(8,128)(2,1)S(1)}, bf16[48,32,4,64]{3,1,0,2:T(8,128)(2,1)}, u32[]{:S(2)}) copy-start(bf16[48,32,4,64]{3,1,0,2:T(8,128)(2,1)} %get-tuple-element.226) | copy-start | bytes 2359300
  111.0 97.4 %collective-permute-start.1 = (bf16[1,32,256]{2,1,0:T(8,128)(2,1)S(1)}, bf16[1,32,256]{2,1,0:T(8,128)(2,1)S(1)}, u32[]{:S(2)}, u32[]{:S(2)}) collective-permute-start(bf16[1,32,256]{2,1,0:T(8,128)(2,1)S(1)} %get-tuple-element.245), channel_id=1, source_target_pairs={{64,0},{128,64},{192,128},{65,1},{129,65},{193,129},{66,2},{130,66... | collective-permute-start | bytes 49160 | tf_op jit(solution)/shard_map/ppermute | solution.py:38
  208.4 0.9 copy-start.9
  209.4 122.0 %collective-permute-start.2 = (bf16[50,1,256]{2,1,0:T(2,128)(2,1)S(1)}, bf16[50,1,256]{2,1,0:T(2,128)(2,1)S(1)}, u32[]{:S(2)}, u32[]{:S(2)}) collective-permute-start(bf16[50,1,256]{2,1,0:T(2,128)(2,1)S(1)} %get-tuple-element.243), channel_id=1, source_target_pairs={{0,4},{4,8},{8,12},{12,16},{16,20},{20,24},{24,28},{28,32},{32,36}... | collective-permute-start | bytes 76808 | tf_op jit(solution)/shard_map/ppermute | solution.py:36
  211.6 119.8 %collective-permute-start.3 = (bf16[50,1,256]{2,1,0:T(2,128)(2,1)S(1)}, bf16[50,1,256]{2,1,0:T(2,128)(2,1)S(1)}, u32[]{:S(2)}, u32[]{:S(2)}) collective-permute-start(bf16[50,1,256]{2,1,0:T(2,128)(2,1)S(1)} %get-tuple-element.244), channel_id=1, source_target_pairs={{4,0},{8,4},{12,8},{16,12},{20,16},{24,20},{28,24},{32,28},{36,32}... | collective-permute-start | bytes 76808 | tf_op jit(solution)/shard_map/ppermute | solution.py:38
  328.8 2.7 copy-start.11
  337.0 32.0 %copy-start.12 = (f32[256]{0:T(256)S(1)}, f32[256]{0:T(256)}, u32[]{:S(2)}) copy-start(f32[256]{0:T(256)} %param.15) | copy-start | bytes 3076
  337.0 32.0 %copy-start.13 = (f32[256]{0:T(256)S(1)}, f32[256]{0:T(256)}, u32[]{:S(2)}) copy-start(f32[256]{0:T(256)} %param.14) | copy-start | bytes 3076
Sparse Core Ops, SparseCore 0:
  107.8 98.2 all-gather.7
where the time goes:
time: 382 us; the launch traced here: 377 us
  blocking collectives  169 us (44%)
  local copies, waits for them, and re-layouts  107 us (28%)
  other arithmetic  62.3 us (16%)
  between operations  13.8 us (4%)
  matrix products  12.6 us (3%)
  starting transfers between devices  9.76 us (3%)
    all_gather x2, blocking collectives, merged_2(): gathered = jax.tree.map(lambda a: lax.all_gather(a, axis), part)  85.1 us
    dynamic_slice x129, local copies, waits for them, and re-layouts, take(): lax.dynamic_index_in_dim(a, source, 0, False)  74.5 us
    all_gather x1, blocking collectives, shards(): agents = lax.all_gather(pooled, ('row', 'col'), axis=0, tiled=True)  52.4 us
    add x63, other arithmetic, join_partials(): earlier[2] * weight_first[..., None] + second[2] * weight_second[..., None]  29.4 us
    psum x1, blocking collectives, shards(): average = lax.psum(summed.sum(-1), 'head') / D  17 us
    psum x1, blocking collectives, shards(): variance = lax.psum((centered * centered).sum(-1), 'head') / D  14.4 us
    slice x2, local copies, waits for them, and re-layouts, rotate_pairs(): lower = segment[..., :quarter]  13 us
  transfers between devices with their start and end apart: 5, of which 0 were waited for; matrix products, arithmetic and copies ran while one was open for 33% of the time, Pallas kernels for 0%

commit v1 on v0

v1 whole, which is shorter than its diff:
```python
import math

import jax
import jax.numpy as jnp
from jax import lax
from jax.experimental import pallas as pl
from jax.experimental.pallas import tpu as pltpu
from jax.sharding import PartitionSpec as P

HD = 64
D = 1024
AGR = 4
TR = 48
TC = 32
CH = 256
N = TR * TC
AGENTS = 256
TILES = 64
LOCAL_HEADS = 4
ROWS = LOCAL_HEADS * AGENTS // TILES
BLOCKS = N // 128

f32 = jnp.float32
bf16 = jnp.bfloat16
epsilon = 1e-05

VMEM_SPEC = pl.BlockSpec(memory_space=pltpu.VMEM)


def call(kernel, out_shape, n_in, scratch=(), flops=0, nbytes=0, name=None):
    outs = jax.tree.map(lambda s: VMEM_SPEC, out_shape)
    return pl.pallas_call(
        kernel,
        out_shape=out_shape,
        in_specs=[VMEM_SPEC] * n_in,
        out_specs=outs,
        scratch_shapes=list(scratch),
        compiler_params=pltpu.CompilerParams(vmem_limit_bytes=32 * 1024 * 1024),
        cost_estimate=pl.CostEstimate(flops=flops, bytes_accessed=nbytes, transcendentals=0),
        name=name,
    )


def shape(dims, dtype):
    return jax.ShapeDtypeStruct(dims, dtype)


def lanes(dims):
    return lax.broadcasted_iota(jnp.int32, dims, len(dims) - 1)


def turn_matrix():
    source = lax.broadcasted_iota(jnp.int32, (CH, CH), 0)
    target = lax.broadcasted_iota(jnp.int32, (CH, CH), 1)
    low = (target & 31) < 16
    minus = jnp.where(low & (source == target + 16), -1.0, 0.0)
    plus = jnp.where((~low) & (source == target - 16), 1.0, 0.0)
    return (minus + plus).astype(bf16)


def sin_cos(angle):
    return jnp.sin(angle), jnp.cos(angle)


def turned(x, matrix, cosine, sine):
    swapped = jnp.dot(x, matrix, preferred_element_type=f32)
    return (x.astype(f32) * cosine + swapped * sine).astype(bf16)


def cell_tables(cos_r, sin_r, cos_c, sin_c, first, rows):
    cosine = jnp.concatenate(
        [cos_r[first + i : first + i + 1, :] * cos_c for i in range(rows)], axis=0
    )
    sine = jnp.concatenate(
        [sin_r[first + i : first + i + 1, :] + sin_c for i in range(rows)], axis=0
    )
    return cosine, sine


def query_kernel(pos_ref, freq_ref, q_ref, tq_ref, agents_ref, tab_r_ref, tab_c_ref, turn_ref):
    freq = freq_ref[...]
    row_pos = pos_ref[0][:, 0:1].astype(f32)
    col_line = pos_ref[1][0:1, :].astype(f32)
    eye = lax.broadcasted_iota(jnp.int32, (TC, TC), 0) == lax.broadcasted_iota(
        jnp.int32, (TC, TC), 1
    )
    col_pos = jnp.sum(jnp.where(eye, jnp.broadcast_to(col_line, (TC, TC)), 0.0), 1, keepdims=True)
    angles = jnp.concatenate([row_pos * freq[0:1, :], col_pos * freq[1:2, :]], axis=0)
    sines, cosines = sin_cos(angles)
    sines = jnp.concatenate([sines, sines], axis=1)
    cosines = jnp.concatenate([cosines, cosines], axis=1)
    tab_r_ref[0] = cosines[:TR]
    tab_r_ref[1] = sines[:TR]
    tab_c_ref[0] = cosines[TR:]
    tab_c_ref[1] = sines[TR:]
    matrix = turn_matrix()
    turn_ref[...] = matrix
    step = N // AGR
    means = []
    for cell in range(AGR):
        cosine, sine = cell_tables(
            cosines[:TR], sines[:TR], cosines[TR:], sines[TR:], cell * (TR // AGR), TR // AGR
        )
        rotated = turned(q_ref[pl.ds(cell * step, step), :], matrix, cosine, sine)
        tq_ref[pl.ds(cell * step, step), :] = rotated
        mean = jnp.sum(rotated.astype(f32), 0, keepdims=True) / step
        means.append(mean.astype(bf16).astype(f32))
    packed = jnp.concatenate([m[:, :128] for m in means] + [m[:, 128:] for m in means], axis=0)
    agents_ref[...] = jnp.broadcast_to(packed[None], (TILES, 8, 128))


def key_kernel(tab_r_ref, tab_c_ref, turn_ref, k_ref, tk_ref):
    matrix = turn_ref[...]
    step = N // AGR
    for cell in range(AGR):
        cosine, sine = cell_tables(
            tab_r_ref[0], tab_r_ref[1], tab_c_ref[0], tab_c_ref[1], cell * (TR // AGR), TR // AGR
        )
        tk_ref[pl.ds(cell * step, step), :] = turned(
            k_ref[pl.ds(cell * step, step), :], matrix, cosine, sine
        )


def agent_pairs(agents_ref, scale):
    pairs = []
    for pair in range(2):
        parts = [agents_ref[pl.ds(4 * pair + k, TILES, stride=8), :] for k in range(AGR)]
        pairs.append((jnp.concatenate(parts, axis=0) * scale).astype(bf16))
    return pairs


def half_mask(dims, parity):
    return (lanes(dims) // HD) == parity


def partial_kernel(agents_ref, tk_ref, v_ref, out_ref, score_ref):
    pairs = agent_pairs(agents_ref, 1.0 / math.sqrt(HD))
    chunk = 512
    for head in range(LOCAL_HEADS):
        pair, parity = head // 2, head % 2
        cols = pl.ds(pair * 128, 128)
        own = pairs[pair]
        own = jnp.where(half_mask(own.shape, parity), own, jnp.zeros_like(own))
        peak = None
        for c in range(N // chunk):
            scores = lax.dot_general(
                own,
                tk_ref[pl.ds(c * chunk, chunk), cols],
                (((1,), (1,)), ((), ())),
                preferred_element_type=f32,
            )
            score_ref[:, pl.ds(c * chunk, chunk)] = scores
            for s in range(chunk // 128):
                piece = scores[:, s * 128 : (s + 1) * 128]
                peak = piece if peak is None else jnp.maximum(peak, piece)
        peak = jnp.max(peak, 1, keepdims=True)
        acc = jnp.zeros((AGENTS, 128), f32)
        for c in range(N // chunk):
            weights = jnp.exp(score_ref[:, pl.ds(c * chunk, chunk)] - peak).astype(bf16)
            block = v_ref[pl.ds(c * chunk, chunk), cols]
            block = jnp.where(half_mask(block.shape, parity), block, jnp.ones_like(block))
            acc = acc + jnp.dot(weights, block, preferred_element_type=f32)
        other = pltpu.roll(acc, HD, 1)
        numer, total = (acc, other) if parity == 0 else (other, acc)
        logs = peak + jnp.log(total)
        values = numer / total
        logs = jnp.max(jnp.where(half_mask(logs.shape, 0), logs, -3e38), 1, keepdims=True)
        first = logs.astype(bf16).astype(f32)
        second = (logs - first).astype(bf16).astype(f32)
        third = logs - first - second
        lane = lanes((AGENTS, 128))
        packed = jnp.where(
            lane < HD,
            values,
            jnp.where(
                lane == HD,
                first,
                jnp.where(lane == HD + 1, second, jnp.where(lane == HD + 2, third, 0.0)),
            ),
        )
        out_ref[pl.ds(head * AGENTS, AGENTS), :] = packed.astype(bf16)


def merge_kernel(parts_ref, out_ref):
    source = lax.broadcasted_iota(jnp.int32, (128, 128), 0)
    picker = jnp.where((source >= HD) & (source < HD + 3), 1.0, 0.0).astype(bf16)
    parts = parts_ref[...]
    logs = jnp.dot(parts, picker, preferred_element_type=f32).reshape(TILES, ROWS, 128)
    values = parts.astype(f32).reshape(TILES, ROWS, 128)
    peak = jnp.max(logs, 0)
    weights = jnp.exp(logs - peak[None])
    merged = jnp.sum(weights * values, 0) / jnp.sum(weights, 0)
    merged = jnp.where(lanes(merged.shape) < HD, merged, 0.0)
    merged = (merged + pltpu.roll(merged, HD, 1)).astype(bf16)
    out_ref[...] = jnp.broadcast_to(merged[None], (TILES, ROWS, 128))


def probability_kernel(agents_ref, tq_ref, prob_ref, recip_ref):
    pairs = agent_pairs(agents_ref, 1.0 / math.sqrt(HD))
    target = [
        jnp.where(half_mask((AGENTS, 128), parity), 1.0, 0.0).astype(bf16) for parity in range(2)
    ]
    owns = []
    for head in range(LOCAL_HEADS):
        own = pairs[head // 2]
        owns.append(jnp.where(half_mask(own.shape, head % 2), own, jnp.zeros_like(own)))
    chunk = 256

    def body(c, carry):
        rows = pl.ds(pl.multiple_of(c * chunk, chunk), chunk)
        for pair in range(2):
            cols = pl.ds(pair * 128, 128)
            queries = tq_ref[rows, cols]
            total = jnp.zeros((chunk, 128), f32)
            for parity in range(2):
                head = 2 * pair + parity
                scores = lax.dot_general(
                    queries, owns[head], (((1,), (1,)), ((), ())), preferred_element_type=f32
                )
                weights = jnp.exp(scores - jnp.max(scores, 1, keepdims=True)).astype(bf16)
                prob_ref[rows, pl.ds(head * AGENTS, AGENTS)] = weights
                total = total + jnp.dot(weights, target[parity], preferred_element_type=f32)
            recip_ref[rows, cols] = 1.0 / total
        return carry

    lax.fori_loop(0, N // chunk, body, 0)


def edge_kernel(left_ref, right_ref, first_ref, last_ref):
    first_ref[...] = left_ref[:, 0, :]
    last_ref[...] = right_ref[:, 15, :]


def line_kernel(v_top_ref, v_bottom_ref, left_ref, right_ref, up_ref, down_ref):
    for v_ref, row, out_ref in ((v_top_ref, 0, up_ref), (v_bottom_ref, TR - 1, down_ref)):
        out_ref[pl.ds(0, TC), :] = v_ref[0]
        left = left_ref[row : row + 1, :].astype(f32)
        right = right_ref[row : row + 1, :].astype(f32)
        tail = jnp.concatenate([left, right, jnp.zeros((14, CH), f32)], axis=0)
        out_ref[pl.ds(TC, 16), :] = tail.astype(bf16)


def conv_kernel(v_ref, left_ref, right_ref, above_ref, below_ref, w_ref, out_ref, l_ref, r_ref):
    l_ref[...] = left_ref[...].astype(f32)
    r_ref[...] = right_ref[...].astype(f32)
    for half in range(2):
        cols = pl.ds(half * 128, 128)
        w = [jnp.broadcast_to(w_ref[t : t + 1, cols], (TC, 128)) for t in range(9)]
        column = lax.broadcasted_iota(jnp.int32, (TC, 128), 0)

        def taps(row, left, right):
            row = row.astype(f32)
            before = jnp.where(column == 0, left, pltpu.roll(row, 1, 0))
            after = jnp.where(column == TC - 1, right, pltpu.roll(row, TC - 1, 0))
            return [before * w[3 * d] + row * w[3 * d + 1] + after * w[3 * d + 2] for d in range(3)]

        tail = above_ref[pl.ds(TC, 16), cols].astype(f32)
        t0 = taps(above_ref[pl.ds(0, TC), cols], tail[0:1], tail[1:2])

        def group(start, carry):
            a, b = carry
            lefts, rights = l_ref[pl.ds(start, 8), cols], r_ref[pl.ds(start, 8), cols]
            for k in range(8):
                t = taps(v_ref[start + k, :, cols], lefts[k : k + 1], rights[k : k + 1])
                if a is not None:
                    at = (start + k - 1) * TC
                    if not isinstance(at, int):
                        at = pl.multiple_of(at, TC)
                    out_ref[pl.ds(at, TC), cols] = a + t[2]
                a, b = b + t[1], t[0]
            return a, b

        carry = group(0, (None, t0[0]))
        a, b = lax.fori_loop(
            1, TR // 8, lambda g, c: group(pl.multiple_of(g * 8, 8), c), carry
        )
        tail = below_ref[pl.ds(TC, 16), cols].astype(f32)
        t = taps(below_ref[pl.ds(0, TC), cols], tail[0:1], tail[1:2])
        out_ref[pl.ds((TR - 1) * TC, TC), cols] = a + t[2]


def attend_kernel(av_ref, prob_ref, recip_ref, conv_ref, sum_ref, stat_ref):
    halves = []
    for pair in range(2):
        pieces = []
        for parity in range(2):
            part = av_ref[pl.ds((2 * pair + parity) * AGENTS, AGENTS), :]
            pieces.append(jnp.where(half_mask(part.shape, parity), part, jnp.zeros_like(part)))
        halves.append(jnp.concatenate(pieces, axis=0))
    eye = lax.broadcasted_iota(jnp.int32, (128, 128), 0) == lanes((128, 128))

    for b in range(BLOCKS):
        rows = pl.ds(b * 128, 128)
        xs = []
        for pair in range(2):
            cols = pl.ds(pair * 128, 128)
            attended = jnp.dot(
                prob_ref[rows, pl.ds(pair * 2 * AGENTS, 2 * AGENTS)],
                halves[pair],
                preferred_element_type=f32,
            )
            x = attended * recip_ref[rows, cols] + conv_ref[rows, cols]
            sum_ref[rows, cols] = x
            xs.append(x)
        mean = jnp.sum(xs[0] + xs[1], 1, keepdims=True) * (1.0 / CH)
        c0, c1 = xs[0] - mean, xs[1] - mean
        squares = jnp.sum(c0 * c0 + c1 * c1, 1, keepdims=True)
        stat_ref[b : b + 1, :] = jnp.sum(jnp.where(eye, mean, 0.0), 0, keepdims=True)
        stat_ref[BLOCKS + b : BLOCKS + b + 1, :] = jnp.sum(
            jnp.where(eye, squares, 0.0), 0, keepdims=True
        )


def norm_kernel(s0_ref, s1_ref, s2_ref, s3_ref, sum_ref, gain_ref, bias_ref, out_ref):
    stats = [s[...] for s in (s0_ref, s1_ref, s2_ref, s3_ref)]
    means = [s[:BLOCKS] for s in stats]
    mean = (means[0] + means[1] + means[2] + means[3]) * 0.25
    squares = sum(s[BLOCKS:] for s in stats)
    for m in means:
        squares = squares + CH * (m - mean) * (m - mean)
    scale = lax.rsqrt(squares * (1.0 / D) + epsilon)
    for b in range(BLOCKS):
        rows = pl.ds(b * 128, 128)
        m = jnp.broadcast_to(mean[b : b + 1], (128, 128)).T
        s = jnp.broadcast_to(scale[b : b + 1], (128, 128)).T
        for half in range(2):
            cols = pl.ds(half * 128, 128)
            out_ref[rows, cols] = (
                (sum_ref[rows, cols] - m) * s * gain_ref[0:1, cols] + bias_ref[0:1, cols]
            ).astype(bf16)


def frequencies():
    lane = jnp.arange(128) % HD
    power = jnp.power(f32(100.0), -(lane % 16).astype(f32) / 16)
    return jnp.stack([jnp.where(lane < 32, power, 0.0), jnp.where(lane < 32, 0.0, power)])


def spread(x):
    return lax.all_to_all(x, ("row", "col"), 0, 0)


def shift(x, axis, step):
    count = lax.axis_size(axis)
    pairs = [(i, i + step) for i in range(count) if 0 <= i + step < count]
    return lax.ppermute(x, axis, pairs)


def shards(queries, keys, values, positions, conv_weight, norm_gain, norm_bias):
    q = queries.reshape(N, CH)
    k = keys.reshape(N, CH)
    v = values.reshape(N, CH)
    mb = 1 << 20
    tq, packed, tab_r, tab_c, turn = call(
        query_kernel,
        (
            shape((N, CH), bf16),
            shape((TILES, 8, 128), f32),
            shape((2, TR, CH), f32),
            shape((2, TC, CH), f32),
            shape((CH, CH), bf16),
        ),
        3,
        nbytes=8 * mb,
        name="turn_queries",
    )(positions, frequencies(), q)
    agents = spread(packed).reshape(TILES * 8, 128)
    tk = call(key_kernel, shape((N, CH), bf16), 4, nbytes=6 * mb, name="turn_keys")(
        tab_r, tab_c, turn, k
    )
    parts = call(
        partial_kernel,
        shape((LOCAL_HEADS * AGENTS, 128), bf16),
        3,
        scratch=[pltpu.VMEM((AGENTS, N), f32)],
        nbytes=20 * mb,
        name="partials",
    )(agents, tk, v)
    received = spread(parts.reshape(TILES, ROWS, 128)).reshape(TILES * ROWS, 128)
    prob, recip = call(
        probability_kernel,
        (shape((N, LOCAL_HEADS * AGENTS), bf16), shape((N, CH), f32)),
        2,
        nbytes=20 * mb,
        name="probabilities",
    )(agents, tq)
    merged = call(merge_kernel, shape((TILES, ROWS, 128), bf16), 1, nbytes=2 * mb, name="merge")(
        received
    )
    agent_values = spread(merged).reshape(TILES * ROWS, 128)

    first, last = pl.pallas_call(
        edge_kernel,
        out_shape=(shape((TR, CH), bf16),) * 2,
        grid=(1,),
        in_specs=[
            pl.BlockSpec((TR, 16, CH), lambda i: (0, 0, 0)),
            pl.BlockSpec((TR, 16, CH), lambda i: (0, 1, 0)),
        ],
        out_specs=(pl.BlockSpec((TR, CH), lambda i: (0, 0)),) * 2,
        name="edges",
    )(values, values)
    left = shift(last, "col", 1)
    right = shift(first, "col", -1)
    up, down = pl.pallas_call(
        line_kernel,
        out_shape=(shape((TC + 16, CH), bf16),) * 2,
        grid=(1,),
        in_specs=[
            pl.BlockSpec((1, TC, CH), lambda i: (0, 0, 0)),
            pl.BlockSpec((1, TC, CH), lambda i: (TR - 1, 0, 0)),
            pl.BlockSpec((TR, CH), lambda i: (0, 0)),
            pl.BlockSpec((TR, CH), lambda i: (0, 0)),
        ],
        out_specs=(pl.BlockSpec((TC + 16, CH), lambda i: (0, 0)),) * 2,
        name="lines",
    )(values, values, left, right)
    above = shift(down, "row", 1)
    below = shift(up, "row", -1)
    convolved = call(
        conv_kernel,
        shape((N, CH), f32),
        6,
        scratch=[pltpu.VMEM((TR, CH), f32), pltpu.VMEM((TR, CH), f32)],
        nbytes=8 * mb,
        name="conv",
    )(values, left, right, above, below, conv_weight)

    summed, stats = call(
        attend_kernel,
        (shape((N, CH), f32), shape((2 * BLOCKS, 128), f32)),
        4,
        nbytes=8 * mb,
        name="attend",
    )(agent_values, prob, recip, convolved)
    heads = lax.axis_size("head")
    others = [
        lax.ppermute(stats, "head", [(i, (i + d) % heads) for i in range(heads)])
        for d in range(1, heads)
    ]
    normed = call(norm_kernel, shape((N, CH), bf16), 7, nbytes=4 * mb, name="norm")(
        stats, *others, summed, norm_gain.reshape(1, CH), norm_bias.reshape(1, CH)
    )
    return normed.reshape(TR, TC, CH)


def solution(mesh):
    in_specs = (
        P("row", "col", "head"),
        P("row", "col", "head"),
        P("row", "col", "head"),
        P(None, "row", "col"),
        P(None, "head"),
        P("head"),
        P("head"),
    )
    out_specs = P("row", "col", "head")
    return jax.shard_map(shards, mesh=mesh, in_specs=in_specs, out_specs=out_specs, check_vma=False)
```

time: 382 us -> 103 us (0.27)
  blocking collectives: 169 us -> 17.8 us
  local copies, waits for them, and re-layouts: 107 us -> 11.1 us
  other arithmetic: 62.3 us -> 0.02 us
  starting transfers between devices: 9.76 us -> 32.4 us
  waiting for transfers between devices: 0.05 us -> 21.6 us
  Pallas kernels: 0 us -> 17.8 us
  between operations: 13.8 us -> 0.17 us
  matrix products: 12.6 us -> 0 us
    all_gather x3 -> x0, blocking collectives: 138 us -> none  [the longest x2 85.1 us: merged_2(): gathered = jax.tree.map(lambda a: lax.all_gather(a, axis), part)]
    dynamic_slice x129 -> x0, local copies, waits for them, and re-layouts: 74.5 us -> none  [take(): lax.dynamic_index_in_dim(a, source, 0, False)]
    psum x2 -> x0, blocking collectives: 31.5 us -> none  [the longest x1 17 us: shards(): average = lax.psum(summed.sum(-1), 'head') / D]
    add x126 -> x0, other arithmetic: 31.1 us -> none  [the longest x63 29.4 us: join_partials(): earlier[2] * weight_first[..., None] + second[2] * weight_second[..., None]]
    all_to_all x0 -> x2, starting transfers between devices: none -> 18.6 us  [spread(): return lax.all_to_all(x, ('row', 'col'), 0, 0)]
    all_to_all x0 -> x1, blocking collectives: none -> 17.8 us  [spread(): return lax.all_to_all(x, ('row', 'col'), 0, 0)]
    pallas_call x0 -> x10, Pallas kernels: none -> 17.8 us  [the longest x1 4.54 us: shards(): call(probability_kernel, (shape((N, LOCAL_HEADS * AGENTS), bf16), shape((...]
    slice x5 -> x0, local copies, waits for them, and re-layouts: 13.6 us -> none  [the longest x2 13 us: rotate_pairs(): lower = segment[..., :quarter]]
  transfers between devices with their start and end apart: 5 -> 9, of which waited for: 0 -> 6; matrix products, arithmetic and copies ran while one was open for 33% -> 0% of each run, Pallas kernels for 0% -> 10%
where the time goes in v1:
time: 103 us; the launch traced here: 101 us
  starting transfers between devices  32.4 us (31%)
  waiting for transfers between devices  21.6 us (21%)
  Pallas kernels  17.8 us (17%)
  blocking collectives  17.8 us (17%)
  local copies, waits for them, and re-layouts  11.1 us (11%)
    all_to_all x2, starting transfers between devices, spread(): return lax.all_to_all(x, ('row', 'col'), 0, 0)  18.6 us
    all_to_all x1, blocking collectives, spread(): return lax.all_to_all(x, ('row', 'col'), 0, 0)  17.8 us
    unnamed x35, local copies, waits for them, and re-layouts  11.1 us
    all_to_all x2, waiting for transfers between devices, spread(): return lax.all_to_all(x, ('row', 'col'), 0, 0)  11 us
    ppermute x4, starting transfers between devices, shift(): return lax.ppermute(x, axis, pairs)  9.29 us
    ppermute x4, waiting for transfers between devices, shift(): return lax.ppermute(x, axis, pairs)  6.48 us
    pallas_call x1, Pallas kernels, shards(): call(probability_kernel, (shape((N, LOCAL_HEADS * AGENTS), bf16), shape((...  4.54 us
    ppermute x3, starting transfers between devices, shards(): lax.ppermute(stats, 'head', [(i, (i + d) % heads) for i in range(heads)])  4.53 us
  transfers between devices with their start and end apart: 9, of which 6 were waited for; matrix products, arithmetic and copies ran while one was open for 0% of the time, Pallas kernels for 10%

profile of v1, /device:TPU:8, one launch (start us, length us, event | category | flops | bytes accessed | tf_op | source)
XLA Modules:
  0.0 100.9 jit_solution(18039541448763315096)
XLA Ops:
  0.0 0.0 copy-start.6
  0.0 0.9 copy.8.pos_ref
  0.9 0.0 copy-start.7
  1.0 1.1 %copy-done.7 = bf16[48,32,256]{2,1,0:T(8,128)(2,1)S(1)} copy-done((bf16[48,32,256]{2,1,0:T(8,128)(2,1)S(1)}, bf16[48,32,256]{2,1,0:T(8,128)(2,1)}, u32[]{:S(2)}) %copy-start.7) | copy-done | bytes 786456
  2.1 0.0 copy-start
  2.1 1.4 %turn_queries.1 = (bf16[1536,256]{1,0:T(8,128)(2,1)S(1)}, f32[64,8,128]{2,1,0:T(8,128)}, f32[2,48,256]{2,1,0:T(8,128)S(1)}, f32[2,32,256]{2,1,0:T(8,128)S(1)}, bf16[256,256]{1,0:T(8,128)(2,1)S(1)}) custom-call(s32[2,48,32]{2,1,0:T(8,128)S(1)} %copy.8.pos_ref, f32[2,128]{1,0:T(2,128)S(1)} %pad_maximum_fusion.freq_ref, bf16[1536,256]{1,0:T(8,128)(2,1)S(1)} %bitcast.17), custom_call_target="tpu_custom_call" | custom-call | bytes 8388608 | tf_op jit(solution)/shard_map/turn_queries/pallas_call | solution.py:354
  3.5 0.0 copy-start.8
  3.5 0.9 copy-done.8
  4.4 12.1 %all-to-all-start = ((f32[64,8,128]{2,1,0:T(8,128)}), f32[64,8,128]{2,1,0:T(8,128)S(1)}, u32[]{:S(2)}, u32[]{:S(2)}) async-start(f32[64,8,128]{2,1,0:T(8,128)} %get-tuple-element.18), calls=%async_computation | async-start | bytes 524288 | tf_op jit(solution)/shard_map/all_to_all | solution.py:340
  16.5 0.0 copy-done.6
  16.5 0.5 turn_keys.1.tk_ref
  17.0 11.0 %all-to-all-done = f32[64,8,128]{2,1,0:T(8,128)S(1)} async-done(((f32[64,8,128]{2,1,0:T(8,128)}), f32[64,8,128]{2,1,0:T(8,128)S(1)}, u32[]{:S(2)}, u32[]{:S(2)}) %all-to-all-start) | async-done | bytes 262176 | tf_op jit(solution)/shard_map/all_to_all | solution.py:340
  28.1 0.0 copy-done
  28.1 3.0 %partials.1 = bf16[1024,128]{1,0:T(8,128)(2,1)S(1)} custom-call(f32[512,128]{1,0:T(8,128)S(1)} %bitcast.11, bf16[1536,256]{1,0:T(8,128)(2,1)S(1)} %turn_keys.1.tk_ref, bf16[1536,256]{1,0:T(8,128)(2,1)S(1)} %bitcast.10), custom_call_target="tpu_custom_call" | custom-call | bytes 20971520 | tf_op jit(solution)/shard_map/partials/pallas_call | solution.py:371
  31.1 17.8 %all_to_all.15 = bf16[64,16,128]{2,1,0:T(8,128)(2,1)S(1)} all-to-all(bf16[64,16,128]{2,1,0:T(8,128)(2,1)S(1)} %bitcast.15), channel_id=1, replica_groups=mesh['row'=4,'col'=16,'head'=4] {'row','col'}, dimensions={0} | all-to-all | bytes 524288 | tf_op jit(solution)/shard_map/all_to_all | solution.py:340
  48.9 1.2 %merge.1 = bf16[64,16,128]{2,1,0:T(8,128)(2,1)} custom-call(bf16[1024,128]{1,0:T(8,128)(2,1)S(1)} %bitcast.14), custom_call_target="tpu_custom_call" | custom-call | bytes 2097152 | tf_op jit(solution)/shard_map/merge/pallas_call | solution.py:387
  50.1 6.5 %all-to-all-start.2 = ((bf16[64,16,128]{2,1,0:T(8,128)(2,1)}), bf16[64,16,128]{2,1,0:T(8,128)(2,1)S(1)}, u32[]{:S(2)}, u32[]{:S(2)}) async-start(bf16[64,16,128]{2,1,0:T(8,128)(2,1)} %merge.1), calls=%async_computation.2 | async-start | bytes 524288 | tf_op jit(solution)/shard_map/all_to_all | solution.py:340
  56.6 0.0 copy-start.1
  56.6 0.0 copy-start.14
  56.6 1.9 %edges.1 = (bf16[48,256]{1,0:T(8,128)(2,1)}, bf16[48,256]{1,0:T(8,128)(2,1)}) custom-call(bf16[48,32,256]{2,1,0:T(8,128)(2,1)} %v_ref.1, bf16[48,32,256]{2,1,0:T(8,128)(2,1)} %v_ref.1), custom_call_target="tpu_custom_call" | custom-call | tf_op jit(solution)/shard_map/edges/pallas_call | solution.py:392
  58.5 2.0 %collective-permute-start = (bf16[48,256]{1,0:T(8,128)(2,1)}, bf16[48,256]{1,0:T(8,128)(2,1)S(1)}, u32[]{:S(2)}, u32[]{:S(2)}) collective-permute-start(bf16[48,256]{1,0:T(8,128)(2,1)} %get-tuple-element.25), channel_id=1, source_target_pairs={{0,4},{4,8},{8,12},{12,16},{16,20},{20,24},{24,28},{28,32},{32,36}... | collective-permute-start | bytes 73736 | tf_op jit(solution)/shard_map/ppermute | solution.py:346
  60.5 1.3 %collective-permute-start.1 = (bf16[48,256]{1,0:T(8,128)(2,1)}, bf16[48,256]{1,0:T(8,128)(2,1)S(1)}, u32[]{:S(2)}, u32[]{:S(2)}) collective-permute-start(bf16[48,256]{1,0:T(8,128)(2,1)} %get-tuple-element.26), channel_id=1, source_target_pairs={{4,0},{8,4},{12,8},{16,12},{20,16},{24,20},{28,24},{32,28},{36,32}... | collective-permute-start | bytes 73736 | tf_op jit(solution)/shard_map/ppermute | solution.py:346
  61.8 0.0 collective-permute-done.left_ref
  61.8 0.0 copy-start.10
  61.8 2.9 %collective-permute-done.1.right_ref = bf16[48,256]{1,0:T(8,128)(2,1)S(1)} collective-permute-done((bf16[48,256]{1,0:T(8,128)(2,1)}, bf16[48,256]{1,0:T(8,128)(2,1)S(1)}, u32[]{:S(2)}, u32[]{:S(2)}) %collective-permute-start.1) | collective-permute-done | bytes 24608 | tf_op jit(solution)/shard_map/ppermute | solution.py:346
  64.8 0.0 copy-done.10
  64.8 0.0 copy-start.12
  64.8 0.6 copy-done.12
  65.4 1.4 %lines.1 = (bf16[48,256]{1,0:T(8,128)(2,1)}, bf16[48,256]{1,0:T(8,128)(2,1)}) custom-call(bf16[48,32,256]{2,1,0:T(8,128)(2,1)} %v_ref.1, bf16[48,32,256]{2,1,0:T(8,128)(2,1)} %v_ref.1, bf16[48,256]{1,0:T(8,128)(2,1)} %copy-done.10, bf16[48,256]{1,0:T(8,128)(2,1)} %copy-done.12), custom_call_target="tpu_custom_call" | custom-call | tf_op jit(solution)/shard_map/lines/pallas_call | solution.py:405
  66.8 0.0 copy-start.9
  66.8 3.6 %collective-permute-start.2 = (bf16[48,256]{1,0:T(8,128)(2,1)}, bf16[48,256]{1,0:T(8,128)(2,1)S(1)}, u32[]{:S(2)}, u32[]{:S(2)}) collective-permute-start(bf16[48,256]{1,0:T(8,128)(2,1)} %get-tuple-element.27), channel_id=1, source_target_pairs={{0,64},{64,128},{128,192},{1,65},{65,129},{129,193},{2,66},{66,130... | collective-permute-start | bytes 73736 | tf_op jit(solution)/shard_map/ppermute | solution.py:346
  70.4 2.4 %collective-permute-start.3 = (bf16[48,256]{1,0:T(8,128)(2,1)}, bf16[48,256]{1,0:T(8,128)(2,1)S(1)}, u32[]{:S(2)}, u32[]{:S(2)}) collective-permute-start(bf16[48,256]{1,0:T(8,128)(2,1)} %get-tuple-element.28), channel_id=1, source_target_pairs={{64,0},{128,64},{192,128},{65,1},{129,65},{193,129},{66,2},{130,66... | collective-permute-start | bytes 73736 | tf_op jit(solution)/shard_map/ppermute | solution.py:346
  72.7 0.1 collective-permute-done.2.above_ref
  72.8 3.5 %collective-permute-done.3.below_ref = bf16[48,256]{1,0:T(8,128)(2,1)S(1)} collective-permute-done((bf16[48,256]{1,0:T(8,128)(2,1)}, bf16[48,256]{1,0:T(8,128)(2,1)S(1)}, u32[]{:S(2)}, u32[]{:S(2)}) %collective-permute-start.3) | collective-permute-done | bytes 24608 | tf_op jit(solution)/shard_map/ppermute | solution.py:346
  76.3 0.0 copy-done.1
  76.3 0.0 copy-done.14
  76.3 0.0 copy-start.11
  76.3 0.7 copy-done.11
  77.0 0.0 copy-start.13
  77.1 0.7 copy-done.13
  77.8 1.3 %conv.1.conv_ref = f32[1536,256]{1,0:T(8,128)S(1)} custom-call(bf16[48,32,256]{2,1,0:T(8,128)(2,1)S(1)} %copy-done.1, bf16[48,256]{1,0:T(8,128)(2,1)S(1)} %copy-done.11, bf16[48,256]{1,0:T(8,128)(2,1)S(1)} %copy-done.13, bf16[48,256]{1,0:T(8,128)(2,1)S(1)} %collective-permute-done.2.above_ref, bf16[48,256]{1,0:T(8,128)(2,1)S(1)} %collective-permute-done.3.below_ref, ...), custom_call_target="tpu_custom_call" | custom-call | bytes 8388608 | tf_op jit(solution)/shard_map/conv/pallas_call | solution.py:420
  79.1 0.0 copy-done.9
  79.1 4.5 %probabilities.1 = (bf16[1536,1024]{1,0:T(8,128)(2,1)S(1)}, f32[1536,256]{1,0:T(8,128)S(1)}) custom-call(f32[512,128]{1,0:T(8,128)S(1)} %bitcast.12, bf16[1536,256]{1,0:T(8,128)(2,1)S(1)} %copy-done.9), custom_call_target="tpu_custom_call" | custom-call | bytes 20971520 | tf_op jit(solution)/shard_map/probabilities/pallas_call | solution.py:380
  83.6 0.0 copy-start.2
  83.6 1.6 %copy-done.2 = bf16[1536,1024]{1,0:T(8,128)(2,1)} copy-done((bf16[1536,1024]{1,0:T(8,128)(2,1)}, bf16[1536,1024]{1,0:T(8,128)(2,1)S(1)}, u32[]{:S(2)}) %copy-start.2) | copy-done | bytes 3145752
  85.3 0.0 copy-start.4
  85.3 1.2 %copy-done.4 = f32[1536,256]{1,0:T(8,128)} copy-done((f32[1536,256]{1,0:T(8,128)}, f32[1536,256]{1,0:T(8,128)S(1)}, u32[]{:S(2)}) %copy-start.4) | copy-done | bytes 1572888
  86.4 0.0 all-to-all-done.2
  86.4 0.0 copy-start.3
  86.4 1.9 %copy-done.3 = bf16[1536,1024]{1,0:T(8,128)(2,1)S(1)} copy-done((bf16[1536,1024]{1,0:T(8,128)(2,1)S(1)}, bf16[1536,1024]{1,0:T(8,128)(2,1)}, u32[]{:S(2)}) %copy-start.3) | copy-done | bytes 3145752
  88.3 0.0 copy-start.5
  88.3 1.4 %copy-done.5 = f32[1536,256]{1,0:T(8,128)S(1)} copy-done((f32[1536,256]{1,0:T(8,128)S(1)}, f32[1536,256]{1,0:T(8,128)}, u32[]{:S(2)}) %copy-start.5) | copy-done | bytes 1572888
  89.7 0.0 copy-start.15
  89.7 0.0 copy-start.16
  89.7 1.2 %attend.1 = (f32[1536,256]{1,0:T(8,128)S(1)}, f32[24,128]{1,0:T(8,128)S(1)}) custom-call(bf16[1024,128]{1,0:T(8,128)(2,1)S(1)} %bitcast.13, bf16[1536,1024]{1,0:T(8,128)(2,1)S(1)} %copy-done.3, f32[1536,256]{1,0:T(8,128)S(1)} %copy-done.5, f32[1536,256]{1,0:T(8,128)S(1)} %conv.1.conv_ref), custom_call_target="tpu_custom_call" | custom-call | bytes 8388608 | tf_op jit(solution)/shard_map/attend/pallas_call | solution.py:429
  90.9 2.8 %collective-permute-start.6 = (f32[24,128]{1,0:T(8,128)S(1)}, f32[24,128]{1,0:T(8,128)S(1)}, u32[]{:S(2)}, u32[]{:S(2)}) collective-permute-start(f32[24,128]{1,0:T(8,128)S(1)} %get-tuple-element.29.s0_ref), channel_id=1, source_target_pairs={{0,3},{1,0},{2,1},{3,2},{4,7},{5,4},{6,5},{7,6},{8,11},{9,8},{10,9... | collective-permute-start | bytes 36872 | tf_op jit(solution)/shard_map/ppermute | solution.py:438
  93.7 0.8 collective-permute-start.5
  94.6 0.9 collective-permute-start.4
  95.4 0.0 collective-permute-done.6.s3_ref
  95.4 3.5 %collective-permute-done.5.s2_ref = f32[24,128]{1,0:T(8,128)S(1)} collective-permute-done((f32[24,128]{1,0:T(8,128)S(1)}, f32[24,128]{1,0:T(8,128)S(1)}, u32[]{:S(2)}, u32[]{:S(2)}) %collective-permute-start.5) | collective-permute-done | bytes 12320 | tf_op jit(solution)/shard_map/ppermute | solution.py:438
  98.9 0.5 collective-permute-done.4.s1_ref
  99.5 0.0 copy-done.15
  99.5 0.0 copy-done.16
  99.5 1.4 %norm.1 = bf16[1536,256]{1,0:T(8,128)(2,1)} custom-call(f32[24,128]{1,0:T(8,128)S(1)} %get-tuple-element.29.s0_ref, f32[24,128]{1,0:T(8,128)S(1)} %collective-permute-done.4.s1_ref, f32[24,128]{1,0:T(8,128)S(1)} %collective-permute-done.5.s2_ref, f32[24,128]{1,0:T(8,128)S(1)} %collective-permute-done.6.s3_ref, f32[1536,256]{1,0:T(8,128)S(1)} %get-tuple-element.30.sum_ref, ...), custom_call_target="tpu_custom_call" | custom-call | bytes 4194304 | tf_op jit(solution)/shard_map/norm/pallas_call | solution.py:441
  (2 shorter events, 0.0 us)
Async XLA Ops:
  0.0 16.5 %copy-start.6 = (bf16[48,32,256]{2,1,0:T(8,128)(2,1)S(1)}, bf16[48,32,256]{2,1,0:T(8,128)(2,1)}, u32[]{:S(2)}) copy-start(bf16[48,32,256]{2,1,0:T(8,128)(2,1)} %param.8) | copy-start | bytes 2359300
  0.9 1.1 %copy-start.7 = (bf16[48,32,256]{2,1,0:T(8,128)(2,1)S(1)}, bf16[48,32,256]{2,1,0:T(8,128)(2,1)}, u32[]{:S(2)}) copy-start(bf16[48,32,256]{2,1,0:T(8,128)(2,1)} %param.7) | copy-start | bytes 2359300
  2.1 26.0 %copy-start = (bf16[48,32,256]{2,1,0:T(8,128)(2,1)S(1)}, bf16[48,32,256]{2,1,0:T(8,128)(2,1)}, u32[]{:S(2)}) copy-start(bf16[48,32,256]{2,1,0:T(8,128)(2,1)} %v_ref.1) | copy-start | bytes 2359300
  3.5 0.9 copy-start.8
  4.4 23.7 %all-to-all-start = ((f32[64,8,128]{2,1,0:T(8,128)}), f32[64,8,128]{2,1,0:T(8,128)S(1)}, u32[]{:S(2)}, u32[]{:S(2)}) async-start(f32[64,8,128]{2,1,0:T(8,128)} %get-tuple-element.18), calls=%async_computation | async-start | bytes 524288 | tf_op jit(solution)/shard_map/all_to_all | solution.py:340
  50.1 36.4 %all-to-all-start.2 = ((bf16[64,16,128]{2,1,0:T(8,128)(2,1)}), bf16[64,16,128]{2,1,0:T(8,128)(2,1)S(1)}, u32[]{:S(2)}, u32[]{:S(2)}) async-start(bf16[64,16,128]{2,1,0:T(8,128)(2,1)} %merge.1), calls=%async_computation.2 | async-start | bytes 524288 | tf_op jit(solution)/shard_map/all_to_all | solution.py:340
  56.6 19.7 %copy-start.1 = (bf16[48,32,256]{2,1,0:T(8,128)(2,1)S(1)}, bf16[48,32,256]{2,1,0:T(8,128)(2,1)}, u32[]{:S(2)}) copy-start(bf16[48,32,256]{2,1,0:T(8,128)(2,1)} %v_ref.1) | copy-start | bytes 2359300
  56.6 19.7 %copy-start.14 = (f32[9,256]{1,0:T(8,128)S(1)}, f32[9,256]{1,0:T(8,128)}, u32[]{:S(2)}) copy-start(f32[9,256]{1,0:T(8,128)} %w_ref.1) | copy-start | bytes 27652
  58.5 3.4 %collective-permute-start = (bf16[48,256]{1,0:T(8,128)(2,1)}, bf16[48,256]{1,0:T(8,128)(2,1)S(1)}, u32[]{:S(2)}, u32[]{:S(2)}) collective-permute-start(bf16[48,256]{1,0:T(8,128)(2,1)} %get-tuple-element.25), channel_id=1, source_target_pairs={{0,4},{4,8},{8,12},{12,16},{16,20},{20,24},{24,28},{28,32},{32,36}... | collective-permute-start | bytes 73736 | tf_op jit(solution)/shard_map/ppermute | solution.py:346
  60.5 4.2 %collective-permute-start.1 = (bf16[48,256]{1,0:T(8,128)(2,1)}, bf16[48,256]{1,0:T(8,128)(2,1)S(1)}, u32[]{:S(2)}, u32[]{:S(2)}) collective-permute-start(bf16[48,256]{1,0:T(8,128)(2,1)} %get-tuple-element.26), channel_id=1, source_target_pairs={{4,0},{8,4},{12,8},{16,12},{20,16},{24,20},{28,24},{32,28},{36,32}... | collective-permute-start | bytes 73736 | tf_op jit(solution)/shard_map/ppermute | solution.py:346
  61.8 2.9 %copy-start.10 = (bf16[48,256]{1,0:T(8,128)(2,1)}, bf16[48,256]{1,0:T(8,128)(2,1)S(1)}, u32[]{:S(2)}) copy-start(bf16[48,256]{1,0:T(8,128)(2,1)S(1)} %collective-permute-done.left_ref) | copy-start | bytes 73732
  64.8 0.6 copy-start.12
  66.8 12.3 %copy-start.9 = (bf16[1536,256]{1,0:T(8,128)(2,1)S(1)}, bf16[1536,256]{1,0:T(8,128)(2,1)}, u32[]{:S(2)}) copy-start(bf16[1536,256]{1,0:T(8,128)(2,1)} %copy-done.8) | copy-start | bytes 2359300
  66.8 6.0 %collective-permute-start.2 = (bf16[48,256]{1,0:T(8,128)(2,1)}, bf16[48,256]{1,0:T(8,128)(2,1)S(1)}, u32[]{:S(2)}, u32[]{:S(2)}) collective-permute-start(bf16[48,256]{1,0:T(8,128)(2,1)} %get-tuple-element.27), channel_id=1, source_target_pairs={{0,64},{64,128},{128,192},{1,65},{65,129},{129,193},{2,66},{66,130... | collective-permute-start | bytes 73736 | tf_op jit(solution)/shard_map/ppermute | solution.py:346
  70.4 5.9 %collective-permute-start.3 = (bf16[48,256]{1,0:T(8,128)(2,1)}, bf16[48,256]{1,0:T(8,128)(2,1)S(1)}, u32[]{:S(2)}, u32[]{:S(2)}) collective-permute-start(bf16[48,256]{1,0:T(8,128)(2,1)} %get-tuple-element.28), channel_id=1, source_target_pairs={{64,0},{128,64},{192,128},{65,1},{129,65},{193,129},{66,2},{130,66... | collective-permute-start | bytes 73736 | tf_op jit(solution)/shard_map/ppermute | solution.py:346
  76.3 0.7 copy-start.11
  77.0 0.7 copy-start.13
  83.6 1.6 %copy-start.2 = (bf16[1536,1024]{1,0:T(8,128)(2,1)}, bf16[1536,1024]{1,0:T(8,128)(2,1)S(1)}, u32[]{:S(2)}) copy-start(bf16[1536,1024]{1,0:T(8,128)(2,1)S(1)} %get-tuple-element.23.prob_ref) | copy-start | bytes 9437188
  85.3 1.2 %copy-start.4 = (f32[1536,256]{1,0:T(8,128)}, f32[1536,256]{1,0:T(8,128)S(1)}, u32[]{:S(2)}) copy-start(f32[1536,256]{1,0:T(8,128)S(1)} %get-tuple-element.24.recip_ref) | copy-start | bytes 4718596
  86.4 1.9 %copy-start.3 = (bf16[1536,1024]{1,0:T(8,128)(2,1)S(1)}, bf16[1536,1024]{1,0:T(8,128)(2,1)}, u32[]{:S(2)}) copy-start(bf16[1536,1024]{1,0:T(8,128)(2,1)} %copy-done.2) | copy-start | bytes 9437188
  88.3 1.4 %copy-start.5 = (f32[1536,256]{1,0:T(8,128)S(1)}, f32[1536,256]{1,0:T(8,128)}, u32[]{:S(2)}) copy-start(f32[1536,256]{1,0:T(8,128)} %copy-done.4) | copy-start | bytes 4718596
  89.7 9.8 %copy-start.15 = (f32[256]{0:T(256)S(1)}, f32[256]{0:T(256)}, u32[]{:S(2)}) copy-start(f32[256]{0:T(256)} %param.12) | copy-start | bytes 3076
  89.7 9.8 %copy-start.16 = (f32[256]{0:T(256)S(1)}, f32[256]{0:T(256)}, u32[]{:S(2)}) copy-start(f32[256]{0:T(256)} %param.13) | copy-start | bytes 3076
  90.9 4.5 %collective-permute-start.6 = (f32[24,128]{1,0:T(8,128)S(1)}, f32[24,128]{1,0:T(8,128)S(1)}, u32[]{:S(2)}, u32[]{:S(2)}) collective-permute-start(f32[24,128]{1,0:T(8,128)S(1)} %get-tuple-element.29.s0_ref), channel_id=1, source_target_pairs={{0,3},{1,0},{2,1},{3,2},{4,7},{5,4},{6,5},{7,6},{8,11},{9,8},{10,9... | collective-permute-start | bytes 36872 | tf_op jit(solution)/shard_map/ppermute | solution.py:438
  93.7 5.2 %collective-permute-start.5 = (f32[24,128]{1,0:T(8,128)S(1)}, f32[24,128]{1,0:T(8,128)S(1)}, u32[]{:S(2)}, u32[]{:S(2)}) collective-permute-start(f32[24,128]{1,0:T(8,128)S(1)} %get-tuple-element.29.s0_ref), channel_id=1, source_target_pairs={{0,2},{1,3},{2,0},{3,1},{4,6},{5,7},{6,4},{7,5},{8,10},{9,11},{10,... | collective-permute-start | bytes 36872 | tf_op jit(solution)/shard_map/ppermute | solution.py:438
  94.6 4.9 %collective-permute-start.4 = (f32[24,128]{1,0:T(8,128)S(1)}, f32[24,128]{1,0:T(8,128)S(1)}, u32[]{:S(2)}, u32[]{:S(2)}) collective-permute-start(f32[24,128]{1,0:T(8,128)S(1)} %get-tuple-element.29.s0_ref), channel_id=1, source_target_pairs={{0,1},{1,2},{2,3},{3,0},{4,5},{5,6},{6,7},{7,4},{8,9},{9,10},{10,1... | collective-permute-start | bytes 36872 | tf_op jit(solution)/shard_map/ppermute | solution.py:438

commit v2 on v1

--- a/solution.py
+++ b/solution.py
@@ -35,7 +35,7 @@
         in_specs=[VMEM_SPEC] * n_in,
         out_specs=outs,
         scratch_shapes=list(scratch),
-        compiler_params=pltpu.CompilerParams(vmem_limit_bytes=32 * 1024 * 1024),
+        compiler_params=pltpu.CompilerParams(vmem_limit_bytes=12 * 1024 * 1024),
         cost_estimate=pl.CostEstimate(flops=flops, bytes_accessed=nbytes, transcendentals=0),
         name=name,
     )
@@ -77,14 +77,23 @@
     return cosine, sine
 
 
-def query_kernel(pos_ref, freq_ref, q_ref, tq_ref, agents_ref, tab_r_ref, tab_c_ref, turn_ref):
+def query_kernel(
+    pos_ref, freq_ref, q_ref, tq_ref, agents_ref, tab_r_ref, tab_c_ref, turn_ref, held_ref, sems
+):
+    step = N // AGR
+    copies = []
+    for cell in range(AGR):
+        part = pl.ds(cell * step, step)
+        copy = pltpu.make_async_copy(q_ref.at[part, :], held_ref.at[part, :], sems.at[cell])
+        copy.start()
+        copies.append(copy)
     freq = freq_ref[...]
-    row_pos = pos_ref[0][:, 0:1].astype(f32)
-    col_line = pos_ref[1][0:1, :].astype(f32)
-    eye = lax.broadcasted_iota(jnp.int32, (TC, TC), 0) == lax.broadcasted_iota(
-        jnp.int32, (TC, TC), 1
-    )
-    col_pos = jnp.sum(jnp.where(eye, jnp.broadcast_to(col_line, (TC, TC)), 0.0), 1, keepdims=True)
+    row_line = pos_ref[0][0:1, :].astype(f32)
+    col_pos = pos_ref[1][:, 0:1].astype(f32)
+    eye = lax.broadcasted_iota(jnp.int32, (TR, TR), 0) == lax.broadcasted_iota(
+        jnp.int32, (TR, TR), 1
+    )
+    row_pos = jnp.sum(jnp.where(eye, jnp.broadcast_to(row_line, (TR, TR)), 0.0), 1, keepdims=True)
     angles = jnp.concatenate([row_pos * freq[0:1, :], col_pos * freq[1:2, :]], axis=0)
     sines, cosines = sin_cos(angles)
     sines = jnp.concatenate([sines, sines], axis=1)
@@ -95,21 +104,23 @@
     tab_c_ref[1] = sines[TR:]
     matrix = turn_matrix()
     turn_ref[...] = matrix
-    step = N // AGR
     means = []
     for cell in range(AGR):
         cosine, sine = cell_tables(
             cosines[:TR], sines[:TR], cosines[TR:], sines[TR:], cell * (TR // AGR), TR // AGR
         )
-        rotated = turned(q_ref[pl.ds(cell * step, step), :], matrix, cosine, sine)
+        copies[cell].wait()
+        rotated = turned(held_ref[pl.ds(cell * step, step), :], matrix, cosine, sine)
         tq_ref[pl.ds(cell * step, step), :] = rotated
         mean = jnp.sum(rotated.astype(f32), 0, keepdims=True) / step
         means.append(mean.astype(bf16).astype(f32))
     packed = jnp.concatenate([m[:, :128] for m in means] + [m[:, 128:] for m in means], axis=0)
-    agents_ref[...] = jnp.broadcast_to(packed[None], (TILES, 8, 128))
-
-
-def key_kernel(tab_r_ref, tab_c_ref, turn_ref, k_ref, tk_ref):
+    agents_ref[...] = jnp.broadcast_to(packed.astype(bf16)[None], (TILES, 8, 128))
+
+
+def key_kernel(tab_r_ref, tab_c_ref, turn_ref, k_ref, v_ref, tk_ref, first_ref, last_ref):
+    first_ref[...] = v_ref[:, 0, :]
+    last_ref[...] = v_ref[:, TC - 1, :]
     matrix = turn_ref[...]
     step = N // AGR
     for cell in range(AGR):
@@ -121,11 +132,12 @@
         )
 
 
-def agent_pairs(agents_ref, scale):
+def agent_pairs(agents_ref, wide_ref, scale):
+    wide_ref[...] = agents_ref[...].astype(f32).reshape(TILES * 8, 128) * scale
     pairs = []
     for pair in range(2):
-        parts = [agents_ref[pl.ds(4 * pair + k, TILES, stride=8), :] for k in range(AGR)]
-        pairs.append((jnp.concatenate(parts, axis=0) * scale).astype(bf16))
+        parts = [wide_ref[pl.ds(4 * pair + k, TILES, stride=8), :] for k in range(AGR)]
+        pairs.append(jnp.concatenate(parts, axis=0).astype(bf16))
     return pairs
 
 
@@ -133,8 +145,8 @@
     return (lanes(dims) // HD) == parity
 
 
-def partial_kernel(agents_ref, tk_ref, v_ref, out_ref, score_ref):
-    pairs = agent_pairs(agents_ref, 1.0 / math.sqrt(HD))
+def partial_kernel(agents_ref, tk_ref, v_ref, out_ref, score_ref, wide_ref):
+    pairs = agent_pairs(agents_ref, wide_ref, 1.0 / math.sqrt(HD))
     chunk = 512
     for head in range(LOCAL_HEADS):
         pair, parity = head // 2, head % 2
@@ -178,28 +190,26 @@
                 jnp.where(lane == HD + 1, second, jnp.where(lane == HD + 2, third, 0.0)),
             ),
         )
-        out_ref[pl.ds(head * AGENTS, AGENTS), :] = packed.astype(bf16)
+        groups = packed.reshape(2, ROWS, 8, 128)
+        out_ref[pl.ds(head * ROWS, ROWS)] = jnp.concatenate([groups[0], groups[1]], 1).astype(bf16)
 
 
 def merge_kernel(parts_ref, out_ref):
     source = lax.broadcasted_iota(jnp.int32, (128, 128), 0)
     picker = jnp.where((source >= HD) & (source < HD + 3), 1.0, 0.0).astype(bf16)
-    parts = parts_ref[...]
+    parts = parts_ref[...].reshape(TILES * ROWS, 128)
     logs = jnp.dot(parts, picker, preferred_element_type=f32).reshape(TILES, ROWS, 128)
     values = parts.astype(f32).reshape(TILES, ROWS, 128)
     peak = jnp.max(logs, 0)
     weights = jnp.exp(logs - peak[None])
     merged = jnp.sum(weights * values, 0) / jnp.sum(weights, 0)
-    merged = jnp.where(lanes(merged.shape) < HD, merged, 0.0)
-    merged = (merged + pltpu.roll(merged, HD, 1)).astype(bf16)
-    out_ref[...] = jnp.broadcast_to(merged[None], (TILES, ROWS, 128))
-
-
-def probability_kernel(agents_ref, tq_ref, prob_ref, recip_ref):
-    pairs = agent_pairs(agents_ref, 1.0 / math.sqrt(HD))
-    target = [
-        jnp.where(half_mask((AGENTS, 128), parity), 1.0, 0.0).astype(bf16) for parity in range(2)
-    ]
+    merged = jnp.where(lanes((8, 128)) < HD, merged[:8], pltpu.roll(merged[8:], HD, 1))
+    out_ref[...] = jnp.broadcast_to(merged.astype(bf16)[None], (TILES, 8, 128))
+
+
+def probability_kernel(agents_ref, tq_ref, prob_ref, wide_ref):
+    pairs = agent_pairs(agents_ref, wide_ref, 1.0 / math.sqrt(HD))
+    ones = jnp.ones((AGENTS, 128), bf16)
     owns = []
     for head in range(LOCAL_HEADS):
         own = pairs[head // 2]
@@ -208,27 +218,21 @@
 
     def body(c, carry):
         rows = pl.ds(pl.multiple_of(c * chunk, chunk), chunk)
-        for pair in range(2):
-            cols = pl.ds(pair * 128, 128)
-            queries = tq_ref[rows, cols]
-            total = jnp.zeros((chunk, 128), f32)
-            for parity in range(2):
-                head = 2 * pair + parity
-                scores = lax.dot_general(
-                    queries, owns[head], (((1,), (1,)), ((), ())), preferred_element_type=f32
-                )
-                weights = jnp.exp(scores - jnp.max(scores, 1, keepdims=True)).astype(bf16)
-                prob_ref[rows, pl.ds(head * AGENTS, AGENTS)] = weights
-                total = total + jnp.dot(weights, target[parity], preferred_element_type=f32)
-            recip_ref[rows, cols] = 1.0 / total
+        for head in range(LOCAL_HEADS):
+            scores = lax.dot_general(
+                tq_ref[rows, pl.ds(head // 2 * 128, 128)],
+                owns[head],
+                (((1,), (1,)), ((), ())),
+                preferred_element_type=f32,
+            )
+            weights = jnp.exp(scores - jnp.max(scores, 1, keepdims=True))
+            total = jnp.dot(weights.astype(bf16), ones, preferred_element_type=f32)
+            scale = 1.0 / total
+            scale = jnp.concatenate([scale, scale], axis=1)
+            prob_ref[rows, pl.ds(head * AGENTS, AGENTS)] = (weights * scale).astype(bf16)
         return carry
 
     lax.fori_loop(0, N // chunk, body, 0)
-
-
-def edge_kernel(left_ref, right_ref, first_ref, last_ref):
-    first_ref[...] = left_ref[:, 0, :]
-    last_ref[...] = right_ref[:, 15, :]
 
 
 def line_kernel(v_top_ref, v_bottom_ref, left_ref, right_ref, up_ref, down_ref):
@@ -279,14 +283,17 @@
         out_ref[pl.ds((TR - 1) * TC, TC), cols] = a + t[2]
 
 
-def attend_kernel(av_ref, prob_ref, recip_ref, conv_ref, sum_ref, stat_ref):
+def attend_kernel(av_ref, prob_ref, conv_ref, sum_ref, stat_ref):
     halves = []
     for pair in range(2):
         pieces = []
         for parity in range(2):
-            part = av_ref[pl.ds((2 * pair + parity) * AGENTS, AGENTS), :]
-            pieces.append(jnp.where(half_mask(part.shape, parity), part, jnp.zeros_like(part)))
-        halves.append(jnp.concatenate(pieces, axis=0))
+            part = av_ref[pl.ds((2 * pair + parity) * ROWS, ROWS)].astype(f32).reshape(128, 128)
+            other = pltpu.roll(part, HD, 1)
+            own = half_mask(part.shape, parity)
+            for piece in (part, other) if parity == 0 else (other, part):
+                pieces.append(jnp.where(own, piece, 0.0))
+        halves.append(jnp.concatenate(pieces, axis=0).astype(bf16))
     eye = lax.broadcasted_iota(jnp.int32, (128, 128), 0) == lanes((128, 128))
 
     for b in range(BLOCKS):
@@ -299,7 +306,7 @@
                 halves[pair],
                 preferred_element_type=f32,
             )
-            x = attended * recip_ref[rows, cols] + conv_ref[rows, cols]
+            x = attended + conv_ref[rows, cols]
             sum_ref[rows, cols] = x
             xs.append(x)
         mean = jnp.sum(xs[0] + xs[1], 1, keepdims=True) * (1.0 / CH)
@@ -346,62 +353,52 @@
     return lax.ppermute(x, axis, pairs)
 
 
+def after(x, *others):
+    return lax.optimization_barrier((x, *others))[0]
+
+
 def shards(queries, keys, values, positions, conv_weight, norm_gain, norm_bias):
     q = queries.reshape(N, CH)
     k = keys.reshape(N, CH)
     v = values.reshape(N, CH)
     mb = 1 << 20
-    tq, packed, tab_r, tab_c, turn = call(
+    wide = pltpu.VMEM((TILES * 8, 128), f32)
+    tq, packed, tab_r, tab_c, turn = pl.pallas_call(
         query_kernel,
-        (
+        out_shape=(
             shape((N, CH), bf16),
-            shape((TILES, 8, 128), f32),
+            shape((TILES, 8, 128), bf16),
             shape((2, TR, CH), f32),
             shape((2, TC, CH), f32),
             shape((CH, CH), bf16),
         ),
-        3,
-        nbytes=8 * mb,
+        in_specs=[VMEM_SPEC, VMEM_SPEC, pl.BlockSpec(memory_space=pltpu.HBM)],
+        out_specs=(VMEM_SPEC,) * 5,
+        scratch_shapes=[pltpu.VMEM((N, CH), bf16), pltpu.SemaphoreType.DMA((AGR,))],
+        compiler_params=pltpu.CompilerParams(vmem_limit_bytes=12 * 1024 * 1024),
+        cost_estimate=pl.CostEstimate(flops=0, bytes_accessed=8 * mb, transcendentals=0),
         name="turn_queries",
-    )(positions, frequencies(), q)
-    agents = spread(packed).reshape(TILES * 8, 128)
-    tk = call(key_kernel, shape((N, CH), bf16), 4, nbytes=6 * mb, name="turn_keys")(
-        tab_r, tab_c, turn, k
-    )
+    )(jnp.swapaxes(positions, 1, 2), frequencies(), q)
+    agents = spread(packed)
+    tk, first, last = call(
+        key_kernel,
+        (shape((N, CH), bf16), shape((TR, CH), bf16), shape((TR, CH), bf16)),
+        5,
+        nbytes=4 * mb,
+        name="turn_keys",
+    )(tab_r, tab_c, turn, k, values)
+    left = shift(last, "col", 1)
+    right = shift(first, "col", -1)
+    agents = after(agents, left, right)
     parts = call(
         partial_kernel,
-        shape((LOCAL_HEADS * AGENTS, 128), bf16),
+        shape((TILES, ROWS, 128), bf16),
         3,
-        scratch=[pltpu.VMEM((AGENTS, N), f32)],
-        nbytes=20 * mb,
+        scratch=[pltpu.VMEM((AGENTS, N), f32), wide],
+        nbytes=10 * mb,
         name="partials",
     )(agents, tk, v)
-    received = spread(parts.reshape(TILES, ROWS, 128)).reshape(TILES * ROWS, 128)
-    prob, recip = call(
-        probability_kernel,
-        (shape((N, LOCAL_HEADS * AGENTS), bf16), shape((N, CH), f32)),
-        2,
-        nbytes=20 * mb,
-        name="probabilities",
-    )(agents, tq)
-    merged = call(merge_kernel, shape((TILES, ROWS, 128), bf16), 1, nbytes=2 * mb, name="merge")(
-        received
-    )
-    agent_values = spread(merged).reshape(TILES * ROWS, 128)
-
-    first, last = pl.pallas_call(
-        edge_kernel,
-        out_shape=(shape((TR, CH), bf16),) * 2,
-        grid=(1,),
-        in_specs=[
-            pl.BlockSpec((TR, 16, CH), lambda i: (0, 0, 0)),
-            pl.BlockSpec((TR, 16, CH), lambda i: (0, 1, 0)),
-        ],
-        out_specs=(pl.BlockSpec((TR, CH), lambda i: (0, 0)),) * 2,
-        name="edges",
-    )(values, values)
-    left = shift(last, "col", 1)
-    right = shift(first, "col", -1)
+    received = spread(parts)
     up, down = pl.pallas_call(
         line_kernel,
         out_shape=(shape((TC + 16, CH), bf16),) * 2,
@@ -417,22 +414,34 @@
     )(values, values, left, right)
     above = shift(down, "row", 1)
     below = shift(up, "row", -1)
+    received = after(received, above, below)
+    merged = call(merge_kernel, shape((TILES, 8, 128), bf16), 1, nbytes=2 * mb, name="merge")(
+        received
+    )
+    agent_values = spread(merged)
+    prob = call(
+        probability_kernel,
+        shape((N, LOCAL_HEADS * AGENTS), bf16),
+        2,
+        scratch=[wide],
+        nbytes=15 * mb,
+        name="probabilities",
+    )(agents, tq)
     convolved = call(
         conv_kernel,
         shape((N, CH), f32),
         6,
         scratch=[pltpu.VMEM((TR, CH), f32), pltpu.VMEM((TR, CH), f32)],
-        nbytes=8 * mb,
+        nbytes=4 * mb,
         name="conv",
     )(values, left, right, above, below, conv_weight)
-
     summed, stats = call(
         attend_kernel,
         (shape((N, CH), f32), shape((2 * BLOCKS, 128), f32)),
-        4,
-        nbytes=8 * mb,
+        3,
+        nbytes=4 * mb,
         name="attend",
-    )(agent_values, prob, recip, convolved)
+    )(agent_values, prob, convolved)
     heads = lax.axis_size("head")
     others = [
         lax.ppermute(stats, "head", [(i, (i + d) % heads) for i in range(heads)])

time: 103 us -> 88 us (0.85); the launches traced: 101 us -> 87.3 us
  blocking collectives: 17.8 us -> 0 us
  starting transfers between devices: 32.4 us -> 46.5 us
  waiting for transfers between devices: 21.6 us -> 12.6 us
  local copies, waits for them, and re-layouts: 11.1 us -> 9.16 us
    all_to_all x1 -> x0, blocking collectives: 17.8 us -> none  [spread(): return lax.all_to_all(x, ('row', 'col'), 0, 0)]
    all_to_all x2 -> x3, starting transfers between devices: 18.6 us -> 32.8 us  [spread(): return lax.all_to_all(x, ('row', 'col'), 0, 0)]
    all_to_all x2 -> x3, waiting for transfers between devices: 11 us -> 2.28 us  [spread(): return lax.all_to_all(x, ('row', 'col'), 0, 0)]
    unnamed x35 -> x32, local copies, waits for them, and re-layouts: 11.1 us -> 9.16 us
    pallas_call x6 -> x5, Pallas kernels: 12.5 us -> 13.5 us  [the longest x1 5.08 us: shards(): call(probability_kernel, shape((N, LOCAL_HEADS * AGENTS), bf16), 2, scrat...]
  transfers between devices with their start and end apart: 9 -> 10, of which waited for: 6 -> 7; matrix products, arithmetic and copies ran while one was open for 0% -> 0% of each run, Pallas kernels for 10% -> 10%
where the time goes in v2:
time: 88 us; the launch traced here: 87.3 us
  starting transfers between devices  46.5 us (53%)
  Pallas kernels  18.8 us (21%)
  waiting for transfers between devices  12.6 us (14%)
  local copies, waits for them, and re-layouts  9.16 us (10%)
    all_to_all x3, starting transfers between devices, spread(): return lax.all_to_all(x, ('row', 'col'), 0, 0)  32.8 us
    ppermute x4, starting transfers between devices, shift(): return lax.ppermute(x, axis, pairs)  9.17 us
    unnamed x32, local copies, waits for them, and re-layouts  9.16 us
    ppermute x4, waiting for transfers between devices, shift(): return lax.ppermute(x, axis, pairs)  6.3 us
    pallas_call x1, Pallas kernels, shards(): call(probability_kernel, shape((N, LOCAL_HEADS * AGENTS), bf16), 2, scrat...  5.08 us
    ppermute x3, starting transfers between devices, shards(): lax.ppermute(stats, 'head', [(i, (i + d) % heads) for i in range(heads)])  4.52 us
    ppermute x3, waiting for transfers between devices, shards(): lax.ppermute(stats, 'head', [(i, (i + d) % heads) for i in range(heads)])  4.02 us
    pallas_call x1, Pallas kernels, shards(): call(partial_kernel, shape((TILES, ROWS, 128), bf16), 3, scratch=[pltpu.V...  3.68 us
  transfers between devices with their start and end apart: 10, of which 7 were waited for; matrix products, arithmetic and copies ran while one was open for 0% of the time, Pallas kernels for 10%

profile of v2, /device:TPU:8, one launch (start us, length us, event | category | flops | bytes accessed | tf_op | source)
XLA Modules:
  0.0 87.3 jit_solution(17029118942946760269)
XLA Ops:
  0.0 0.0 copy-start
  0.0 0.0 copy-start.5
  0.0 1.2 %copy-done.5 = bf16[48,32,256]{2,1,0:T(8,128)(2,1)S(1)} copy-done((bf16[48,32,256]{2,1,0:T(8,128)(2,1)S(1)}, bf16[48,32,256]{2,1,0:T(8,128)(2,1)}, u32[]{:S(2)}) %copy-start.5) | copy-done | bytes 786456
  1.2 0.0 copy-start.12
  1.2 0.8 copy-done.12
  2.0 3.0 %turn_queries.1 = (bf16[1536,256]{1,0:T(8,128)(2,1)S(1)}, bf16[64,8,128]{2,1,0:T(8,128)(2,1)}, f32[2,48,256]{2,1,0:T(8,128)S(1)}, f32[2,32,256]{2,1,0:T(8,128)S(1)}, bf16[256,256]{1,0:T(8,128)(2,1)S(1)}) custom-call(s32[2,32,48]{2,1,0:T(8,128)S(1)} %bitcast.10, f32[2,128]{1,0:T(2,128)S(1)} %pad_maximum_fusion.freq_ref, bf16[1536,256]{1,0:T(8,128)(2,1)S(1)} %bitcast.9), custom_call_target="tpu_custom_call" | custom-call | bytes 8388608 | tf_op jit(solution)/shard_map/turn_queries/pallas_call | solution.py:366
  5.0 0.0 copy-start.6
  5.1 0.9 copy-done.6
  5.9 12.1 %all-to-all-start = ((bf16[64,8,128]{2,1,0:T(8,128)(2,1)}), bf16[64,8,128]{2,1,0:T(8,128)(2,1)S(1)}, u32[]{:S(2)}, u32[]{:S(2)}) async-start(bf16[64,8,128]{2,1,0:T(8,128)(2,1)} %get-tuple-element.19), calls=%async_computation | async-start | bytes 262144 | tf_op jit(solution)/shard_map/all_to_all | solution.py:347
  18.0 0.0 copy-done
  18.1 0.0 copy-start.4
  18.1 1.1 %copy-done.4 = bf16[48,32,256]{2,1,0:T(8,128)(2,1)S(1)} copy-done((bf16[48,32,256]{2,1,0:T(8,128)(2,1)S(1)}, bf16[48,32,256]{2,1,0:T(8,128)(2,1)}, u32[]{:S(2)}) %copy-start.4) | copy-done | bytes 786456
  19.2 0.6 turn_keys.1
  19.8 2.1 %collective-permute-start = (bf16[48,256]{1,0:T(8,128)(2,1)S(1)}, bf16[48,256]{1,0:T(8,128)(2,1)S(1)}, u32[]{:S(2)}, u32[]{:S(2)}) collective-permute-start(bf16[48,256]{1,0:T(8,128)(2,1)S(1)} %get-tuple-element.23), channel_id=1, source_target_pairs={{0,4},{4,8},{8,12},{12,16},{16,20},{20,24},{24,28},{28,32},{32,36}... | collective-permute-start | bytes 73736 | tf_op jit(solution)/shard_map/ppermute | solution.py:353
  21.8 1.3 %collective-permute-start.1 = (bf16[48,256]{1,0:T(8,128)(2,1)S(1)}, bf16[48,256]{1,0:T(8,128)(2,1)S(1)}, u32[]{:S(2)}, u32[]{:S(2)}) collective-permute-start(bf16[48,256]{1,0:T(8,128)(2,1)S(1)} %get-tuple-element.24), channel_id=1, source_target_pairs={{4,0},{8,4},{12,8},{16,12},{20,16},{24,20},{28,24},{32,28},{36,32}... | collective-permute-start | bytes 73736 | tf_op jit(solution)/shard_map/ppermute | solution.py:353
  23.1 0.0 collective-permute-done.left_ref
  23.1 0.0 copy-start.8
  23.1 2.7 %collective-permute-done.1.right_ref = bf16[48,256]{1,0:T(8,128)(2,1)S(1)} collective-permute-done((bf16[48,256]{1,0:T(8,128)(2,1)S(1)}, bf16[48,256]{1,0:T(8,128)(2,1)S(1)}, u32[]{:S(2)}, u32[]{:S(2)}) %collective-permute-start.1) | collective-permute-done | bytes 24608 | tf_op jit(solution)/shard_map/ppermute | solution.py:353
  25.8 0.0 copy-start.10
  25.8 1.6 %all-to-all-done.agents_ref = bf16[64,8,128]{2,1,0:T(8,128)(2,1)S(1)} async-done(((bf16[64,8,128]{2,1,0:T(8,128)(2,1)}), bf16[64,8,128]{2,1,0:T(8,128)(2,1)S(1)}, u32[]{:S(2)}, u32[]{:S(2)}) %all-to-all-start) | async-done | bytes 131104 | tf_op jit(solution)/shard_map/all_to_all | solution.py:347
  27.4 3.7 %partials.1 = bf16[64,16,128]{2,1,0:T(8,128)(2,1)} custom-call(bf16[64,8,128]{2,1,0:T(8,128)(2,1)S(1)} %all-to-all-done.agents_ref, bf16[1536,256]{1,0:T(8,128)(2,1)S(1)} %get-tuple-element.26.tk_ref, bf16[1536,256]{1,0:T(8,128)(2,1)S(1)} %bitcast.7), custom_call_target="tpu_custom_call" | custom-call | bytes 10485760 | tf_op jit(solution)/shard_map/partials/pallas_call | solution.py:393
  31.1 0.0 copy-start.1
  31.1 0.0 copy-start.13
  31.1 11.3 %all-to-all-start.1 = ((bf16[64,16,128]{2,1,0:T(8,128)(2,1)}), bf16[64,16,128]{2,1,0:T(8,128)(2,1)S(1)}, u32[]{:S(2)}, u32[]{:S(2)}) async-start(bf16[64,16,128]{2,1,0:T(8,128)(2,1)} %partials.1), calls=%async_computation.1 | async-start | bytes 524288 | tf_op jit(solution)/shard_map/all_to_all | solution.py:347
  42.5 0.0 copy-done.8
  42.5 0.0 copy-done.10
  42.5 1.4 %lines.1 = (bf16[48,256]{1,0:T(8,128)(2,1)}, bf16[48,256]{1,0:T(8,128)(2,1)}) custom-call(bf16[48,32,256]{2,1,0:T(8,128)(2,1)} %v_ref.3, bf16[48,32,256]{2,1,0:T(8,128)(2,1)} %v_ref.3, bf16[48,256]{1,0:T(8,128)(2,1)} %copy-done.8, bf16[48,256]{1,0:T(8,128)(2,1)} %copy-done.10), custom_call_target="tpu_custom_call" | custom-call | tf_op jit(solution)/shard_map/lines/pallas_call | solution.py:402
  43.9 3.5 %collective-permute-start.2 = (bf16[48,256]{1,0:T(8,128)(2,1)}, bf16[48,256]{1,0:T(8,128)(2,1)S(1)}, u32[]{:S(2)}, u32[]{:S(2)}) collective-permute-start(bf16[48,256]{1,0:T(8,128)(2,1)} %get-tuple-element.27), channel_id=1, source_target_pairs={{0,64},{64,128},{128,192},{1,65},{65,129},{129,193},{2,66},{66,130... | collective-permute-start | bytes 73736 | tf_op jit(solution)/shard_map/ppermute | solution.py:353
  47.4 2.4 %collective-permute-start.3 = (bf16[48,256]{1,0:T(8,128)(2,1)}, bf16[48,256]{1,0:T(8,128)(2,1)S(1)}, u32[]{:S(2)}, u32[]{:S(2)}) collective-permute-start(bf16[48,256]{1,0:T(8,128)(2,1)} %get-tuple-element.28), channel_id=1, source_target_pairs={{64,0},{128,64},{192,128},{65,1},{129,65},{193,129},{66,2},{130,66... | collective-permute-start | bytes 73736 | tf_op jit(solution)/shard_map/ppermute | solution.py:353
  49.7 0.7 collective-permute-done.2.above_ref
  50.4 2.9 %collective-permute-done.3.below_ref = bf16[48,256]{1,0:T(8,128)(2,1)S(1)} collective-permute-done((bf16[48,256]{1,0:T(8,128)(2,1)}, bf16[48,256]{1,0:T(8,128)(2,1)S(1)}, u32[]{:S(2)}, u32[]{:S(2)}) %collective-permute-start.3) | collective-permute-done | bytes 24608 | tf_op jit(solution)/shard_map/ppermute | solution.py:353
  53.3 0.7 all-to-all-done.1.parts_ref
  54.0 1.1 %merge.1 = bf16[64,8,128]{2,1,0:T(8,128)(2,1)} custom-call(bf16[64,16,128]{2,1,0:T(8,128)(2,1)S(1)} %all-to-all-done.1.parts_ref), custom_call_target="tpu_custom_call" | custom-call | bytes 2097152 | tf_op jit(solution)/shard_map/merge/pallas_call | solution.py:418
  55.1 9.3 %all-to-all-start.2 = ((bf16[64,8,128]{2,1,0:T(8,128)(2,1)}), bf16[64,8,128]{2,1,0:T(8,128)(2,1)S(1)}, u32[]{:S(2)}, u32[]{:S(2)}) async-start(bf16[64,8,128]{2,1,0:T(8,128)(2,1)} %merge.1), calls=%async_computation.2 | async-start | bytes 262144 | tf_op jit(solution)/shard_map/all_to_all | solution.py:347
  64.5 0.0 copy-done.1
  64.5 0.0 copy-done.13
  64.5 0.0 copy-start.9
  64.5 0.7 copy-done.9
  65.2 0.0 copy-start.11
  65.2 0.7 copy-done.11
  66.0 1.3 %conv.1.conv_ref = f32[1536,256]{1,0:T(8,128)S(1)} custom-call(bf16[48,32,256]{2,1,0:T(8,128)(2,1)S(1)} %copy-done.1, bf16[48,256]{1,0:T(8,128)(2,1)S(1)} %copy-done.9, bf16[48,256]{1,0:T(8,128)(2,1)S(1)} %copy-done.11, bf16[48,256]{1,0:T(8,128)(2,1)S(1)} %collective-permute-done.2.above_ref, bf16[48,256]{1,0:T(8,128)(2,1)S(1)} %collective-permute-done.3.below_ref, ...), custom_call_target="tpu_custom_call" | custom-call | bytes 4194304 | tf_op jit(solution)/shard_map/conv/pallas_call | solution.py:430
  67.3 0.0 copy-start.2
  67.3 1.2 %copy-done.2 = f32[1536,256]{1,0:T(8,128)} copy-done((f32[1536,256]{1,0:T(8,128)}, f32[1536,256]{1,0:T(8,128)S(1)}, u32[]{:S(2)}) %copy-start.2) | copy-done | bytes 1572888
  68.5 0.0 copy-start.7
  68.5 1.1 %copy-done.7 = bf16[1536,256]{1,0:T(8,128)(2,1)S(1)} copy-done((bf16[1536,256]{1,0:T(8,128)(2,1)S(1)}, bf16[1536,256]{1,0:T(8,128)(2,1)}, u32[]{:S(2)}) %copy-start.7) | copy-done | bytes 786456
  69.6 5.1 %probabilities.1.prob_ref = bf16[1536,1024]{1,0:T(8,128)(2,1)S(1)} custom-call(bf16[64,8,128]{2,1,0:T(8,128)(2,1)S(1)} %all-to-all-done.agents_ref, bf16[1536,256]{1,0:T(8,128)(2,1)S(1)} %copy-done.7), custom_call_target="tpu_custom_call" | custom-call | bytes 15728640 | tf_op jit(solution)/shard_map/probabilities/pallas_call | solution.py:422
  74.7 0.0 all-to-all-done.2.av_ref
  74.7 0.0 copy-start.3
  74.7 1.4 %copy-done.3 = f32[1536,256]{1,0:T(8,128)S(1)} copy-done((f32[1536,256]{1,0:T(8,128)S(1)}, f32[1536,256]{1,0:T(8,128)}, u32[]{:S(2)}) %copy-start.3) | copy-done | bytes 1572888
  76.1 0.0 copy-start.14
  76.1 0.0 copy-start.15
  76.1 1.2 %attend.1 = (f32[1536,256]{1,0:T(8,128)S(1)}, f32[24,128]{1,0:T(8,128)S(1)}) custom-call(bf16[64,8,128]{2,1,0:T(8,128)(2,1)S(1)} %all-to-all-done.2.av_ref, bf16[1536,1024]{1,0:T(8,128)(2,1)S(1)} %probabilities.1.prob_ref, f32[1536,256]{1,0:T(8,128)S(1)} %copy-done.3), custom_call_target="tpu_custom_call" | custom-call | bytes 4194304 | tf_op jit(solution)/shard_map/attend/pallas_call | solution.py:438
  77.3 2.8 %collective-permute-start.6 = (f32[24,128]{1,0:T(8,128)S(1)}, f32[24,128]{1,0:T(8,128)S(1)}, u32[]{:S(2)}, u32[]{:S(2)}) collective-permute-start(f32[24,128]{1,0:T(8,128)S(1)} %get-tuple-element.31.s0_ref), channel_id=1, source_target_pairs={{0,3},{1,0},{2,1},{3,2},{4,7},{5,4},{6,5},{7,6},{8,11},{9,8},{10,9... | collective-permute-start | bytes 36872 | tf_op jit(solution)/shard_map/ppermute | solution.py:447
  80.2 0.8 collective-permute-start.5
  81.0 0.9 %collective-permute-start.4 = (f32[24,128]{1,0:T(8,128)S(1)}, f32[24,128]{1,0:T(8,128)S(1)}, u32[]{:S(2)}, u32[]{:S(2)}) collective-permute-start(f32[24,128]{1,0:T(8,128)S(1)} %get-tuple-element.31.s0_ref), channel_id=1, source_target_pairs={{0,1},{1,2},{2,3},{3,0},{4,5},{5,6},{6,7},{7,4},{8,9},{9,10},{10,1... | collective-permute-start | bytes 36872 | tf_op jit(solution)/shard_map/ppermute | solution.py:447
  81.8 0.0 collective-permute-done.6.s3_ref
  81.9 3.5 %collective-permute-done.5.s2_ref = f32[24,128]{1,0:T(8,128)S(1)} collective-permute-done((f32[24,128]{1,0:T(8,128)S(1)}, f32[24,128]{1,0:T(8,128)S(1)}, u32[]{:S(2)}, u32[]{:S(2)}) %collective-permute-start.5) | collective-permute-done | bytes 12320 | tf_op jit(solution)/shard_map/ppermute | solution.py:447
  85.4 0.5 collective-permute-done.4.s1_ref
  85.9 0.0 copy-done.14
  85.9 0.0 copy-done.15
  85.9 1.4 %norm.1 = bf16[1536,256]{1,0:T(8,128)(2,1)} custom-call(f32[24,128]{1,0:T(8,128)S(1)} %get-tuple-element.31.s0_ref, f32[24,128]{1,0:T(8,128)S(1)} %collective-permute-done.4.s1_ref, f32[24,128]{1,0:T(8,128)S(1)} %collective-permute-done.5.s2_ref, f32[24,128]{1,0:T(8,128)S(1)} %collective-permute-done.6.s3_ref, f32[1536,256]{1,0:T(8,128)S(1)} %get-tuple-element.32.sum_ref, ...), custom_call_target="tpu_custom_call" | custom-call | bytes 4194304 | tf_op jit(solution)/shard_map/norm/pallas_call | solution.py:450
  (2 shorter events, 0.0 us)
Async XLA Ops:
  0.0 18.0 %copy-start = (bf16[48,32,256]{2,1,0:T(8,128)(2,1)S(1)}, bf16[48,32,256]{2,1,0:T(8,128)(2,1)}, u32[]{:S(2)}) copy-start(bf16[48,32,256]{2,1,0:T(8,128)(2,1)} %v_ref.3) | copy-start | bytes 2359300
  0.0 1.2 %copy-start.5 = (bf16[48,32,256]{2,1,0:T(8,128)(2,1)S(1)}, bf16[48,32,256]{2,1,0:T(8,128)(2,1)}, u32[]{:S(2)}) copy-start(bf16[48,32,256]{2,1,0:T(8,128)(2,1)} %param.7) | copy-start | bytes 2359300
  1.2 0.8 copy-start.12
  5.0 0.9 %copy-start.6 = (bf16[1536,256]{1,0:T(8,128)(2,1)}, bf16[1536,256]{1,0:T(8,128)(2,1)S(1)}, u32[]{:S(2)}) copy-start(bf16[1536,256]{1,0:T(8,128)(2,1)S(1)} %get-tuple-element.30.tq_ref) | copy-start | bytes 2359300
  5.9 21.5 %all-to-all-start = ((bf16[64,8,128]{2,1,0:T(8,128)(2,1)}), bf16[64,8,128]{2,1,0:T(8,128)(2,1)S(1)}, u32[]{:S(2)}, u32[]{:S(2)}) async-start(bf16[64,8,128]{2,1,0:T(8,128)(2,1)} %get-tuple-element.19), calls=%async_computation | async-start | bytes 262144 | tf_op jit(solution)/shard_map/all_to_all | solution.py:347
  18.1 1.1 %copy-start.4 = (bf16[48,32,256]{2,1,0:T(8,128)(2,1)S(1)}, bf16[48,32,256]{2,1,0:T(8,128)(2,1)}, u32[]{:S(2)}) copy-start(bf16[48,32,256]{2,1,0:T(8,128)(2,1)} %param.8) | copy-start | bytes 2359300
  19.8 3.4 %collective-permute-start = (bf16[48,256]{1,0:T(8,128)(2,1)S(1)}, bf16[48,256]{1,0:T(8,128)(2,1)S(1)}, u32[]{:S(2)}, u32[]{:S(2)}) collective-permute-start(bf16[48,256]{1,0:T(8,128)(2,1)S(1)} %get-tuple-element.23), channel_id=1, source_target_pairs={{0,4},{4,8},{8,12},{12,16},{16,20},{20,24},{24,28},{28,32},{32,36}... | collective-permute-start | bytes 73736 | tf_op jit(solution)/shard_map/ppermute | solution.py:353
  21.8 4.0 %collective-permute-start.1 = (bf16[48,256]{1,0:T(8,128)(2,1)S(1)}, bf16[48,256]{1,0:T(8,128)(2,1)S(1)}, u32[]{:S(2)}, u32[]{:S(2)}) collective-permute-start(bf16[48,256]{1,0:T(8,128)(2,1)S(1)} %get-tuple-element.24), channel_id=1, source_target_pairs={{4,0},{8,4},{12,8},{16,12},{20,16},{24,20},{28,24},{32,28},{36,32}... | collective-permute-start | bytes 73736 | tf_op jit(solution)/shard_map/ppermute | solution.py:353
  23.1 19.3 %copy-start.8 = (bf16[48,256]{1,0:T(8,128)(2,1)}, bf16[48,256]{1,0:T(8,128)(2,1)S(1)}, u32[]{:S(2)}) copy-start(bf16[48,256]{1,0:T(8,128)(2,1)S(1)} %collective-permute-done.left_ref) | copy-start | bytes 73732
  25.8 16.6 %copy-start.10 = (bf16[48,256]{1,0:T(8,128)(2,1)}, bf16[48,256]{1,0:T(8,128)(2,1)S(1)}, u32[]{:S(2)}) copy-start(bf16[48,256]{1,0:T(8,128)(2,1)S(1)} %collective-permute-done.1.right_ref) | copy-start | bytes 73732
  31.1 33.4 %copy-start.1 = (bf16[48,32,256]{2,1,0:T(8,128)(2,1)S(1)}, bf16[48,32,256]{2,1,0:T(8,128)(2,1)}, u32[]{:S(2)}) copy-start(bf16[48,32,256]{2,1,0:T(8,128)(2,1)} %v_ref.3) | copy-start | bytes 2359300
  31.1 33.4 %copy-start.13 = (f32[9,256]{1,0:T(8,128)S(1)}, f32[9,256]{1,0:T(8,128)}, u32[]{:S(2)}) copy-start(f32[9,256]{1,0:T(8,128)} %w_ref.1) | copy-start | bytes 27652
  31.1 22.9 %all-to-all-start.1 = ((bf16[64,16,128]{2,1,0:T(8,128)(2,1)}), bf16[64,16,128]{2,1,0:T(8,128)(2,1)S(1)}, u32[]{:S(2)}, u32[]{:S(2)}) async-start(bf16[64,16,128]{2,1,0:T(8,128)(2,1)} %partials.1), calls=%async_computation.1 | async-start | bytes 524288 | tf_op jit(solution)/shard_map/all_to_all | solution.py:347
  43.9 6.5 %collective-permute-start.2 = (bf16[48,256]{1,0:T(8,128)(2,1)}, bf16[48,256]{1,0:T(8,128)(2,1)S(1)}, u32[]{:S(2)}, u32[]{:S(2)}) collective-permute-start(bf16[48,256]{1,0:T(8,128)(2,1)} %get-tuple-element.27), channel_id=1, source_target_pairs={{0,64},{64,128},{128,192},{1,65},{65,129},{129,193},{2,66},{66,130... | collective-permute-start | bytes 73736 | tf_op jit(solution)/shard_map/ppermute | solution.py:353
  47.4 6.0 %collective-permute-start.3 = (bf16[48,256]{1,0:T(8,128)(2,1)}, bf16[48,256]{1,0:T(8,128)(2,1)S(1)}, u32[]{:S(2)}, u32[]{:S(2)}) collective-permute-start(bf16[48,256]{1,0:T(8,128)(2,1)} %get-tuple-element.28), channel_id=1, source_target_pairs={{64,0},{128,64},{192,128},{65,1},{129,65},{193,129},{66,2},{130,66... | collective-permute-start | bytes 73736 | tf_op jit(solution)/shard_map/ppermute | solution.py:353
  55.1 19.5 %all-to-all-start.2 = ((bf16[64,8,128]{2,1,0:T(8,128)(2,1)}), bf16[64,8,128]{2,1,0:T(8,128)(2,1)S(1)}, u32[]{:S(2)}, u32[]{:S(2)}) async-start(bf16[64,8,128]{2,1,0:T(8,128)(2,1)} %merge.1), calls=%async_computation.2 | async-start | bytes 262144 | tf_op jit(solution)/shard_map/all_to_all | solution.py:347
  64.5 0.7 copy-start.9
  65.2 0.7 copy-start.11
  67.3 1.2 %copy-start.2 = (f32[1536,256]{1,0:T(8,128)}, f32[1536,256]{1,0:T(8,128)S(1)}, u32[]{:S(2)}) copy-start(f32[1536,256]{1,0:T(8,128)S(1)} %conv.1.conv_ref) | copy-start | bytes 4718596
  68.5 1.1 %copy-start.7 = (bf16[1536,256]{1,0:T(8,128)(2,1)S(1)}, bf16[1536,256]{1,0:T(8,128)(2,1)}, u32[]{:S(2)}) copy-start(bf16[1536,256]{1,0:T(8,128)(2,1)} %copy-done.6) | copy-start | bytes 2359300
  74.7 1.4 %copy-start.3 = (f32[1536,256]{1,0:T(8,128)S(1)}, f32[1536,256]{1,0:T(8,128)}, u32[]{:S(2)}) copy-start(f32[1536,256]{1,0:T(8,128)} %copy-done.2) | copy-start | bytes 4718596
  76.1 9.8 %copy-start.14 = (f32[256]{0:T(256)S(1)}, f32[256]{0:T(256)}, u32[]{:S(2)}) copy-start(f32[256]{0:T(256)} %param.12) | copy-start | bytes 3076
  76.1 9.8 %copy-start.15 = (f32[256]{0:T(256)S(1)}, f32[256]{0:T(256)}, u32[]{:S(2)}) copy-start(f32[256]{0:T(256)} %param.13) | copy-start | bytes 3076
  77.3 4.5 %collective-permute-start.6 = (f32[24,128]{1,0:T(8,128)S(1)}, f32[24,128]{1,0:T(8,128)S(1)}, u32[]{:S(2)}, u32[]{:S(2)}) collective-permute-start(f32[24,128]{1,0:T(8,128)S(1)} %get-tuple-element.31.s0_ref), channel_id=1, source_target_pairs={{0,3},{1,0},{2,1},{3,2},{4,7},{5,4},{6,5},{7,6},{8,11},{9,8},{10,9... | collective-permute-start | bytes 36872 | tf_op jit(solution)/shard_map/ppermute | solution.py:447
  80.2 5.2 %collective-permute-start.5 = (f32[24,128]{1,0:T(8,128)S(1)}, f32[24,128]{1,0:T(8,128)S(1)}, u32[]{:S(2)}, u32[]{:S(2)}) collective-permute-start(f32[24,128]{1,0:T(8,128)S(1)} %get-tuple-element.31.s0_ref), channel_id=1, source_target_pairs={{0,2},{1,3},{2,0},{3,1},{4,6},{5,7},{6,4},{7,5},{8,10},{9,11},{10,... | collective-permute-start | bytes 36872 | tf_op jit(solution)/shard_map/ppermute | solution.py:447
  81.0 4.9 %collective-permute-start.4 = (f32[24,128]{1,0:T(8,128)S(1)}, f32[24,128]{1,0:T(8,128)S(1)}, u32[]{:S(2)}, u32[]{:S(2)}) collective-permute-start(f32[24,128]{1,0:T(8,128)S(1)} %get-tuple-element.31.s0_ref), channel_id=1, source_target_pairs={{0,1},{1,2},{2,3},{3,0},{4,5},{5,6},{6,7},{7,4},{8,9},{9,10},{10,1... | collective-permute-start | bytes 36872 | tf_op jit(solution)/shard_map/ppermute | solution.py:447

commit v3 on v2

--- a/solution.py
+++ b/solution.py
@@ -25,24 +25,47 @@
 epsilon = 1e-05
 
 VMEM_SPEC = pl.BlockSpec(memory_space=pltpu.VMEM)
-
-
-def call(kernel, out_shape, n_in, scratch=(), flops=0, nbytes=0, name=None):
-    outs = jax.tree.map(lambda s: VMEM_SPEC, out_shape)
-    return pl.pallas_call(
+HBM_SPEC = pl.BlockSpec(memory_space=pltpu.HBM)
+
+
+def call(kernel, outs, in_spaces, scratch=(), nbytes=0, name=None, out_spaces=None):
+    fn = pl.pallas_call(
         kernel,
-        out_shape=out_shape,
-        in_specs=[VMEM_SPEC] * n_in,
-        out_specs=outs,
+        out_shape=outs,
+        in_specs=[HBM_SPEC if c == "h" else VMEM_SPEC for c in in_spaces],
+        out_specs=(
+            tuple(HBM_SPEC if c == "h" else VMEM_SPEC for c in out_spaces or " " * len(outs))
+            if isinstance(outs, tuple)
+            else VMEM_SPEC
+        ),
         scratch_shapes=list(scratch),
         compiler_params=pltpu.CompilerParams(vmem_limit_bytes=12 * 1024 * 1024),
-        cost_estimate=pl.CostEstimate(flops=flops, bytes_accessed=nbytes, transcendentals=0),
+        cost_estimate=pl.CostEstimate(flops=0, bytes_accessed=nbytes, transcendentals=0),
         name=name,
     )
+
+    def run(*args):
+        spaces = {"h": pltpu.HBM, "v": pltpu.VMEM}
+        return fn(
+            *[
+                pltpu.with_memory_space_constraint(x, spaces[c]) if c in spaces else x
+                for x, c in zip(args, in_spaces, strict=True)
+            ]
+        )
+
+    return run
 
 
 def shape(dims, dtype):
     return jax.ShapeDtypeStruct(dims, dtype)
+
+
+def near(dims, dtype):
+    return pltpu.VMEM(dims, dtype)
+
+
+def far(dims, dtype):
+    return pltpu.HBM(dims, dtype)
 
 
 def lanes(dims):
@@ -77,24 +100,47 @@
     return cosine, sine
 
 
+def slots(block):
+    twice = jnp.concatenate([block, block], axis=0).astype(bf16)
+    return jnp.broadcast_to(twice[None], (TILES // 2, 16, 128)).reshape(TILES * 8, 128)
+
+
 def query_kernel(
-    pos_ref, freq_ref, q_ref, tq_ref, agents_ref, tab_r_ref, tab_c_ref, turn_ref, held_ref, sems
+    pos_ref,
+    q_ref,
+    tq_ref,
+    agents_ref,
+    tab_r_ref,
+    tab_c_ref,
+    turn_ref,
+    held_ref,
+    done_ref,
+    spot_ref,
+    sems,
 ):
     step = N // AGR
+    place = pltpu.make_async_copy(pos_ref, spot_ref, sems.at[AGR])
+    place.start()
     copies = []
     for cell in range(AGR):
         part = pl.ds(cell * step, step)
         copy = pltpu.make_async_copy(q_ref.at[part, :], held_ref.at[part, :], sems.at[cell])
         copy.start()
         copies.append(copy)
-    freq = freq_ref[...]
-    row_line = pos_ref[0][0:1, :].astype(f32)
-    col_pos = pos_ref[1][:, 0:1].astype(f32)
+    matrix = turn_matrix()
+    turn_ref[...] = matrix
+    lane = lanes((1, 128)) % HD
+    power = jnp.exp((lane % 16).astype(f32) * f32(-math.log(100.0) / 16))
+    freq_r = jnp.where(lane < 32, power, 0.0)
+    freq_c = jnp.where(lane < 32, 0.0, power)
+    place.wait()
+    row_line = spot_ref[0][0:1, :].astype(f32)
+    col_pos = spot_ref[1][:, 0:1].astype(f32)
     eye = lax.broadcasted_iota(jnp.int32, (TR, TR), 0) == lax.broadcasted_iota(
         jnp.int32, (TR, TR), 1
     )
     row_pos = jnp.sum(jnp.where(eye, jnp.broadcast_to(row_line, (TR, TR)), 0.0), 1, keepdims=True)
-    angles = jnp.concatenate([row_pos * freq[0:1, :], col_pos * freq[1:2, :]], axis=0)
+    angles = jnp.concatenate([row_pos * freq_r, col_pos * freq_c], axis=0)
     sines, cosines = sin_cos(angles)
     sines = jnp.concatenate([sines, sines], axis=1)
     cosines = jnp.concatenate([cosines, cosines], axis=1)
@@ -102,8 +148,6 @@
     tab_r_ref[1] = sines[:TR]
     tab_c_ref[0] = cosines[TR:]
     tab_c_ref[1] = sines[TR:]
-    matrix = turn_matrix()
-    turn_ref[...] = matrix
     means = []
     for cell in range(AGR):
         cosine, sine = cell_tables(
@@ -111,14 +155,34 @@
         )
         copies[cell].wait()
         rotated = turned(held_ref[pl.ds(cell * step, step), :], matrix, cosine, sine)
-        tq_ref[pl.ds(cell * step, step), :] = rotated
+        part = pl.ds(cell * step, step)
+        done_ref[part, :] = rotated
+        copies[cell] = pltpu.make_async_copy(
+            done_ref.at[part, :], tq_ref.at[part, :], sems.at[AGR + 1 + cell]
+        )
+        copies[cell].start()
         mean = jnp.sum(rotated.astype(f32), 0, keepdims=True) / step
         means.append(mean.astype(bf16).astype(f32))
     packed = jnp.concatenate([m[:, :128] for m in means] + [m[:, 128:] for m in means], axis=0)
-    agents_ref[...] = jnp.broadcast_to(packed.astype(bf16)[None], (TILES, 8, 128))
-
-
-def key_kernel(tab_r_ref, tab_c_ref, turn_ref, k_ref, v_ref, tk_ref, first_ref, last_ref):
+    agents_ref[...] = slots(packed)
+    for copy in copies:
+        copy.wait()
+
+
+def key_kernel(
+    tab_r_ref,
+    tab_c_ref,
+    turn_ref,
+    k_ref,
+    v_ref,
+    tk_ref,
+    first_ref,
+    last_ref,
+    top_ref,
+    bottom_ref,
+):
+    top_ref[...] = v_ref[0]
+    bottom_ref[...] = v_ref[TR - 1]
     first_ref[...] = v_ref[:, 0, :]
     last_ref[...] = v_ref[:, TC - 1, :]
     matrix = turn_ref[...]
@@ -132,12 +196,15 @@
         )
 
 
-def agent_pairs(agents_ref, wide_ref, scale):
-    wide_ref[...] = agents_ref[...].astype(f32).reshape(TILES * 8, 128) * scale
+def agent_pairs(agents_ref, scale):
+    target = lax.broadcasted_iota(jnp.int32, (AGENTS, TILES * 8), 0)
+    source = lax.broadcasted_iota(jnp.int32, (AGENTS, TILES * 8), 1)
+    agents = agents_ref[...]
     pairs = []
     for pair in range(2):
-        parts = [wide_ref[pl.ds(4 * pair + k, TILES, stride=8), :] for k in range(AGR)]
-        pairs.append(jnp.concatenate(parts, axis=0).astype(bf16))
+        wanted = (target & (TILES - 1)) * 8 + (target // TILES) + 4 * pair
+        pick = jnp.where(source == wanted, scale, 0.0).astype(bf16)
+        pairs.append(jnp.dot(pick, agents, preferred_element_type=f32).astype(bf16))
     return pairs
 
 
@@ -145,8 +212,8 @@
     return (lanes(dims) // HD) == parity
 
 
-def partial_kernel(agents_ref, tk_ref, v_ref, out_ref, score_ref, wide_ref):
-    pairs = agent_pairs(agents_ref, wide_ref, 1.0 / math.sqrt(HD))
+def partial_kernel(agents_ref, tk_ref, v_ref, out_ref, score_ref):
+    pairs = agent_pairs(agents_ref, 1.0 / math.sqrt(HD))
     chunk = 512
     for head in range(LOCAL_HEADS):
         pair, parity = head // 2, head % 2
@@ -191,36 +258,45 @@
             ),
         )
         groups = packed.reshape(2, ROWS, 8, 128)
-        out_ref[pl.ds(head * ROWS, ROWS)] = jnp.concatenate([groups[0], groups[1]], 1).astype(bf16)
+        groups = jnp.concatenate([groups[0], groups[1]], 1).reshape(AGENTS, 128)
+        out_ref[pl.ds(head * AGENTS, AGENTS), :] = groups.astype(bf16)
 
 
 def merge_kernel(parts_ref, out_ref):
     source = lax.broadcasted_iota(jnp.int32, (128, 128), 0)
     picker = jnp.where((source >= HD) & (source < HD + 3), 1.0, 0.0).astype(bf16)
-    parts = parts_ref[...].reshape(TILES * ROWS, 128)
+    parts = parts_ref[...]
     logs = jnp.dot(parts, picker, preferred_element_type=f32).reshape(TILES, ROWS, 128)
     values = parts.astype(f32).reshape(TILES, ROWS, 128)
     peak = jnp.max(logs, 0)
     weights = jnp.exp(logs - peak[None])
     merged = jnp.sum(weights * values, 0) / jnp.sum(weights, 0)
     merged = jnp.where(lanes((8, 128)) < HD, merged[:8], pltpu.roll(merged[8:], HD, 1))
-    out_ref[...] = jnp.broadcast_to(merged.astype(bf16)[None], (TILES, 8, 128))
-
-
-def probability_kernel(agents_ref, tq_ref, prob_ref, wide_ref):
-    pairs = agent_pairs(agents_ref, wide_ref, 1.0 / math.sqrt(HD))
+    out_ref[...] = slots(merged)
+
+
+def probability_kernel(agents_ref, tq_ref, prob_ref, held_ref, sems):
+    chunk = 256
+
+    def fetch(c):
+        rows = pl.ds(pl.multiple_of(c * chunk, chunk), chunk)
+        return pltpu.make_async_copy(tq_ref.at[rows, :], held_ref.at[rows, :], sems.at[c])
+
+    for c in range(N // chunk):
+        fetch(c).start()
+    pairs = agent_pairs(agents_ref, 1.0 / math.sqrt(HD))
     ones = jnp.ones((AGENTS, 128), bf16)
     owns = []
     for head in range(LOCAL_HEADS):
         own = pairs[head // 2]
         owns.append(jnp.where(half_mask(own.shape, head % 2), own, jnp.zeros_like(own)))
-    chunk = 256
 
     def body(c, carry):
+        fetch(c).wait()
         rows = pl.ds(pl.multiple_of(c * chunk, chunk), chunk)
         for head in range(LOCAL_HEADS):
             scores = lax.dot_general(
-                tq_ref[rows, pl.ds(head // 2 * 128, 128)],
+                held_ref[rows, pl.ds(head // 2 * 128, 128)],
                 owns[head],
                 (((1,), (1,)), ((), ())),
                 preferred_element_type=f32,
@@ -235,9 +311,9 @@
     lax.fori_loop(0, N // chunk, body, 0)
 
 
-def line_kernel(v_top_ref, v_bottom_ref, left_ref, right_ref, up_ref, down_ref):
-    for v_ref, row, out_ref in ((v_top_ref, 0, up_ref), (v_bottom_ref, TR - 1, down_ref)):
-        out_ref[pl.ds(0, TC), :] = v_ref[0]
+def line_kernel(top_ref, bottom_ref, left_ref, right_ref, up_ref, down_ref):
+    for line_ref, row, out_ref in ((top_ref, 0, up_ref), (bottom_ref, TR - 1, down_ref)):
+        out_ref[pl.ds(0, TC), :] = line_ref[...]
         left = left_ref[row : row + 1, :].astype(f32)
         right = right_ref[row : row + 1, :].astype(f32)
         tail = jnp.concatenate([left, right, jnp.zeros((14, CH), f32)], axis=0)
@@ -283,12 +359,20 @@
         out_ref[pl.ds((TR - 1) * TC, TC), cols] = a + t[2]
 
 
-def attend_kernel(av_ref, prob_ref, conv_ref, sum_ref, stat_ref):
+def attend_kernel(av_ref, prob_ref, conv_hbm_ref, sum_ref, stat_ref, conv_ref, sems):
+    step = N // AGR
+    copies = []
+    for c in range(AGR):
+        part = pl.ds(c * step, step)
+        copies.append(
+            pltpu.make_async_copy(conv_hbm_ref.at[part, :], conv_ref.at[part, :], sems.at[c])
+        )
+        copies[c].start()
     halves = []
     for pair in range(2):
         pieces = []
         for parity in range(2):
-            part = av_ref[pl.ds((2 * pair + parity) * ROWS, ROWS)].astype(f32).reshape(128, 128)
+            part = av_ref[pl.ds((2 * pair + parity) * 128, 128), :].astype(f32)
             other = pltpu.roll(part, HD, 1)
             own = half_mask(part.shape, parity)
             for piece in (part, other) if parity == 0 else (other, part):
@@ -297,6 +381,8 @@
     eye = lax.broadcasted_iota(jnp.int32, (128, 128), 0) == lanes((128, 128))
 
     for b in range(BLOCKS):
+        if b * 128 % step == 0:
+            copies[b * 128 // step].wait()
         rows = pl.ds(b * 128, 128)
         xs = []
         for pair in range(2):
@@ -337,14 +423,9 @@
             ).astype(bf16)
 
 
-def frequencies():
-    lane = jnp.arange(128) % HD
-    power = jnp.power(f32(100.0), -(lane % 16).astype(f32) / 16)
-    return jnp.stack([jnp.where(lane < 32, power, 0.0), jnp.where(lane < 32, 0.0, power)])
-
-
 def spread(x):
-    return lax.all_to_all(x, ("row", "col"), 0, 0)
+    slot = x.reshape(TILES, x.shape[0] // TILES, 128)
+    return lax.all_to_all(slot, ("row", "col"), 0, 0).reshape(x.shape)
 
 
 def shift(x, axis, step):
@@ -362,83 +443,78 @@
     k = keys.reshape(N, CH)
     v = values.reshape(N, CH)
     mb = 1 << 20
-    wide = pltpu.VMEM((TILES * 8, 128), f32)
-    tq, packed, tab_r, tab_c, turn = pl.pallas_call(
+    tq, packed, tab_r, tab_c, turn = call(
         query_kernel,
-        out_shape=(
-            shape((N, CH), bf16),
-            shape((TILES, 8, 128), bf16),
-            shape((2, TR, CH), f32),
-            shape((2, TC, CH), f32),
-            shape((CH, CH), bf16),
+        (
+            far((N, CH), bf16),
+            shape((TILES * 8, 128), bf16),
+            near((2, TR, CH), f32),
+            near((2, TC, CH), f32),
+            near((CH, CH), bf16),
         ),
-        in_specs=[VMEM_SPEC, VMEM_SPEC, pl.BlockSpec(memory_space=pltpu.HBM)],
-        out_specs=(VMEM_SPEC,) * 5,
-        scratch_shapes=[pltpu.VMEM((N, CH), bf16), pltpu.SemaphoreType.DMA((AGR,))],
-        compiler_params=pltpu.CompilerParams(vmem_limit_bytes=12 * 1024 * 1024),
-        cost_estimate=pl.CostEstimate(flops=0, bytes_accessed=8 * mb, transcendentals=0),
+        "hh",
+        scratch=[
+            pltpu.VMEM((N, CH), bf16),
+            pltpu.VMEM((N, CH), bf16),
+            pltpu.VMEM((2, TC, TR), jnp.int32),
+            pltpu.SemaphoreType.DMA((2 * AGR + 1,)),
+        ],
+        out_spaces="h    ",
+        nbytes=8 * mb,
         name="turn_queries",
-    )(jnp.swapaxes(positions, 1, 2), frequencies(), q)
+    )(jnp.swapaxes(positions, 1, 2), q)
     agents = spread(packed)
-    tk, first, last = call(
+    tk, first, last, top, bottom = call(
         key_kernel,
-        (shape((N, CH), bf16), shape((TR, CH), bf16), shape((TR, CH), bf16)),
-        5,
+        (near((N, CH), bf16),) + (near((TR, CH), bf16),) * 2 + (near((TC, CH), bf16),) * 2,
+        "vvv  ",
         nbytes=4 * mb,
         name="turn_keys",
     )(tab_r, tab_c, turn, k, values)
     left = shift(last, "col", 1)
     right = shift(first, "col", -1)
-    agents = after(agents, left, right)
     parts = call(
         partial_kernel,
-        shape((TILES, ROWS, 128), bf16),
-        3,
-        scratch=[pltpu.VMEM((AGENTS, N), f32), wide],
+        shape((TILES * ROWS, 128), bf16),
+        " v ",
+        scratch=[pltpu.VMEM((AGENTS, N), f32)],
         nbytes=10 * mb,
         name="partials",
     )(agents, tk, v)
+    parts = after(parts, left, right)
     received = spread(parts)
-    up, down = pl.pallas_call(
-        line_kernel,
-        out_shape=(shape((TC + 16, CH), bf16),) * 2,
-        grid=(1,),
-        in_specs=[
-            pl.BlockSpec((1, TC, CH), lambda i: (0, 0, 0)),
-            pl.BlockSpec((1, TC, CH), lambda i: (TR - 1, 0, 0)),
-            pl.BlockSpec((TR, CH), lambda i: (0, 0)),
-            pl.BlockSpec((TR, CH), lambda i: (0, 0)),
-        ],
-        out_specs=(pl.BlockSpec((TC + 16, CH), lambda i: (0, 0)),) * 2,
-        name="lines",
-    )(values, values, left, right)
+    up, down = call(
+        line_kernel, (near((TC + 16, CH), bf16),) * 2, "vvvv", nbytes=mb // 4, name="lines"
+    )(top, bottom, left, right)
     above = shift(down, "row", 1)
     below = shift(up, "row", -1)
-    received = after(received, above, below)
-    merged = call(merge_kernel, shape((TILES, 8, 128), bf16), 1, nbytes=2 * mb, name="merge")(
+    received = after(received, up, down)
+    merged = call(merge_kernel, shape((TILES * 8, 128), bf16), " ", nbytes=2 * mb, name="merge")(
         received
     )
+    merged = after(merged, above, below)
     agent_values = spread(merged)
     prob = call(
         probability_kernel,
-        shape((N, LOCAL_HEADS * AGENTS), bf16),
-        2,
-        scratch=[wide],
+        near((N, LOCAL_HEADS * AGENTS), bf16),
+        " h",
+        scratch=[pltpu.VMEM((N, CH), bf16), pltpu.SemaphoreType.DMA((N // 256,))],
         nbytes=15 * mb,
         name="probabilities",
     )(agents, tq)
     convolved = call(
         conv_kernel,
-        shape((N, CH), f32),
-        6,
+        far((N, CH), f32),
+        " vvvv ",
         scratch=[pltpu.VMEM((TR, CH), f32), pltpu.VMEM((TR, CH), f32)],
         nbytes=4 * mb,
         name="conv",
     )(values, left, right, above, below, conv_weight)
     summed, stats = call(
         attend_kernel,
-        (shape((N, CH), f32), shape((2 * BLOCKS, 128), f32)),
-        3,
+        (near((N, CH), f32), near((2 * BLOCKS, 128), f32)),
+        " vh",
+        scratch=[pltpu.VMEM((N, CH), f32), pltpu.SemaphoreType.DMA((AGR,))],
         nbytes=4 * mb,
         name="attend",
     )(agent_values, prob, convolved)
@@ -447,7 +523,7 @@
         lax.ppermute(stats, "head", [(i, (i + d) % heads) for i in range(heads)])
         for d in range(1, heads)
     ]
-    normed = call(norm_kernel, shape((N, CH), bf16), 7, nbytes=4 * mb, name="norm")(
+    normed = call(norm_kernel, shape((N, CH), bf16), "v   v  ", nbytes=4 * mb, name="norm")(
         stats, *others, summed, norm_gain.reshape(1, CH), norm_bias.reshape(1, CH)
     )
     return normed.reshape(TR, TC, CH)

time: 88 us -> 80.8 us (0.918)
  local copies, waits for them, and re-layouts: 9.16 us -> 1.14 us
  starting transfers between devices: 46.5 us -> 41.8 us
  Pallas kernels: 18.8 us -> 22.1 us
  waiting for transfers between devices: 12.6 us -> 15 us
    all_to_all x3, waiting for transfers between devices: 2.28 us -> 10.9 us  [spread(): return lax.all_to_all(slot, ('row', 'col'), 0, 0).reshape(x.shape)]
    unnamed x32 -> x10, local copies, waits for them, and re-layouts: 9.16 us -> 1.14 us
    ppermute x4, waiting for transfers between devices: 6.3 us -> 0.01 us  [shift(): return lax.ppermute(x, axis, pairs)]
    all_to_all x3, starting transfers between devices: 32.8 us -> 28.1 us  [spread(): return lax.all_to_all(slot, ('row', 'col'), 0, 0).reshape(x.shape)]
    pallas_call x9, Pallas kernels: 18.8 us -> 22.1 us  [run(): fn(*[pltpu.with_memory_space_constraint(x, spaces[c]) if c in spaces else...]
  transfers between devices with their start and end apart: 10 -> 10, of which waited for: 7 -> 5; matrix products, arithmetic and copies ran while one was open for 0% -> 0% of each run, Pallas kernels for 10% -> 17%
where the time goes in v3:
time: 80.8 us; the launch traced here: 80.1 us
  starting transfers between devices  41.8 us (52%)
  Pallas kernels  22.1 us (27%)
  waiting for transfers between devices  15 us (19%)
  local copies, waits for them, and re-layouts  1.14 us (1%)
    all_to_all x3, starting transfers between devices, spread(): return lax.all_to_all(slot, ('row', 'col'), 0, 0).reshape(x.shape)  28.1 us
    pallas_call x9, Pallas kernels, run(): fn(*[pltpu.with_memory_space_constraint(x, spaces[c]) if c in spaces else...  22.1 us
    all_to_all x3, waiting for transfers between devices, spread(): return lax.all_to_all(slot, ('row', 'col'), 0, 0).reshape(x.shape)  10.9 us
    ppermute x4, starting transfers between devices, shift(): return lax.ppermute(x, axis, pairs)  9.19 us
    ppermute x3, starting transfers between devices, shards(): lax.ppermute(stats, 'head', [(i, (i + d) % heads) for i in range(heads)])  4.52 us
    ppermute x3, waiting for transfers between devices, shards(): lax.ppermute(stats, 'head', [(i, (i + d) % heads) for i in range(heads)])  4.02 us
  transfers between devices with their start and end apart: 10, of which 5 were waited for; matrix products, arithmetic and copies ran while one was open for 0% of the time, Pallas kernels for 17%

profile of v3, /device:TPU:8, one launch (start us, length us, event | category | flops | bytes accessed | tf_op | source)
XLA Modules:
  0.0 80.1 jit_solution(3701663519401720297)
XLA Ops:
  0.0 0.0 copy-start
  0.0 3.5 %turn_queries.1 = (bf16[1536,256]{1,0:T(8,128)(2,1)}, bf16[512,128]{1,0:T(8,128)(2,1)}, f32[2,48,256]{2,1,0:T(8,128)S(1)}, f32[2,32,256]{2,1,0:T(8,128)S(1)}, bf16[256,256]{1,0:T(8,128)(2,1)S(1)}) custom-call(s32[2,32,48]{2,1,0:T(8,128)} %bitcast.22, bf16[1536,256]{1,0:T(8,128)(2,1)} %bitcast.21), custom_call_target="tpu_custom_call" | custom-call | bytes 8388608 | tf_op jit(solution)/shard_map/turn_queries/pallas_call | solution.py:49
  3.6 12.1 %all-to-all-start = ((bf16[64,8,128]{2,1,0:T(8,128)(2,1)}), bf16[64,8,128]{2,1,0:T(8,128)(2,1)S(1)}, u32[]{:S(2)}, u32[]{:S(2)}) async-start(bf16[64,8,128]{2,1,0:T(8,128)(2,1)} %bitcast.2), calls=%async_computation | async-start | bytes 262144 | tf_op jit(solution)/shard_map/all_to_all | solution.py:428
  15.7 0.0 copy-done
  15.7 0.0 copy-start.1
  15.7 1.1 %copy-done.1 = bf16[48,32,256]{2,1,0:T(8,128)(2,1)S(1)} copy-done((bf16[48,32,256]{2,1,0:T(8,128)(2,1)S(1)}, bf16[48,32,256]{2,1,0:T(8,128)(2,1)}, u32[]{:S(2)}) %copy-start.1) | copy-done | bytes 786456
  16.8 0.6 turn_keys.1
  17.4 2.1 %collective-permute-start = (bf16[48,256]{1,0:T(8,128)(2,1)S(1)}, bf16[48,256]{1,0:T(8,128)(2,1)S(1)}, u32[]{:S(2)}, u32[]{:S(2)}) collective-permute-start(bf16[48,256]{1,0:T(8,128)(2,1)S(1)} %get-tuple-element.27), channel_id=1, source_target_pairs={{0,4},{4,8},{8,12},{12,16},{16,20},{20,24},{24,28},{28,32},{32,36}... | collective-permute-start | bytes 73736 | tf_op jit(solution)/shard_map/ppermute | solution.py:434
  19.5 1.3 %collective-permute-start.1 = (bf16[48,256]{1,0:T(8,128)(2,1)S(1)}, bf16[48,256]{1,0:T(8,128)(2,1)S(1)}, u32[]{:S(2)}, u32[]{:S(2)}) collective-permute-start(bf16[48,256]{1,0:T(8,128)(2,1)S(1)} %get-tuple-element.28), channel_id=1, source_target_pairs={{4,0},{8,4},{12,8},{16,12},{20,16},{24,20},{28,24},{32,28},{36,32}... | collective-permute-start | bytes 73736 | tf_op jit(solution)/shard_map/ppermute | solution.py:434
  20.8 4.3 %all-to-all-done = bf16[64,8,128]{2,1,0:T(8,128)(2,1)S(1)} async-done(((bf16[64,8,128]{2,1,0:T(8,128)(2,1)}), bf16[64,8,128]{2,1,0:T(8,128)(2,1)S(1)}, u32[]{:S(2)}, u32[]{:S(2)}) %all-to-all-start) | async-done | bytes 131104 | tf_op jit(solution)/shard_map/all_to_all | solution.py:428
  25.1 0.0 copy-start.2
  25.1 3.9 %partials.1 = bf16[1024,128]{1,0:T(8,128)(2,1)} custom-call(bf16[512,128]{1,0:T(8,128)(2,1)S(1)} %bitcast.14, bf16[1536,256]{1,0:T(8,128)(2,1)S(1)} %get-tuple-element.26.tk_ref, bf16[1536,256]{1,0:T(8,128)(2,1)S(1)} %bitcast.13), custom_call_target="tpu_custom_call" | custom-call | bytes 10485760 | tf_op jit(solution)/shard_map/partials/pallas_call | solution.py:49
  28.9 0.0 collective-permute-done.left_ref
  28.9 0.0 collective-permute-done.1.right_ref
  28.9 9.4 %all-to-all-start.1 = ((bf16[64,16,128]{2,1,0:T(8,128)(2,1)}), bf16[64,16,128]{2,1,0:T(8,128)(2,1)S(1)}, u32[]{:S(2)}, u32[]{:S(2)}) async-start(bf16[64,16,128]{2,1,0:T(8,128)(2,1)} %bitcast.6), calls=%async_computation.1 | async-start | bytes 524288 | tf_op jit(solution)/shard_map/all_to_all | solution.py:428
  38.4 2.4 %collective-permute-start.3 = (bf16[48,256]{1,0:T(8,128)(2,1)S(1)}, bf16[48,256]{1,0:T(8,128)(2,1)S(1)}, u32[]{:S(2)}, u32[]{:S(2)}) collective-permute-start(bf16[48,256]{1,0:T(8,128)(2,1)S(1)} %get-tuple-element.32), channel_id=1, source_target_pairs={{64,0},{128,64},{192,128},{65,1},{129,65},{193,129},{66,2},{130,66... | collective-permute-start | bytes 73736 | tf_op jit(solution)/shard_map/ppermute | solution.py:434
  40.8 3.5 %collective-permute-start.2 = (bf16[48,256]{1,0:T(8,128)(2,1)S(1)}, bf16[48,256]{1,0:T(8,128)(2,1)S(1)}, u32[]{:S(2)}, u32[]{:S(2)}) collective-permute-start(bf16[48,256]{1,0:T(8,128)(2,1)S(1)} %get-tuple-element.33), channel_id=1, source_target_pairs={{0,64},{64,128},{128,192},{1,65},{65,129},{129,193},{2,66},{66,130... | collective-permute-start | bytes 73736 | tf_op jit(solution)/shard_map/ppermute | solution.py:434
  44.3 5.7 %all-to-all-done.1 = bf16[64,16,128]{2,1,0:T(8,128)(2,1)S(1)} async-done(((bf16[64,16,128]{2,1,0:T(8,128)(2,1)}), bf16[64,16,128]{2,1,0:T(8,128)(2,1)S(1)}, u32[]{:S(2)}, u32[]{:S(2)}) %all-to-all-start.1) | async-done | bytes 262176 | tf_op jit(solution)/shard_map/all_to_all | solution.py:428
  49.9 1.1 %merge.1 = bf16[512,128]{1,0:T(8,128)(2,1)} custom-call(bf16[1024,128]{1,0:T(8,128)(2,1)S(1)} %bitcast.16), custom_call_target="tpu_custom_call" | custom-call | bytes 2097152 | tf_op jit(solution)/shard_map/merge/pallas_call | solution.py:49
  51.1 0.0 collective-permute-done.3.below_ref
  51.1 0.0 collective-permute-done.2.above_ref
  51.1 6.5 %all-to-all-start.2 = ((bf16[64,8,128]{2,1,0:T(8,128)(2,1)}), bf16[64,8,128]{2,1,0:T(8,128)(2,1)S(1)}, u32[]{:S(2)}, u32[]{:S(2)}) async-start(bf16[64,8,128]{2,1,0:T(8,128)(2,1)} %bitcast.8), calls=%async_computation.2 | async-start | bytes 262144 | tf_op jit(solution)/shard_map/all_to_all | solution.py:428
  57.6 0.0 copy-done.2
  57.6 2.5 %conv.1.conv_hbm_ref = f32[1536,256]{1,0:T(8,128)} custom-call(bf16[48,32,256]{2,1,0:T(8,128)(2,1)S(1)} %copy-done, bf16[48,256]{1,0:T(8,128)(2,1)S(1)} %collective-permute-done.left_ref, bf16[48,256]{1,0:T(8,128)(2,1)S(1)} %collective-permute-done.1.right_ref, bf16[48,256]{1,0:T(8,128)(2,1)S(1)} %collective-permute-done.2.above_ref, ...), custom_call_target="tpu_custom_call" | custom-call | bytes 4194304 | tf_op jit(solution)/shard_map/conv/pallas_call | solution.py:49
  60.0 6.0 %probabilities.1.prob_ref = bf16[1536,1024]{1,0:T(8,128)(2,1)S(1)} custom-call(bf16[512,128]{1,0:T(8,128)(2,1)S(1)} %bitcast.15, bf16[1536,256]{1,0:T(8,128)(2,1)} %get-tuple-element.36.tq_ref), custom_call_target="tpu_custom_call" | custom-call | bytes 15728640 | tf_op jit(solution)/shard_map/probabilities/pallas_call | solution.py:49
  66.0 0.9 %all-to-all-done.2 = bf16[64,8,128]{2,1,0:T(8,128)(2,1)S(1)} async-done(((bf16[64,8,128]{2,1,0:T(8,128)(2,1)}), bf16[64,8,128]{2,1,0:T(8,128)(2,1)S(1)}, u32[]{:S(2)}, u32[]{:S(2)}) %all-to-all-start.2) | async-done | bytes 131104 | tf_op jit(solution)/shard_map/all_to_all | solution.py:428
  67.0 0.0 copy-start.3
  67.0 0.0 copy-start.4
  67.0 3.1 %attend.1 = (f32[1536,256]{1,0:T(8,128)S(1)}, f32[24,128]{1,0:T(8,128)S(1)}) custom-call(bf16[512,128]{1,0:T(8,128)(2,1)S(1)} %bitcast.18, bf16[1536,1024]{1,0:T(8,128)(2,1)S(1)} %probabilities.1.prob_ref, f32[1536,256]{1,0:T(8,128)} %conv.1.conv_hbm_ref), custom_call_target="tpu_custom_call" | custom-call | bytes 4194304 | tf_op jit(solution)/shard_map/attend/pallas_call | solution.py:49
  70.1 2.8 %collective-permute-start.6 = (f32[24,128]{1,0:T(8,128)S(1)}, f32[24,128]{1,0:T(8,128)S(1)}, u32[]{:S(2)}, u32[]{:S(2)}) collective-permute-start(f32[24,128]{1,0:T(8,128)S(1)} %get-tuple-element.37.s0_ref), channel_id=1, source_target_pairs={{0,3},{1,0},{2,1},{3,2},{4,7},{5,4},{6,5},{7,6},{8,11},{9,8},{10,9... | collective-permute-start | bytes 36872 | tf_op jit(solution)/shard_map/ppermute | solution.py:523
  73.0 0.8 collective-permute-start.5
  73.8 0.9 %collective-permute-start.4 = (f32[24,128]{1,0:T(8,128)S(1)}, f32[24,128]{1,0:T(8,128)S(1)}, u32[]{:S(2)}, u32[]{:S(2)}) collective-permute-start(f32[24,128]{1,0:T(8,128)S(1)} %get-tuple-element.37.s0_ref), channel_id=1, source_target_pairs={{0,1},{1,2},{2,3},{3,0},{4,5},{5,6},{6,7},{7,4},{8,9},{9,10},{10,1... | collective-permute-start | bytes 36872 | tf_op jit(solution)/shard_map/ppermute | solution.py:523
  74.7 0.0 collective-permute-done.6.s3_ref
  74.7 3.5 %collective-permute-done.5.s2_ref = f32[24,128]{1,0:T(8,128)S(1)} collective-permute-done((f32[24,128]{1,0:T(8,128)S(1)}, f32[24,128]{1,0:T(8,128)S(1)}, u32[]{:S(2)}, u32[]{:S(2)}) %collective-permute-start.5) | collective-permute-done | bytes 12320 | tf_op jit(solution)/shard_map/ppermute | solution.py:523
  78.2 0.5 collective-permute-done.4.s1_ref
  78.7 0.0 copy-done.3
  78.7 0.0 copy-done.4
  78.7 1.4 %norm.1 = bf16[1536,256]{1,0:T(8,128)(2,1)} custom-call(f32[24,128]{1,0:T(8,128)S(1)} %get-tuple-element.37.s0_ref, f32[24,128]{1,0:T(8,128)S(1)} %collective-permute-done.4.s1_ref, f32[24,128]{1,0:T(8,128)S(1)} %collective-permute-done.5.s2_ref, f32[24,128]{1,0:T(8,128)S(1)} %collective-permute-done.6.s3_ref, f32[1536,256]{1,0:T(8,128)S(1)} %get-tuple-element.38.sum_ref, ...), custom_call_target="tpu_custom_call" | custom-call | bytes 4194304 | tf_op jit(solution)/shard_map/norm/pallas_call | solution.py:49
  (1 shorter events, 0.0 us)
Async XLA Ops:
  0.0 15.7 %copy-start = (bf16[48,32,256]{2,1,0:T(8,128)(2,1)S(1)}, bf16[48,32,256]{2,1,0:T(8,128)(2,1)}, u32[]{:S(2)}) copy-start(bf16[48,32,256]{2,1,0:T(8,128)(2,1)} %v_ref.3) | copy-start | bytes 2359300
  3.6 21.5 %all-to-all-start = ((bf16[64,8,128]{2,1,0:T(8,128)(2,1)}), bf16[64,8,128]{2,1,0:T(8,128)(2,1)S(1)}, u32[]{:S(2)}, u32[]{:S(2)}) async-start(bf16[64,8,128]{2,1,0:T(8,128)(2,1)} %bitcast.2), calls=%async_computation | async-start | bytes 262144 | tf_op jit(solution)/shard_map/all_to_all | solution.py:428
  15.7 1.1 %copy-start.1 = (bf16[48,32,256]{2,1,0:T(8,128)(2,1)S(1)}, bf16[48,32,256]{2,1,0:T(8,128)(2,1)}, u32[]{:S(2)}) copy-start(bf16[48,32,256]{2,1,0:T(8,128)(2,1)} %param.8) | copy-start | bytes 2359300
  17.4 11.5 %collective-permute-start = (bf16[48,256]{1,0:T(8,128)(2,1)S(1)}, bf16[48,256]{1,0:T(8,128)(2,1)S(1)}, u32[]{:S(2)}, u32[]{:S(2)}) collective-permute-start(bf16[48,256]{1,0:T(8,128)(2,1)S(1)} %get-tuple-element.27), channel_id=1, source_target_pairs={{0,4},{4,8},{8,12},{12,16},{16,20},{20,24},{24,28},{28,32},{32,36}... | collective-permute-start | bytes 73736 | tf_op jit(solution)/shard_map/ppermute | solution.py:434
  19.5 9.5 %collective-permute-start.1 = (bf16[48,256]{1,0:T(8,128)(2,1)S(1)}, bf16[48,256]{1,0:T(8,128)(2,1)S(1)}, u32[]{:S(2)}, u32[]{:S(2)}) collective-permute-start(bf16[48,256]{1,0:T(8,128)(2,1)S(1)} %get-tuple-element.28), channel_id=1, source_target_pairs={{4,0},{8,4},{12,8},{16,12},{20,16},{24,20},{28,24},{32,28},{36,32}... | collective-permute-start | bytes 73736 | tf_op jit(solution)/shard_map/ppermute | solution.py:434
  25.1 32.5 %copy-start.2 = (f32[9,256]{1,0:T(8,128)S(1)}, f32[9,256]{1,0:T(8,128)}, u32[]{:S(2)}) copy-start(f32[9,256]{1,0:T(8,128)} %w_ref.1) | copy-start | bytes 27652
  28.9 21.0 %all-to-all-start.1 = ((bf16[64,16,128]{2,1,0:T(8,128)(2,1)}), bf16[64,16,128]{2,1,0:T(8,128)(2,1)S(1)}, u32[]{:S(2)}, u32[]{:S(2)}) async-start(bf16[64,16,128]{2,1,0:T(8,128)(2,1)} %bitcast.6), calls=%async_computation.1 | async-start | bytes 524288 | tf_op jit(solution)/shard_map/all_to_all | solution.py:428
  38.4 12.7 %collective-permute-start.3 = (bf16[48,256]{1,0:T(8,128)(2,1)S(1)}, bf16[48,256]{1,0:T(8,128)(2,1)S(1)}, u32[]{:S(2)}, u32[]{:S(2)}) collective-permute-start(bf16[48,256]{1,0:T(8,128)(2,1)S(1)} %get-tuple-element.32), channel_id=1, source_target_pairs={{64,0},{128,64},{192,128},{65,1},{129,65},{193,129},{66,2},{130,66... | collective-permute-start | bytes 73736 | tf_op jit(solution)/shard_map/ppermute | solution.py:434
  40.8 10.3 %collective-permute-start.2 = (bf16[48,256]{1,0:T(8,128)(2,1)S(1)}, bf16[48,256]{1,0:T(8,128)(2,1)S(1)}, u32[]{:S(2)}, u32[]{:S(2)}) collective-permute-start(bf16[48,256]{1,0:T(8,128)(2,1)S(1)} %get-tuple-element.33), channel_id=1, source_target_pairs={{0,64},{64,128},{128,192},{1,65},{65,129},{129,193},{2,66},{66,130... | collective-permute-start | bytes 73736 | tf_op jit(solution)/shard_map/ppermute | solution.py:434
  51.1 15.9 %all-to-all-start.2 = ((bf16[64,8,128]{2,1,0:T(8,128)(2,1)}), bf16[64,8,128]{2,1,0:T(8,128)(2,1)S(1)}, u32[]{:S(2)}, u32[]{:S(2)}) async-start(bf16[64,8,128]{2,1,0:T(8,128)(2,1)} %bitcast.8), calls=%async_computation.2 | async-start | bytes 262144 | tf_op jit(solution)/shard_map/all_to_all | solution.py:428
  67.0 11.7 %copy-start.3 = (f32[256]{0:T(256)S(1)}, f32[256]{0:T(256)}, u32[]{:S(2)}) copy-start(f32[256]{0:T(256)} %param.12) | copy-start | bytes 3076
  67.0 11.7 %copy-start.4 = (f32[256]{0:T(256)S(1)}, f32[256]{0:T(256)}, u32[]{:S(2)}) copy-start(f32[256]{0:T(256)} %param.13) | copy-start | bytes 3076
  70.1 4.5 %collective-permute-start.6 = (f32[24,128]{1,0:T(8,128)S(1)}, f32[24,128]{1,0:T(8,128)S(1)}, u32[]{:S(2)}, u32[]{:S(2)}) collective-permute-start(f32[24,128]{1,0:T(8,128)S(1)} %get-tuple-element.37.s0_ref), channel_id=1, source_target_pairs={{0,3},{1,0},{2,1},{3,2},{4,7},{5,4},{6,5},{7,6},{8,11},{9,8},{10,9... | collective-permute-start | bytes 36872 | tf_op jit(solution)/shard_map/ppermute | solution.py:523
  73.0 5.2 %collective-permute-start.5 = (f32[24,128]{1,0:T(8,128)S(1)}, f32[24,128]{1,0:T(8,128)S(1)}, u32[]{:S(2)}, u32[]{:S(2)}) collective-permute-start(f32[24,128]{1,0:T(8,128)S(1)} %get-tuple-element.37.s0_ref), channel_id=1, source_target_pairs={{0,2},{1,3},{2,0},{3,1},{4,6},{5,7},{6,4},{7,5},{8,10},{9,11},{10,... | collective-permute-start | bytes 36872 | tf_op jit(solution)/shard_map/ppermute | solution.py:523
  73.8 4.9 %collective-permute-start.4 = (f32[24,128]{1,0:T(8,128)S(1)}, f32[24,128]{1,0:T(8,128)S(1)}, u32[]{:S(2)}, u32[]{:S(2)}) collective-permute-start(f32[24,128]{1,0:T(8,128)S(1)} %get-tuple-element.37.s0_ref), channel_id=1, source_target_pairs={{0,1},{1,2},{2,3},{3,0},{4,5},{5,6},{6,7},{7,4},{8,9},{9,10},{10,1... | collective-permute-start | bytes 36872 | tf_op jit(solution)/shard_map/ppermute | solution.py:523

commit v4 on v3

--- a/solution.py
+++ b/solution.py
@@ -39,7 +39,7 @@
             else VMEM_SPEC
         ),
         scratch_shapes=list(scratch),
-        compiler_params=pltpu.CompilerParams(vmem_limit_bytes=12 * 1024 * 1024),
+        compiler_params=pltpu.CompilerParams(vmem_limit_bytes=20 * 1024 * 1024),
         cost_estimate=pl.CostEstimate(flops=0, bytes_accessed=nbytes, transcendentals=0),
         name=name,
     )
@@ -108,13 +108,11 @@
 def query_kernel(
     pos_ref,
     q_ref,
-    tq_ref,
     agents_ref,
     tab_r_ref,
     tab_c_ref,
     turn_ref,
     held_ref,
-    done_ref,
     spot_ref,
     sems,
 ):
@@ -155,45 +153,62 @@
         )
         copies[cell].wait()
         rotated = turned(held_ref[pl.ds(cell * step, step), :], matrix, cosine, sine)
-        part = pl.ds(cell * step, step)
-        done_ref[part, :] = rotated
-        copies[cell] = pltpu.make_async_copy(
-            done_ref.at[part, :], tq_ref.at[part, :], sems.at[AGR + 1 + cell]
-        )
-        copies[cell].start()
         mean = jnp.sum(rotated.astype(f32), 0, keepdims=True) / step
         means.append(mean.astype(bf16).astype(f32))
     packed = jnp.concatenate([m[:, :128] for m in means] + [m[:, 128:] for m in means], axis=0)
     agents_ref[...] = slots(packed)
-    for copy in copies:
-        copy.wait()
 
 
 def key_kernel(
     tab_r_ref,
     tab_c_ref,
     turn_ref,
+    v_ref,
     k_ref,
-    v_ref,
+    q_ref,
     tk_ref,
+    tq_ref,
     first_ref,
     last_ref,
     top_ref,
     bottom_ref,
+    k_held_ref,
+    q_held_ref,
+    done_ref,
+    v_held_ref,
+    sems,
 ):
-    top_ref[...] = v_ref[0]
-    bottom_ref[...] = v_ref[TR - 1]
-    first_ref[...] = v_ref[:, 0, :]
-    last_ref[...] = v_ref[:, TC - 1, :]
+    step = N // AGR
+    parts = [pl.ds(cell * step, step) for cell in range(AGR)]
+
+    def moves(source, target, first):
+        return [
+            pltpu.make_async_copy(source.at[part, :], target.at[part, :], sems.at[first + i])
+            for i, part in enumerate(parts)
+        ]
+
+    k_in, q_in = moves(k_ref, k_held_ref, 0), moves(q_ref, q_held_ref, AGR)
+    q_out = moves(done_ref, tq_ref, 2 * AGR)
+    v_in = pltpu.make_async_copy(v_ref, v_held_ref, sems.at[3 * AGR])
+    for copy in q_in + k_in + [v_in]:
+        copy.start()
     matrix = turn_ref[...]
-    step = N // AGR
-    for cell in range(AGR):
+    for cell, part in enumerate(parts):
         cosine, sine = cell_tables(
             tab_r_ref[0], tab_r_ref[1], tab_c_ref[0], tab_c_ref[1], cell * (TR // AGR), TR // AGR
         )
-        tk_ref[pl.ds(cell * step, step), :] = turned(
-            k_ref[pl.ds(cell * step, step), :], matrix, cosine, sine
-        )
+        q_in[cell].wait()
+        done_ref[part, :] = turned(q_held_ref[part, :], matrix, cosine, sine)
+        q_out[cell].start()
+        k_in[cell].wait()
+        tk_ref[part, :] = turned(k_held_ref[part, :], matrix, cosine, sine)
+    v_in.wait()
+    top_ref[...] = v_held_ref[0]
+    bottom_ref[...] = v_held_ref[TR - 1]
+    first_ref[...] = v_held_ref[:, 0, :]
+    last_ref[...] = v_held_ref[:, TC - 1, :]
+    for copy in q_out:
+        copy.wait()
 
 
 def agent_pairs(agents_ref, scale):
@@ -212,7 +227,9 @@
     return (lanes(dims) // HD) == parity
 
 
-def partial_kernel(agents_ref, tk_ref, v_ref, out_ref, score_ref):
+def partial_kernel(agents_ref, tk_ref, v_hbm_ref, out_ref, score_ref, v_ref, sem):
+    fetch = pltpu.make_async_copy(v_hbm_ref, v_ref, sem)
+    fetch.start()
     pairs = agent_pairs(agents_ref, 1.0 / math.sqrt(HD))
     chunk = 512
     for head in range(LOCAL_HEADS):
@@ -234,6 +251,8 @@
                 peak = piece if peak is None else jnp.maximum(peak, piece)
         peak = jnp.max(peak, 1, keepdims=True)
         acc = jnp.zeros((AGENTS, 128), f32)
+        if head == 0:
+            fetch.wait()
         for c in range(N // chunk):
             weights = jnp.exp(score_ref[:, pl.ds(c * chunk, chunk)] - peak).astype(bf16)
             block = v_ref[pl.ds(c * chunk, chunk), cols]
@@ -275,7 +294,24 @@
     out_ref[...] = slots(merged)
 
 
-def probability_kernel(agents_ref, tq_ref, prob_ref, held_ref, sems):
+def probability_kernel(
+    agents_ref,
+    tq_ref,
+    v_ref,
+    left_ref,
+    right_ref,
+    above_ref,
+    below_ref,
+    w_ref,
+    prob_ref,
+    conv_ref,
+    held_ref,
+    v_held_ref,
+    total_ref,
+    l_ref,
+    r_ref,
+    sems,
+):
     chunk = 256
 
     def fetch(c):
@@ -284,7 +320,15 @@
 
     for c in range(N // chunk):
         fetch(c).start()
+    v_in = pltpu.make_async_copy(v_ref, v_held_ref, sems.at[N // chunk])
+    conv_out = pltpu.make_async_copy(total_ref, conv_ref, sems.at[N // chunk + 1])
+    v_in.start()
     pairs = agent_pairs(agents_ref, 1.0 / math.sqrt(HD))
+    v_in.wait()
+    convolve(
+        v_held_ref, left_ref, right_ref, above_ref, below_ref, w_ref, total_ref, l_ref, r_ref
+    )
+    conv_out.start()
     ones = jnp.ones((AGENTS, 128), bf16)
     owns = []
     for head in range(LOCAL_HEADS):
@@ -309,6 +353,7 @@
         return carry
 
     lax.fori_loop(0, N // chunk, body, 0)
+    conv_out.wait()
 
 
 def line_kernel(top_ref, bottom_ref, left_ref, right_ref, up_ref, down_ref):
@@ -320,11 +365,15 @@
         out_ref[pl.ds(TC, 16), :] = tail.astype(bf16)
 
 
-def conv_kernel(v_ref, left_ref, right_ref, above_ref, below_ref, w_ref, out_ref, l_ref, r_ref):
+def convolve(v_ref, left_ref, right_ref, above_ref, below_ref, w_ref, out_ref, l_ref, r_ref):
     l_ref[...] = left_ref[...].astype(f32)
     r_ref[...] = right_ref[...].astype(f32)
     for half in range(2):
         cols = pl.ds(half * 128, 128)
+
+        def put(at, total):
+            out_ref[pl.ds(at, TC), cols] = total
+
         w = [jnp.broadcast_to(w_ref[t : t + 1, cols], (TC, 128)) for t in range(9)]
         column = lax.broadcasted_iota(jnp.int32, (TC, 128), 0)
 
@@ -346,7 +395,7 @@
                     at = (start + k - 1) * TC
                     if not isinstance(at, int):
                         at = pl.multiple_of(at, TC)
-                    out_ref[pl.ds(at, TC), cols] = a + t[2]
+                    put(at, a + t[2])
                 a, b = b + t[1], t[0]
             return a, b
 
@@ -356,19 +405,13 @@
         )
         tail = below_ref[pl.ds(TC, 16), cols].astype(f32)
         t = taps(below_ref[pl.ds(0, TC), cols], tail[0:1], tail[1:2])
-        out_ref[pl.ds((TR - 1) * TC, TC), cols] = a + t[2]
-
-
-def attend_kernel(av_ref, prob_ref, conv_hbm_ref, sum_ref, stat_ref, conv_ref, sems):
-    step = N // AGR
-    copies = []
-    for c in range(AGR):
-        part = pl.ds(c * step, step)
-        copies.append(
-            pltpu.make_async_copy(conv_hbm_ref.at[part, :], conv_ref.at[part, :], sems.at[c])
-        )
-        copies[c].start()
-    halves = []
+        put((TR - 1) * TC, a + t[2])
+
+
+def attend_kernel(av_ref, prob_ref, conv_hbm_ref, sum_ref, stat_ref, conv_ref, sem):
+    fetch = pltpu.make_async_copy(conv_hbm_ref, conv_ref, sem)
+    fetch.start()
+    eye = lax.broadcasted_iota(jnp.int32, (128, 128), 0) == lanes((128, 128))
     for pair in range(2):
         pieces = []
         for parity in range(2):
@@ -377,34 +420,30 @@
             own = half_mask(part.shape, parity)
             for piece in (part, other) if parity == 0 else (other, part):
                 pieces.append(jnp.where(own, piece, 0.0))
-        halves.append(jnp.concatenate(pieces, axis=0).astype(bf16))
-    eye = lax.broadcasted_iota(jnp.int32, (128, 128), 0) == lanes((128, 128))
-
-    for b in range(BLOCKS):
-        if b * 128 % step == 0:
-            copies[b * 128 // step].wait()
-        rows = pl.ds(b * 128, 128)
-        xs = []
-        for pair in range(2):
-            cols = pl.ds(pair * 128, 128)
-            attended = jnp.dot(
+        agent_values = jnp.concatenate(pieces, axis=0).astype(bf16)
+        for b in range(N // 512):
+            rows = pl.ds(b * 512, 512)
+            sum_ref[rows, pl.ds(pair * 128, 128)] = jnp.dot(
                 prob_ref[rows, pl.ds(pair * 2 * AGENTS, 2 * AGENTS)],
-                halves[pair],
+                agent_values,
                 preferred_element_type=f32,
             )
-            x = attended + conv_ref[rows, cols]
-            sum_ref[rows, cols] = x
-            xs.append(x)
-        mean = jnp.sum(xs[0] + xs[1], 1, keepdims=True) * (1.0 / CH)
-        c0, c1 = xs[0] - mean, xs[1] - mean
-        squares = jnp.sum(c0 * c0 + c1 * c1, 1, keepdims=True)
+    fetch.wait()
+    for b in range(BLOCKS):
+        rows = pl.ds(b * 128, 128)
+        x = sum_ref[rows, :] + conv_ref[rows, :]
+        sum_ref[rows, :] = x
+        mean = jnp.sum(x[:, :128] + x[:, 128:], 1, keepdims=True) * (1.0 / CH)
+        x = x - mean
+        x = x * x
+        squares = jnp.sum(x[:, :128] + x[:, 128:], 1, keepdims=True)
         stat_ref[b : b + 1, :] = jnp.sum(jnp.where(eye, mean, 0.0), 0, keepdims=True)
         stat_ref[BLOCKS + b : BLOCKS + b + 1, :] = jnp.sum(
             jnp.where(eye, squares, 0.0), 0, keepdims=True
         )
 
 
-def norm_kernel(s0_ref, s1_ref, s2_ref, s3_ref, sum_ref, gain_ref, bias_ref, out_ref):
+def norm_kernel(s0_ref, s1_ref, s2_ref, s3_ref, sum_ref, gain_ref, bias_ref, out_ref, done_ref, sems):
     stats = [s[...] for s in (s0_ref, s1_ref, s2_ref, s3_ref)]
     means = [s[:BLOCKS] for s in stats]
     mean = (means[0] + means[1] + means[2] + means[3]) * 0.25
@@ -412,15 +451,26 @@
     for m in means:
         squares = squares + CH * (m - mean) * (m - mean)
     scale = lax.rsqrt(squares * (1.0 / D) + epsilon)
+    step = N // AGR
+    copies = []
     for b in range(BLOCKS):
         rows = pl.ds(b * 128, 128)
         m = jnp.broadcast_to(mean[b : b + 1], (128, 128)).T
         s = jnp.broadcast_to(scale[b : b + 1], (128, 128)).T
         for half in range(2):
             cols = pl.ds(half * 128, 128)
-            out_ref[rows, cols] = (
+            done_ref[rows, cols] = (
                 (sum_ref[rows, cols] - m) * s * gain_ref[0:1, cols] + bias_ref[0:1, cols]
             ).astype(bf16)
+        if (b + 1) * 128 % step == 0:
+            part = pl.ds((b + 1) * 128 - step, step)
+            copy = pltpu.make_async_copy(
+                done_ref.at[part, :], out_ref.at[part, :], sems.at[len(copies)]
+            )
+            copy.start()
+            copies.append(copy)
+    for copy in copies:
+        copy.wait()
 
 
 def spread(x):
@@ -443,10 +493,9 @@
     k = keys.reshape(N, CH)
     v = values.reshape(N, CH)
     mb = 1 << 20
-    tq, packed, tab_r, tab_c, turn = call(
+    packed, tab_r, tab_c, turn = call(
         query_kernel,
         (
-            far((N, CH), bf16),
             shape((TILES * 8, 128), bf16),
             near((2, TR, CH), f32),
             near((2, TC, CH), f32),
@@ -455,29 +504,36 @@
         "hh",
         scratch=[
             pltpu.VMEM((N, CH), bf16),
-            pltpu.VMEM((N, CH), bf16),
             pltpu.VMEM((2, TC, TR), jnp.int32),
-            pltpu.SemaphoreType.DMA((2 * AGR + 1,)),
+            pltpu.SemaphoreType.DMA((AGR + 1,)),
         ],
-        out_spaces="h    ",
         nbytes=8 * mb,
-        name="turn_queries",
+        name="pool_queries",
     )(jnp.swapaxes(positions, 1, 2), q)
     agents = spread(packed)
-    tk, first, last, top, bottom = call(
+    tk, tq, first, last, top, bottom = call(
         key_kernel,
-        (near((N, CH), bf16),) + (near((TR, CH), bf16),) * 2 + (near((TC, CH), bf16),) * 2,
-        "vvv  ",
+        (near((N, CH), bf16), far((N, CH), bf16))
+        + (near((TR, CH), bf16),) * 2
+        + (near((TC, CH), bf16),) * 2,
+        "vvvhhh",
+        scratch=[pltpu.VMEM((N, CH), bf16)] * 3
+        + [pltpu.VMEM((TR, TC, CH), bf16), pltpu.SemaphoreType.DMA((3 * AGR + 1,))],
         nbytes=4 * mb,
+        out_spaces=" h    ",
         name="turn_keys",
-    )(tab_r, tab_c, turn, k, values)
+    )(tab_r, tab_c, turn, values, k, q)
     left = shift(last, "col", 1)
     right = shift(first, "col", -1)
     parts = call(
         partial_kernel,
         shape((TILES * ROWS, 128), bf16),
-        " v ",
-        scratch=[pltpu.VMEM((AGENTS, N), f32)],
+        " vh",
+        scratch=[
+            pltpu.VMEM((AGENTS, N), f32),
+            pltpu.VMEM((N, CH), bf16),
+            pltpu.SemaphoreType.DMA(()),
+        ],
         nbytes=10 * mb,
         name="partials",
     )(agents, tk, v)
@@ -494,27 +550,27 @@
     )
     merged = after(merged, above, below)
     agent_values = spread(merged)
-    prob = call(
+    prob, convolved = call(
         probability_kernel,
-        near((N, LOCAL_HEADS * AGENTS), bf16),
-        " h",
-        scratch=[pltpu.VMEM((N, CH), bf16), pltpu.SemaphoreType.DMA((N // 256,))],
-        nbytes=15 * mb,
+        (near((N, LOCAL_HEADS * AGENTS), bf16), far((N, CH), f32)),
+        " hhvvvv ",
+        scratch=[
+            pltpu.VMEM((N, CH), bf16),
+            pltpu.VMEM((TR, TC, CH), bf16),
+            pltpu.VMEM((N, CH), f32),
+            pltpu.VMEM((TR, CH), f32),
+            pltpu.VMEM((TR, CH), f32),
+            pltpu.SemaphoreType.DMA((N // 256 + 2,)),
+        ],
+        nbytes=20 * mb,
+        out_spaces=" h",
         name="probabilities",
-    )(agents, tq)
-    convolved = call(
-        conv_kernel,
-        far((N, CH), f32),
-        " vvvv ",
-        scratch=[pltpu.VMEM((TR, CH), f32), pltpu.VMEM((TR, CH), f32)],
-        nbytes=4 * mb,
-        name="conv",
-    )(values, left, right, above, below, conv_weight)
+    )(agents, tq, values, left, right, above, below, conv_weight)
     summed, stats = call(
         attend_kernel,
         (near((N, CH), f32), near((2 * BLOCKS, 128), f32)),
         " vh",
-        scratch=[pltpu.VMEM((N, CH), f32), pltpu.SemaphoreType.DMA((AGR,))],
+        scratch=[pltpu.VMEM((N, CH), f32), pltpu.SemaphoreType.DMA(())],
         nbytes=4 * mb,
         name="attend",
     )(agent_values, prob, convolved)
@@ -523,9 +579,17 @@
         lax.ppermute(stats, "head", [(i, (i + d) % heads) for i in range(heads)])
         for d in range(1, heads)
     ]
-    normed = call(norm_kernel, shape((N, CH), bf16), "v   v  ", nbytes=4 * mb, name="norm")(
+    normed = call(
+        norm_kernel,
+        (shape((N, CH), bf16),),
+        "v   v  ",
+        scratch=[pltpu.VMEM((N, CH), bf16), pltpu.SemaphoreType.DMA((AGR,))],
+        nbytes=4 * mb,
+        out_spaces="h",
+        name="norm",
+    )(
         stats, *others, summed, norm_gain.reshape(1, CH), norm_bias.reshape(1, CH)
-    )
+    )[0]
     return normed.reshape(TR, TC, CH)
 
 

time: 80.8 us -> 82.1 us (1.016)
  starting transfers between devices: 41.8 us -> 43.7 us
  Pallas kernels: 22.1 us -> 23.7 us
  waiting for transfers between devices: 15 us -> 13.6 us
  local copies, waits for them, and re-layouts: 1.14 us -> 0.01 us
    all_to_all x3, starting transfers between devices: 28.1 us -> 30 us  [spread(): return lax.all_to_all(slot, ('row', 'col'), 0, 0).reshape(x.shape)]
    pallas_call x9 -> x8, Pallas kernels: 22.1 us -> 23.7 us  [run(): fn(*[pltpu.with_memory_space_constraint(x, spaces[c]) if c in spaces else...]
    all_to_all x3, waiting for transfers between devices: 10.9 us -> 9.55 us  [spread(): return lax.all_to_all(slot, ('row', 'col'), 0, 0).reshape(x.shape)]
    unnamed x10 -> x6, local copies, waits for them, and re-layouts: 1.14 us -> 0.01 us
  transfers between devices with their start and end apart: 10 -> 10, of which waited for: 5 -> 5; matrix products, arithmetic and copies ran while one was open for 0% -> 0% of each run, Pallas kernels for 17% -> 21%
where the time goes in v4:
time: 82.1 us; the launch traced here: 81.3 us
  starting transfers between devices  43.7 us (53%)
  Pallas kernels  23.7 us (29%)
  waiting for transfers between devices  13.6 us (17%)
    all_to_all x3, starting transfers between devices, spread(): return lax.all_to_all(slot, ('row', 'col'), 0, 0).reshape(x.shape)  30 us
    pallas_call x8, Pallas kernels, run(): fn(*[pltpu.with_memory_space_constraint(x, spaces[c]) if c in spaces else...  23.7 us
    all_to_all x3, waiting for transfers between devices, spread(): return lax.all_to_all(slot, ('row', 'col'), 0, 0).reshape(x.shape)  9.55 us
    ppermute x4, starting transfers between devices, shift(): return lax.ppermute(x, axis, pairs)  9.19 us
    ppermute x3, starting transfers between devices, shards(): lax.ppermute(stats, 'head', [(i, (i + d) % heads) for i in range(heads)])  4.53 us
    ppermute x3, waiting for transfers between devices, shards(): lax.ppermute(stats, 'head', [(i, (i + d) % heads) for i in range(heads)])  4.02 us
  transfers between devices with their start and end apart: 10, of which 5 were waited for; matrix products, arithmetic and copies ran while one was open for 0% of the time, Pallas kernels for 21%

profile of v4, /device:TPU:8, one launch (start us, length us, event | category | flops | bytes accessed | tf_op | source)
XLA Modules:
  0.0 81.3 jit_solution(9436423694548062731)
XLA Ops:
  0.0 2.8 %pool_queries.1 = (bf16[512,128]{1,0:T(8,128)(2,1)}, f32[2,48,256]{2,1,0:T(8,128)S(1)}, f32[2,32,256]{2,1,0:T(8,128)S(1)}, bf16[256,256]{1,0:T(8,128)(2,1)S(1)}) custom-call(s32[2,32,48]{2,1,0:T(8,128)} %bitcast.23, bf16[1536,256]{1,0:T(8,128)(2,1)} %bitcast.20), custom_call_target="tpu_custom_call" | custom-call | bytes 8388608 | tf_op jit(solution)/shard_map/pool_queries/pallas_call | solution.py:49
  2.8 12.1 %all-to-all-start = ((bf16[64,8,128]{2,1,0:T(8,128)(2,1)}), bf16[64,8,128]{2,1,0:T(8,128)(2,1)S(1)}, u32[]{:S(2)}, u32[]{:S(2)}) async-start(bf16[64,8,128]{2,1,0:T(8,128)(2,1)} %bitcast.2), calls=%async_computation | async-start | bytes 262144 | tf_op jit(solution)/shard_map/all_to_all | solution.py:478
  14.9 3.6 %turn_keys.1 = (bf16[1536,256]{1,0:T(8,128)(2,1)S(1)}, bf16[1536,256]{1,0:T(8,128)(2,1)}, bf16[48,256]{1,0:T(8,128)(2,1)S(1)}, bf16[48,256]{1,0:T(8,128)(2,1)S(1...) custom-call(f32[2,48,256]{2,1,0:T(8,128)S(1)} %get-tuple-element.25.tab_r_ref, ...), custom_call_target="tpu_custom_call" | custom-call | bytes 4194304 | tf_op jit(solution)/shard_map/turn_keys/pallas_call | solution.py:49
  18.6 2.1 %collective-permute-start = (bf16[48,256]{1,0:T(8,128)(2,1)S(1)}, bf16[48,256]{1,0:T(8,128)(2,1)S(1)}, u32[]{:S(2)}, u32[]{:S(2)}) collective-permute-start(bf16[48,256]{1,0:T(8,128)(2,1)S(1)} %get-tuple-element.29), channel_id=1, source_target_pairs={{0,4},{4,8},{8,12},{12,16},{16,20},{20,24},{24,28},{28,32},{32,36}... | collective-permute-start | bytes 73736 | tf_op jit(solution)/shard_map/ppermute | solution.py:484
  20.6 1.3 %collective-permute-start.1 = (bf16[48,256]{1,0:T(8,128)(2,1)S(1)}, bf16[48,256]{1,0:T(8,128)(2,1)S(1)}, u32[]{:S(2)}, u32[]{:S(2)}) collective-permute-start(bf16[48,256]{1,0:T(8,128)(2,1)S(1)} %get-tuple-element.30), channel_id=1, source_target_pairs={{4,0},{8,4},{12,8},{16,12},{20,16},{24,20},{28,24},{32,28},{36,32}... | collective-permute-start | bytes 73736 | tf_op jit(solution)/shard_map/ppermute | solution.py:484
  21.9 2.4 %all-to-all-done = bf16[64,8,128]{2,1,0:T(8,128)(2,1)S(1)} async-done(((bf16[64,8,128]{2,1,0:T(8,128)(2,1)}), bf16[64,8,128]{2,1,0:T(8,128)(2,1)S(1)}, u32[]{:S(2)}, u32[]{:S(2)}) %all-to-all-start) | async-done | bytes 131104 | tf_op jit(solution)/shard_map/all_to_all | solution.py:478
  24.3 0.0 copy-start
  24.3 4.6 %partials.1 = bf16[1024,128]{1,0:T(8,128)(2,1)} custom-call(bf16[512,128]{1,0:T(8,128)(2,1)S(1)} %bitcast.13, bf16[1536,256]{1,0:T(8,128)(2,1)S(1)} %get-tuple-element.28.tk_ref, bf16[1536,256]{1,0:T(8,128)(2,1)} %bitcast.19), custom_call_target="tpu_custom_call" | custom-call | bytes 10485760 | tf_op jit(solution)/shard_map/partials/pallas_call | solution.py:49
  29.0 0.0 collective-permute-done.left_ref
  29.0 0.0 collective-permute-done.1.right_ref
  29.0 11.4 %all-to-all-start.1 = ((bf16[64,16,128]{2,1,0:T(8,128)(2,1)}), bf16[64,16,128]{2,1,0:T(8,128)(2,1)S(1)}, u32[]{:S(2)}, u32[]{:S(2)}) async-start(bf16[64,16,128]{2,1,0:T(8,128)(2,1)} %bitcast.6), calls=%async_computation.1 | async-start | bytes 524288 | tf_op jit(solution)/shard_map/all_to_all | solution.py:478
  40.4 2.4 %collective-permute-start.3 = (bf16[48,256]{1,0:T(8,128)(2,1)S(1)}, bf16[48,256]{1,0:T(8,128)(2,1)S(1)}, u32[]{:S(2)}, u32[]{:S(2)}) collective-permute-start(bf16[48,256]{1,0:T(8,128)(2,1)S(1)} %get-tuple-element.34), channel_id=1, source_target_pairs={{64,0},{128,64},{192,128},{65,1},{129,65},{193,129},{66,2},{130,66... | collective-permute-start | bytes 73736 | tf_op jit(solution)/shard_map/ppermute | solution.py:484
  42.8 3.5 %collective-permute-start.2 = (bf16[48,256]{1,0:T(8,128)(2,1)S(1)}, bf16[48,256]{1,0:T(8,128)(2,1)S(1)}, u32[]{:S(2)}, u32[]{:S(2)}) collective-permute-start(bf16[48,256]{1,0:T(8,128)(2,1)S(1)} %get-tuple-element.35), channel_id=1, source_target_pairs={{0,64},{64,128},{128,192},{1,65},{65,129},{129,193},{2,66},{66,130... | collective-permute-start | bytes 73736 | tf_op jit(solution)/shard_map/ppermute | solution.py:484
  46.3 5.7 %all-to-all-done.1 = bf16[64,16,128]{2,1,0:T(8,128)(2,1)S(1)} async-done(((bf16[64,16,128]{2,1,0:T(8,128)(2,1)}), bf16[64,16,128]{2,1,0:T(8,128)(2,1)S(1)}, u32[]{:S(2)}, u32[]{:S(2)}) %all-to-all-start.1) | async-done | bytes 262176 | tf_op jit(solution)/shard_map/all_to_all | solution.py:478
  51.9 1.1 %merge.1 = bf16[512,128]{1,0:T(8,128)(2,1)} custom-call(bf16[1024,128]{1,0:T(8,128)(2,1)S(1)} %bitcast.15), custom_call_target="tpu_custom_call" | custom-call | bytes 2097152 | tf_op jit(solution)/shard_map/merge/pallas_call | solution.py:49
  53.1 0.0 collective-permute-done.3.below_ref
  53.1 0.0 collective-permute-done.2.above_ref
  53.1 6.5 %all-to-all-start.2 = ((bf16[64,8,128]{2,1,0:T(8,128)(2,1)}), bf16[64,8,128]{2,1,0:T(8,128)(2,1)S(1)}, u32[]{:S(2)}, u32[]{:S(2)}) async-start(bf16[64,8,128]{2,1,0:T(8,128)(2,1)} %bitcast.8), calls=%async_computation.2 | async-start | bytes 262144 | tf_op jit(solution)/shard_map/all_to_all | solution.py:478
  59.6 0.0 copy-done
  59.6 7.9 %probabilities.1 = (bf16[1536,1024]{1,0:T(8,128)(2,1)S(1)}, f32[1536,256]{1,0:T(8,128)}) custom-call(bf16[512,128]{1,0:T(8,128)(2,1)S(1)} %bitcast.14, bf16[1536,256]{1,0:T(8,128)(2,1)} %get-tuple-element.38.tq_ref, bf16[48,32,256]{2,1,0:T(8,128)(2,1)} %v_ref.3, bf16[48,256]{1,0:T(8,128)(2,1)S(1)} %collective-permute-done.left_ref, ...), custom_call_target="tpu_custom_call" | custom-call | bytes 20971520 | tf_op jit(solution)/shard_map/probabilities/pallas_call | solution.py:49
  67.5 1.5 %all-to-all-done.2 = bf16[64,8,128]{2,1,0:T(8,128)(2,1)S(1)} async-done(((bf16[64,8,128]{2,1,0:T(8,128)(2,1)}), bf16[64,8,128]{2,1,0:T(8,128)(2,1)S(1)}, u32[]{:S(2)}, u32[]{:S(2)}) %all-to-all-start.2) | async-done | bytes 131104 | tf_op jit(solution)/shard_map/all_to_all | solution.py:478
  69.0 0.0 copy-start.1
  69.0 0.0 copy-start.2
  69.0 2.4 %attend.1 = (f32[1536,256]{1,0:T(8,128)S(1)}, f32[24,128]{1,0:T(8,128)S(1)}) custom-call(bf16[512,128]{1,0:T(8,128)(2,1)S(1)} %bitcast.16, bf16[1536,1024]{1,0:T(8,128)(2,1)S(1)} %get-tuple-element.39.prob_ref, f32[1536,256]{1,0:T(8,128)} %get-tuple-element.40.conv_hbm_ref), custom_call_target="tpu_custom_call" | custom-call | bytes 4194304 | tf_op jit(solution)/shard_map/attend/pallas_call | solution.py:49
  71.4 2.8 %collective-permute-start.6 = (f32[24,128]{1,0:T(8,128)S(1)}, f32[24,128]{1,0:T(8,128)S(1)}, u32[]{:S(2)}, u32[]{:S(2)}) collective-permute-start(f32[24,128]{1,0:T(8,128)S(1)} %get-tuple-element.41.s0_ref), channel_id=1, source_target_pairs={{0,3},{1,0},{2,1},{3,2},{4,7},{5,4},{6,5},{7,6},{8,11},{9,8},{10,9... | collective-permute-start | bytes 36872 | tf_op jit(solution)/shard_map/ppermute | solution.py:579
  74.2 0.8 collective-permute-start.5
  75.0 0.9 %collective-permute-start.4 = (f32[24,128]{1,0:T(8,128)S(1)}, f32[24,128]{1,0:T(8,128)S(1)}, u32[]{:S(2)}, u32[]{:S(2)}) collective-permute-start(f32[24,128]{1,0:T(8,128)S(1)} %get-tuple-element.41.s0_ref), channel_id=1, source_target_pairs={{0,1},{1,2},{2,3},{3,0},{4,5},{5,6},{6,7},{7,4},{8,9},{9,10},{10,1... | collective-permute-start | bytes 36872 | tf_op jit(solution)/shard_map/ppermute | solution.py:579
  75.9 0.0 collective-permute-done.6.s3_ref
  75.9 3.5 %collective-permute-done.5.s2_ref = f32[24,128]{1,0:T(8,128)S(1)} collective-permute-done((f32[24,128]{1,0:T(8,128)S(1)}, f32[24,128]{1,0:T(8,128)S(1)}, u32[]{:S(2)}, u32[]{:S(2)}) %collective-permute-start.5) | collective-permute-done | bytes 12320 | tf_op jit(solution)/shard_map/ppermute | solution.py:579
  79.4 0.5 collective-permute-done.4.s1_ref
  79.9 0.0 copy-done.1
  79.9 0.0 copy-done.2
  79.9 1.2 %norm.1 = bf16[1536,256]{1,0:T(8,128)(2,1)} custom-call(f32[24,128]{1,0:T(8,128)S(1)} %get-tuple-element.41.s0_ref, f32[24,128]{1,0:T(8,128)S(1)} %collective-permute-done.4.s1_ref, f32[24,128]{1,0:T(8,128)S(1)} %collective-permute-done.5.s2_ref, f32[24,128]{1,0:T(8,128)S(1)} %collective-permute-done.6.s3_ref, f32[1536,256]{1,0:T(8,128)S(1)} %get-tuple-element.42.sum_ref, ...), custom_call_target="tpu_custom_call" | custom-call | bytes 4194304 | tf_op jit(solution)/shard_map/norm/pallas_call | solution.py:49
  (1 shorter events, 0.0 us)
Async XLA Ops:
  2.8 21.5 %all-to-all-start = ((bf16[64,8,128]{2,1,0:T(8,128)(2,1)}), bf16[64,8,128]{2,1,0:T(8,128)(2,1)S(1)}, u32[]{:S(2)}, u32[]{:S(2)}) async-start(bf16[64,8,128]{2,1,0:T(8,128)(2,1)} %bitcast.2), calls=%async_computation | async-start | bytes 262144 | tf_op jit(solution)/shard_map/all_to_all | solution.py:478
  18.6 10.4 %collective-permute-start = (bf16[48,256]{1,0:T(8,128)(2,1)S(1)}, bf16[48,256]{1,0:T(8,128)(2,1)S(1)}, u32[]{:S(2)}, u32[]{:S(2)}) collective-permute-start(bf16[48,256]{1,0:T(8,128)(2,1)S(1)} %get-tuple-element.29), channel_id=1, source_target_pairs={{0,4},{4,8},{8,12},{12,16},{16,20},{20,24},{24,28},{28,32},{32,36}... | collective-permute-start | bytes 73736 | tf_op jit(solution)/shard_map/ppermute | solution.py:484
  20.6 8.4 %collective-permute-start.1 = (bf16[48,256]{1,0:T(8,128)(2,1)S(1)}, bf16[48,256]{1,0:T(8,128)(2,1)S(1)}, u32[]{:S(2)}, u32[]{:S(2)}) collective-permute-start(bf16[48,256]{1,0:T(8,128)(2,1)S(1)} %get-tuple-element.30), channel_id=1, source_target_pairs={{4,0},{8,4},{12,8},{16,12},{20,16},{24,20},{28,24},{32,28},{36,32}... | collective-permute-start | bytes 73736 | tf_op jit(solution)/shard_map/ppermute | solution.py:484
  24.3 35.3 %copy-start = (f32[9,256]{1,0:T(8,128)S(1)}, f32[9,256]{1,0:T(8,128)}, u32[]{:S(2)}) copy-start(f32[9,256]{1,0:T(8,128)} %w_ref.1) | copy-start | bytes 27652
  29.0 22.9 %all-to-all-start.1 = ((bf16[64,16,128]{2,1,0:T(8,128)(2,1)}), bf16[64,16,128]{2,1,0:T(8,128)(2,1)S(1)}, u32[]{:S(2)}, u32[]{:S(2)}) async-start(bf16[64,16,128]{2,1,0:T(8,128)(2,1)} %bitcast.6), calls=%async_computation.1 | async-start | bytes 524288 | tf_op jit(solution)/shard_map/all_to_all | solution.py:478
  40.4 12.7 %collective-permute-start.3 = (bf16[48,256]{1,0:T(8,128)(2,1)S(1)}, bf16[48,256]{1,0:T(8,128)(2,1)S(1)}, u32[]{:S(2)}, u32[]{:S(2)}) collective-permute-start(bf16[48,256]{1,0:T(8,128)(2,1)S(1)} %get-tuple-element.34), channel_id=1, source_target_pairs={{64,0},{128,64},{192,128},{65,1},{129,65},{193,129},{66,2},{130,66... | collective-permute-start | bytes 73736 | tf_op jit(solution)/shard_map/ppermute | solution.py:484
  42.8 10.3 %collective-permute-start.2 = (bf16[48,256]{1,0:T(8,128)(2,1)S(1)}, bf16[48,256]{1,0:T(8,128)(2,1)S(1)}, u32[]{:S(2)}, u32[]{:S(2)}) collective-permute-start(bf16[48,256]{1,0:T(8,128)(2,1)S(1)} %get-tuple-element.35), channel_id=1, source_target_pairs={{0,64},{64,128},{128,192},{1,65},{65,129},{129,193},{2,66},{66,130... | collective-permute-start | bytes 73736 | tf_op jit(solution)/shard_map/ppermute | solution.py:484
  53.1 15.9 %all-to-all-start.2 = ((bf16[64,8,128]{2,1,0:T(8,128)(2,1)}), bf16[64,8,128]{2,1,0:T(8,128)(2,1)S(1)}, u32[]{:S(2)}, u32[]{:S(2)}) async-start(bf16[64,8,128]{2,1,0:T(8,128)(2,1)} %bitcast.8), calls=%async_computation.2 | async-start | bytes 262144 | tf_op jit(solution)/shard_map/all_to_all | solution.py:478
  69.0 10.9 %copy-start.1 = (f32[256]{0:T(256)S(1)}, f32[256]{0:T(256)}, u32[]{:S(2)}) copy-start(f32[256]{0:T(256)} %param.12) | copy-start | bytes 3076
  69.0 10.9 %copy-start.2 = (f32[256]{0:T(256)S(1)}, f32[256]{0:T(256)}, u32[]{:S(2)}) copy-start(f32[256]{0:T(256)} %param.13) | copy-start | bytes 3076
  71.4 4.5 %collective-permute-start.6 = (f32[24,128]{1,0:T(8,128)S(1)}, f32[24,128]{1,0:T(8,128)S(1)}, u32[]{:S(2)}, u32[]{:S(2)}) collective-permute-start(f32[24,128]{1,0:T(8,128)S(1)} %get-tuple-element.41.s0_ref), channel_id=1, source_target_pairs={{0,3},{1,0},{2,1},{3,2},{4,7},{5,4},{6,5},{7,6},{8,11},{9,8},{10,9... | collective-permute-start | bytes 36872 | tf_op jit(solution)/shard_map/ppermute | solution.py:579
  74.2 5.2 %collective-permute-start.5 = (f32[24,128]{1,0:T(8,128)S(1)}, f32[24,128]{1,0:T(8,128)S(1)}, u32[]{:S(2)}, u32[]{:S(2)}) collective-permute-start(f32[24,128]{1,0:T(8,128)S(1)} %get-tuple-element.41.s0_ref), channel_id=1, source_target_pairs={{0,2},{1,3},{2,0},{3,1},{4,6},{5,7},{6,4},{7,5},{8,10},{9,11},{10,... | collective-permute-start | bytes 36872 | tf_op jit(solution)/shard_map/ppermute | solution.py:579
  75.0 4.9 %collective-permute-start.4 = (f32[24,128]{1,0:T(8,128)S(1)}, f32[24,128]{1,0:T(8,128)S(1)}, u32[]{:S(2)}, u32[]{:S(2)}) collective-permute-start(f32[24,128]{1,0:T(8,128)S(1)} %get-tuple-element.41.s0_ref), channel_id=1, source_target_pairs={{0,1},{1,2},{2,3},{3,0},{4,5},{5,6},{6,7},{7,4},{8,9},{9,10},{10,1... | collective-permute-start | bytes 36872 | tf_op jit(solution)/shard_map/ppermute | solution.py:579

commit v5 on v4

--- a/solution.py
+++ b/solution.py
@@ -90,7 +90,14 @@
     return (x.astype(f32) * cosine + swapped * sine).astype(bf16)
 
 
-def cell_tables(cos_r, sin_r, cos_c, sin_c, first, rows):
+def split_tables(cosines, sines):
+    cosines = jnp.concatenate([cosines, cosines], axis=1)
+    sines = jnp.concatenate([sines, sines], axis=1)
+    return cosines[:TR], sines[:TR], cosines[TR:], sines[TR:]
+
+
+def cell_tables(tables, first, rows):
+    cos_r, sin_r, cos_c, sin_c = tables
     cosine = jnp.concatenate(
         [cos_r[first + i : first + i + 1, :] * cos_c for i in range(rows)], axis=0
     )
@@ -109,9 +116,7 @@
     pos_ref,
     q_ref,
     agents_ref,
-    tab_r_ref,
-    tab_c_ref,
-    turn_ref,
+    tab_ref,
     held_ref,
     spot_ref,
     sems,
@@ -126,7 +131,6 @@
         copy.start()
         copies.append(copy)
     matrix = turn_matrix()
-    turn_ref[...] = matrix
     lane = lanes((1, 128)) % HD
     power = jnp.exp((lane % 16).astype(f32) * f32(-math.log(100.0) / 16))
     freq_r = jnp.where(lane < 32, power, 0.0)
@@ -140,17 +144,12 @@
     row_pos = jnp.sum(jnp.where(eye, jnp.broadcast_to(row_line, (TR, TR)), 0.0), 1, keepdims=True)
     angles = jnp.concatenate([row_pos * freq_r, col_pos * freq_c], axis=0)
     sines, cosines = sin_cos(angles)
-    sines = jnp.concatenate([sines, sines], axis=1)
-    cosines = jnp.concatenate([cosines, cosines], axis=1)
-    tab_r_ref[0] = cosines[:TR]
-    tab_r_ref[1] = sines[:TR]
-    tab_c_ref[0] = cosines[TR:]
-    tab_c_ref[1] = sines[TR:]
+    tab_ref[0] = cosines
+    tab_ref[1] = sines
+    tables = split_tables(cosines, sines)
     means = []
     for cell in range(AGR):
-        cosine, sine = cell_tables(
-            cosines[:TR], sines[:TR], cosines[TR:], sines[TR:], cell * (TR // AGR), TR // AGR
-        )
+        cosine, sine = cell_tables(tables, cell * (TR // AGR), TR // AGR)
         copies[cell].wait()
         rotated = turned(held_ref[pl.ds(cell * step, step), :], matrix, cosine, sine)
         mean = jnp.sum(rotated.astype(f32), 0, keepdims=True) / step
@@ -160,55 +159,40 @@
 
 
 def key_kernel(
-    tab_r_ref,
-    tab_c_ref,
-    turn_ref,
+    tab_hbm_ref,
     v_ref,
     k_ref,
-    q_ref,
     tk_ref,
-    tq_ref,
     first_ref,
     last_ref,
     top_ref,
     bottom_ref,
-    k_held_ref,
-    q_held_ref,
-    done_ref,
-    v_held_ref,
+    tab_ref,
+    held_ref,
     sems,
 ):
     step = N // AGR
-    parts = [pl.ds(cell * step, step) for cell in range(AGR)]
-
-    def moves(source, target, first):
-        return [
-            pltpu.make_async_copy(source.at[part, :], target.at[part, :], sems.at[first + i])
-            for i, part in enumerate(parts)
-        ]
-
-    k_in, q_in = moves(k_ref, k_held_ref, 0), moves(q_ref, q_held_ref, AGR)
-    q_out = moves(done_ref, tq_ref, 2 * AGR)
-    v_in = pltpu.make_async_copy(v_ref, v_held_ref, sems.at[3 * AGR])
-    for copy in q_in + k_in + [v_in]:
-        copy.start()
-    matrix = turn_ref[...]
-    for cell, part in enumerate(parts):
-        cosine, sine = cell_tables(
-            tab_r_ref[0], tab_r_ref[1], tab_c_ref[0], tab_c_ref[1], cell * (TR // AGR), TR // AGR
+    table = pltpu.make_async_copy(tab_hbm_ref, tab_ref, sems.at[AGR])
+    table.start()
+    copies = []
+    for cell in range(AGR):
+        part = pl.ds(cell * step, step)
+        copies.append(
+            pltpu.make_async_copy(k_ref.at[part, :], held_ref.at[part, :], sems.at[cell])
         )
-        q_in[cell].wait()
-        done_ref[part, :] = turned(q_held_ref[part, :], matrix, cosine, sine)
-        q_out[cell].start()
-        k_in[cell].wait()
-        tk_ref[part, :] = turned(k_held_ref[part, :], matrix, cosine, sine)
-    v_in.wait()
-    top_ref[...] = v_held_ref[0]
-    bottom_ref[...] = v_held_ref[TR - 1]
-    first_ref[...] = v_held_ref[:, 0, :]
-    last_ref[...] = v_held_ref[:, TC - 1, :]
-    for copy in q_out:
-        copy.wait()
+        copies[cell].start()
+    top_ref[...] = v_ref[0]
+    bottom_ref[...] = v_ref[TR - 1]
+    first_ref[...] = v_ref[:, 0, :]
+    last_ref[...] = v_ref[:, TC - 1, :]
+    matrix = turn_matrix()
+    table.wait()
+    tables = split_tables(tab_ref[0], tab_ref[1])
+    for cell in range(AGR):
+        part = pl.ds(cell * step, step)
+        cosine, sine = cell_tables(tables, cell * (TR // AGR), TR // AGR)
+        copies[cell].wait()
+        tk_ref[part, :] = turned(held_ref[part, :], matrix, cosine, sine)
 
 
 def agent_pairs(agents_ref, scale):
@@ -227,9 +211,7 @@
     return (lanes(dims) // HD) == parity
 
 
-def partial_kernel(agents_ref, tk_ref, v_hbm_ref, out_ref, score_ref, v_ref, sem):
-    fetch = pltpu.make_async_copy(v_hbm_ref, v_ref, sem)
-    fetch.start()
+def partial_kernel(agents_ref, tk_ref, v_ref, out_ref, score_ref):
     pairs = agent_pairs(agents_ref, 1.0 / math.sqrt(HD))
     chunk = 512
     for head in range(LOCAL_HEADS):
@@ -251,8 +233,6 @@
                 peak = piece if peak is None else jnp.maximum(peak, piece)
         peak = jnp.max(peak, 1, keepdims=True)
         acc = jnp.zeros((AGENTS, 128), f32)
-        if head == 0:
-            fetch.wait()
         for c in range(N // chunk):
             weights = jnp.exp(score_ref[:, pl.ds(c * chunk, chunk)] - peak).astype(bf16)
             block = v_ref[pl.ds(c * chunk, chunk), cols]
@@ -294,41 +274,20 @@
     out_ref[...] = slots(merged)
 
 
-def probability_kernel(
-    agents_ref,
-    tq_ref,
-    v_ref,
-    left_ref,
-    right_ref,
-    above_ref,
-    below_ref,
-    w_ref,
-    prob_ref,
-    conv_ref,
-    held_ref,
-    v_held_ref,
-    total_ref,
-    l_ref,
-    r_ref,
-    sems,
-):
+def probability_kernel(agents_ref, tab_hbm_ref, q_ref, prob_ref, tab_ref, held_ref, sems):
     chunk = 256
+    table = pltpu.make_async_copy(tab_hbm_ref, tab_ref, sems.at[N // chunk])
+    table.start()
 
     def fetch(c):
         rows = pl.ds(pl.multiple_of(c * chunk, chunk), chunk)
-        return pltpu.make_async_copy(tq_ref.at[rows, :], held_ref.at[rows, :], sems.at[c])
+        return pltpu.make_async_copy(q_ref.at[rows, :], held_ref.at[rows, :], sems.at[c])
 
     for c in range(N // chunk):
         fetch(c).start()
-    v_in = pltpu.make_async_copy(v_ref, v_held_ref, sems.at[N // chunk])
-    conv_out = pltpu.make_async_copy(total_ref, conv_ref, sems.at[N // chunk + 1])
-    v_in.start()
     pairs = agent_pairs(agents_ref, 1.0 / math.sqrt(HD))
-    v_in.wait()
-    convolve(
-        v_held_ref, left_ref, right_ref, above_ref, below_ref, w_ref, total_ref, l_ref, r_ref
-    )
-    conv_out.start()
+    matrix = turn_matrix()
+    table.wait()
     ones = jnp.ones((AGENTS, 128), bf16)
     owns = []
     for head in range(LOCAL_HEADS):
@@ -338,9 +297,15 @@
     def body(c, carry):
         fetch(c).wait()
         rows = pl.ds(pl.multiple_of(c * chunk, chunk), chunk)
+        lines = pl.ds(pl.multiple_of(c * (chunk // TC), chunk // TC), chunk // TC)
+        near_rows = [tab_ref[i, lines, :] for i in range(2)]
+        near_cols = [tab_ref[i, pl.ds(TR, TC), :] for i in range(2)]
+        tables = [jnp.concatenate([t, t], axis=1) for t in near_rows + near_cols]
+        cosine, sine = cell_tables(tables, 0, chunk // TC)
+        queries = turned(held_ref[rows, :], matrix, cosine, sine)
         for head in range(LOCAL_HEADS):
             scores = lax.dot_general(
-                held_ref[rows, pl.ds(head // 2 * 128, 128)],
+                queries[:, head // 2 * 128 : head // 2 * 128 + 128],
                 owns[head],
                 (((1,), (1,)), ((), ())),
                 preferred_element_type=f32,
@@ -353,7 +318,6 @@
         return carry
 
     lax.fori_loop(0, N // chunk, body, 0)
-    conv_out.wait()
 
 
 def line_kernel(top_ref, bottom_ref, left_ref, right_ref, up_ref, down_ref):
@@ -365,7 +329,22 @@
         out_ref[pl.ds(TC, 16), :] = tail.astype(bf16)
 
 
-def convolve(v_ref, left_ref, right_ref, above_ref, below_ref, w_ref, out_ref, l_ref, r_ref):
+def conv_kernel(
+    v_hbm_ref,
+    left_ref,
+    right_ref,
+    above_ref,
+    below_ref,
+    w_ref,
+    out_ref,
+    v_ref,
+    l_ref,
+    r_ref,
+    sem,
+):
+    fetch = pltpu.make_async_copy(v_hbm_ref, v_ref, sem)
+    fetch.start()
+    fetch.wait()
     l_ref[...] = left_ref[...].astype(f32)
     r_ref[...] = right_ref[...].astype(f32)
     for half in range(2):
@@ -493,14 +472,9 @@
     k = keys.reshape(N, CH)
     v = values.reshape(N, CH)
     mb = 1 << 20
-    packed, tab_r, tab_c, turn = call(
+    packed, table = call(
         query_kernel,
-        (
-            shape((TILES * 8, 128), bf16),
-            near((2, TR, CH), f32),
-            near((2, TC, CH), f32),
-            near((CH, CH), bf16),
-        ),
+        (far((TILES * 8, 128), bf16), far((2, TR + TC, 128), f32)),
         "hh",
         scratch=[
             pltpu.VMEM((N, CH), bf16),
@@ -511,61 +485,65 @@
         name="pool_queries",
     )(jnp.swapaxes(positions, 1, 2), q)
     agents = spread(packed)
-    tk, tq, first, last, top, bottom = call(
+    held_table = pltpu.VMEM((2, TR + TC, 128), f32)
+    tk, first, last, top, bottom = call(
         key_kernel,
-        (near((N, CH), bf16), far((N, CH), bf16))
+        (near((N, CH), bf16),)
         + (near((TR, CH), bf16),) * 2
         + (near((TC, CH), bf16),) * 2,
-        "vvvhhh",
-        scratch=[pltpu.VMEM((N, CH), bf16)] * 3
-        + [pltpu.VMEM((TR, TC, CH), bf16), pltpu.SemaphoreType.DMA((3 * AGR + 1,))],
+        "h h",
+        scratch=[held_table, pltpu.VMEM((N, CH), bf16), pltpu.SemaphoreType.DMA((AGR + 1,))],
         nbytes=4 * mb,
-        out_spaces=" h    ",
         name="turn_keys",
-    )(tab_r, tab_c, turn, values, k, q)
+    )(table, values, k)
     left = shift(last, "col", 1)
     right = shift(first, "col", -1)
     parts = call(
         partial_kernel,
-        shape((TILES * ROWS, 128), bf16),
-        " vh",
-        scratch=[
-            pltpu.VMEM((AGENTS, N), f32),
-            pltpu.VMEM((N, CH), bf16),
-            pltpu.SemaphoreType.DMA(()),
-        ],
+        far((TILES * ROWS, 128), bf16),
+        " v ",
+        scratch=[pltpu.VMEM((AGENTS, N), f32)],
         nbytes=10 * mb,
         name="partials",
     )(agents, tk, v)
-    parts = after(parts, left, right)
-    received = spread(parts)
     up, down = call(
-        line_kernel, (near((TC + 16, CH), bf16),) * 2, "vvvv", nbytes=mb // 4, name="lines"
-    )(top, bottom, left, right)
+        line_kernel,
+        (near((TC + 16, CH), bf16),) * 2,
+        "vv  ",
+        nbytes=mb // 4,
+        name="lines",
+    )(top, bottom, *lax.optimization_barrier((left, right, agents))[:2])
     above = shift(down, "row", 1)
     below = shift(up, "row", -1)
-    received = after(received, up, down)
-    merged = call(merge_kernel, shape((TILES * 8, 128), bf16), " ", nbytes=2 * mb, name="merge")(
+    parts = after(parts, above, below)
+    received = spread(parts)
+    prob = call(
+        probability_kernel,
+        near((N, LOCAL_HEADS * AGENTS), bf16),
+        " hh",
+        scratch=[
+            held_table,
+            pltpu.VMEM((N, CH), bf16),
+            pltpu.SemaphoreType.DMA((N // 256 + 1,)),
+        ],
+        nbytes=20 * mb,
+        name="probabilities",
+    )(agents, table, q)
+    received = after(received, prob)
+    merged = call(merge_kernel, far((TILES * 8, 128), bf16), " ", nbytes=2 * mb, name="merge")(
         received
     )
-    merged = after(merged, above, below)
     agent_values = spread(merged)
-    prob, convolved = call(
-        probability_kernel,
-        (near((N, LOCAL_HEADS * AGENTS), bf16), far((N, CH), f32)),
-        " hhvvvv ",
-        scratch=[
-            pltpu.VMEM((N, CH), bf16),
-            pltpu.VMEM((TR, TC, CH), bf16),
-            pltpu.VMEM((N, CH), f32),
-            pltpu.VMEM((TR, CH), f32),
-            pltpu.VMEM((TR, CH), f32),
-            pltpu.SemaphoreType.DMA((N // 256 + 2,)),
-        ],
-        nbytes=20 * mb,
-        out_spaces=" h",
-        name="probabilities",
-    )(agents, tq, values, left, right, above, below, conv_weight)
+    convolved = call(
+        conv_kernel,
+        far((N, CH), f32),
+        "h     ",
+        scratch=[pltpu.VMEM((TR, TC, CH), bf16)]
+        + [pltpu.VMEM((TR, CH), f32)] * 2
+        + [pltpu.SemaphoreType.DMA(())],
+        nbytes=6 * mb,
+        name="conv",
+    )(values, left, right, above, below, conv_weight)
     summed, stats = call(
         attend_kernel,
         (near((N, CH), f32), near((2 * BLOCKS, 128), f32)),

time: 82.1 us -> 87.8 us (1.069)
  local copies, waits for them, and re-layouts: 0.01 us -> 3.55 us
  waiting for transfers between devices: 13.6 us -> 16.8 us
  Pallas kernels: 23.7 us -> 22.7 us
    unnamed x6 -> x24, local copies, waits for them, and re-layouts: 0.01 us -> 3.55 us
    ppermute x4, waiting for transfers between devices: 0.01 us -> 2.71 us  [shift(): return lax.ppermute(x, axis, pairs)]
    pallas_call x8 -> x9, Pallas kernels: 23.7 us -> 22.7 us  [run(): fn(*[pltpu.with_memory_space_constraint(x, spaces[c]) if c in spaces else...]
  transfers between devices with their start and end apart: 10 -> 10, of which waited for: 5 -> 6; matrix products, arithmetic and copies ran while one was open for 0% -> 0% of each run, Pallas kernels for 21% -> 17%
where the time goes in v5:
time: 87.8 us; the launch traced here: 86.7 us
  starting transfers between devices  43.6 us (50%)
  Pallas kernels  22.7 us (26%)
  waiting for transfers between devices  16.8 us (19%)
  local copies, waits for them, and re-layouts  3.55 us (4%)
    all_to_all x3, starting transfers between devices, spread(): return lax.all_to_all(slot, ('row', 'col'), 0, 0).reshape(x.shape)  29.9 us
    pallas_call x9, Pallas kernels, run(): fn(*[pltpu.with_memory_space_constraint(x, spaces[c]) if c in spaces else...  22.7 us
    all_to_all x3, waiting for transfers between devices, spread(): return lax.all_to_all(slot, ('row', 'col'), 0, 0).reshape(x.shape)  10 us
    ppermute x4, starting transfers between devices, shift(): return lax.ppermute(x, axis, pairs)  9.19 us
    ppermute x3, starting transfers between devices, shards(): lax.ppermute(stats, 'head', [(i, (i + d) % heads) for i in range(heads)])  4.53 us
    ppermute x3, waiting for transfers between devices, shards(): lax.ppermute(stats, 'head', [(i, (i + d) % heads) for i in range(heads)])  4.01 us
    unnamed x24, local copies, waits for them, and re-layouts  3.55 us
    ppermute x4, waiting for transfers between devices, shift(): return lax.ppermute(x, axis, pairs)  2.71 us
  transfers between devices with their start and end apart: 10, of which 6 were waited for; matrix products, arithmetic and copies ran while one was open for 0% of the time, Pallas kernels for 17%

profile of v5, /device:TPU:8, one launch (start us, length us, event | category | flops | bytes accessed | tf_op | source)
XLA Modules:
  0.0 86.7 jit_solution(8340297286794090929)
XLA Ops:
  0.0 0.0 copy-start
  0.0 2.9 %pool_queries.1 = (bf16[512,128]{1,0:T(8,128)(2,1)}, f32[2,80,128]{2,1,0:T(8,128)}) custom-call(s32[2,32,48]{2,1,0:T(8,128)} %bitcast.26, bf16[1536,256]{1,0:T(8,128)(2,1)} %bitcast.20), custom_call_target="tpu_custom_call" | custom-call | bytes 8388608 | tf_op jit(solution)/shard_map/pool_queries/pallas_call | solution.py:49
  2.9 12.1 %all-to-all-start = ((bf16[64,8,128]{2,1,0:T(8,128)(2,1)}), bf16[64,8,128]{2,1,0:T(8,128)(2,1)S(1)}, u32[]{:S(2)}, u32[]{:S(2)}) async-start(bf16[64,8,128]{2,1,0:T(8,128)(2,1)} %bitcast.25), calls=%async_computation | async-start | bytes 262144 | tf_op jit(solution)/shard_map/all_to_all | solution.py:457
  15.0 0.0 copy-done
  15.0 2.0 %turn_keys.1 = (bf16[1536,256]{1,0:T(8,128)(2,1)S(1)}, bf16[48,256]{1,0:T(8,128)(2,1)S(1)}, bf16[48,256]{1,0:T(8,128)(2,1)S(1)}, bf16[32,256]{1,0:T(8,128)(2,1)S(1)}, bf16[32,256]{1,0:T(8,128)(2,1)S(1)}) custom-call(f32[2,80,128]{2,1,0:T(8,128)} %get-tuple-element.21.tab_hbm_ref, bf16[48,32,256]{2,1,0:T(8,128)(2,1)S(1)} %copy-done, bf16[1536,256]{1,0:T(8,128)(2,1)} %bitcast.23), custom_call_target="tpu_custom_call" | custom-call | bytes 4194304 | tf_op jit(solution)/shard_map/turn_keys/pallas_call | solution.py:49
  17.0 2.1 %collective-permute-start = (bf16[48,256]{1,0:T(8,128)(2,1)S(1)}, bf16[48,256]{1,0:T(8,128)(2,1)S(1)}, u32[]{:S(2)}, u32[]{:S(2)}) collective-permute-start(bf16[48,256]{1,0:T(8,128)(2,1)S(1)} %get-tuple-element.25), channel_id=1, source_target_pairs={{0,4},{4,8},{8,12},{12,16},{16,20},{20,24},{24,28},{28,32},{32,36}... | collective-permute-start | bytes 73736 | tf_op jit(solution)/shard_map/ppermute | solution.py:463
  19.1 1.3 %collective-permute-start.1 = (bf16[48,256]{1,0:T(8,128)(2,1)S(1)}, bf16[48,256]{1,0:T(8,128)(2,1)S(1)}, u32[]{:S(2)}, u32[]{:S(2)}) collective-permute-start(bf16[48,256]{1,0:T(8,128)(2,1)S(1)} %get-tuple-element.26), channel_id=1, source_target_pairs={{4,0},{8,4},{12,8},{16,12},{20,16},{24,20},{28,24},{32,28},{36,32}... | collective-permute-start | bytes 73736 | tf_op jit(solution)/shard_map/ppermute | solution.py:463
  20.4 0.0 collective-permute-done.left_ref
  20.4 0.0 copy-start.1
  20.4 2.7 %collective-permute-done.1.right_ref = bf16[48,256]{1,0:T(8,128)(2,1)S(1)} collective-permute-done((bf16[48,256]{1,0:T(8,128)(2,1)S(1)}, bf16[48,256]{1,0:T(8,128)(2,1)S(1)}, u32[]{:S(2)}, u32[]{:S(2)}) %collective-permute-start.1) | collective-permute-done | bytes 24608 | tf_op jit(solution)/shard_map/ppermute | solution.py:463
  23.1 0.0 copy-start.3
  23.1 1.3 %all-to-all-done = bf16[64,8,128]{2,1,0:T(8,128)(2,1)S(1)} async-done(((bf16[64,8,128]{2,1,0:T(8,128)(2,1)}), bf16[64,8,128]{2,1,0:T(8,128)(2,1)S(1)}, u32[]{:S(2)}, u32[]{:S(2)}) %all-to-all-start) | async-done | bytes 131104 | tf_op jit(solution)/shard_map/all_to_all | solution.py:457
  24.4 3.1 %collective-permute-start.2 = (bf16[48,256]{1,0:T(8,128)(2,1)S(1)}, bf16[48,256]{1,0:T(8,128)(2,1)S(1)}, u32[]{:S(2)}, u32[]{:S(2)}) collective-permute-start(bf16[48,256]{1,0:T(8,128)(2,1)S(1)} %get-tuple-element.29), channel_id=1, source_target_pairs={{0,64},{64,128},{128,192},{1,65},{65,129},{129,193},{2,66},{66,130... | collective-permute-start | bytes 73736 | tf_op jit(solution)/shard_map/ppermute | solution.py:463
  27.5 2.8 %collective-permute-start.3 = (bf16[48,256]{1,0:T(8,128)(2,1)S(1)}, bf16[48,256]{1,0:T(8,128)(2,1)S(1)}, u32[]{:S(2)}, u32[]{:S(2)}) collective-permute-start(bf16[48,256]{1,0:T(8,128)(2,1)S(1)} %get-tuple-element.30), channel_id=1, source_target_pairs={{64,0},{128,64},{192,128},{65,1},{129,65},{193,129},{66,2},{130,66... | collective-permute-start | bytes 73736 | tf_op jit(solution)/shard_map/ppermute | solution.py:463
  30.3 3.9 %partials.1 = bf16[1024,128]{1,0:T(8,128)(2,1)} custom-call(bf16[512,128]{1,0:T(8,128)(2,1)S(1)} %bitcast.14, bf16[1536,256]{1,0:T(8,128)(2,1)S(1)} %get-tuple-element.22.tk_ref, bf16[1536,256]{1,0:T(8,128)(2,1)S(1)} %bitcast.13), custom_call_target="tpu_custom_call" | custom-call | bytes 10485760 | tf_op jit(solution)/shard_map/partials/pallas_call | solution.py:49
  34.1 0.0 collective-permute-done.2.above_ref
  34.1 0.0 copy-start.5
  34.1 0.0 collective-permute-done.3.below_ref
  34.1 0.0 copy-start.7
  34.2 0.0 copy-done.1
  34.2 0.0 copy-done.3
  34.2 0.6 copy-done.5
  34.7 0.0 copy-done.7
  34.8 11.3 %all-to-all-start.1 = ((bf16[64,16,128]{2,1,0:T(8,128)(2,1)}), bf16[64,16,128]{2,1,0:T(8,128)(2,1)S(1)}, u32[]{:S(2)}, u32[]{:S(2)}) async-start(bf16[64,16,128]{2,1,0:T(8,128)(2,1)} %bitcast.22), calls=%async_computation.1 | async-start | bytes 524288 | tf_op jit(solution)/shard_map/all_to_all | solution.py:457
  46.0 0.0 copy-start.9
  46.0 5.6 %probabilities.1.prob_ref = bf16[1536,1024]{1,0:T(8,128)(2,1)S(1)} custom-call(bf16[512,128]{1,0:T(8,128)(2,1)S(1)} %bitcast.15, f32[2,80,128]{2,1,0:T(8,128)} %get-tuple-element.21.tab_hbm_ref, bf16[1536,256]{1,0:T(8,128)(2,1)} %bitcast.21), custom_call_target="tpu_custom_call" | custom-call | bytes 20971520 | tf_op jit(solution)/shard_map/probabilities/pallas_call | solution.py:49
  51.6 5.9 %all-to-all-done.1 = bf16[64,16,128]{2,1,0:T(8,128)(2,1)S(1)} async-done(((bf16[64,16,128]{2,1,0:T(8,128)(2,1)}), bf16[64,16,128]{2,1,0:T(8,128)(2,1)S(1)}, u32[]{:S(2)}, u32[]{:S(2)}) %all-to-all-start.1) | async-done | bytes 262176 | tf_op jit(solution)/shard_map/all_to_all | solution.py:457
  57.6 1.1 %merge.1 = bf16[512,128]{1,0:T(8,128)(2,1)} custom-call(bf16[1024,128]{1,0:T(8,128)(2,1)S(1)} %bitcast.16), custom_call_target="tpu_custom_call" | custom-call | bytes 2097152 | tf_op jit(solution)/shard_map/merge/pallas_call | solution.py:49
  58.7 6.5 %all-to-all-start.2 = ((bf16[64,8,128]{2,1,0:T(8,128)(2,1)}), bf16[64,8,128]{2,1,0:T(8,128)(2,1)S(1)}, u32[]{:S(2)}, u32[]{:S(2)}) async-start(bf16[64,8,128]{2,1,0:T(8,128)(2,1)} %bitcast.24), calls=%async_computation.2 | async-start | bytes 262144 | tf_op jit(solution)/shard_map/all_to_all | solution.py:457
  65.2 0.0 copy-done.9
  65.2 0.0 copy-start.2
  65.2 0.7 copy-done.2
  65.9 0.0 copy-start.4
  65.9 0.7 copy-done.4
  66.7 0.0 copy-start.6
  66.7 0.7 copy-done.6
  67.4 0.0 copy-start.8
  67.4 0.7 copy-done.8
  68.2 3.6 %conv.1.conv_hbm_ref = f32[1536,256]{1,0:T(8,128)} custom-call(bf16[48,32,256]{2,1,0:T(8,128)(2,1)} %v_hbm_ref.1, bf16[48,256]{1,0:T(8,128)(2,1)S(1)} %copy-done.2, bf16[48,256]{1,0:T(8,128)(2,1)S(1)} %copy-done.4, bf16[48,256]{1,0:T(8,128)(2,1)S(1)} %copy-done.6, bf16[48,256]{1,0:T(8,128)(2,1)S(1)} %copy-done.8, f32[9,256]{1,0:T(8,128)S(1)} %copy-done.9), custom_call_target="tpu_custom_call" | custom-call | bytes 6291456 | tf_op jit(solution)/shard_map/conv/pallas_call | solution.py:49
  71.8 2.8 %all-to-all-done.2 = bf16[64,8,128]{2,1,0:T(8,128)(2,1)S(1)} async-done(((bf16[64,8,128]{2,1,0:T(8,128)(2,1)}), bf16[64,8,128]{2,1,0:T(8,128)(2,1)S(1)}, u32[]{:S(2)}, u32[]{:S(2)}) %all-to-all-start.2) | async-done | bytes 131104 | tf_op jit(solution)/shard_map/all_to_all | solution.py:457
  74.6 0.0 copy-start.10
  74.6 0.0 copy-start.11
  74.6 2.4 %attend.1 = (f32[1536,256]{1,0:T(8,128)S(1)}, f32[24,128]{1,0:T(8,128)S(1)}) custom-call(bf16[512,128]{1,0:T(8,128)(2,1)S(1)} %bitcast.17, bf16[1536,1024]{1,0:T(8,128)(2,1)S(1)} %probabilities.1.prob_ref, f32[1536,256]{1,0:T(8,128)} %conv.1.conv_hbm_ref), custom_call_target="tpu_custom_call" | custom-call | bytes 4194304 | tf_op jit(solution)/shard_map/attend/pallas_call | solution.py:49
  77.0 2.8 %collective-permute-start.6 = (f32[24,128]{1,0:T(8,128)S(1)}, f32[24,128]{1,0:T(8,128)S(1)}, u32[]{:S(2)}, u32[]{:S(2)}) collective-permute-start(f32[24,128]{1,0:T(8,128)S(1)} %get-tuple-element.33.s0_ref), channel_id=1, source_target_pairs={{0,3},{1,0},{2,1},{3,2},{4,7},{5,4},{6,5},{7,6},{8,11},{9,8},{10,9... | collective-permute-start | bytes 36872 | tf_op jit(solution)/shard_map/ppermute | solution.py:557
  79.8 0.8 collective-permute-start.5
  80.6 0.9 %collective-permute-start.4 = (f32[24,128]{1,0:T(8,128)S(1)}, f32[24,128]{1,0:T(8,128)S(1)}, u32[]{:S(2)}, u32[]{:S(2)}) collective-permute-start(f32[24,128]{1,0:T(8,128)S(1)} %get-tuple-element.33.s0_ref), channel_id=1, source_target_pairs={{0,1},{1,2},{2,3},{3,0},{4,5},{5,6},{6,7},{7,4},{8,9},{9,10},{10,1... | collective-permute-start | bytes 36872 | tf_op jit(solution)/shard_map/ppermute | solution.py:557
  81.5 0.0 collective-permute-done.6.s3_ref
  81.5 3.5 %collective-permute-done.5.s2_ref = f32[24,128]{1,0:T(8,128)S(1)} collective-permute-done((f32[24,128]{1,0:T(8,128)S(1)}, f32[24,128]{1,0:T(8,128)S(1)}, u32[]{:S(2)}, u32[]{:S(2)}) %collective-permute-start.5) | collective-permute-done | bytes 12320 | tf_op jit(solution)/shard_map/ppermute | solution.py:557
  85.0 0.5 collective-permute-done.4.s1_ref
  85.5 0.0 copy-done.10
  85.5 0.0 copy-done.11
  85.5 1.2 %norm.1 = bf16[1536,256]{1,0:T(8,128)(2,1)} custom-call(f32[24,128]{1,0:T(8,128)S(1)} %get-tuple-element.33.s0_ref, f32[24,128]{1,0:T(8,128)S(1)} %collective-permute-done.4.s1_ref, f32[24,128]{1,0:T(8,128)S(1)} %collective-permute-done.5.s2_ref, f32[24,128]{1,0:T(8,128)S(1)} %collective-permute-done.6.s3_ref, f32[1536,256]{1,0:T(8,128)S(1)} %get-tuple-element.34.sum_ref, ...), custom_call_target="tpu_custom_call" | custom-call | bytes 4194304 | tf_op jit(solution)/shard_map/norm/pallas_call | solution.py:49
  (1 shorter events, 0.0 us)
Async XLA Ops:
  0.0 15.0 %copy-start = (bf16[48,32,256]{2,1,0:T(8,128)(2,1)S(1)}, bf16[48,32,256]{2,1,0:T(8,128)(2,1)}, u32[]{:S(2)}) copy-start(bf16[48,32,256]{2,1,0:T(8,128)(2,1)} %v_hbm_ref.1) | copy-start | bytes 2359300
  2.9 21.5 %all-to-all-start = ((bf16[64,8,128]{2,1,0:T(8,128)(2,1)}), bf16[64,8,128]{2,1,0:T(8,128)(2,1)S(1)}, u32[]{:S(2)}, u32[]{:S(2)}) async-start(bf16[64,8,128]{2,1,0:T(8,128)(2,1)} %bitcast.25), calls=%async_computation | async-start | bytes 262144 | tf_op jit(solution)/shard_map/all_to_all | solution.py:457
  17.0 3.4 %collective-permute-start = (bf16[48,256]{1,0:T(8,128)(2,1)S(1)}, bf16[48,256]{1,0:T(8,128)(2,1)S(1)}, u32[]{:S(2)}, u32[]{:S(2)}) collective-permute-start(bf16[48,256]{1,0:T(8,128)(2,1)S(1)} %get-tuple-element.25), channel_id=1, source_target_pairs={{0,4},{4,8},{8,12},{12,16},{16,20},{20,24},{24,28},{28,32},{32,36}... | collective-permute-start | bytes 73736 | tf_op jit(solution)/shard_map/ppermute | solution.py:463
  19.1 4.0 %collective-permute-start.1 = (bf16[48,256]{1,0:T(8,128)(2,1)S(1)}, bf16[48,256]{1,0:T(8,128)(2,1)S(1)}, u32[]{:S(2)}, u32[]{:S(2)}) collective-permute-start(bf16[48,256]{1,0:T(8,128)(2,1)S(1)} %get-tuple-element.26), channel_id=1, source_target_pairs={{4,0},{8,4},{12,8},{16,12},{20,16},{24,20},{28,24},{32,28},{36,32}... | collective-permute-start | bytes 73736 | tf_op jit(solution)/shard_map/ppermute | solution.py:463
  20.4 13.7 %copy-start.1 = (bf16[48,256]{1,0:T(8,128)(2,1)}, bf16[48,256]{1,0:T(8,128)(2,1)S(1)}, u32[]{:S(2)}) copy-start(bf16[48,256]{1,0:T(8,128)(2,1)S(1)} %collective-permute-done.left_ref) | copy-start | bytes 73732
  23.1 11.0 %copy-start.3 = (bf16[48,256]{1,0:T(8,128)(2,1)}, bf16[48,256]{1,0:T(8,128)(2,1)S(1)}, u32[]{:S(2)}) copy-start(bf16[48,256]{1,0:T(8,128)(2,1)S(1)} %collective-permute-done.1.right_ref) | copy-start | bytes 73732
  24.4 9.7 %collective-permute-start.2 = (bf16[48,256]{1,0:T(8,128)(2,1)S(1)}, bf16[48,256]{1,0:T(8,128)(2,1)S(1)}, u32[]{:S(2)}, u32[]{:S(2)}) collective-permute-start(bf16[48,256]{1,0:T(8,128)(2,1)S(1)} %get-tuple-element.29), channel_id=1, source_target_pairs={{0,64},{64,128},{128,192},{1,65},{65,129},{129,193},{2,66},{66,130... | collective-permute-start | bytes 73736 | tf_op jit(solution)/shard_map/ppermute | solution.py:463
  27.5 6.6 %collective-permute-start.3 = (bf16[48,256]{1,0:T(8,128)(2,1)S(1)}, bf16[48,256]{1,0:T(8,128)(2,1)S(1)}, u32[]{:S(2)}, u32[]{:S(2)}) collective-permute-start(bf16[48,256]{1,0:T(8,128)(2,1)S(1)} %get-tuple-element.30), channel_id=1, source_target_pairs={{64,0},{128,64},{192,128},{65,1},{129,65},{193,129},{66,2},{130,66... | collective-permute-start | bytes 73736 | tf_op jit(solution)/shard_map/ppermute | solution.py:463
  34.1 0.6 copy-start.5
  34.1 0.6 copy-start.7
  34.8 22.8 %all-to-all-start.1 = ((bf16[64,16,128]{2,1,0:T(8,128)(2,1)}), bf16[64,16,128]{2,1,0:T(8,128)(2,1)S(1)}, u32[]{:S(2)}, u32[]{:S(2)}) async-start(bf16[64,16,128]{2,1,0:T(8,128)(2,1)} %bitcast.22), calls=%async_computation.1 | async-start | bytes 524288 | tf_op jit(solution)/shard_map/all_to_all | solution.py:457
  46.0 19.2 %copy-start.9 = (f32[9,256]{1,0:T(8,128)S(1)}, f32[9,256]{1,0:T(8,128)}, u32[]{:S(2)}) copy-start(f32[9,256]{1,0:T(8,128)} %w_ref.1) | copy-start | bytes 27652
  58.7 15.9 %all-to-all-start.2 = ((bf16[64,8,128]{2,1,0:T(8,128)(2,1)}), bf16[64,8,128]{2,1,0:T(8,128)(2,1)S(1)}, u32[]{:S(2)}, u32[]{:S(2)}) async-start(bf16[64,8,128]{2,1,0:T(8,128)(2,1)} %bitcast.24), calls=%async_computation.2 | async-start | bytes 262144 | tf_op jit(solution)/shard_map/all_to_all | solution.py:457
  65.2 0.7 copy-start.2
  65.9 0.7 copy-start.4
  66.7 0.7 copy-start.6
  67.4 0.7 copy-start.8
  74.6 10.9 %copy-start.10 = (f32[256]{0:T(256)S(1)}, f32[256]{0:T(256)}, u32[]{:S(2)}) copy-start(f32[256]{0:T(256)} %param.12) | copy-start | bytes 3076
  74.6 10.9 %copy-start.11 = (f32[256]{0:T(256)S(1)}, f32[256]{0:T(256)}, u32[]{:S(2)}) copy-start(f32[256]{0:T(256)} %param.13) | copy-start | bytes 3076
  77.0 4.5 %collective-permute-start.6 = (f32[24,128]{1,0:T(8,128)S(1)}, f32[24,128]{1,0:T(8,128)S(1)}, u32[]{:S(2)}, u32[]{:S(2)}) collective-permute-start(f32[24,128]{1,0:T(8,128)S(1)} %get-tuple-element.33.s0_ref), channel_id=1, source_target_pairs={{0,3},{1,0},{2,1},{3,2},{4,7},{5,4},{6,5},{7,6},{8,11},{9,8},{10,9... | collective-permute-start | bytes 36872 | tf_op jit(solution)/shard_map/ppermute | solution.py:557
  79.8 5.2 %collective-permute-start.5 = (f32[24,128]{1,0:T(8,128)S(1)}, f32[24,128]{1,0:T(8,128)S(1)}, u32[]{:S(2)}, u32[]{:S(2)}) collective-permute-start(f32[24,128]{1,0:T(8,128)S(1)} %get-tuple-element.33.s0_ref), channel_id=1, source_target_pairs={{0,2},{1,3},{2,0},{3,1},{4,6},{5,7},{6,4},{7,5},{8,10},{9,11},{10,... | collective-permute-start | bytes 36872 | tf_op jit(solution)/shard_map/ppermute | solution.py:557
  80.6 4.9 %collective-permute-start.4 = (f32[24,128]{1,0:T(8,128)S(1)}, f32[24,128]{1,0:T(8,128)S(1)}, u32[]{:S(2)}, u32[]{:S(2)}) collective-permute-start(f32[24,128]{1,0:T(8,128)S(1)} %get-tuple-element.33.s0_ref), channel_id=1, source_target_pairs={{0,1},{1,2},{2,3},{3,0},{4,5},{5,6},{6,7},{7,4},{8,9},{9,10},{10,1... | collective-permute-start | bytes 36872 | tf_op jit(solution)/shard_map/ppermute | solution.py:557

commit v6 on v5

--- a/solution.py
+++ b/solution.py
@@ -165,8 +165,6 @@
     tk_ref,
     first_ref,
     last_ref,
-    top_ref,
-    bottom_ref,
     tab_ref,
     held_ref,
     sems,
@@ -181,8 +179,6 @@
             pltpu.make_async_copy(k_ref.at[part, :], held_ref.at[part, :], sems.at[cell])
         )
         copies[cell].start()
-    top_ref[...] = v_ref[0]
-    bottom_ref[...] = v_ref[TR - 1]
     first_ref[...] = v_ref[:, 0, :]
     last_ref[...] = v_ref[:, TC - 1, :]
     matrix = turn_matrix()
@@ -320,9 +316,23 @@
     lax.fori_loop(0, N // chunk, body, 0)
 
 
-def line_kernel(top_ref, bottom_ref, left_ref, right_ref, up_ref, down_ref):
-    for line_ref, row, out_ref in ((top_ref, 0, up_ref), (bottom_ref, TR - 1, down_ref)):
-        out_ref[pl.ds(0, TC), :] = line_ref[...]
+def line_kernel(v_ref, left_hbm_ref, right_hbm_ref, up_ref, down_ref, left_ref, right_ref, sems):
+    copies = [
+        pltpu.make_async_copy(source, target, sems.at[i])
+        for i, (source, target) in enumerate(
+            (
+                (v_ref.at[0], up_ref.at[pl.ds(0, TC), :]),
+                (v_ref.at[TR - 1], down_ref.at[pl.ds(0, TC), :]),
+                (left_hbm_ref, left_ref),
+                (right_hbm_ref, right_ref),
+            )
+        )
+    ]
+    for copy in copies:
+        copy.start()
+    for copy in copies:
+        copy.wait()
+    for row, out_ref in ((0, up_ref), (TR - 1, down_ref)):
         left = left_ref[row : row + 1, :].astype(f32)
         right = right_ref[row : row + 1, :].astype(f32)
         tail = jnp.concatenate([left, right, jnp.zeros((14, CH), f32)], axis=0)
@@ -331,20 +341,29 @@
 
 def conv_kernel(
     v_hbm_ref,
-    left_ref,
-    right_ref,
+    left_hbm_ref,
+    right_hbm_ref,
     above_ref,
     below_ref,
     w_ref,
     out_ref,
     v_ref,
+    left_ref,
+    right_ref,
     l_ref,
     r_ref,
-    sem,
+    sems,
 ):
-    fetch = pltpu.make_async_copy(v_hbm_ref, v_ref, sem)
-    fetch.start()
-    fetch.wait()
+    copies = [
+        pltpu.make_async_copy(source, target, sems.at[i])
+        for i, (source, target) in enumerate(
+            ((left_hbm_ref, left_ref), (right_hbm_ref, right_ref), (v_hbm_ref, v_ref))
+        )
+    ]
+    for copy in copies:
+        copy.start()
+    for copy in copies:
+        copy.wait()
     l_ref[...] = left_ref[...].astype(f32)
     r_ref[...] = right_ref[...].astype(f32)
     for half in range(2):
@@ -486,18 +505,14 @@
     )(jnp.swapaxes(positions, 1, 2), q)
     agents = spread(packed)
     held_table = pltpu.VMEM((2, TR + TC, 128), f32)
-    tk, first, last, top, bottom = call(
+    tk, first, last = call(
         key_kernel,
-        (near((N, CH), bf16),)
-        + (near((TR, CH), bf16),) * 2
-        + (near((TC, CH), bf16),) * 2,
+        (near((N, CH), bf16),) + (far((TR, CH), bf16),) * 2,
         "h h",
         scratch=[held_table, pltpu.VMEM((N, CH), bf16), pltpu.SemaphoreType.DMA((AGR + 1,))],
         nbytes=4 * mb,
         name="turn_keys",
     )(table, values, k)
-    left = shift(last, "col", 1)
-    right = shift(first, "col", -1)
     parts = call(
         partial_kernel,
         far((TILES * ROWS, 128), bf16),
@@ -506,16 +521,9 @@
         nbytes=10 * mb,
         name="partials",
     )(agents, tk, v)
-    up, down = call(
-        line_kernel,
-        (near((TC + 16, CH), bf16),) * 2,
-        "vv  ",
-        nbytes=mb // 4,
-        name="lines",
-    )(top, bottom, *lax.optimization_barrier((left, right, agents))[:2])
-    above = shift(down, "row", 1)
-    below = shift(up, "row", -1)
-    parts = after(parts, above, below)
+    last, first, parts = lax.optimization_barrier((last, first, parts))
+    left = shift(last, "col", 1)
+    right = shift(first, "col", -1)
     received = spread(parts)
     prob = call(
         probability_kernel,
@@ -529,18 +537,30 @@
         nbytes=20 * mb,
         name="probabilities",
     )(agents, table, q)
-    received = after(received, prob)
+    received = after(received, prob, left, right)
     merged = call(merge_kernel, far((TILES * 8, 128), bf16), " ", nbytes=2 * mb, name="merge")(
         received
     )
+    left, right, merged = lax.optimization_barrier((left, right, merged))
+    up, down = call(
+        line_kernel,
+        (near((TC + 16, CH), bf16),) * 2,
+        "hhh",
+        scratch=[pltpu.VMEM((TR, CH), bf16)] * 2 + [pltpu.SemaphoreType.DMA((4,))],
+        nbytes=mb // 4,
+        name="lines",
+    )(values, left, right)
+    above = shift(down, "row", 1)
+    below = shift(up, "row", -1)
     agent_values = spread(merged)
     convolved = call(
         conv_kernel,
         far((N, CH), f32),
-        "h     ",
+        "hhh   ",
         scratch=[pltpu.VMEM((TR, TC, CH), bf16)]
+        + [pltpu.VMEM((TR, CH), bf16)] * 2
         + [pltpu.VMEM((TR, CH), f32)] * 2
-        + [pltpu.SemaphoreType.DMA(())],
+        + [pltpu.SemaphoreType.DMA((3,))],
         nbytes=6 * mb,
         name="conv",
     )(values, left, right, above, below, conv_weight)

time: 87.8 us -> 85 us (0.968)
  local copies, waits for them, and re-layouts: 3.55 us -> 0.61 us
  Pallas kernels: 22.7 us -> 23.9 us
    unnamed x24 -> x10, local copies, waits for them, and re-layouts: 3.55 us -> 0.61 us
    pallas_call x9, Pallas kernels: 22.7 us -> 23.9 us  [run(): fn(*[pltpu.with_memory_space_constraint(x, spaces[c]) if c in spaces else...]
  transfers between devices with their start and end apart: 10 -> 10, of which waited for: 6 -> 5; matrix products, arithmetic and copies ran while one was open for 0% -> 0% of each run, Pallas kernels for 17% -> 15%
where the time goes in v6:
time: 85 us; the launch traced here: 84.5 us
  starting transfers between devices  43.1 us (51%)
  Pallas kernels  23.9 us (28%)
  waiting for transfers between devices  16.6 us (20%)
    all_to_all x3, starting transfers between devices, spread(): return lax.all_to_all(slot, ('row', 'col'), 0, 0).reshape(x.shape)  29.4 us
    pallas_call x9, Pallas kernels, run(): fn(*[pltpu.with_memory_space_constraint(x, spaces[c]) if c in spaces else...  23.9 us
    all_to_all x3, waiting for transfers between devices, spread(): return lax.all_to_all(slot, ('row', 'col'), 0, 0).reshape(x.shape)  9.28 us
    ppermute x4, starting transfers between devices, shift(): return lax.ppermute(x, axis, pairs)  9.19 us
    ppermute x3, starting transfers between devices, shards(): lax.ppermute(stats, 'head', [(i, (i + d) % heads) for i in range(heads)])  4.52 us
    ppermute x3, waiting for transfers between devices, shards(): lax.ppermute(stats, 'head', [(i, (i + d) % heads) for i in range(heads)])  4.02 us
    ppermute x4, waiting for transfers between devices, shift(): return lax.ppermute(x, axis, pairs)  3.34 us
  transfers between devices with their start and end apart: 10, of which 5 were waited for; matrix products, arithmetic and copies ran while one was open for 0% of the time, Pallas kernels for 15%

profile of v6, /device:TPU:8, one launch (start us, length us, event | category | flops | bytes accessed | tf_op | source)
XLA Modules:
  0.0 84.5 jit_solution(1148130540193880354)
XLA Ops:
  0.0 0.0 copy-start
  0.0 2.9 %pool_queries.1 = (bf16[512,128]{1,0:T(8,128)(2,1)}, f32[2,80,128]{2,1,0:T(8,128)}) custom-call(s32[2,32,48]{2,1,0:T(8,128)} %bitcast.26, bf16[1536,256]{1,0:T(8,128)(2,1)} %bitcast.20), custom_call_target="tpu_custom_call" | custom-call | bytes 8388608 | tf_op jit(solution)/shard_map/pool_queries/pallas_call | solution.py:49
  2.9 12.1 %all-to-all-start = ((bf16[64,8,128]{2,1,0:T(8,128)(2,1)}), bf16[64,8,128]{2,1,0:T(8,128)(2,1)S(1)}, u32[]{:S(2)}, u32[]{:S(2)}) async-start(bf16[64,8,128]{2,1,0:T(8,128)(2,1)} %bitcast.25), calls=%async_computation | async-start | bytes 262144 | tf_op jit(solution)/shard_map/all_to_all | solution.py:476
  15.0 0.0 copy-done
  15.0 2.4 %turn_keys.1 = (bf16[1536,256]{1,0:T(8,128)(2,1)S(1)}, bf16[48,256]{1,0:T(8,128)(2,1)}, bf16[48,256]{1,0:T(8,128)(2,1)}) custom-call(f32[2,80,128]{2,1,0:T(8,128)} %get-tuple-element.21.tab_hbm_ref, bf16[48,32,256]{2,1,0:T(8,128)(2,1)S(1)} %copy-done, bf16[1536,256]{1,0:T(8,128)(2,1)} %bitcast.23), custom_call_target="tpu_custom_call" | custom-call | bytes 4194304 | tf_op jit(solution)/shard_map/turn_keys/pallas_call | solution.py:49
  17.4 7.0 %all-to-all-done = bf16[64,8,128]{2,1,0:T(8,128)(2,1)S(1)} async-done(((bf16[64,8,128]{2,1,0:T(8,128)(2,1)}), bf16[64,8,128]{2,1,0:T(8,128)(2,1)S(1)}, u32[]{:S(2)}, u32[]{:S(2)}) %all-to-all-start) | async-done | bytes 131104 | tf_op jit(solution)/shard_map/all_to_all | solution.py:476
  24.4 3.9 %partials.1 = bf16[1024,128]{1,0:T(8,128)(2,1)} custom-call(bf16[512,128]{1,0:T(8,128)(2,1)S(1)} %bitcast.14, bf16[1536,256]{1,0:T(8,128)(2,1)S(1)} %get-tuple-element.25.tk_ref, bf16[1536,256]{1,0:T(8,128)(2,1)S(1)} %bitcast.13), custom_call_target="tpu_custom_call" | custom-call | bytes 10485760 | tf_op jit(solution)/shard_map/partials/pallas_call | solution.py:49
  28.3 5.8 %all-to-all-start.1 = ((bf16[64,16,128]{2,1,0:T(8,128)(2,1)}), bf16[64,16,128]{2,1,0:T(8,128)(2,1)S(1)}, u32[]{:S(2)}, u32[]{:S(2)}) async-start(bf16[64,16,128]{2,1,0:T(8,128)(2,1)} %bitcast.22), calls=%async_computation.1 | async-start | bytes 524288 | tf_op jit(solution)/shard_map/all_to_all | solution.py:476
  34.1 0.0 copy-start.1
  34.1 2.1 %collective-permute-start = (bf16[48,256]{1,0:T(8,128)(2,1)}, bf16[48,256]{1,0:T(8,128)(2,1)S(1)}, u32[]{:S(2)}, u32[]{:S(2)}) collective-permute-start(bf16[48,256]{1,0:T(8,128)(2,1)} %get-tuple-element.26), channel_id=1, source_target_pairs={{0,4},{4,8},{8,12},{12,16},{16,20},{20,24},{24,28},{28,32},{32,36}... | collective-permute-start | bytes 73736 | tf_op jit(solution)/shard_map/ppermute | solution.py:482
  36.2 1.3 %collective-permute-start.1 = (bf16[48,256]{1,0:T(8,128)(2,1)}, bf16[48,256]{1,0:T(8,128)(2,1)}, u32[]{:S(2)}, u32[]{:S(2)}) collective-permute-start(bf16[48,256]{1,0:T(8,128)(2,1)} %get-tuple-element.27), channel_id=1, source_target_pairs={{4,0},{8,4},{12,8},{16,12},{20,16},{24,20},{28,24},{32,28},{36,32}... | collective-permute-start | bytes 73736 | tf_op jit(solution)/shard_map/ppermute | solution.py:482
  37.5 5.6 %probabilities.1.prob_ref = bf16[1536,1024]{1,0:T(8,128)(2,1)S(1)} custom-call(bf16[512,128]{1,0:T(8,128)(2,1)S(1)} %bitcast.15, f32[2,80,128]{2,1,0:T(8,128)} %get-tuple-element.21.tab_hbm_ref, bf16[1536,256]{1,0:T(8,128)(2,1)} %bitcast.21), custom_call_target="tpu_custom_call" | custom-call | bytes 20971520 | tf_op jit(solution)/shard_map/probabilities/pallas_call | solution.py:49
  43.1 0.0 collective-permute-done.left_hbm_ref
  43.1 0.0 copy-start.4
  43.1 0.6 copy-done.4
  43.7 0.0 collective-permute-done.1.right_hbm_ref
  43.7 2.3 %all-to-all-done.1 = bf16[64,16,128]{2,1,0:T(8,128)(2,1)S(1)} async-done(((bf16[64,16,128]{2,1,0:T(8,128)(2,1)}), bf16[64,16,128]{2,1,0:T(8,128)(2,1)S(1)}, u32[]{:S(2)}, u32[]{:S(2)}) %all-to-all-start.1) | async-done | bytes 262176 | tf_op jit(solution)/shard_map/all_to_all | solution.py:476
  46.0 1.1 %merge.1 = bf16[512,128]{1,0:T(8,128)(2,1)} custom-call(bf16[1024,128]{1,0:T(8,128)(2,1)S(1)} %bitcast.16), custom_call_target="tpu_custom_call" | custom-call | bytes 2097152 | tf_op jit(solution)/shard_map/merge/pallas_call | solution.py:49
  47.1 11.5 %all-to-all-start.2 = ((bf16[64,8,128]{2,1,0:T(8,128)(2,1)}), bf16[64,8,128]{2,1,0:T(8,128)(2,1)S(1)}, u32[]{:S(2)}, u32[]{:S(2)}) async-start(bf16[64,8,128]{2,1,0:T(8,128)(2,1)} %bitcast.24), calls=%async_computation.2 | async-start | bytes 262144 | tf_op jit(solution)/shard_map/all_to_all | solution.py:476
  58.6 0.8 lines.1
  59.5 3.5 %collective-permute-start.2 = (bf16[48,256]{1,0:T(8,128)(2,1)S(1)}, bf16[48,256]{1,0:T(8,128)(2,1)S(1)}, u32[]{:S(2)}, u32[]{:S(2)}) collective-permute-start(bf16[48,256]{1,0:T(8,128)(2,1)S(1)} %get-tuple-element.33), channel_id=1, source_target_pairs={{0,64},{64,128},{128,192},{1,65},{65,129},{129,193},{2,66},{66,130... | collective-permute-start | bytes 73736 | tf_op jit(solution)/shard_map/ppermute | solution.py:482
  62.9 2.4 %collective-permute-start.3 = (bf16[48,256]{1,0:T(8,128)(2,1)S(1)}, bf16[48,256]{1,0:T(8,128)(2,1)S(1)}, u32[]{:S(2)}, u32[]{:S(2)}) collective-permute-start(bf16[48,256]{1,0:T(8,128)(2,1)S(1)} %get-tuple-element.34), channel_id=1, source_target_pairs={{64,0},{128,64},{192,128},{65,1},{129,65},{193,129},{66,2},{130,66... | collective-permute-start | bytes 73736 | tf_op jit(solution)/shard_map/ppermute | solution.py:482
  65.3 0.0 collective-permute-done.2.above_ref
  65.3 3.3 %collective-permute-done.3.below_ref = bf16[48,256]{1,0:T(8,128)(2,1)S(1)} collective-permute-done((bf16[48,256]{1,0:T(8,128)(2,1)S(1)}, bf16[48,256]{1,0:T(8,128)(2,1)S(1)}, u32[]{:S(2)}, u32[]{:S(2)}) %collective-permute-start.3) | collective-permute-done | bytes 24608 | tf_op jit(solution)/shard_map/ppermute | solution.py:482
  68.7 0.0 copy-done.1
  68.7 3.6 %conv.1.conv_hbm_ref = f32[1536,256]{1,0:T(8,128)} custom-call(bf16[48,32,256]{2,1,0:T(8,128)(2,1)} %v_hbm_ref.1, bf16[48,256]{1,0:T(8,128)(2,1)} %copy-done.4, bf16[48,256]{1,0:T(8,128)(2,1)} %collective-permute-done.1.right_hbm_ref, bf16[48,256]{1,0:T(8,128)(2,1)S(1)} %collective-permute-done.2.above_ref, ...), custom_call_target="tpu_custom_call" | custom-call | bytes 6291456 | tf_op jit(solution)/shard_map/conv/pallas_call | solution.py:49
  72.3 0.0 all-to-all-done.2
  72.3 0.0 copy-start.2
  72.3 0.0 copy-start.3
  72.3 2.4 %attend.1 = (f32[1536,256]{1,0:T(8,128)S(1)}, f32[24,128]{1,0:T(8,128)S(1)}) custom-call(bf16[512,128]{1,0:T(8,128)(2,1)S(1)} %bitcast.17, bf16[1536,1024]{1,0:T(8,128)(2,1)S(1)} %probabilities.1.prob_ref, f32[1536,256]{1,0:T(8,128)} %conv.1.conv_hbm_ref), custom_call_target="tpu_custom_call" | custom-call | bytes 4194304 | tf_op jit(solution)/shard_map/attend/pallas_call | solution.py:49
  74.7 2.8 %collective-permute-start.6 = (f32[24,128]{1,0:T(8,128)S(1)}, f32[24,128]{1,0:T(8,128)S(1)}, u32[]{:S(2)}, u32[]{:S(2)}) collective-permute-start(f32[24,128]{1,0:T(8,128)S(1)} %get-tuple-element.35.s0_ref), channel_id=1, source_target_pairs={{0,3},{1,0},{2,1},{3,2},{4,7},{5,4},{6,5},{7,6},{8,11},{9,8},{10,9... | collective-permute-start | bytes 36872 | tf_op jit(solution)/shard_map/ppermute | solution.py:577
  77.5 0.8 collective-permute-start.5
  78.3 0.9 %collective-permute-start.4 = (f32[24,128]{1,0:T(8,128)S(1)}, f32[24,128]{1,0:T(8,128)S(1)}, u32[]{:S(2)}, u32[]{:S(2)}) collective-permute-start(f32[24,128]{1,0:T(8,128)S(1)} %get-tuple-element.35.s0_ref), channel_id=1, source_target_pairs={{0,1},{1,2},{2,3},{3,0},{4,5},{5,6},{6,7},{7,4},{8,9},{9,10},{10,1... | collective-permute-start | bytes 36872 | tf_op jit(solution)/shard_map/ppermute | solution.py:577
  79.2 0.0 collective-permute-done.6.s3_ref
  79.2 3.5 %collective-permute-done.5.s2_ref = f32[24,128]{1,0:T(8,128)S(1)} collective-permute-done((f32[24,128]{1,0:T(8,128)S(1)}, f32[24,128]{1,0:T(8,128)S(1)}, u32[]{:S(2)}, u32[]{:S(2)}) %collective-permute-start.5) | collective-permute-done | bytes 12320 | tf_op jit(solution)/shard_map/ppermute | solution.py:577
  82.7 0.5 collective-permute-done.4.s1_ref
  83.2 0.0 copy-done.2
  83.3 0.0 copy-done.3
  83.3 1.2 %norm.1 = bf16[1536,256]{1,0:T(8,128)(2,1)} custom-call(f32[24,128]{1,0:T(8,128)S(1)} %get-tuple-element.35.s0_ref, f32[24,128]{1,0:T(8,128)S(1)} %collective-permute-done.4.s1_ref, f32[24,128]{1,0:T(8,128)S(1)} %collective-permute-done.5.s2_ref, f32[24,128]{1,0:T(8,128)S(1)} %collective-permute-done.6.s3_ref, f32[1536,256]{1,0:T(8,128)S(1)} %get-tuple-element.36.sum_ref, ...), custom_call_target="tpu_custom_call" | custom-call | bytes 4194304 | tf_op jit(solution)/shard_map/norm/pallas_call | solution.py:49
Async XLA Ops:
  0.0 15.0 %copy-start = (bf16[48,32,256]{2,1,0:T(8,128)(2,1)S(1)}, bf16[48,32,256]{2,1,0:T(8,128)(2,1)}, u32[]{:S(2)}) copy-start(bf16[48,32,256]{2,1,0:T(8,128)(2,1)} %v_hbm_ref.1) | copy-start | bytes 2359300
  2.9 21.5 %all-to-all-start = ((bf16[64,8,128]{2,1,0:T(8,128)(2,1)}), bf16[64,8,128]{2,1,0:T(8,128)(2,1)S(1)}, u32[]{:S(2)}, u32[]{:S(2)}) async-start(bf16[64,8,128]{2,1,0:T(8,128)(2,1)} %bitcast.25), calls=%async_computation | async-start | bytes 262144 | tf_op jit(solution)/shard_map/all_to_all | solution.py:476
  28.3 17.7 %all-to-all-start.1 = ((bf16[64,16,128]{2,1,0:T(8,128)(2,1)}), bf16[64,16,128]{2,1,0:T(8,128)(2,1)S(1)}, u32[]{:S(2)}, u32[]{:S(2)}) async-start(bf16[64,16,128]{2,1,0:T(8,128)(2,1)} %bitcast.22), calls=%async_computation.1 | async-start | bytes 524288 | tf_op jit(solution)/shard_map/all_to_all | solution.py:476
  34.1 34.5 %copy-start.1 = (f32[9,256]{1,0:T(8,128)S(1)}, f32[9,256]{1,0:T(8,128)}, u32[]{:S(2)}) copy-start(f32[9,256]{1,0:T(8,128)} %w_ref.1) | copy-start | bytes 27652
  34.1 9.0 %collective-permute-start = (bf16[48,256]{1,0:T(8,128)(2,1)}, bf16[48,256]{1,0:T(8,128)(2,1)S(1)}, u32[]{:S(2)}, u32[]{:S(2)}) collective-permute-start(bf16[48,256]{1,0:T(8,128)(2,1)} %get-tuple-element.26), channel_id=1, source_target_pairs={{0,4},{4,8},{8,12},{12,16},{16,20},{20,24},{24,28},{28,32},{32,36}... | collective-permute-start | bytes 73736 | tf_op jit(solution)/shard_map/ppermute | solution.py:482
  36.2 7.5 %collective-permute-start.1 = (bf16[48,256]{1,0:T(8,128)(2,1)}, bf16[48,256]{1,0:T(8,128)(2,1)}, u32[]{:S(2)}, u32[]{:S(2)}) collective-permute-start(bf16[48,256]{1,0:T(8,128)(2,1)} %get-tuple-element.27), channel_id=1, source_target_pairs={{4,0},{8,4},{12,8},{16,12},{20,16},{24,20},{28,24},{32,28},{36,32}... | collective-permute-start | bytes 73736 | tf_op jit(solution)/shard_map/ppermute | solution.py:482
  43.1 0.6 copy-start.4
  47.1 25.2 %all-to-all-start.2 = ((bf16[64,8,128]{2,1,0:T(8,128)(2,1)}), bf16[64,8,128]{2,1,0:T(8,128)(2,1)S(1)}, u32[]{:S(2)}, u32[]{:S(2)}) async-start(bf16[64,8,128]{2,1,0:T(8,128)(2,1)} %bitcast.24), calls=%async_computation.2 | async-start | bytes 262144 | tf_op jit(solution)/shard_map/all_to_all | solution.py:476
  59.5 5.9 %collective-permute-start.2 = (bf16[48,256]{1,0:T(8,128)(2,1)S(1)}, bf16[48,256]{1,0:T(8,128)(2,1)S(1)}, u32[]{:S(2)}, u32[]{:S(2)}) collective-permute-start(bf16[48,256]{1,0:T(8,128)(2,1)S(1)} %get-tuple-element.33), channel_id=1, source_target_pairs={{0,64},{64,128},{128,192},{1,65},{65,129},{129,193},{2,66},{66,130... | collective-permute-start | bytes 73736 | tf_op jit(solution)/shard_map/ppermute | solution.py:482
  62.9 5.7 %collective-permute-start.3 = (bf16[48,256]{1,0:T(8,128)(2,1)S(1)}, bf16[48,256]{1,0:T(8,128)(2,1)S(1)}, u32[]{:S(2)}, u32[]{:S(2)}) collective-permute-start(bf16[48,256]{1,0:T(8,128)(2,1)S(1)} %get-tuple-element.34), channel_id=1, source_target_pairs={{64,0},{128,64},{192,128},{65,1},{129,65},{193,129},{66,2},{130,66... | collective-permute-start | bytes 73736 | tf_op jit(solution)/shard_map/ppermute | solution.py:482
  72.3 10.9 %copy-start.2 = (f32[256]{0:T(256)S(1)}, f32[256]{0:T(256)}, u32[]{:S(2)}) copy-start(f32[256]{0:T(256)} %param.12) | copy-start | bytes 3076
  72.3 10.9 %copy-start.3 = (f32[256]{0:T(256)S(1)}, f32[256]{0:T(256)}, u32[]{:S(2)}) copy-start(f32[256]{0:T(256)} %param.13) | copy-start | bytes 3076
  74.7 4.5 %collective-permute-start.6 = (f32[24,128]{1,0:T(8,128)S(1)}, f32[24,128]{1,0:T(8,128)S(1)}, u32[]{:S(2)}, u32[]{:S(2)}) collective-permute-start(f32[24,128]{1,0:T(8,128)S(1)} %get-tuple-element.35.s0_ref), channel_id=1, source_target_pairs={{0,3},{1,0},{2,1},{3,2},{4,7},{5,4},{6,5},{7,6},{8,11},{9,8},{10,9... | collective-permute-start | bytes 36872 | tf_op jit(solution)/shard_map/ppermute | solution.py:577
  77.5 5.2 %collective-permute-start.5 = (f32[24,128]{1,0:T(8,128)S(1)}, f32[24,128]{1,0:T(8,128)S(1)}, u32[]{:S(2)}, u32[]{:S(2)}) collective-permute-start(f32[24,128]{1,0:T(8,128)S(1)} %get-tuple-element.35.s0_ref), channel_id=1, source_target_pairs={{0,2},{1,3},{2,0},{3,1},{4,6},{5,7},{6,4},{7,5},{8,10},{9,11},{10,... | collective-permute-start | bytes 36872 | tf_op jit(solution)/shard_map/ppermute | solution.py:577
  78.3 4.9 %collective-permute-start.4 = (f32[24,128]{1,0:T(8,128)S(1)}, f32[24,128]{1,0:T(8,128)S(1)}, u32[]{:S(2)}, u32[]{:S(2)}) collective-permute-start(f32[24,128]{1,0:T(8,128)S(1)} %get-tuple-element.35.s0_ref), channel_id=1, source_target_pairs={{0,1},{1,2},{2,3},{3,0},{4,5},{5,6},{6,7},{7,4},{8,9},{9,10},{10,1... | collective-permute-start | bytes 36872 | tf_op jit(solution)/shard_map/ppermute | solution.py:577

commit v7 on v6

--- a/solution.py
+++ b/solution.py
@@ -158,13 +158,21 @@
     agents_ref[...] = slots(packed)
 
 
+def even_core():
+    return lax.rem(lax.axis_index("col"), 2) == 0
+
+
+def even_row():
+    return lax.rem(lax.axis_index("row"), 2) == 0
+
+
 def key_kernel(
     tab_hbm_ref,
     v_ref,
     k_ref,
     tk_ref,
-    first_ref,
-    last_ref,
+    near_ref,
+    far_ref,
     tab_ref,
     held_ref,
     sems,
@@ -179,8 +187,10 @@
             pltpu.make_async_copy(k_ref.at[part, :], held_ref.at[part, :], sems.at[cell])
         )
         copies[cell].start()
-    first_ref[...] = v_ref[:, 0, :]
-    last_ref[...] = v_ref[:, TC - 1, :]
+    first, last = v_ref[:, 0, :], v_ref[:, TC - 1, :]
+    even = even_core()
+    near_ref[...] = jnp.where(even, last, first)
+    far_ref[...] = jnp.where(even, first, last)
     matrix = turn_matrix()
     table.wait()
     tables = split_tables(tab_ref[0], tab_ref[1])
@@ -316,15 +326,26 @@
     lax.fori_loop(0, N // chunk, body, 0)
 
 
-def line_kernel(v_ref, left_hbm_ref, right_hbm_ref, up_ref, down_ref, left_ref, right_ref, sems):
+def line_kernel(
+    v_ref,
+    near_hbm_ref,
+    far_hbm_ref,
+    mate_ref,
+    rest_ref,
+    top_ref,
+    bottom_ref,
+    near_ref,
+    far_ref,
+    sems,
+):
     copies = [
         pltpu.make_async_copy(source, target, sems.at[i])
         for i, (source, target) in enumerate(
             (
-                (v_ref.at[0], up_ref.at[pl.ds(0, TC), :]),
-                (v_ref.at[TR - 1], down_ref.at[pl.ds(0, TC), :]),
-                (left_hbm_ref, left_ref),
-                (right_hbm_ref, right_ref),
+                (v_ref.at[0], top_ref),
+                (v_ref.at[TR - 1], bottom_ref),
+                (near_hbm_ref, near_ref),
+                (far_hbm_ref, far_ref),
             )
         )
     ]
@@ -332,42 +353,68 @@
         copy.start()
     for copy in copies:
         copy.wait()
-    for row, out_ref in ((0, up_ref), (TR - 1, down_ref)):
-        left = left_ref[row : row + 1, :].astype(f32)
-        right = right_ref[row : row + 1, :].astype(f32)
+    lines = []
+    for row, line_ref in ((0, top_ref), (TR - 1, bottom_ref)):
+        mate = near_ref[row : row + 1, :].astype(f32)
+        rest = far_ref[row : row + 1, :].astype(f32)
+        left = jnp.where(even_core(), rest, mate)
+        right = jnp.where(even_core(), mate, rest)
         tail = jnp.concatenate([left, right, jnp.zeros((14, CH), f32)], axis=0)
-        out_ref[pl.ds(TC, 16), :] = tail.astype(bf16)
+        lines.append(jnp.concatenate([line_ref[...].astype(f32), tail], axis=0))
+    mate_ref[...] = jnp.where(even_row(), lines[1], lines[0]).astype(bf16)
+    rest_ref[...] = jnp.where(even_row(), lines[0], lines[1]).astype(bf16)
 
 
 def conv_kernel(
     v_hbm_ref,
-    left_hbm_ref,
-    right_hbm_ref,
+    near_hbm_ref,
+    far_hbm_ref,
+    mate_ref,
+    rest_ref,
+    w_ref,
+    out_hbm_ref,
+    v_ref,
+    near_ref,
+    far_ref,
     above_ref,
     below_ref,
-    w_ref,
-    out_ref,
-    v_ref,
-    left_ref,
-    right_ref,
     l_ref,
     r_ref,
+    out_ref,
     sems,
 ):
     copies = [
-        pltpu.make_async_copy(source, target, sems.at[i])
-        for i, (source, target) in enumerate(
-            ((left_hbm_ref, left_ref), (right_hbm_ref, right_ref), (v_hbm_ref, v_ref))
-        )
+        pltpu.make_async_copy(near_hbm_ref, near_ref, sems.at[0]),
+        pltpu.make_async_copy(far_hbm_ref, far_ref, sems.at[1]),
     ]
+    for half in range(2):
+        cols = pl.ds(half * 128, 128)
+        copies.append(
+            pltpu.make_async_copy(
+                v_hbm_ref.at[:, :, cols], v_ref.at[:, :, cols], sems.at[2 + half]
+            )
+        )
+    outs = []
+    for half in range(2):
+        cols = pl.ds(half * 128, 128)
+        outs.append(
+            pltpu.make_async_copy(
+                out_ref.at[:, cols], out_hbm_ref.at[:, cols], sems.at[4 + half]
+            )
+        )
     for copy in copies:
         copy.start()
-    for copy in copies:
-        copy.wait()
-    l_ref[...] = left_ref[...].astype(f32)
-    r_ref[...] = right_ref[...].astype(f32)
+    mate, rest = mate_ref[...].astype(f32), rest_ref[...].astype(f32)
+    above_ref[...] = jnp.where(even_row(), rest, mate)
+    below_ref[...] = jnp.where(even_row(), mate, rest)
+    copies[0].wait()
+    copies[1].wait()
+    mate, rest = near_ref[...].astype(f32), far_ref[...].astype(f32)
+    l_ref[...] = jnp.where(even_core(), rest, mate)
+    r_ref[...] = jnp.where(even_core(), mate, rest)
     for half in range(2):
         cols = pl.ds(half * 128, 128)
+        copies[2 + half].wait()
 
         def put(at, total):
             out_ref[pl.ds(at, TC), cols] = total
@@ -381,7 +428,7 @@
             after = jnp.where(column == TC - 1, right, pltpu.roll(row, TC - 1, 0))
             return [before * w[3 * d] + row * w[3 * d + 1] + after * w[3 * d + 2] for d in range(3)]
 
-        tail = above_ref[pl.ds(TC, 16), cols].astype(f32)
+        tail = above_ref[pl.ds(TC, 8), cols]
         t0 = taps(above_ref[pl.ds(0, TC), cols], tail[0:1], tail[1:2])
 
         def group(start, carry):
@@ -401,9 +448,12 @@
         a, b = lax.fori_loop(
             1, TR // 8, lambda g, c: group(pl.multiple_of(g * 8, 8), c), carry
         )
-        tail = below_ref[pl.ds(TC, 16), cols].astype(f32)
+        tail = below_ref[pl.ds(TC, 8), cols]
         t = taps(below_ref[pl.ds(0, TC), cols], tail[0:1], tail[1:2])
         put((TR - 1) * TC, a + t[2])
+        outs[half].start()
+    for copy in outs:
+        copy.wait()
 
 
 def attend_kernel(av_ref, prob_ref, conv_hbm_ref, sum_ref, stat_ref, conv_ref, sem):
@@ -476,10 +526,12 @@
     return lax.all_to_all(slot, ("row", "col"), 0, 0).reshape(x.shape)
 
 
-def shift(x, axis, step):
-    count = lax.axis_size(axis)
-    pairs = [(i, i + step) for i in range(count) if 0 <= i + step < count]
-    return lax.ppermute(x, axis, pairs)
+def swap(x, axis, pairs):
+    return lax.ppermute(x, axis, [p for i, j in pairs for p in ((i, j), (j, i))])
+
+
+def chain(axis, first):
+    return [(i, i + 1) for i in range(first, lax.axis_size(axis) - 1, 2)]
 
 
 def after(x, *others):
@@ -505,7 +557,7 @@
     )(jnp.swapaxes(positions, 1, 2), q)
     agents = spread(packed)
     held_table = pltpu.VMEM((2, TR + TC, 128), f32)
-    tk, first, last = call(
+    tk, inner, outer = call(
         key_kernel,
         (near((N, CH), bf16),) + (far((TR, CH), bf16),) * 2,
         "h h",
@@ -521,10 +573,28 @@
         nbytes=10 * mb,
         name="partials",
     )(agents, tk, v)
-    last, first, parts = lax.optimization_barrier((last, first, parts))
-    left = shift(last, "col", 1)
-    right = shift(first, "col", -1)
+    inner, outer, parts = lax.optimization_barrier((inner, outer, parts))
+    inner = swap(inner, "col", chain("col", 0))
+    outer = swap(outer, "col", chain("col", 1))
     received = spread(parts)
+    mate, rest = call(
+        line_kernel,
+        (near((TC + 16, CH), bf16),) * 2,
+        "hhh",
+        scratch=[pltpu.VMEM((TC, CH), bf16)] * 2
+        + [pltpu.VMEM((TR, CH), bf16)] * 2
+        + [pltpu.SemaphoreType.DMA((4,))],
+        nbytes=mb // 4,
+        name="lines",
+    )(values, inner, outer)
+    received = after(received, mate, rest)
+    mate = swap(mate, "row", chain("row", 0))
+    rest = swap(rest, "row", chain("row", 1))
+    merged = call(merge_kernel, far((TILES * 8, 128), bf16), " ", nbytes=2 * mb, name="merge")(
+        received
+    )
+    merged = after(merged, mate, rest)
+    agent_values = spread(merged)
     prob = call(
         probability_kernel,
         near((N, LOCAL_HEADS * AGENTS), bf16),
@@ -536,34 +606,20 @@
         ],
         nbytes=20 * mb,
         name="probabilities",
-    )(agents, table, q)
-    received = after(received, prob, left, right)
-    merged = call(merge_kernel, far((TILES * 8, 128), bf16), " ", nbytes=2 * mb, name="merge")(
-        received
-    )
-    left, right, merged = lax.optimization_barrier((left, right, merged))
-    up, down = call(
-        line_kernel,
-        (near((TC + 16, CH), bf16),) * 2,
-        "hhh",
-        scratch=[pltpu.VMEM((TR, CH), bf16)] * 2 + [pltpu.SemaphoreType.DMA((4,))],
-        nbytes=mb // 4,
-        name="lines",
-    )(values, left, right)
-    above = shift(down, "row", 1)
-    below = shift(up, "row", -1)
-    agent_values = spread(merged)
+    )(after(agents, merged), table, q)
     convolved = call(
         conv_kernel,
-        far((N, CH), f32),
+        (far((N, CH), f32),),
         "hhh   ",
         scratch=[pltpu.VMEM((TR, TC, CH), bf16)]
         + [pltpu.VMEM((TR, CH), bf16)] * 2
+        + [pltpu.VMEM((TC + 16, CH), f32)] * 2
         + [pltpu.VMEM((TR, CH), f32)] * 2
-        + [pltpu.SemaphoreType.DMA((3,))],
+        + [pltpu.VMEM((N, CH), f32), pltpu.SemaphoreType.DMA((6,))],
         nbytes=6 * mb,
+        out_spaces="h",
         name="conv",
-    )(values, left, right, above, below, conv_weight)
+    )(values, inner, outer, mate, rest, conv_weight)[0]
     summed, stats = call(
         attend_kernel,
         (near((N, CH), f32), near((2 * BLOCKS, 128), f32)),
@@ -574,8 +630,7 @@
     )(agent_values, prob, convolved)
     heads = lax.axis_size("head")
     others = [
-        lax.ppermute(stats, "head", [(i, (i + d) % heads) for i in range(heads)])
-        for d in range(1, heads)
+        lax.ppermute(stats, "head", [(i, i ^ d) for i in range(heads)]) for d in range(1, heads)
     ]
     normed = call(
         norm_kernel,

time: 85 us -> 82.5 us (0.971)
  starting transfers between devices: 43.1 us -> 40.9 us
  waiting for transfers between devices: 16.6 us -> 15.4 us
    ppermute x7, starting transfers between devices: 13.7 us -> 9.88 us  [the longest x4 5.7 us: swap(): lax.ppermute(x, axis, [p for i, j in pairs for p in ((i, j), (j, i))])]
    ppermute x7, waiting for transfers between devices: 7.36 us -> 4.26 us  [the longest x3 3.87 us: shards(): lax.ppermute(stats, 'head', [(i, i ^ d) for i in range(heads)])]
    all_to_all x3, waiting for transfers between devices: 9.28 us -> 11.2 us  [spread(): return lax.all_to_all(slot, ('row', 'col'), 0, 0).reshape(x.shape)]
    all_to_all x3, starting transfers between devices: 29.4 us -> 31 us  [spread(): return lax.all_to_all(slot, ('row', 'col'), 0, 0).reshape(x.shape)]
  transfers between devices with their start and end apart: 10 -> 10, of which waited for: 5 -> 6; matrix products, arithmetic and copies ran while one was open for 0% -> 0% of each run, Pallas kernels for 15% -> 16%
where the time goes in v7:
time: 82.5 us; the launch traced here: 81.4 us
  starting transfers between devices  40.9 us (50%)
  Pallas kernels  23.6 us (29%)
  waiting for transfers between devices  15.4 us (19%)
  local copies, waits for them, and re-layouts  1.21 us (1%)
    all_to_all x3, starting transfers between devices, spread(): return lax.all_to_all(slot, ('row', 'col'), 0, 0).reshape(x.shape)  31 us
    pallas_call x9, Pallas kernels, run(): fn(*[pltpu.with_memory_space_constraint(x, spaces[c]) if c in spaces else...  23.6 us
    all_to_all x3, waiting for transfers between devices, spread(): return lax.all_to_all(slot, ('row', 'col'), 0, 0).reshape(x.shape)  11.2 us
    ppermute x4, starting transfers between devices, swap(): lax.ppermute(x, axis, [p for i, j in pairs for p in ((i, j), (j, i))])  5.7 us
    ppermute x3, starting transfers between devices, shards(): lax.ppermute(stats, 'head', [(i, i ^ d) for i in range(heads)])  4.18 us
    ppermute x3, waiting for transfers between devices, shards(): lax.ppermute(stats, 'head', [(i, i ^ d) for i in range(heads)])  3.87 us
  transfers between devices with their start and end apart: 10, of which 6 were waited for; matrix products, arithmetic and copies ran while one was open for 0% of the time, Pallas kernels for 16%

profile of v7, /device:TPU:8, one launch (start us, length us, event | category | flops | bytes accessed | tf_op | source)
XLA Modules:
  0.0 81.4 jit_solution(5683143967867060039)
XLA Ops:
  0.0 0.0 copy-start
  0.0 2.9 %pool_queries.1 = (bf16[512,128]{1,0:T(8,128)(2,1)}, f32[2,80,128]{2,1,0:T(8,128)}) custom-call(s32[2,32,48]{2,1,0:T(8,128)} %bitcast.26, bf16[1536,256]{1,0:T(8,128)(2,1)} %bitcast.20), custom_call_target="tpu_custom_call" | custom-call | bytes 8388608 | tf_op jit(solution)/shard_map/pool_queries/pallas_call | solution.py:49
  2.9 12.1 %all-to-all-start = ((bf16[64,8,128]{2,1,0:T(8,128)(2,1)}), bf16[64,8,128]{2,1,0:T(8,128)(2,1)S(1)}, u32[]{:S(2)}, u32[]{:S(2)}) async-start(bf16[64,8,128]{2,1,0:T(8,128)(2,1)} %bitcast.25), calls=%async_computation | async-start | bytes 262144 | tf_op jit(solution)/shard_map/all_to_all | solution.py:526
  15.0 0.0 copy-done
  15.0 2.4 %turn_keys.1 = (bf16[1536,256]{1,0:T(8,128)(2,1)S(1)}, bf16[48,256]{1,0:T(8,128)(2,1)}, bf16[48,256]{1,0:T(8,128)(2,1)}) custom-call(f32[2,80,128]{2,1,0:T(8,128)} %get-tuple-element.20.tab_hbm_ref, bf16[48,32,256]{2,1,0:T(8,128)(2,1)S(1)} %copy-done, bf16[1536,256]{1,0:T(8,128)(2,1)} %bitcast.23), custom_call_target="tpu_custom_call" | custom-call | bytes 4194304 | tf_op jit(solution)/shard_map/turn_keys/pallas_call | solution.py:49
  17.4 0.0 copy-start.7
  17.4 0.0 copy-start.6
  17.4 7.0 %all-to-all-done = bf16[64,8,128]{2,1,0:T(8,128)(2,1)S(1)} async-done(((bf16[64,8,128]{2,1,0:T(8,128)(2,1)}), bf16[64,8,128]{2,1,0:T(8,128)(2,1)S(1)}, u32[]{:S(2)}, u32[]{:S(2)}) %all-to-all-start) | async-done | bytes 131104 | tf_op jit(solution)/shard_map/all_to_all | solution.py:526
  24.4 0.0 copy-start.1
  24.4 3.9 %partials.1 = bf16[1024,128]{1,0:T(8,128)(2,1)} custom-call(bf16[512,128]{1,0:T(8,128)(2,1)S(1)} %bitcast.14, bf16[1536,256]{1,0:T(8,128)(2,1)S(1)} %get-tuple-element.24.tk_ref, bf16[1536,256]{1,0:T(8,128)(2,1)S(1)} %bitcast.13), custom_call_target="tpu_custom_call" | custom-call | bytes 10485760 | tf_op jit(solution)/shard_map/partials/pallas_call | solution.py:49
  28.3 5.8 %all-to-all-start.1 = ((bf16[64,16,128]{2,1,0:T(8,128)(2,1)}), bf16[64,16,128]{2,1,0:T(8,128)(2,1)S(1)}, u32[]{:S(2)}, u32[]{:S(2)}) async-start(bf16[64,16,128]{2,1,0:T(8,128)(2,1)} %bitcast.22), calls=%async_computation.1 | async-start | bytes 524288 | tf_op jit(solution)/shard_map/all_to_all | solution.py:526
  34.1 0.0 copy-done.7
  34.1 0.2 collective-permute-start
  34.4 0.0 copy-done.6
  34.4 0.7 collective-permute-start.1
  35.0 0.4 collective-permute-done.near_hbm_ref
  35.4 0.0 copy-start.4
  35.4 0.0 collective-permute-done.1.far_hbm_ref
  35.4 0.6 copy-done.4
  36.0 0.0 copy-start.5
  36.0 0.6 copy-done.5
  36.6 0.8 %lines.1 = (bf16[48,256]{1,0:T(8,128)(2,1)S(1)}, bf16[48,256]{1,0:T(8,128)(2,1)S(1)}) custom-call(bf16[48,32,256]{2,1,0:T(8,128)(2,1)} %v_hbm_ref.1, bf16[48,256]{1,0:T(8,128)(2,1)} %copy-done.4, bf16[48,256]{1,0:T(8,128)(2,1)} %copy-done.5), custom_call_target="tpu_custom_call" | custom-call | bytes 262144 | tf_op jit(solution)/shard_map/lines/pallas_call | solution.py:49
  37.5 0.5 collective-permute-start.2
  38.0 4.3 %collective-permute-start.3 = (bf16[48,256]{1,0:T(8,128)(2,1)S(1)}, bf16[48,256]{1,0:T(8,128)(2,1)S(1)}, u32[]{:S(2)}, u32[]{:S(2)}) collective-permute-start(bf16[48,256]{1,0:T(8,128)(2,1)S(1)} %get-tuple-element.29), channel_id=1, source_target_pairs={{64,128},{128,64},{65,129},{129,65},{66,130},{130,66},{67,131},{13... | collective-permute-start | bytes 73736 | tf_op jit(solution)/shard_map/ppermute | solution.py:530
  42.3 3.7 %all-to-all-done.1 = bf16[64,16,128]{2,1,0:T(8,128)(2,1)S(1)} async-done(((bf16[64,16,128]{2,1,0:T(8,128)(2,1)}), bf16[64,16,128]{2,1,0:T(8,128)(2,1)S(1)}, u32[]{:S(2)}, u32[]{:S(2)}) %all-to-all-start.1) | async-done | bytes 262176 | tf_op jit(solution)/shard_map/all_to_all | solution.py:526
  46.0 1.1 %merge.1 = bf16[512,128]{1,0:T(8,128)(2,1)} custom-call(bf16[1024,128]{1,0:T(8,128)(2,1)S(1)} %bitcast.16), custom_call_target="tpu_custom_call" | custom-call | bytes 2097152 | tf_op jit(solution)/shard_map/merge/pallas_call | solution.py:49
  47.1 0.0 collective-permute-done.2.mate_ref
  47.1 0.0 collective-permute-done.3.rest_ref
  47.1 13.1 %all-to-all-start.2 = ((bf16[64,8,128]{2,1,0:T(8,128)(2,1)}), bf16[64,8,128]{2,1,0:T(8,128)(2,1)S(1)}, u32[]{:S(2)}, u32[]{:S(2)}) async-start(bf16[64,8,128]{2,1,0:T(8,128)(2,1)} %bitcast.24), calls=%async_computation.2 | async-start | bytes 262144 | tf_op jit(solution)/shard_map/all_to_all | solution.py:526
  60.2 0.0 copy-done.1
  60.2 3.3 %conv.1.conv_hbm_ref = f32[1536,256]{1,0:T(8,128)} custom-call(bf16[48,32,256]{2,1,0:T(8,128)(2,1)} %v_hbm_ref.1, bf16[48,256]{1,0:T(8,128)(2,1)} %copy-done.4, bf16[48,256]{1,0:T(8,128)(2,1)} %copy-done.5, bf16[48,256]{1,0:T(8,128)(2,1)S(1)} %collective-permute-done.2.mate_ref, bf16[48,256]{1,0:T(8,128)(2,1)S(1)} %collective-permute-done.3.rest_ref, ...), custom_call_target="tpu_custom_call" | custom-call | bytes 6291456 | tf_op jit(solution)/shard_map/conv/pallas_call | solution.py:49
  63.5 5.6 %probabilities.1.prob_ref = bf16[1536,1024]{1,0:T(8,128)(2,1)S(1)} custom-call(bf16[512,128]{1,0:T(8,128)(2,1)S(1)} %bitcast.15, f32[2,80,128]{2,1,0:T(8,128)} %get-tuple-element.20.tab_hbm_ref, bf16[1536,256]{1,0:T(8,128)(2,1)} %bitcast.21), custom_call_target="tpu_custom_call" | custom-call | bytes 20971520 | tf_op jit(solution)/shard_map/probabilities/pallas_call | solution.py:49
  69.1 0.5 all-to-all-done.2
  69.6 0.0 copy-start.2
  69.6 0.0 copy-start.3
  69.6 2.4 %attend.1 = (f32[1536,256]{1,0:T(8,128)S(1)}, f32[24,128]{1,0:T(8,128)S(1)}) custom-call(bf16[512,128]{1,0:T(8,128)(2,1)S(1)} %bitcast.17, bf16[1536,1024]{1,0:T(8,128)(2,1)S(1)} %probabilities.1.prob_ref, f32[1536,256]{1,0:T(8,128)} %conv.1.conv_hbm_ref), custom_call_target="tpu_custom_call" | custom-call | bytes 4194304 | tf_op jit(solution)/shard_map/attend/pallas_call | solution.py:49
  72.0 2.8 %collective-permute-start.6 = (f32[24,128]{1,0:T(8,128)S(1)}, f32[24,128]{1,0:T(8,128)S(1)}, u32[]{:S(2)}, u32[]{:S(2)}) collective-permute-start(f32[24,128]{1,0:T(8,128)S(1)} %get-tuple-element.33.s0_ref), channel_id=1, source_target_pairs={{0,3},{1,2},{2,1},{3,0},{4,7},{5,6},{6,5},{7,4},{8,11},{9,10},{10,... | collective-permute-start | bytes 36872 | tf_op jit(solution)/shard_map/ppermute | solution.py:633
  74.8 0.8 collective-permute-start.5
  75.6 0.5 collective-permute-start.4
  76.2 0.8 collective-permute-done.6.s3_ref
  77.0 3.1 %collective-permute-done.5.s2_ref = f32[24,128]{1,0:T(8,128)S(1)} collective-permute-done((f32[24,128]{1,0:T(8,128)S(1)}, f32[24,128]{1,0:T(8,128)S(1)}, u32[]{:S(2)}, u32[]{:S(2)}) %collective-permute-start.5) | collective-permute-done | bytes 12320 | tf_op jit(solution)/shard_map/ppermute | solution.py:633
  80.0 0.0 collective-permute-done.4.s1_ref
  80.0 0.0 copy-done.2
  80.0 0.0 copy-done.3
  80.0 1.2 %norm.1 = bf16[1536,256]{1,0:T(8,128)(2,1)} custom-call(f32[24,128]{1,0:T(8,128)S(1)} %get-tuple-element.33.s0_ref, f32[24,128]{1,0:T(8,128)S(1)} %collective-permute-done.4.s1_ref, f32[24,128]{1,0:T(8,128)S(1)} %collective-permute-done.5.s2_ref, f32[24,128]{1,0:T(8,128)S(1)} %collective-permute-done.6.s3_ref, f32[1536,256]{1,0:T(8,128)S(1)} %get-tuple-element.34.sum_ref, ...), custom_call_target="tpu_custom_call" | custom-call | bytes 4194304 | tf_op jit(solution)/shard_map/norm/pallas_call | solution.py:49
Async XLA Ops:
  0.0 15.0 %copy-start = (bf16[48,32,256]{2,1,0:T(8,128)(2,1)S(1)}, bf16[48,32,256]{2,1,0:T(8,128)(2,1)}, u32[]{:S(2)}) copy-start(bf16[48,32,256]{2,1,0:T(8,128)(2,1)} %v_hbm_ref.1) | copy-start | bytes 2359300
  2.9 21.5 %all-to-all-start = ((bf16[64,8,128]{2,1,0:T(8,128)(2,1)}), bf16[64,8,128]{2,1,0:T(8,128)(2,1)S(1)}, u32[]{:S(2)}, u32[]{:S(2)}) async-start(bf16[64,8,128]{2,1,0:T(8,128)(2,1)} %bitcast.25), calls=%async_computation | async-start | bytes 262144 | tf_op jit(solution)/shard_map/all_to_all | solution.py:526
  17.4 16.7 %copy-start.7 = (bf16[48,256]{1,0:T(8,128)(2,1)S(1)}, bf16[48,256]{1,0:T(8,128)(2,1)}, u32[]{:S(2)}) copy-start(bf16[48,256]{1,0:T(8,128)(2,1)} %get-tuple-element.26) | copy-start | bytes 73732
  17.4 16.9 %copy-start.6 = (bf16[48,256]{1,0:T(8,128)(2,1)S(1)}, bf16[48,256]{1,0:T(8,128)(2,1)}, u32[]{:S(2)}) copy-start(bf16[48,256]{1,0:T(8,128)(2,1)} %get-tuple-element.27) | copy-start | bytes 73732
  24.4 35.8 %copy-start.1 = (f32[9,256]{1,0:T(8,128)S(1)}, f32[9,256]{1,0:T(8,128)}, u32[]{:S(2)}) copy-start(f32[9,256]{1,0:T(8,128)} %w_ref.1) | copy-start | bytes 27652
  28.3 17.7 %all-to-all-start.1 = ((bf16[64,16,128]{2,1,0:T(8,128)(2,1)}), bf16[64,16,128]{2,1,0:T(8,128)(2,1)S(1)}, u32[]{:S(2)}, u32[]{:S(2)}) async-start(bf16[64,16,128]{2,1,0:T(8,128)(2,1)} %bitcast.22), calls=%async_computation.1 | async-start | bytes 524288 | tf_op jit(solution)/shard_map/all_to_all | solution.py:526
  34.1 1.3 %collective-permute-start = (bf16[48,256]{1,0:T(8,128)(2,1)S(1)}, bf16[48,256]{1,0:T(8,128)(2,1)S(1)}, u32[]{:S(2)}, u32[]{:S(2)}) collective-permute-start(bf16[48,256]{1,0:T(8,128)(2,1)S(1)} %copy-done.7), channel_id=1, source_target_pairs={{0,4},{4,0},{8,12},{12,8},{16,20},{20,16},{24,28},{28,24},{32,36},... | collective-permute-start | bytes 73736 | tf_op jit(solution)/shard_map/ppermute | solution.py:530
  34.4 1.0 %collective-permute-start.1 = (bf16[48,256]{1,0:T(8,128)(2,1)S(1)}, bf16[48,256]{1,0:T(8,128)(2,1)S(1)}, u32[]{:S(2)}, u32[]{:S(2)}) collective-permute-start(bf16[48,256]{1,0:T(8,128)(2,1)S(1)} %copy-done.6), channel_id=1, source_target_pairs={{4,8},{8,4},{12,16},{16,12},{20,24},{24,20},{28,32},{32,28},{36,40... | collective-permute-start | bytes 73736 | tf_op jit(solution)/shard_map/ppermute | solution.py:530
  35.4 0.6 copy-start.4
  36.0 0.6 copy-start.5
  37.5 9.7 %collective-permute-start.2 = (bf16[48,256]{1,0:T(8,128)(2,1)S(1)}, bf16[48,256]{1,0:T(8,128)(2,1)S(1)}, u32[]{:S(2)}, u32[]{:S(2)}) collective-permute-start(bf16[48,256]{1,0:T(8,128)(2,1)S(1)} %get-tuple-element.28), channel_id=1, source_target_pairs={{0,64},{64,0},{128,192},{192,128},{1,65},{65,1},{129,193},{193,129... | collective-permute-start | bytes 73736 | tf_op jit(solution)/shard_map/ppermute | solution.py:530
  38.0 9.2 %collective-permute-start.3 = (bf16[48,256]{1,0:T(8,128)(2,1)S(1)}, bf16[48,256]{1,0:T(8,128)(2,1)S(1)}, u32[]{:S(2)}, u32[]{:S(2)}) collective-permute-start(bf16[48,256]{1,0:T(8,128)(2,1)S(1)} %get-tuple-element.29), channel_id=1, source_target_pairs={{64,128},{128,64},{65,129},{129,65},{66,130},{130,66},{67,131},{13... | collective-permute-start | bytes 73736 | tf_op jit(solution)/shard_map/ppermute | solution.py:530
  47.1 22.5 %all-to-all-start.2 = ((bf16[64,8,128]{2,1,0:T(8,128)(2,1)}), bf16[64,8,128]{2,1,0:T(8,128)(2,1)S(1)}, u32[]{:S(2)}, u32[]{:S(2)}) async-start(bf16[64,8,128]{2,1,0:T(8,128)(2,1)} %bitcast.24), calls=%async_computation.2 | async-start | bytes 262144 | tf_op jit(solution)/shard_map/all_to_all | solution.py:526
  69.6 10.4 %copy-start.2 = (f32[256]{0:T(256)S(1)}, f32[256]{0:T(256)}, u32[]{:S(2)}) copy-start(f32[256]{0:T(256)} %param.12) | copy-start | bytes 3076
  69.6 10.4 %copy-start.3 = (f32[256]{0:T(256)S(1)}, f32[256]{0:T(256)}, u32[]{:S(2)}) copy-start(f32[256]{0:T(256)} %param.13) | copy-start | bytes 3076
  72.0 5.0 %collective-permute-start.6 = (f32[24,128]{1,0:T(8,128)S(1)}, f32[24,128]{1,0:T(8,128)S(1)}, u32[]{:S(2)}, u32[]{:S(2)}) collective-permute-start(f32[24,128]{1,0:T(8,128)S(1)} %get-tuple-element.33.s0_ref), channel_id=1, source_target_pairs={{0,3},{1,2},{2,1},{3,0},{4,7},{5,6},{6,5},{7,4},{8,11},{9,10},{10,... | collective-permute-start | bytes 36872 | tf_op jit(solution)/shard_map/ppermute | solution.py:633
  74.8 5.2 %collective-permute-start.5 = (f32[24,128]{1,0:T(8,128)S(1)}, f32[24,128]{1,0:T(8,128)S(1)}, u32[]{:S(2)}, u32[]{:S(2)}) collective-permute-start(f32[24,128]{1,0:T(8,128)S(1)} %get-tuple-element.33.s0_ref), channel_id=1, source_target_pairs={{0,2},{1,3},{2,0},{3,1},{4,6},{5,7},{6,4},{7,5},{8,10},{9,11},{10,... | collective-permute-start | bytes 36872 | tf_op jit(solution)/shard_map/ppermute | solution.py:633
  75.6 4.4 %collective-permute-start.4 = (f32[24,128]{1,0:T(8,128)S(1)}, f32[24,128]{1,0:T(8,128)S(1)}, u32[]{:S(2)}, u32[]{:S(2)}) collective-permute-start(f32[24,128]{1,0:T(8,128)S(1)} %get-tuple-element.33.s0_ref), channel_id=1, source_target_pairs={{0,1},{1,0},{2,3},{3,2},{4,5},{5,4},{6,7},{7,6},{8,9},{9,8},{10,11... | collective-permute-start | bytes 36872 | tf_op jit(solution)/shard_map/ppermute | solution.py:633

commit v8 on v7

--- a/solution.py
+++ b/solution.py
@@ -456,9 +456,15 @@
         copy.wait()
 
 
-def attend_kernel(av_ref, prob_ref, conv_hbm_ref, sum_ref, stat_ref, conv_ref, sem):
-    fetch = pltpu.make_async_copy(conv_hbm_ref, conv_ref, sem)
-    fetch.start()
+def attend_kernel(av_ref, prob_ref, conv_hbm_ref, sum_ref, stat_ref, conv_ref, sems):
+    step = N // AGR
+    copies = []
+    for c in range(AGR):
+        part = pl.ds(c * step, step)
+        copies.append(
+            pltpu.make_async_copy(conv_hbm_ref.at[part, :], conv_ref.at[part, :], sems.at[c])
+        )
+        copies[c].start()
     eye = lax.broadcasted_iota(jnp.int32, (128, 128), 0) == lanes((128, 128))
     for pair in range(2):
         pieces = []
@@ -476,8 +482,9 @@
                 agent_values,
                 preferred_element_type=f32,
             )
-    fetch.wait()
     for b in range(BLOCKS):
+        if b * 128 % step == 0:
+            copies[b * 128 // step].wait()
         rows = pl.ds(b * 128, 128)
         x = sum_ref[rows, :] + conv_ref[rows, :]
         sum_ref[rows, :] = x
@@ -573,9 +580,9 @@
         nbytes=10 * mb,
         name="partials",
     )(agents, tk, v)
-    inner, outer, parts = lax.optimization_barrier((inner, outer, parts))
     inner = swap(inner, "col", chain("col", 0))
     outer = swap(outer, "col", chain("col", 1))
+    parts, inner, outer = lax.optimization_barrier((parts, inner, outer))
     received = spread(parts)
     mate, rest = call(
         line_kernel,
@@ -624,7 +631,7 @@
         attend_kernel,
         (near((N, CH), f32), near((2 * BLOCKS, 128), f32)),
         " vh",
-        scratch=[pltpu.VMEM((N, CH), f32), pltpu.SemaphoreType.DMA(())],
+        scratch=[pltpu.VMEM((N, CH), f32), pltpu.SemaphoreType.DMA((AGR,))],
         nbytes=4 * mb,
         name="attend",
     )(agent_values, prob, convolved)

time: 82.5 us -> 75.9 us (0.920)
  starting transfers between devices: 40.9 us -> 34.7 us
  local copies, waits for them, and re-layouts: 1.21 us -> 0.02 us
  waiting for transfers between devices: 15.4 us -> 16.3 us
    all_to_all x3, starting transfers between devices: 31 us -> 24.9 us  [spread(): return lax.all_to_all(slot, ('row', 'col'), 0, 0).reshape(x.shape)]
    all_to_all x3, waiting for transfers between devices: 11.2 us -> 12.4 us  [spread(): return lax.all_to_all(slot, ('row', 'col'), 0, 0).reshape(x.shape)]
    unnamed x16 -> x12, local copies, waits for them, and re-layouts: 1.21 us -> 0.02 us
  transfers between devices with their start and end apart: 10 -> 10, of which waited for: 6 -> 5; matrix products, arithmetic and copies ran while one was open for 0% -> 0% of each run, Pallas kernels for 16% -> 23%
where the time goes in v8:
time: 75.9 us; the launch traced here: 74.9 us
  starting transfers between devices  34.7 us (46%)
  Pallas kernels  23.5 us (31%)
  waiting for transfers between devices  16.3 us (21%)
    all_to_all x3, starting transfers between devices, spread(): return lax.all_to_all(slot, ('row', 'col'), 0, 0).reshape(x.shape)  24.9 us
    pallas_call x9, Pallas kernels, run(): fn(*[pltpu.with_memory_space_constraint(x, spaces[c]) if c in spaces else...  23.5 us
    all_to_all x3, waiting for transfers between devices, spread(): return lax.all_to_all(slot, ('row', 'col'), 0, 0).reshape(x.shape)  12.4 us
    ppermute x4, starting transfers between devices, swap(): lax.ppermute(x, axis, [p for i, j in pairs for p in ((i, j), (j, i))])  5.7 us
    ppermute x3, starting transfers between devices, shards(): lax.ppermute(stats, 'head', [(i, i ^ d) for i in range(heads)])  4.18 us
    ppermute x3, waiting for transfers between devices, shards(): lax.ppermute(stats, 'head', [(i, i ^ d) for i in range(heads)])  3.87 us
  transfers between devices with their start and end apart: 10, of which 5 were waited for; matrix products, arithmetic and copies ran while one was open for 0% of the time, Pallas kernels for 23%

profile of v8, /device:TPU:8, one launch (start us, length us, event | category | flops | bytes accessed | tf_op | source)
XLA Modules:
  0.0 74.9 jit_solution(11341615266532596364)
XLA Ops:
  0.0 0.0 copy-start
  0.0 2.9 %pool_queries.1 = (bf16[512,128]{1,0:T(8,128)(2,1)}, f32[2,80,128]{2,1,0:T(8,128)}) custom-call(s32[2,32,48]{2,1,0:T(8,128)} %bitcast.26, bf16[1536,256]{1,0:T(8,128)(2,1)} %bitcast.20), custom_call_target="tpu_custom_call" | custom-call | bytes 8388608 | tf_op jit(solution)/shard_map/pool_queries/pallas_call | solution.py:49
  2.9 12.1 %all-to-all-start = ((bf16[64,8,128]{2,1,0:T(8,128)(2,1)}), bf16[64,8,128]{2,1,0:T(8,128)(2,1)S(1)}, u32[]{:S(2)}, u32[]{:S(2)}) async-start(bf16[64,8,128]{2,1,0:T(8,128)(2,1)} %bitcast.25), calls=%async_computation | async-start | bytes 262144 | tf_op jit(solution)/shard_map/all_to_all | solution.py:533
  15.0 0.0 copy-done
  15.0 2.4 %turn_keys.1 = (bf16[1536,256]{1,0:T(8,128)(2,1)S(1)}, bf16[48,256]{1,0:T(8,128)(2,1)}, bf16[48,256]{1,0:T(8,128)(2,1)}) custom-call(f32[2,80,128]{2,1,0:T(8,128)} %get-tuple-element.21.tab_hbm_ref, bf16[48,32,256]{2,1,0:T(8,128)(2,1)S(1)} %copy-done, bf16[1536,256]{1,0:T(8,128)(2,1)} %bitcast.23), custom_call_target="tpu_custom_call" | custom-call | bytes 4194304 | tf_op jit(solution)/shard_map/turn_keys/pallas_call | solution.py:49
  17.4 0.2 collective-permute-start
  17.7 0.7 collective-permute-start.1
  18.3 6.1 %all-to-all-done = bf16[64,8,128]{2,1,0:T(8,128)(2,1)S(1)} async-done(((bf16[64,8,128]{2,1,0:T(8,128)(2,1)}), bf16[64,8,128]{2,1,0:T(8,128)(2,1)S(1)}, u32[]{:S(2)}, u32[]{:S(2)}) %all-to-all-start) | async-done | bytes 131104 | tf_op jit(solution)/shard_map/all_to_all | solution.py:533
  24.4 0.0 copy-start.1
  24.4 3.9 %partials.1 = bf16[1024,128]{1,0:T(8,128)(2,1)} custom-call(bf16[512,128]{1,0:T(8,128)(2,1)S(1)} %bitcast.14, bf16[1536,256]{1,0:T(8,128)(2,1)S(1)} %get-tuple-element.22.tk_ref, bf16[1536,256]{1,0:T(8,128)(2,1)S(1)} %bitcast.13), custom_call_target="tpu_custom_call" | custom-call | bytes 10485760 | tf_op jit(solution)/shard_map/partials/pallas_call | solution.py:49
  28.3 0.0 collective-permute-done.near_hbm_ref
  28.3 0.0 copy-start.4
  28.3 0.0 collective-permute-done.1.far_hbm_ref
  28.3 0.0 copy-start.5
  28.3 6.2 %all-to-all-start.1 = ((bf16[64,16,128]{2,1,0:T(8,128)(2,1)}), bf16[64,16,128]{2,1,0:T(8,128)(2,1)S(1)}, u32[]{:S(2)}, u32[]{:S(2)}) async-start(bf16[64,16,128]{2,1,0:T(8,128)(2,1)} %bitcast.22), calls=%async_computation.1 | async-start | bytes 524288 | tf_op jit(solution)/shard_map/all_to_all | solution.py:533
  34.5 0.0 copy-done.4
  34.6 0.0 copy-done.5
  34.6 0.8 %lines.1 = (bf16[48,256]{1,0:T(8,128)(2,1)S(1)}, bf16[48,256]{1,0:T(8,128)(2,1)S(1)}) custom-call(bf16[48,32,256]{2,1,0:T(8,128)(2,1)} %v_hbm_ref.1, bf16[48,256]{1,0:T(8,128)(2,1)} %copy-done.4, bf16[48,256]{1,0:T(8,128)(2,1)} %copy-done.5), custom_call_target="tpu_custom_call" | custom-call | bytes 262144 | tf_op jit(solution)/shard_map/lines/pallas_call | solution.py:49
  35.4 0.5 collective-permute-start.2
  35.9 4.3 %collective-permute-start.3 = (bf16[48,256]{1,0:T(8,128)(2,1)S(1)}, bf16[48,256]{1,0:T(8,128)(2,1)S(1)}, u32[]{:S(2)}, u32[]{:S(2)}) collective-permute-start(bf16[48,256]{1,0:T(8,128)(2,1)S(1)} %get-tuple-element.29), channel_id=1, source_target_pairs={{64,128},{128,64},{65,129},{129,65},{66,130},{130,66},{67,131},{13... | collective-permute-start | bytes 73736 | tf_op jit(solution)/shard_map/ppermute | solution.py:537
  40.2 5.8 %all-to-all-done.1 = bf16[64,16,128]{2,1,0:T(8,128)(2,1)S(1)} async-done(((bf16[64,16,128]{2,1,0:T(8,128)(2,1)}), bf16[64,16,128]{2,1,0:T(8,128)(2,1)S(1)}, u32[]{:S(2)}, u32[]{:S(2)}) %all-to-all-start.1) | async-done | bytes 262176 | tf_op jit(solution)/shard_map/all_to_all | solution.py:533
  46.1 1.1 %merge.1 = bf16[512,128]{1,0:T(8,128)(2,1)} custom-call(bf16[1024,128]{1,0:T(8,128)(2,1)S(1)} %bitcast.16), custom_call_target="tpu_custom_call" | custom-call | bytes 2097152 | tf_op jit(solution)/shard_map/merge/pallas_call | solution.py:49
  47.2 0.0 collective-permute-done.2.mate_ref
  47.2 0.0 collective-permute-done.3.rest_ref
  47.2 6.5 %all-to-all-start.2 = ((bf16[64,8,128]{2,1,0:T(8,128)(2,1)}), bf16[64,8,128]{2,1,0:T(8,128)(2,1)S(1)}, u32[]{:S(2)}, u32[]{:S(2)}) async-start(bf16[64,8,128]{2,1,0:T(8,128)(2,1)} %bitcast.24), calls=%async_computation.2 | async-start | bytes 262144 | tf_op jit(solution)/shard_map/all_to_all | solution.py:533
  53.7 0.0 copy-done.1
  53.7 3.3 %conv.1.conv_hbm_ref = f32[1536,256]{1,0:T(8,128)} custom-call(bf16[48,32,256]{2,1,0:T(8,128)(2,1)} %v_hbm_ref.1, bf16[48,256]{1,0:T(8,128)(2,1)} %copy-done.4, bf16[48,256]{1,0:T(8,128)(2,1)} %copy-done.5, bf16[48,256]{1,0:T(8,128)(2,1)S(1)} %collective-permute-done.2.mate_ref, bf16[48,256]{1,0:T(8,128)(2,1)S(1)} %collective-permute-done.3.rest_ref, ...), custom_call_target="tpu_custom_call" | custom-call | bytes 6291456 | tf_op jit(solution)/shard_map/conv/pallas_call | solution.py:49
  57.0 5.6 %probabilities.1.prob_ref = bf16[1536,1024]{1,0:T(8,128)(2,1)S(1)} custom-call(bf16[512,128]{1,0:T(8,128)(2,1)S(1)} %bitcast.15, f32[2,80,128]{2,1,0:T(8,128)} %get-tuple-element.21.tab_hbm_ref, bf16[1536,256]{1,0:T(8,128)(2,1)} %bitcast.21), custom_call_target="tpu_custom_call" | custom-call | bytes 20971520 | tf_op jit(solution)/shard_map/probabilities/pallas_call | solution.py:49
  62.6 0.5 all-to-all-done.2
  63.1 0.0 copy-start.2
  63.1 0.0 copy-start.3
  63.1 2.3 %attend.1 = (f32[1536,256]{1,0:T(8,128)S(1)}, f32[24,128]{1,0:T(8,128)S(1)}) custom-call(bf16[512,128]{1,0:T(8,128)(2,1)S(1)} %bitcast.17, bf16[1536,1024]{1,0:T(8,128)(2,1)S(1)} %probabilities.1.prob_ref, f32[1536,256]{1,0:T(8,128)} %conv.1.conv_hbm_ref), custom_call_target="tpu_custom_call" | custom-call | bytes 4194304 | tf_op jit(solution)/shard_map/attend/pallas_call | solution.py:49
  65.5 2.8 %collective-permute-start.6 = (f32[24,128]{1,0:T(8,128)S(1)}, f32[24,128]{1,0:T(8,128)S(1)}, u32[]{:S(2)}, u32[]{:S(2)}) collective-permute-start(f32[24,128]{1,0:T(8,128)S(1)} %get-tuple-element.33.s0_ref), channel_id=1, source_target_pairs={{0,3},{1,2},{2,1},{3,0},{4,7},{5,6},{6,5},{7,4},{8,11},{9,10},{10,... | collective-permute-start | bytes 36872 | tf_op jit(solution)/shard_map/ppermute | solution.py:640
  68.3 0.8 %collective-permute-start.5 = (f32[24,128]{1,0:T(8,128)S(1)}, f32[24,128]{1,0:T(8,128)S(1)}, u32[]{:S(2)}, u32[]{:S(2)}) collective-permute-start(f32[24,128]{1,0:T(8,128)S(1)} %get-tuple-element.33.s0_ref), channel_id=1, source_target_pairs={{0,2},{1,3},{2,0},{3,1},{4,6},{5,7},{6,4},{7,5},{8,10},{9,11},{10,... | collective-permute-start | bytes 36872 | tf_op jit(solution)/shard_map/ppermute | solution.py:640
  69.1 0.5 collective-permute-start.4
  69.6 0.8 %collective-permute-done.6.s3_ref = f32[24,128]{1,0:T(8,128)S(1)} collective-permute-done((f32[24,128]{1,0:T(8,128)S(1)}, f32[24,128]{1,0:T(8,128)S(1)}, u32[]{:S(2)}, u32[]{:S(2)}) %collective-permute-start.6) | collective-permute-done | bytes 12320 | tf_op jit(solution)/shard_map/ppermute | solution.py:640
  70.5 3.1 %collective-permute-done.5.s2_ref = f32[24,128]{1,0:T(8,128)S(1)} collective-permute-done((f32[24,128]{1,0:T(8,128)S(1)}, f32[24,128]{1,0:T(8,128)S(1)}, u32[]{:S(2)}, u32[]{:S(2)}) %collective-permute-start.5) | collective-permute-done | bytes 12320 | tf_op jit(solution)/shard_map/ppermute | solution.py:640
  73.5 0.0 collective-permute-done.4.s1_ref
  73.5 0.0 copy-done.2
  73.5 0.0 copy-done.3
  73.5 1.2 %norm.1 = bf16[1536,256]{1,0:T(8,128)(2,1)} custom-call(f32[24,128]{1,0:T(8,128)S(1)} %get-tuple-element.33.s0_ref, f32[24,128]{1,0:T(8,128)S(1)} %collective-permute-done.4.s1_ref, f32[24,128]{1,0:T(8,128)S(1)} %collective-permute-done.5.s2_ref, f32[24,128]{1,0:T(8,128)S(1)} %collective-permute-done.6.s3_ref, f32[1536,256]{1,0:T(8,128)S(1)} %get-tuple-element.34.sum_ref, ...), custom_call_target="tpu_custom_call" | custom-call | bytes 4194304 | tf_op jit(solution)/shard_map/norm/pallas_call | solution.py:49
Async XLA Ops:
  0.0 15.0 %copy-start = (bf16[48,32,256]{2,1,0:T(8,128)(2,1)S(1)}, bf16[48,32,256]{2,1,0:T(8,128)(2,1)}, u32[]{:S(2)}) copy-start(bf16[48,32,256]{2,1,0:T(8,128)(2,1)} %v_hbm_ref.1) | copy-start | bytes 2359300
  2.9 21.5 %all-to-all-start = ((bf16[64,8,128]{2,1,0:T(8,128)(2,1)}), bf16[64,8,128]{2,1,0:T(8,128)(2,1)S(1)}, u32[]{:S(2)}, u32[]{:S(2)}) async-start(bf16[64,8,128]{2,1,0:T(8,128)(2,1)} %bitcast.25), calls=%async_computation | async-start | bytes 262144 | tf_op jit(solution)/shard_map/all_to_all | solution.py:533
  17.4 10.9 %collective-permute-start = (bf16[48,256]{1,0:T(8,128)(2,1)}, bf16[48,256]{1,0:T(8,128)(2,1)S(1)}, u32[]{:S(2)}, u32[]{:S(2)}) collective-permute-start(bf16[48,256]{1,0:T(8,128)(2,1)} %get-tuple-element.23), channel_id=1, source_target_pairs={{0,4},{4,0},{8,12},{12,8},{16,20},{20,16},{24,28},{28,24},{32,36},... | collective-permute-start | bytes 73736 | tf_op jit(solution)/shard_map/ppermute | solution.py:537
  17.7 10.6 %collective-permute-start.1 = (bf16[48,256]{1,0:T(8,128)(2,1)}, bf16[48,256]{1,0:T(8,128)(2,1)S(1)}, u32[]{:S(2)}, u32[]{:S(2)}) collective-permute-start(bf16[48,256]{1,0:T(8,128)(2,1)} %get-tuple-element.24), channel_id=1, source_target_pairs={{4,8},{8,4},{12,16},{16,12},{20,24},{24,20},{28,32},{32,28},{36,40... | collective-permute-start | bytes 73736 | tf_op jit(solution)/shard_map/ppermute | solution.py:537
  24.4 29.3 %copy-start.1 = (f32[9,256]{1,0:T(8,128)S(1)}, f32[9,256]{1,0:T(8,128)}, u32[]{:S(2)}) copy-start(f32[9,256]{1,0:T(8,128)} %w_ref.1) | copy-start | bytes 27652
  28.3 6.3 %copy-start.4 = (bf16[48,256]{1,0:T(8,128)(2,1)}, bf16[48,256]{1,0:T(8,128)(2,1)S(1)}, u32[]{:S(2)}) copy-start(bf16[48,256]{1,0:T(8,128)(2,1)S(1)} %collective-permute-done.near_hbm_ref) | copy-start | bytes 73732
  28.3 6.3 %copy-start.5 = (bf16[48,256]{1,0:T(8,128)(2,1)}, bf16[48,256]{1,0:T(8,128)(2,1)S(1)}, u32[]{:S(2)}) copy-start(bf16[48,256]{1,0:T(8,128)(2,1)S(1)} %collective-permute-done.1.far_hbm_ref) | copy-start | bytes 73732
  28.3 17.8 %all-to-all-start.1 = ((bf16[64,16,128]{2,1,0:T(8,128)(2,1)}), bf16[64,16,128]{2,1,0:T(8,128)(2,1)S(1)}, u32[]{:S(2)}, u32[]{:S(2)}) async-start(bf16[64,16,128]{2,1,0:T(8,128)(2,1)} %bitcast.22), calls=%async_computation.1 | async-start | bytes 524288 | tf_op jit(solution)/shard_map/all_to_all | solution.py:533
  35.4 11.8 %collective-permute-start.2 = (bf16[48,256]{1,0:T(8,128)(2,1)S(1)}, bf16[48,256]{1,0:T(8,128)(2,1)S(1)}, u32[]{:S(2)}, u32[]{:S(2)}) collective-permute-start(bf16[48,256]{1,0:T(8,128)(2,1)S(1)} %get-tuple-element.28), channel_id=1, source_target_pairs={{0,64},{64,0},{128,192},{192,128},{1,65},{65,1},{129,193},{193,129... | collective-permute-start | bytes 73736 | tf_op jit(solution)/shard_map/ppermute | solution.py:537
  35.9 11.3 %collective-permute-start.3 = (bf16[48,256]{1,0:T(8,128)(2,1)S(1)}, bf16[48,256]{1,0:T(8,128)(2,1)S(1)}, u32[]{:S(2)}, u32[]{:S(2)}) collective-permute-start(bf16[48,256]{1,0:T(8,128)(2,1)S(1)} %get-tuple-element.29), channel_id=1, source_target_pairs={{64,128},{128,64},{65,129},{129,65},{66,130},{130,66},{67,131},{13... | collective-permute-start | bytes 73736 | tf_op jit(solution)/shard_map/ppermute | solution.py:537
  47.2 15.9 %all-to-all-start.2 = ((bf16[64,8,128]{2,1,0:T(8,128)(2,1)}), bf16[64,8,128]{2,1,0:T(8,128)(2,1)S(1)}, u32[]{:S(2)}, u32[]{:S(2)}) async-start(bf16[64,8,128]{2,1,0:T(8,128)(2,1)} %bitcast.24), calls=%async_computation.2 | async-start | bytes 262144 | tf_op jit(solution)/shard_map/all_to_all | solution.py:533
  63.1 10.4 %copy-start.2 = (f32[256]{0:T(256)S(1)}, f32[256]{0:T(256)}, u32[]{:S(2)}) copy-start(f32[256]{0:T(256)} %param.12) | copy-start | bytes 3076
  63.1 10.4 %copy-start.3 = (f32[256]{0:T(256)S(1)}, f32[256]{0:T(256)}, u32[]{:S(2)}) copy-start(f32[256]{0:T(256)} %param.13) | copy-start | bytes 3076
  65.5 5.0 %collective-permute-start.6 = (f32[24,128]{1,0:T(8,128)S(1)}, f32[24,128]{1,0:T(8,128)S(1)}, u32[]{:S(2)}, u32[]{:S(2)}) collective-permute-start(f32[24,128]{1,0:T(8,128)S(1)} %get-tuple-element.33.s0_ref), channel_id=1, source_target_pairs={{0,3},{1,2},{2,1},{3,0},{4,7},{5,6},{6,5},{7,4},{8,11},{9,10},{10,... | collective-permute-start | bytes 36872 | tf_op jit(solution)/shard_map/ppermute | solution.py:640
  68.3 5.2 %collective-permute-start.5 = (f32[24,128]{1,0:T(8,128)S(1)}, f32[24,128]{1,0:T(8,128)S(1)}, u32[]{:S(2)}, u32[]{:S(2)}) collective-permute-start(f32[24,128]{1,0:T(8,128)S(1)} %get-tuple-element.33.s0_ref), channel_id=1, source_target_pairs={{0,2},{1,3},{2,0},{3,1},{4,6},{5,7},{6,4},{7,5},{8,10},{9,11},{10,... | collective-permute-start | bytes 36872 | tf_op jit(solution)/shard_map/ppermute | solution.py:640
  69.1 4.4 %collective-permute-start.4 = (f32[24,128]{1,0:T(8,128)S(1)}, f32[24,128]{1,0:T(8,128)S(1)}, u32[]{:S(2)}, u32[]{:S(2)}) collective-permute-start(f32[24,128]{1,0:T(8,128)S(1)} %get-tuple-element.33.s0_ref), channel_id=1, source_target_pairs={{0,1},{1,0},{2,3},{3,2},{4,5},{5,4},{6,7},{7,6},{8,9},{9,8},{10,11... | collective-permute-start | bytes 36872 | tf_op jit(solution)/shard_map/ppermute | solution.py:640

commit v9 on v8

--- a/solution.py
+++ b/solution.py
@@ -326,28 +326,10 @@
     lax.fori_loop(0, N // chunk, body, 0)
 
 
-def line_kernel(
-    v_ref,
-    near_hbm_ref,
-    far_hbm_ref,
-    mate_ref,
-    rest_ref,
-    top_ref,
-    bottom_ref,
-    near_ref,
-    far_ref,
-    sems,
-):
+def line_kernel(v_ref, near_ref, far_ref, mate_ref, rest_ref, top_ref, bottom_ref, sems):
     copies = [
-        pltpu.make_async_copy(source, target, sems.at[i])
-        for i, (source, target) in enumerate(
-            (
-                (v_ref.at[0], top_ref),
-                (v_ref.at[TR - 1], bottom_ref),
-                (near_hbm_ref, near_ref),
-                (far_hbm_ref, far_ref),
-            )
-        )
+        pltpu.make_async_copy(v_ref.at[0], top_ref, sems.at[0]),
+        pltpu.make_async_copy(v_ref.at[TR - 1], bottom_ref, sems.at[1]),
     ]
     for copy in copies:
         copy.start()
@@ -366,16 +348,13 @@
 
 
 def conv_kernel(
-    v_hbm_ref,
-    near_hbm_ref,
-    far_hbm_ref,
+    v_ref,
+    near_ref,
+    far_ref,
     mate_ref,
     rest_ref,
     w_ref,
     out_hbm_ref,
-    v_ref,
-    near_ref,
-    far_ref,
     above_ref,
     below_ref,
     l_ref,
@@ -383,38 +362,22 @@
     out_ref,
     sems,
 ):
-    copies = [
-        pltpu.make_async_copy(near_hbm_ref, near_ref, sems.at[0]),
-        pltpu.make_async_copy(far_hbm_ref, far_ref, sems.at[1]),
-    ]
-    for half in range(2):
-        cols = pl.ds(half * 128, 128)
-        copies.append(
-            pltpu.make_async_copy(
-                v_hbm_ref.at[:, :, cols], v_ref.at[:, :, cols], sems.at[2 + half]
-            )
-        )
     outs = []
     for half in range(2):
         cols = pl.ds(half * 128, 128)
         outs.append(
             pltpu.make_async_copy(
-                out_ref.at[:, cols], out_hbm_ref.at[:, cols], sems.at[4 + half]
+                out_ref.at[:, cols], out_hbm_ref.at[:, cols], sems.at[half]
             )
         )
-    for copy in copies:
-        copy.start()
     mate, rest = mate_ref[...].astype(f32), rest_ref[...].astype(f32)
     above_ref[...] = jnp.where(even_row(), rest, mate)
     below_ref[...] = jnp.where(even_row(), mate, rest)
-    copies[0].wait()
-    copies[1].wait()
     mate, rest = near_ref[...].astype(f32), far_ref[...].astype(f32)
     l_ref[...] = jnp.where(even_core(), rest, mate)
     r_ref[...] = jnp.where(even_core(), mate, rest)
     for half in range(2):
         cols = pl.ds(half * 128, 128)
-        copies[2 + half].wait()
 
         def put(at, total):
             out_ref[pl.ds(at, TC), cols] = total
@@ -587,10 +550,8 @@
     mate, rest = call(
         line_kernel,
         (near((TC + 16, CH), bf16),) * 2,
-        "hhh",
-        scratch=[pltpu.VMEM((TC, CH), bf16)] * 2
-        + [pltpu.VMEM((TR, CH), bf16)] * 2
-        + [pltpu.SemaphoreType.DMA((4,))],
+        "hvv",
+        scratch=[pltpu.VMEM((TC, CH), bf16)] * 2 + [pltpu.SemaphoreType.DMA((2,))],
         nbytes=mb // 4,
         name="lines",
     )(values, inner, outer)
@@ -617,12 +578,10 @@
     convolved = call(
         conv_kernel,
         (far((N, CH), f32),),
-        "hhh   ",
-        scratch=[pltpu.VMEM((TR, TC, CH), bf16)]
-        + [pltpu.VMEM((TR, CH), bf16)] * 2
-        + [pltpu.VMEM((TC + 16, CH), f32)] * 2
+        " vvvv ",
+        scratch=[pltpu.VMEM((TC + 16, CH), f32)] * 2
         + [pltpu.VMEM((TR, CH), f32)] * 2
-        + [pltpu.VMEM((N, CH), f32), pltpu.SemaphoreType.DMA((6,))],
+        + [pltpu.VMEM((N, CH), f32), pltpu.SemaphoreType.DMA((2,))],
         nbytes=6 * mb,
         out_spaces="h",
         name="conv",

time: 75.9 us -> 76 us (level)
  Pallas kernels: 23.5 us -> 22.3 us
  waiting for transfers between devices: 16.3 us -> 17.5 us
    all_to_all x3, waiting for transfers between devices: 12.4 us -> 13.6 us  [spread(): return lax.all_to_all(slot, ('row', 'col'), 0, 0).reshape(x.shape)]
    pallas_call x9, Pallas kernels: 23.5 us -> 22.3 us  [run(): fn(*[pltpu.with_memory_space_constraint(x, spaces[c]) if c in spaces else...]
  transfers between devices with their start and end apart: 10 -> 10, of which waited for: 5 -> 5; matrix products, arithmetic and copies ran while one was open for 0% -> 0% of each run, Pallas kernels for 23% -> 21%
where the time goes in v9:
time: 76 us; the launch traced here: 74.9 us
  starting transfers between devices  34.7 us (46%)
  Pallas kernels  22.3 us (29%)
  waiting for transfers between devices  17.5 us (23%)
    all_to_all x3, starting transfers between devices, spread(): return lax.all_to_all(slot, ('row', 'col'), 0, 0).reshape(x.shape)  24.8 us
    pallas_call x9, Pallas kernels, run(): fn(*[pltpu.with_memory_space_constraint(x, spaces[c]) if c in spaces else...  22.3 us
    all_to_all x3, waiting for transfers between devices, spread(): return lax.all_to_all(slot, ('row', 'col'), 0, 0).reshape(x.shape)  13.6 us
    ppermute x4, starting transfers between devices, swap(): lax.ppermute(x, axis, [p for i, j in pairs for p in ((i, j), (j, i))])  5.7 us
    ppermute x3, starting transfers between devices, shards(): lax.ppermute(stats, 'head', [(i, i ^ d) for i in range(heads)])  4.18 us
    ppermute x3, waiting for transfers between devices, shards(): lax.ppermute(stats, 'head', [(i, i ^ d) for i in range(heads)])  3.87 us
  transfers between devices with their start and end apart: 10, of which 5 were waited for; matrix products, arithmetic and copies ran while one was open for 0% of the time, Pallas kernels for 21%

profile of v9, /device:TPU:8, one launch (start us, length us, event | category | flops | bytes accessed | tf_op | source)
XLA Modules:
  0.0 74.9 jit_solution(10998608897557292761)
XLA Ops:
  0.0 0.0 copy-start
  0.0 2.9 %pool_queries.1 = (bf16[512,128]{1,0:T(8,128)(2,1)}, f32[2,80,128]{2,1,0:T(8,128)}) custom-call(s32[2,32,48]{2,1,0:T(8,128)} %bitcast.26, bf16[1536,256]{1,0:T(8,128)(2,1)} %bitcast.20), custom_call_target="tpu_custom_call" | custom-call | bytes 8388608 | tf_op jit(solution)/shard_map/pool_queries/pallas_call | solution.py:49
  2.9 12.1 %all-to-all-start = ((bf16[64,8,128]{2,1,0:T(8,128)(2,1)}), bf16[64,8,128]{2,1,0:T(8,128)(2,1)S(1)}, u32[]{:S(2)}, u32[]{:S(2)}) async-start(bf16[64,8,128]{2,1,0:T(8,128)(2,1)} %bitcast.25), calls=%async_computation | async-start | bytes 262144 | tf_op jit(solution)/shard_map/all_to_all | solution.py:496
  15.0 0.0 copy-done
  15.0 2.4 %turn_keys.1 = (bf16[1536,256]{1,0:T(8,128)(2,1)S(1)}, bf16[48,256]{1,0:T(8,128)(2,1)}, bf16[48,256]{1,0:T(8,128)(2,1)}) custom-call(f32[2,80,128]{2,1,0:T(8,128)} %get-tuple-element.21.tab_hbm_ref, bf16[48,32,256]{2,1,0:T(8,128)(2,1)S(1)} %copy-done, bf16[1536,256]{1,0:T(8,128)(2,1)} %bitcast.23), custom_call_target="tpu_custom_call" | custom-call | bytes 4194304 | tf_op jit(solution)/shard_map/turn_keys/pallas_call | solution.py:49
  17.4 0.2 collective-permute-start
  17.6 0.7 collective-permute-start.1
  18.3 6.1 %all-to-all-done = bf16[64,8,128]{2,1,0:T(8,128)(2,1)S(1)} async-done(((bf16[64,8,128]{2,1,0:T(8,128)(2,1)}), bf16[64,8,128]{2,1,0:T(8,128)(2,1)S(1)}, u32[]{:S(2)}, u32[]{:S(2)}) %all-to-all-start) | async-done | bytes 131104 | tf_op jit(solution)/shard_map/all_to_all | solution.py:496
  24.4 0.0 copy-start.1
  24.4 0.0 copy-start.2
  24.4 3.9 %partials.1 = bf16[1024,128]{1,0:T(8,128)(2,1)} custom-call(bf16[512,128]{1,0:T(8,128)(2,1)S(1)} %bitcast.14, bf16[1536,256]{1,0:T(8,128)(2,1)S(1)} %get-tuple-element.22.tk_ref, bf16[1536,256]{1,0:T(8,128)(2,1)S(1)} %bitcast.13), custom_call_target="tpu_custom_call" | custom-call | bytes 10485760 | tf_op jit(solution)/shard_map/partials/pallas_call | solution.py:49
  28.3 0.0 collective-permute-done.near_ref
  28.3 0.0 collective-permute-done.1.far_ref
  28.3 6.2 %all-to-all-start.1 = ((bf16[64,16,128]{2,1,0:T(8,128)(2,1)}), bf16[64,16,128]{2,1,0:T(8,128)(2,1)S(1)}, u32[]{:S(2)}, u32[]{:S(2)}) async-start(bf16[64,16,128]{2,1,0:T(8,128)(2,1)} %bitcast.22), calls=%async_computation.1 | async-start | bytes 524288 | tf_op jit(solution)/shard_map/all_to_all | solution.py:496
  34.5 0.8 %lines.1 = (bf16[48,256]{1,0:T(8,128)(2,1)S(1)}, bf16[48,256]{1,0:T(8,128)(2,1)S(1)}) custom-call(bf16[48,32,256]{2,1,0:T(8,128)(2,1)} %v_ref.5, bf16[48,256]{1,0:T(8,128)(2,1)S(1)} %collective-permute-done.near_ref, bf16[48,256]{1,0:T(8,128)(2,1)S(1)} %collective-permute-done.1.far_ref), custom_call_target="tpu_custom_call" | custom-call | bytes 262144 | tf_op jit(solution)/shard_map/lines/pallas_call | solution.py:49
  35.3 0.5 collective-permute-start.2
  35.8 4.3 %collective-permute-start.3 = (bf16[48,256]{1,0:T(8,128)(2,1)S(1)}, bf16[48,256]{1,0:T(8,128)(2,1)S(1)}, u32[]{:S(2)}, u32[]{:S(2)}) collective-permute-start(bf16[48,256]{1,0:T(8,128)(2,1)S(1)} %get-tuple-element.29), channel_id=1, source_target_pairs={{64,128},{128,64},{65,129},{129,65},{66,130},{130,66},{67,131},{13... | collective-permute-start | bytes 73736 | tf_op jit(solution)/shard_map/ppermute | solution.py:500
  40.1 5.9 %all-to-all-done.1 = bf16[64,16,128]{2,1,0:T(8,128)(2,1)S(1)} async-done(((bf16[64,16,128]{2,1,0:T(8,128)(2,1)}), bf16[64,16,128]{2,1,0:T(8,128)(2,1)S(1)}, u32[]{:S(2)}, u32[]{:S(2)}) %all-to-all-start.1) | async-done | bytes 262176 | tf_op jit(solution)/shard_map/all_to_all | solution.py:496
  46.1 1.1 %merge.1 = bf16[512,128]{1,0:T(8,128)(2,1)} custom-call(bf16[1024,128]{1,0:T(8,128)(2,1)S(1)} %bitcast.16), custom_call_target="tpu_custom_call" | custom-call | bytes 2097152 | tf_op jit(solution)/shard_map/merge/pallas_call | solution.py:49
  47.2 0.0 collective-permute-done.2.mate_ref
  47.2 0.0 collective-permute-done.3.rest_ref
  47.2 6.5 %all-to-all-start.2 = ((bf16[64,8,128]{2,1,0:T(8,128)(2,1)}), bf16[64,8,128]{2,1,0:T(8,128)(2,1)S(1)}, u32[]{:S(2)}, u32[]{:S(2)}) async-start(bf16[64,8,128]{2,1,0:T(8,128)(2,1)} %bitcast.24), calls=%async_computation.2 | async-start | bytes 262144 | tf_op jit(solution)/shard_map/all_to_all | solution.py:496
  53.7 0.0 copy-done.1
  53.7 0.0 copy-done.2
  53.7 2.2 %conv.1.conv_hbm_ref = f32[1536,256]{1,0:T(8,128)} custom-call(bf16[48,32,256]{2,1,0:T(8,128)(2,1)S(1)} %copy-done.1, bf16[48,256]{1,0:T(8,128)(2,1)S(1)} %collective-permute-done.near_ref, bf16[48,256]{1,0:T(8,128)(2,1)S(1)} %collective-permute-done.1.far_ref, bf16[48,256]{1,0:T(8,128)(2,1)S(1)} %collective-permute-done.2.mate_ref, ...), custom_call_target="tpu_custom_call" | custom-call | bytes 6291456 | tf_op jit(solution)/shard_map/conv/pallas_call | solution.py:49
  55.9 5.6 %probabilities.1.prob_ref = bf16[1536,1024]{1,0:T(8,128)(2,1)S(1)} custom-call(bf16[512,128]{1,0:T(8,128)(2,1)S(1)} %bitcast.15, f32[2,80,128]{2,1,0:T(8,128)} %get-tuple-element.21.tab_hbm_ref, bf16[1536,256]{1,0:T(8,128)(2,1)} %bitcast.21), custom_call_target="tpu_custom_call" | custom-call | bytes 20971520 | tf_op jit(solution)/shard_map/probabilities/pallas_call | solution.py:49
  61.6 1.6 %all-to-all-done.2 = bf16[64,8,128]{2,1,0:T(8,128)(2,1)S(1)} async-done(((bf16[64,8,128]{2,1,0:T(8,128)(2,1)}), bf16[64,8,128]{2,1,0:T(8,128)(2,1)S(1)}, u32[]{:S(2)}, u32[]{:S(2)}) %all-to-all-start.2) | async-done | bytes 131104 | tf_op jit(solution)/shard_map/all_to_all | solution.py:496
  63.1 0.0 copy-start.3
  63.1 0.0 copy-start.4
  63.1 2.3 %attend.1 = (f32[1536,256]{1,0:T(8,128)S(1)}, f32[24,128]{1,0:T(8,128)S(1)}) custom-call(bf16[512,128]{1,0:T(8,128)(2,1)S(1)} %bitcast.17, bf16[1536,1024]{1,0:T(8,128)(2,1)S(1)} %probabilities.1.prob_ref, f32[1536,256]{1,0:T(8,128)} %conv.1.conv_hbm_ref), custom_call_target="tpu_custom_call" | custom-call | bytes 4194304 | tf_op jit(solution)/shard_map/attend/pallas_call | solution.py:49
  65.4 2.8 %collective-permute-start.6 = (f32[24,128]{1,0:T(8,128)S(1)}, f32[24,128]{1,0:T(8,128)S(1)}, u32[]{:S(2)}, u32[]{:S(2)}) collective-permute-start(f32[24,128]{1,0:T(8,128)S(1)} %get-tuple-element.33.s0_ref), channel_id=1, source_target_pairs={{0,3},{1,2},{2,1},{3,0},{4,7},{5,6},{6,5},{7,4},{8,11},{9,10},{10,... | collective-permute-start | bytes 36872 | tf_op jit(solution)/shard_map/ppermute | solution.py:599
  68.3 0.8 %collective-permute-start.5 = (f32[24,128]{1,0:T(8,128)S(1)}, f32[24,128]{1,0:T(8,128)S(1)}, u32[]{:S(2)}, u32[]{:S(2)}) collective-permute-start(f32[24,128]{1,0:T(8,128)S(1)} %get-tuple-element.33.s0_ref), channel_id=1, source_target_pairs={{0,2},{1,3},{2,0},{3,1},{4,6},{5,7},{6,4},{7,5},{8,10},{9,11},{10,... | collective-permute-start | bytes 36872 | tf_op jit(solution)/shard_map/ppermute | solution.py:599
  69.1 0.5 collective-permute-start.4
  69.6 0.8 %collective-permute-done.6.s3_ref = f32[24,128]{1,0:T(8,128)S(1)} collective-permute-done((f32[24,128]{1,0:T(8,128)S(1)}, f32[24,128]{1,0:T(8,128)S(1)}, u32[]{:S(2)}, u32[]{:S(2)}) %collective-permute-start.6) | collective-permute-done | bytes 12320 | tf_op jit(solution)/shard_map/ppermute | solution.py:599
  70.4 3.1 %collective-permute-done.5.s2_ref = f32[24,128]{1,0:T(8,128)S(1)} collective-permute-done((f32[24,128]{1,0:T(8,128)S(1)}, f32[24,128]{1,0:T(8,128)S(1)}, u32[]{:S(2)}, u32[]{:S(2)}) %collective-permute-start.5) | collective-permute-done | bytes 12320 | tf_op jit(solution)/shard_map/ppermute | solution.py:599
  73.5 0.0 collective-permute-done.4.s1_ref
  73.5 0.0 copy-done.3
  73.5 0.0 copy-done.4
  73.5 1.2 %norm.1 = bf16[1536,256]{1,0:T(8,128)(2,1)} custom-call(f32[24,128]{1,0:T(8,128)S(1)} %get-tuple-element.33.s0_ref, f32[24,128]{1,0:T(8,128)S(1)} %collective-permute-done.4.s1_ref, f32[24,128]{1,0:T(8,128)S(1)} %collective-permute-done.5.s2_ref, f32[24,128]{1,0:T(8,128)S(1)} %collective-permute-done.6.s3_ref, f32[1536,256]{1,0:T(8,128)S(1)} %get-tuple-element.34.sum_ref, ...), custom_call_target="tpu_custom_call" | custom-call | bytes 4194304 | tf_op jit(solution)/shard_map/norm/pallas_call | solution.py:49
Async XLA Ops:
  0.0 15.0 %copy-start = (bf16[48,32,256]{2,1,0:T(8,128)(2,1)S(1)}, bf16[48,32,256]{2,1,0:T(8,128)(2,1)}, u32[]{:S(2)}) copy-start(bf16[48,32,256]{2,1,0:T(8,128)(2,1)} %v_ref.5) | copy-start | bytes 2359300
  2.9 21.5 %all-to-all-start = ((bf16[64,8,128]{2,1,0:T(8,128)(2,1)}), bf16[64,8,128]{2,1,0:T(8,128)(2,1)S(1)}, u32[]{:S(2)}, u32[]{:S(2)}) async-start(bf16[64,8,128]{2,1,0:T(8,128)(2,1)} %bitcast.25), calls=%async_computation | async-start | bytes 262144 | tf_op jit(solution)/shard_map/all_to_all | solution.py:496
  17.4 10.9 %collective-permute-start = (bf16[48,256]{1,0:T(8,128)(2,1)}, bf16[48,256]{1,0:T(8,128)(2,1)S(1)}, u32[]{:S(2)}, u32[]{:S(2)}) collective-permute-start(bf16[48,256]{1,0:T(8,128)(2,1)} %get-tuple-element.23), channel_id=1, source_target_pairs={{0,4},{4,0},{8,12},{12,8},{16,20},{20,16},{24,28},{28,24},{32,36},... | collective-permute-start | bytes 73736 | tf_op jit(solution)/shard_map/ppermute | solution.py:500
  17.6 10.6 %collective-permute-start.1 = (bf16[48,256]{1,0:T(8,128)(2,1)}, bf16[48,256]{1,0:T(8,128)(2,1)S(1)}, u32[]{:S(2)}, u32[]{:S(2)}) collective-permute-start(bf16[48,256]{1,0:T(8,128)(2,1)} %get-tuple-element.24), channel_id=1, source_target_pairs={{4,8},{8,4},{12,16},{16,12},{20,24},{24,20},{28,32},{32,28},{36,40... | collective-permute-start | bytes 73736 | tf_op jit(solution)/shard_map/ppermute | solution.py:500
  24.4 29.3 %copy-start.1 = (bf16[48,32,256]{2,1,0:T(8,128)(2,1)S(1)}, bf16[48,32,256]{2,1,0:T(8,128)(2,1)}, u32[]{:S(2)}) copy-start(bf16[48,32,256]{2,1,0:T(8,128)(2,1)} %v_ref.5) | copy-start | bytes 2359300
  24.4 29.3 %copy-start.2 = (f32[9,256]{1,0:T(8,128)S(1)}, f32[9,256]{1,0:T(8,128)}, u32[]{:S(2)}) copy-start(f32[9,256]{1,0:T(8,128)} %w_ref.1) | copy-start | bytes 27652
  28.3 17.8 %all-to-all-start.1 = ((bf16[64,16,128]{2,1,0:T(8,128)(2,1)}), bf16[64,16,128]{2,1,0:T(8,128)(2,1)S(1)}, u32[]{:S(2)}, u32[]{:S(2)}) async-start(bf16[64,16,128]{2,1,0:T(8,128)(2,1)} %bitcast.22), calls=%async_computation.1 | async-start | bytes 524288 | tf_op jit(solution)/shard_map/all_to_all | solution.py:496
  35.3 11.9 %collective-permute-start.2 = (bf16[48,256]{1,0:T(8,128)(2,1)S(1)}, bf16[48,256]{1,0:T(8,128)(2,1)S(1)}, u32[]{:S(2)}, u32[]{:S(2)}) collective-permute-start(bf16[48,256]{1,0:T(8,128)(2,1)S(1)} %get-tuple-element.28), channel_id=1, source_target_pairs={{0,64},{64,0},{128,192},{192,128},{1,65},{65,1},{129,193},{193,129... | collective-permute-start | bytes 73736 | tf_op jit(solution)/shard_map/ppermute | solution.py:500
  35.8 11.4 %collective-permute-start.3 = (bf16[48,256]{1,0:T(8,128)(2,1)S(1)}, bf16[48,256]{1,0:T(8,128)(2,1)S(1)}, u32[]{:S(2)}, u32[]{:S(2)}) collective-permute-start(bf16[48,256]{1,0:T(8,128)(2,1)S(1)} %get-tuple-element.29), channel_id=1, source_target_pairs={{64,128},{128,64},{65,129},{129,65},{66,130},{130,66},{67,131},{13... | collective-permute-start | bytes 73736 | tf_op jit(solution)/shard_map/ppermute | solution.py:500
  47.2 15.9 %all-to-all-start.2 = ((bf16[64,8,128]{2,1,0:T(8,128)(2,1)}), bf16[64,8,128]{2,1,0:T(8,128)(2,1)S(1)}, u32[]{:S(2)}, u32[]{:S(2)}) async-start(bf16[64,8,128]{2,1,0:T(8,128)(2,1)} %bitcast.24), calls=%async_computation.2 | async-start | bytes 262144 | tf_op jit(solution)/shard_map/all_to_all | solution.py:496
  63.1 10.4 %copy-start.3 = (f32[256]{0:T(256)S(1)}, f32[256]{0:T(256)}, u32[]{:S(2)}) copy-start(f32[256]{0:T(256)} %param.12) | copy-start | bytes 3076
  63.1 10.4 %copy-start.4 = (f32[256]{0:T(256)S(1)}, f32[256]{0:T(256)}, u32[]{:S(2)}) copy-start(f32[256]{0:T(256)} %param.13) | copy-start | bytes 3076
  65.4 5.0 %collective-permute-start.6 = (f32[24,128]{1,0:T(8,128)S(1)}, f32[24,128]{1,0:T(8,128)S(1)}, u32[]{:S(2)}, u32[]{:S(2)}) collective-permute-start(f32[24,128]{1,0:T(8,128)S(1)} %get-tuple-element.33.s0_ref), channel_id=1, source_target_pairs={{0,3},{1,2},{2,1},{3,0},{4,7},{5,6},{6,5},{7,4},{8,11},{9,10},{10,... | collective-permute-start | bytes 36872 | tf_op jit(solution)/shard_map/ppermute | solution.py:599
  68.3 5.2 %collective-permute-start.5 = (f32[24,128]{1,0:T(8,128)S(1)}, f32[24,128]{1,0:T(8,128)S(1)}, u32[]{:S(2)}, u32[]{:S(2)}) collective-permute-start(f32[24,128]{1,0:T(8,128)S(1)} %get-tuple-element.33.s0_ref), channel_id=1, source_target_pairs={{0,2},{1,3},{2,0},{3,1},{4,6},{5,7},{6,4},{7,5},{8,10},{9,11},{10,... | collective-permute-start | bytes 36872 | tf_op jit(solution)/shard_map/ppermute | solution.py:599
  69.1 4.4 %collective-permute-start.4 = (f32[24,128]{1,0:T(8,128)S(1)}, f32[24,128]{1,0:T(8,128)S(1)}, u32[]{:S(2)}, u32[]{:S(2)}) collective-permute-start(f32[24,128]{1,0:T(8,128)S(1)} %get-tuple-element.33.s0_ref), channel_id=1, source_target_pairs={{0,1},{1,0},{2,3},{3,2},{4,5},{5,4},{6,7},{7,6},{8,9},{9,8},{10,11... | collective-permute-start | bytes 36872 | tf_op jit(solution)/shard_map/ppermute | solution.py:599

commit v10 on v9

--- a/solution.py
+++ b/solution.py
@@ -201,15 +201,12 @@
         tk_ref[part, :] = turned(held_ref[part, :], matrix, cosine, sine)
 
 
-def agent_pairs(agents_ref, scale):
-    target = lax.broadcasted_iota(jnp.int32, (AGENTS, TILES * 8), 0)
-    source = lax.broadcasted_iota(jnp.int32, (AGENTS, TILES * 8), 1)
-    agents = agents_ref[...]
+def agent_pairs(agents_ref, wide_ref, scale):
+    wide_ref[...] = agents_ref[...].astype(f32) * scale
     pairs = []
     for pair in range(2):
-        wanted = (target & (TILES - 1)) * 8 + (target // TILES) + 4 * pair
-        pick = jnp.where(source == wanted, scale, 0.0).astype(bf16)
-        pairs.append(jnp.dot(pick, agents, preferred_element_type=f32).astype(bf16))
+        parts = [wide_ref[pl.ds(4 * pair + k, TILES, stride=8), :] for k in range(AGR)]
+        pairs.append(jnp.concatenate(parts, axis=0).astype(bf16))
     return pairs
 
 
@@ -217,8 +214,8 @@
     return (lanes(dims) // HD) == parity
 
 
-def partial_kernel(agents_ref, tk_ref, v_ref, out_ref, score_ref):
-    pairs = agent_pairs(agents_ref, 1.0 / math.sqrt(HD))
+def partial_kernel(agents_ref, tk_ref, v_ref, out_ref, score_ref, wide_ref):
+    pairs = agent_pairs(agents_ref, wide_ref, 1.0 / math.sqrt(HD))
     chunk = 512
     for head in range(LOCAL_HEADS):
         pair, parity = head // 2, head % 2
@@ -280,18 +277,8 @@
     out_ref[...] = slots(merged)
 
 
-def probability_kernel(agents_ref, tab_hbm_ref, q_ref, prob_ref, tab_ref, held_ref, sems):
-    chunk = 256
-    table = pltpu.make_async_copy(tab_hbm_ref, tab_ref, sems.at[N // chunk])
-    table.start()
-
-    def fetch(c):
-        rows = pl.ds(pl.multiple_of(c * chunk, chunk), chunk)
-        return pltpu.make_async_copy(q_ref.at[rows, :], held_ref.at[rows, :], sems.at[c])
-
-    for c in range(N // chunk):
-        fetch(c).start()
-    pairs = agent_pairs(agents_ref, 1.0 / math.sqrt(HD))
+def probabilities(pairs, tab_ref, table, held_ref, fetches, prob_ref):
+    chunk = N // len(fetches)
     matrix = turn_matrix()
     table.wait()
     ones = jnp.ones((AGENTS, 128), bf16)
@@ -299,15 +286,11 @@
     for head in range(LOCAL_HEADS):
         own = pairs[head // 2]
         owns.append(jnp.where(half_mask(own.shape, head % 2), own, jnp.zeros_like(own)))
-
-    def body(c, carry):
-        fetch(c).wait()
-        rows = pl.ds(pl.multiple_of(c * chunk, chunk), chunk)
-        lines = pl.ds(pl.multiple_of(c * (chunk // TC), chunk // TC), chunk // TC)
-        near_rows = [tab_ref[i, lines, :] for i in range(2)]
-        near_cols = [tab_ref[i, pl.ds(TR, TC), :] for i in range(2)]
-        tables = [jnp.concatenate([t, t], axis=1) for t in near_rows + near_cols]
-        cosine, sine = cell_tables(tables, 0, chunk // TC)
+    tables = split_tables(tab_ref[0], tab_ref[1])
+    for c, fetch in enumerate(fetches):
+        rows = pl.ds(c * chunk, chunk)
+        cosine, sine = cell_tables(tables, c * (chunk // TC), chunk // TC)
+        fetch.wait()
         queries = turned(held_ref[rows, :], matrix, cosine, sine)
         for head in range(LOCAL_HEADS):
             scores = lax.dot_general(
@@ -321,9 +304,6 @@
             scale = 1.0 / total
             scale = jnp.concatenate([scale, scale], axis=1)
             prob_ref[rows, pl.ds(head * AGENTS, AGENTS)] = (weights * scale).astype(bf16)
-        return carry
-
-    lax.fori_loop(0, N // chunk, body, 0)
 
 
 def line_kernel(v_ref, near_ref, far_ref, mate_ref, rest_ref, top_ref, bottom_ref, sems):
@@ -347,14 +327,22 @@
     rest_ref[...] = jnp.where(even_row(), lines[0], lines[1]).astype(bf16)
 
 
-def conv_kernel(
-    v_ref,
+def local_kernel(
+    agents_ref,
+    tab_hbm_ref,
+    q_ref,
+    v_hbm_ref,
     near_ref,
     far_ref,
     mate_ref,
     rest_ref,
     w_ref,
+    prob_ref,
     out_hbm_ref,
+    wide_ref,
+    tab_ref,
+    held_ref,
+    v_ref,
     above_ref,
     below_ref,
     l_ref,
@@ -362,12 +350,28 @@
     out_ref,
     sems,
 ):
+    v_fetches = []
+    for half in range(2):
+        cols = pl.ds(half * 128, 128)
+        v_fetches.append(
+            pltpu.make_async_copy(v_hbm_ref.at[:, :, cols], v_ref.at[:, :, cols], sems.at[half])
+        )
+    table = pltpu.make_async_copy(tab_hbm_ref, tab_ref, sems.at[2])
+    q_fetches = []
+    for c in range(3):
+        part = pl.ds(c * (N // 3), N // 3)
+        q_fetches.append(
+            pltpu.make_async_copy(q_ref.at[part, :], held_ref.at[part, :], sems.at[3 + c])
+        )
+    for copy in v_fetches + [table] + q_fetches:
+        copy.start()
+    pairs = agent_pairs(agents_ref, wide_ref, 1.0 / math.sqrt(HD))
     outs = []
     for half in range(2):
         cols = pl.ds(half * 128, 128)
         outs.append(
             pltpu.make_async_copy(
-                out_ref.at[:, cols], out_hbm_ref.at[:, cols], sems.at[half]
+                out_ref.at[:, cols], out_hbm_ref.at[:, cols], sems.at[6 + half]
             )
         )
     mate, rest = mate_ref[...].astype(f32), rest_ref[...].astype(f32)
@@ -378,6 +382,7 @@
     r_ref[...] = jnp.where(even_core(), mate, rest)
     for half in range(2):
         cols = pl.ds(half * 128, 128)
+        v_fetches[half].wait()
 
         def put(at, total):
             out_ref[pl.ds(at, TC), cols] = total
@@ -415,6 +420,7 @@
         t = taps(below_ref[pl.ds(0, TC), cols], tail[0:1], tail[1:2])
         put((TR - 1) * TC, a + t[2])
         outs[half].start()
+    probabilities(pairs, tab_ref, table, held_ref, q_fetches, prob_ref)
     for copy in outs:
         copy.wait()
 
@@ -513,6 +519,7 @@
     k = keys.reshape(N, CH)
     v = values.reshape(N, CH)
     mb = 1 << 20
+    wide = pltpu.VMEM((TILES * 8, 128), f32)
     packed, table = call(
         query_kernel,
         (far((TILES * 8, 128), bf16), far((2, TR + TC, 128), f32)),
@@ -539,7 +546,7 @@
         partial_kernel,
         far((TILES * ROWS, 128), bf16),
         " v ",
-        scratch=[pltpu.VMEM((AGENTS, N), f32)],
+        scratch=[pltpu.VMEM((AGENTS, N), f32), wide],
         nbytes=10 * mb,
         name="partials",
     )(agents, tk, v)
@@ -563,29 +570,26 @@
     )
     merged = after(merged, mate, rest)
     agent_values = spread(merged)
-    prob = call(
-        probability_kernel,
-        near((N, LOCAL_HEADS * AGENTS), bf16),
-        " hh",
+    prob, convolved = call(
+        local_kernel,
+        (near((N, LOCAL_HEADS * AGENTS), bf16), far((N, CH), f32)),
+        " hhhvvvv ",
         scratch=[
+            wide,
             held_table,
             pltpu.VMEM((N, CH), bf16),
-            pltpu.SemaphoreType.DMA((N // 256 + 1,)),
+            pltpu.VMEM((TR, TC, CH), bf16),
+            pltpu.VMEM((TC + 16, CH), f32),
+            pltpu.VMEM((TC + 16, CH), f32),
+            pltpu.VMEM((TR, CH), f32),
+            pltpu.VMEM((TR, CH), f32),
+            pltpu.VMEM((N, CH), f32),
+            pltpu.SemaphoreType.DMA((8,)),
         ],
         nbytes=20 * mb,
-        name="probabilities",
-    )(after(agents, merged), table, q)
-    convolved = call(
-        conv_kernel,
-        (far((N, CH), f32),),
-        " vvvv ",
-        scratch=[pltpu.VMEM((TC + 16, CH), f32)] * 2
-        + [pltpu.VMEM((TR, CH), f32)] * 2
-        + [pltpu.VMEM((N, CH), f32), pltpu.SemaphoreType.DMA((2,))],
-        nbytes=6 * mb,
-        out_spaces="h",
-        name="conv",
-    )(values, inner, outer, mate, rest, conv_weight)[0]
+        out_spaces=" h",
+        name="conv_and_probabilities",
+    )(after(agents, merged), table, q, values, inner, outer, mate, rest, conv_weight)
     summed, stats = call(
         attend_kernel,
         (near((N, CH), f32), near((2 * BLOCKS, 128), f32)),

time: 76 us -> 76 us (level)
  Pallas kernels: 22.3 us -> 19.9 us
  waiting for transfers between devices: 17.5 us -> 19.7 us
    pallas_call x9 -> x8, Pallas kernels: 22.3 us -> 19.9 us  [run(): fn(*[pltpu.with_memory_space_constraint(x, spaces[c]) if c in spaces else...]
    all_to_all x3, waiting for transfers between devices: 13.6 us -> 15.9 us  [spread(): return lax.all_to_all(slot, ('row', 'col'), 0, 0).reshape(x.shape)]
  transfers between devices with their start and end apart: 10 -> 10, of which waited for: 5 -> 5; matrix products, arithmetic and copies ran while one was open for 0% -> 0% of each run, Pallas kernels for 21% -> 18%
where the time goes in v10:
time: 76 us; the launch traced here: 74.9 us
  starting transfers between devices  34.9 us (46%)
  Pallas kernels  19.9 us (26%)
  waiting for transfers between devices  19.7 us (26%)
    all_to_all x3, starting transfers between devices, spread(): return lax.all_to_all(slot, ('row', 'col'), 0, 0).reshape(x.shape)  25 us
    pallas_call x8, Pallas kernels, run(): fn(*[pltpu.with_memory_space_constraint(x, spaces[c]) if c in spaces else...  19.9 us
    all_to_all x3, waiting for transfers between devices, spread(): return lax.all_to_all(slot, ('row', 'col'), 0, 0).reshape(x.shape)  15.9 us
    ppermute x4, starting transfers between devices, swap(): lax.ppermute(x, axis, [p for i, j in pairs for p in ((i, j), (j, i))])  5.7 us
    ppermute x3, starting transfers between devices, shards(): lax.ppermute(stats, 'head', [(i, i ^ d) for i in range(heads)])  4.18 us
    ppermute x3, waiting for transfers between devices, shards(): lax.ppermute(stats, 'head', [(i, i ^ d) for i in range(heads)])  3.87 us
  transfers between devices with their start and end apart: 10, of which 5 were waited for; matrix products, arithmetic and copies ran while one was open for 0% of the time, Pallas kernels for 18%

profile of v10, /device:TPU:8, one launch (start us, length us, event | category | flops | bytes accessed | tf_op | source)
XLA Modules:
  0.0 74.9 jit_solution(10175442817506921644)
XLA Ops:
  0.0 0.0 copy-start
  0.0 2.9 %pool_queries.1 = (bf16[512,128]{1,0:T(8,128)(2,1)}, f32[2,80,128]{2,1,0:T(8,128)}) custom-call(s32[2,32,48]{2,1,0:T(8,128)} %bitcast.26, bf16[1536,256]{1,0:T(8,128)(2,1)} %bitcast.20), custom_call_target="tpu_custom_call" | custom-call | bytes 8388608 | tf_op jit(solution)/shard_map/pool_queries/pallas_call | solution.py:49
  2.9 12.1 %all-to-all-start = ((bf16[64,8,128]{2,1,0:T(8,128)(2,1)}), bf16[64,8,128]{2,1,0:T(8,128)(2,1)S(1)}, u32[]{:S(2)}, u32[]{:S(2)}) async-start(bf16[64,8,128]{2,1,0:T(8,128)(2,1)} %bitcast.25), calls=%async_computation | async-start | bytes 262144 | tf_op jit(solution)/shard_map/all_to_all | solution.py:502
  15.0 0.0 copy-done
  15.0 2.4 %turn_keys.1 = (bf16[1536,256]{1,0:T(8,128)(2,1)S(1)}, bf16[48,256]{1,0:T(8,128)(2,1)}, bf16[48,256]{1,0:T(8,128)(2,1)}) custom-call(f32[2,80,128]{2,1,0:T(8,128)} %get-tuple-element.23.tab_hbm_ref, bf16[48,32,256]{2,1,0:T(8,128)(2,1)S(1)} %copy-done, bf16[1536,256]{1,0:T(8,128)(2,1)} %bitcast.23), custom_call_target="tpu_custom_call" | custom-call | bytes 4194304 | tf_op jit(solution)/shard_map/turn_keys/pallas_call | solution.py:49
  17.4 0.2 collective-permute-start
  17.6 0.7 collective-permute-start.1
  18.3 6.1 %all-to-all-done = bf16[64,8,128]{2,1,0:T(8,128)(2,1)S(1)} async-done(((bf16[64,8,128]{2,1,0:T(8,128)(2,1)}), bf16[64,8,128]{2,1,0:T(8,128)(2,1)S(1)}, u32[]{:S(2)}, u32[]{:S(2)}) %all-to-all-start) | async-done | bytes 131104 | tf_op jit(solution)/shard_map/all_to_all | solution.py:502
  24.4 0.0 copy-start.1
  24.4 3.7 %partials.1 = bf16[1024,128]{1,0:T(8,128)(2,1)} custom-call(bf16[512,128]{1,0:T(8,128)(2,1)S(1)} %bitcast.14, bf16[1536,256]{1,0:T(8,128)(2,1)S(1)} %get-tuple-element.24.tk_ref, bf16[1536,256]{1,0:T(8,128)(2,1)S(1)} %bitcast.13), custom_call_target="tpu_custom_call" | custom-call | bytes 10485760 | tf_op jit(solution)/shard_map/partials/pallas_call | solution.py:49
  28.1 0.0 collective-permute-done.near_ref
  28.1 0.0 collective-permute-done.1.far_ref
  28.1 6.4 %all-to-all-start.1 = ((bf16[64,16,128]{2,1,0:T(8,128)(2,1)}), bf16[64,16,128]{2,1,0:T(8,128)(2,1)S(1)}, u32[]{:S(2)}, u32[]{:S(2)}) async-start(bf16[64,16,128]{2,1,0:T(8,128)(2,1)} %bitcast.22), calls=%async_computation.1 | async-start | bytes 524288 | tf_op jit(solution)/shard_map/all_to_all | solution.py:502
  34.5 0.8 %lines.1 = (bf16[48,256]{1,0:T(8,128)(2,1)S(1)}, bf16[48,256]{1,0:T(8,128)(2,1)S(1)}) custom-call(bf16[48,32,256]{2,1,0:T(8,128)(2,1)} %v_hbm_ref.1, bf16[48,256]{1,0:T(8,128)(2,1)S(1)} %collective-permute-done.near_ref, bf16[48,256]{1,0:T(8,128)(2,1)S(1)} %collective-permute-done.1.far_ref), custom_call_target="tpu_custom_call" | custom-call | bytes 262144 | tf_op jit(solution)/shard_map/lines/pallas_call | solution.py:49
  35.3 0.5 collective-permute-start.2
  35.8 4.3 %collective-permute-start.3 = (bf16[48,256]{1,0:T(8,128)(2,1)S(1)}, bf16[48,256]{1,0:T(8,128)(2,1)S(1)}, u32[]{:S(2)}, u32[]{:S(2)}) collective-permute-start(bf16[48,256]{1,0:T(8,128)(2,1)S(1)} %get-tuple-element.31), channel_id=1, source_target_pairs={{64,128},{128,64},{65,129},{129,65},{66,130},{130,66},{67,131},{13... | collective-permute-start | bytes 73736 | tf_op jit(solution)/shard_map/ppermute | solution.py:506
  40.1 5.9 %all-to-all-done.1 = bf16[64,16,128]{2,1,0:T(8,128)(2,1)S(1)} async-done(((bf16[64,16,128]{2,1,0:T(8,128)(2,1)}), bf16[64,16,128]{2,1,0:T(8,128)(2,1)S(1)}, u32[]{:S(2)}, u32[]{:S(2)}) %all-to-all-start.1) | async-done | bytes 262176 | tf_op jit(solution)/shard_map/all_to_all | solution.py:502
  46.1 1.1 %merge.1 = bf16[512,128]{1,0:T(8,128)(2,1)} custom-call(bf16[1024,128]{1,0:T(8,128)(2,1)S(1)} %bitcast.16), custom_call_target="tpu_custom_call" | custom-call | bytes 2097152 | tf_op jit(solution)/shard_map/merge/pallas_call | solution.py:49
  47.2 0.0 collective-permute-done.2.mate_ref
  47.2 0.0 collective-permute-done.3.rest_ref
  47.2 6.5 %all-to-all-start.2 = ((bf16[64,8,128]{2,1,0:T(8,128)(2,1)}), bf16[64,8,128]{2,1,0:T(8,128)(2,1)S(1)}, u32[]{:S(2)}, u32[]{:S(2)}) async-start(bf16[64,8,128]{2,1,0:T(8,128)(2,1)} %bitcast.24), calls=%async_computation.2 | async-start | bytes 262144 | tf_op jit(solution)/shard_map/all_to_all | solution.py:502
  53.7 0.0 copy-done.1
  53.7 5.6 %conv_and_probabilities.1 = (bf16[1536,1024]{1,0:T(8,128)(2,1)S(1)}, f32[1536,256]{1,0:T(8,128)}) custom-call(bf16[512,128]{1,0:T(8,128)(2,1)S(1)} %bitcast.15, f32[2,80,128]{2,1,0:T(8,128)} %get-tuple-element.23.tab_hbm_ref, bf16[1536,256]{1,0:T(8,128)(2,1)} %bitcast.21, bf16[48,32,256]{2,1,0:T(8,128)(2,1)} %v_hbm_ref.1, ...), custom_call_target="tpu_custom_call" | custom-call | bytes 20971520 | tf_op jit(solution)/shard_map/conv_and_probabilities/pallas_call | solution.py:49
  59.3 3.8 %all-to-all-done.2 = bf16[64,8,128]{2,1,0:T(8,128)(2,1)S(1)} async-done(((bf16[64,8,128]{2,1,0:T(8,128)(2,1)}), bf16[64,8,128]{2,1,0:T(8,128)(2,1)S(1)}, u32[]{:S(2)}, u32[]{:S(2)}) %all-to-all-start.2) | async-done | bytes 131104 | tf_op jit(solution)/shard_map/all_to_all | solution.py:502
  63.1 0.0 copy-start.2
  63.1 0.0 copy-start.3
  63.1 2.3 %attend.1 = (f32[1536,256]{1,0:T(8,128)S(1)}, f32[24,128]{1,0:T(8,128)S(1)}) custom-call(bf16[512,128]{1,0:T(8,128)(2,1)S(1)} %bitcast.17, bf16[1536,1024]{1,0:T(8,128)(2,1)S(1)} %get-tuple-element.35.prob_ref, f32[1536,256]{1,0:T(8,128)} %get-tuple-element.36.conv_hbm_ref), custom_call_target="tpu_custom_call" | custom-call | bytes 4194304 | tf_op jit(solution)/shard_map/attend/pallas_call | solution.py:49
  65.4 2.8 %collective-permute-start.6 = (f32[24,128]{1,0:T(8,128)S(1)}, f32[24,128]{1,0:T(8,128)S(1)}, u32[]{:S(2)}, u32[]{:S(2)}) collective-permute-start(f32[24,128]{1,0:T(8,128)S(1)} %get-tuple-element.37.s0_ref), channel_id=1, source_target_pairs={{0,3},{1,2},{2,1},{3,0},{4,7},{5,6},{6,5},{7,4},{8,11},{9,10},{10,... | collective-permute-start | bytes 36872 | tf_op jit(solution)/shard_map/ppermute | solution.py:603
  68.3 0.8 %collective-permute-start.5 = (f32[24,128]{1,0:T(8,128)S(1)}, f32[24,128]{1,0:T(8,128)S(1)}, u32[]{:S(2)}, u32[]{:S(2)}) collective-permute-start(f32[24,128]{1,0:T(8,128)S(1)} %get-tuple-element.37.s0_ref), channel_id=1, source_target_pairs={{0,2},{1,3},{2,0},{3,1},{4,6},{5,7},{6,4},{7,5},{8,10},{9,11},{10,... | collective-permute-start | bytes 36872 | tf_op jit(solution)/shard_map/ppermute | solution.py:603
  69.1 0.5 collective-permute-start.4
  69.6 0.8 %collective-permute-done.6.s3_ref = f32[24,128]{1,0:T(8,128)S(1)} collective-permute-done((f32[24,128]{1,0:T(8,128)S(1)}, f32[24,128]{1,0:T(8,128)S(1)}, u32[]{:S(2)}, u32[]{:S(2)}) %collective-permute-start.6) | collective-permute-done | bytes 12320 | tf_op jit(solution)/shard_map/ppermute | solution.py:603
  70.4 3.1 %collective-permute-done.5.s2_ref = f32[24,128]{1,0:T(8,128)S(1)} collective-permute-done((f32[24,128]{1,0:T(8,128)S(1)}, f32[24,128]{1,0:T(8,128)S(1)}, u32[]{:S(2)}, u32[]{:S(2)}) %collective-permute-start.5) | collective-permute-done | bytes 12320 | tf_op jit(solution)/shard_map/ppermute | solution.py:603
  73.5 0.0 collective-permute-done.4.s1_ref
  73.5 0.0 copy-done.2
  73.5 0.0 copy-done.3
  73.5 1.2 %norm.1 = bf16[1536,256]{1,0:T(8,128)(2,1)} custom-call(f32[24,128]{1,0:T(8,128)S(1)} %get-tuple-element.37.s0_ref, f32[24,128]{1,0:T(8,128)S(1)} %collective-permute-done.4.s1_ref, f32[24,128]{1,0:T(8,128)S(1)} %collective-permute-done.5.s2_ref, f32[24,128]{1,0:T(8,128)S(1)} %collective-permute-done.6.s3_ref, f32[1536,256]{1,0:T(8,128)S(1)} %get-tuple-element.38.sum_ref, ...), custom_call_target="tpu_custom_call" | custom-call | bytes 4194304 | tf_op jit(solution)/shard_map/norm/pallas_call | solution.py:49
Async XLA Ops:
  0.0 15.0 %copy-start = (bf16[48,32,256]{2,1,0:T(8,128)(2,1)S(1)}, bf16[48,32,256]{2,1,0:T(8,128)(2,1)}, u32[]{:S(2)}) copy-start(bf16[48,32,256]{2,1,0:T(8,128)(2,1)} %v_hbm_ref.1) | copy-start | bytes 2359300
  2.9 21.5 %all-to-all-start = ((bf16[64,8,128]{2,1,0:T(8,128)(2,1)}), bf16[64,8,128]{2,1,0:T(8,128)(2,1)S(1)}, u32[]{:S(2)}, u32[]{:S(2)}) async-start(bf16[64,8,128]{2,1,0:T(8,128)(2,1)} %bitcast.25), calls=%async_computation | async-start | bytes 262144 | tf_op jit(solution)/shard_map/all_to_all | solution.py:502
  17.4 10.7 %collective-permute-start = (bf16[48,256]{1,0:T(8,128)(2,1)}, bf16[48,256]{1,0:T(8,128)(2,1)S(1)}, u32[]{:S(2)}, u32[]{:S(2)}) collective-permute-start(bf16[48,256]{1,0:T(8,128)(2,1)} %get-tuple-element.25), channel_id=1, source_target_pairs={{0,4},{4,0},{8,12},{12,8},{16,20},{20,16},{24,28},{28,24},{32,36},... | collective-permute-start | bytes 73736 | tf_op jit(solution)/shard_map/ppermute | solution.py:506
  17.6 10.5 %collective-permute-start.1 = (bf16[48,256]{1,0:T(8,128)(2,1)}, bf16[48,256]{1,0:T(8,128)(2,1)S(1)}, u32[]{:S(2)}, u32[]{:S(2)}) collective-permute-start(bf16[48,256]{1,0:T(8,128)(2,1)} %get-tuple-element.26), channel_id=1, source_target_pairs={{4,8},{8,4},{12,16},{16,12},{20,24},{24,20},{28,32},{32,28},{36,40... | collective-permute-start | bytes 73736 | tf_op jit(solution)/shard_map/ppermute | solution.py:506
  24.4 29.3 %copy-start.1 = (f32[9,256]{1,0:T(8,128)S(1)}, f32[9,256]{1,0:T(8,128)}, u32[]{:S(2)}) copy-start(f32[9,256]{1,0:T(8,128)} %w_ref.1) | copy-start | bytes 27652
  28.1 18.0 %all-to-all-start.1 = ((bf16[64,16,128]{2,1,0:T(8,128)(2,1)}), bf16[64,16,128]{2,1,0:T(8,128)(2,1)S(1)}, u32[]{:S(2)}, u32[]{:S(2)}) async-start(bf16[64,16,128]{2,1,0:T(8,128)(2,1)} %bitcast.22), calls=%async_computation.1 | async-start | bytes 524288 | tf_op jit(solution)/shard_map/all_to_all | solution.py:502
  35.3 11.9 %collective-permute-start.2 = (bf16[48,256]{1,0:T(8,128)(2,1)S(1)}, bf16[48,256]{1,0:T(8,128)(2,1)S(1)}, u32[]{:S(2)}, u32[]{:S(2)}) collective-permute-start(bf16[48,256]{1,0:T(8,128)(2,1)S(1)} %get-tuple-element.30), channel_id=1, source_target_pairs={{0,64},{64,0},{128,192},{192,128},{1,65},{65,1},{129,193},{193,129... | collective-permute-start | bytes 73736 | tf_op jit(solution)/shard_map/ppermute | solution.py:506
  35.8 11.4 %collective-permute-start.3 = (bf16[48,256]{1,0:T(8,128)(2,1)S(1)}, bf16[48,256]{1,0:T(8,128)(2,1)S(1)}, u32[]{:S(2)}, u32[]{:S(2)}) collective-permute-start(bf16[48,256]{1,0:T(8,128)(2,1)S(1)} %get-tuple-element.31), channel_id=1, source_target_pairs={{64,128},{128,64},{65,129},{129,65},{66,130},{130,66},{67,131},{13... | collective-permute-start | bytes 73736 | tf_op jit(solution)/shard_map/ppermute | solution.py:506
  47.2 15.9 %all-to-all-start.2 = ((bf16[64,8,128]{2,1,0:T(8,128)(2,1)}), bf16[64,8,128]{2,1,0:T(8,128)(2,1)S(1)}, u32[]{:S(2)}, u32[]{:S(2)}) async-start(bf16[64,8,128]{2,1,0:T(8,128)(2,1)} %bitcast.24), calls=%async_computation.2 | async-start | bytes 262144 | tf_op jit(solution)/shard_map/all_to_all | solution.py:502
  63.1 10.4 %copy-start.2 = (f32[256]{0:T(256)S(1)}, f32[256]{0:T(256)}, u32[]{:S(2)}) copy-start(f32[256]{0:T(256)} %param.12) | copy-start | bytes 3076
  63.1 10.4 %copy-start.3 = (f32[256]{0:T(256)S(1)}, f32[256]{0:T(256)}, u32[]{:S(2)}) copy-start(f32[256]{0:T(256)} %param.13) | copy-start | bytes 3076
  65.4 5.0 %collective-permute-start.6 = (f32[24,128]{1,0:T(8,128)S(1)}, f32[24,128]{1,0:T(8,128)S(1)}, u32[]{:S(2)}, u32[]{:S(2)}) collective-permute-start(f32[24,128]{1,0:T(8,128)S(1)} %get-tuple-element.37.s0_ref), channel_id=1, source_target_pairs={{0,3},{1,2},{2,1},{3,0},{4,7},{5,6},{6,5},{7,4},{8,11},{9,10},{10,... | collective-permute-start | bytes 36872 | tf_op jit(solution)/shard_map/ppermute | solution.py:603
  68.3 5.2 %collective-permute-start.5 = (f32[24,128]{1,0:T(8,128)S(1)}, f32[24,128]{1,0:T(8,128)S(1)}, u32[]{:S(2)}, u32[]{:S(2)}) collective-permute-start(f32[24,128]{1,0:T(8,128)S(1)} %get-tuple-element.37.s0_ref), channel_id=1, source_target_pairs={{0,2},{1,3},{2,0},{3,1},{4,6},{5,7},{6,4},{7,5},{8,10},{9,11},{10,... | collective-permute-start | bytes 36872 | tf_op jit(solution)/shard_map/ppermute | solution.py:603
  69.1 4.4 %collective-permute-start.4 = (f32[24,128]{1,0:T(8,128)S(1)}, f32[24,128]{1,0:T(8,128)S(1)}, u32[]{:S(2)}, u32[]{:S(2)}) collective-permute-start(f32[24,128]{1,0:T(8,128)S(1)} %get-tuple-element.37.s0_ref), channel_id=1, source_target_pairs={{0,1},{1,0},{2,3},{3,2},{4,5},{5,4},{6,7},{7,6},{8,9},{9,8},{10,11... | collective-permute-start | bytes 36872 | tf_op jit(solution)/shard_map/ppermute | solution.py:603

commit v11 on v10

--- a/solution.py
+++ b/solution.py
@@ -17,7 +17,8 @@
 AGENTS = 256
 TILES = 64
 LOCAL_HEADS = 4
-ROWS = LOCAL_HEADS * AGENTS // TILES
+PEERS = TILES // 2
+PIECES = 4
 BLOCKS = N // 128
 
 f32 = jnp.float32
@@ -159,7 +160,7 @@
 
 
 def even_core():
-    return lax.rem(lax.axis_index("col"), 2) == 0
+    return lax.axis_index("core") == 0
 
 
 def even_row():
@@ -171,12 +172,9 @@
     v_ref,
     k_ref,
     tk_ref,
-    near_ref,
-    far_ref,
-    tab_ref,
-    held_ref,
-    sems,
+    *refs,
 ):
+    sends, (near_ref, far_ref, tab_ref, held_ref, sems) = refs[:PIECES], refs[PIECES:]
     step = N // AGR
     table = pltpu.make_async_copy(tab_hbm_ref, tab_ref, sems.at[AGR])
     table.start()
@@ -191,6 +189,11 @@
     even = even_core()
     near_ref[...] = jnp.where(even, last, first)
     far_ref[...] = jnp.where(even, first, last)
+    other = jnp.where(even, v_ref[:, :, 128:], v_ref[:, :, :128])
+    other = other.reshape(N, 128)
+    size = 2 * N // PIECES
+    for i in range(PIECES // 2):
+        sends[PIECES // 2 + i][...] = other[i * size : (i + 1) * size]
     matrix = turn_matrix()
     table.wait()
     tables = split_tables(tab_ref[0], tab_ref[1])
@@ -198,7 +201,13 @@
         part = pl.ds(cell * step, step)
         cosine, sine = cell_tables(tables, cell * (TR // AGR), TR // AGR)
         copies[cell].wait()
-        tk_ref[part, :] = turned(held_ref[part, :], matrix, cosine, sine)
+        keys = turned(held_ref[part, :], matrix, cosine, sine)
+        tk_ref[part, :] = jnp.where(even, keys[:, :128], keys[:, 128:])
+        keys = jnp.where(even, keys[:, 128:], keys[:, :128])
+        span = math.gcd(size, step)
+        for at in range(0, step, span):
+            to = cell * step + at
+            sends[to // size][pl.ds(to % size, span), :] = keys[at : at + span]
 
 
 def agent_pairs(agents_ref, wide_ref, scale):
@@ -214,19 +223,31 @@
     return (lanes(dims) // HD) == parity
 
 
-def partial_kernel(agents_ref, tk_ref, v_ref, out_ref, score_ref, wide_ref):
+def partial_kernel(agents_ref, tk_ref, v_ref, *refs):
+    got, (out_ref, score_ref, wide_ref) = refs[:PIECES], refs[PIECES:]
+    size = 2 * N // PIECES
     pairs = agent_pairs(agents_ref, wide_ref, 1.0 / math.sqrt(HD))
-    chunk = 512
-    for head in range(LOCAL_HEADS):
-        pair, parity = head // 2, head % 2
-        cols = pl.ds(pair * 128, 128)
-        own = pairs[pair]
+    mine = jnp.where(even_core(), pairs[0], pairs[1])
+    offset = pl.multiple_of(lax.axis_index("core") * 128, 128)
+    chunk = 512 if size % 512 == 0 else 384
+
+    def part(c, which):
+        at = c * chunk % N
+        if c * chunk >= N:
+            at = at + which * N
+            return got[at // size][pl.ds(at % size, chunk), :]
+        if which == 0:
+            return tk_ref[pl.ds(at, chunk), :]
+        return v_ref[pl.ds(at, chunk), pl.ds(offset, 128)]
+
+    for parity in range(2):
+        own = mine
         own = jnp.where(half_mask(own.shape, parity), own, jnp.zeros_like(own))
         peak = None
-        for c in range(N // chunk):
+        for c in range(2 * N // chunk):
             scores = lax.dot_general(
                 own,
-                tk_ref[pl.ds(c * chunk, chunk), cols],
+                part(c, 0),
                 (((1,), (1,)), ((), ())),
                 preferred_element_type=f32,
             )
@@ -236,9 +257,9 @@
                 peak = piece if peak is None else jnp.maximum(peak, piece)
         peak = jnp.max(peak, 1, keepdims=True)
         acc = jnp.zeros((AGENTS, 128), f32)
-        for c in range(N // chunk):
+        for c in range(2 * N // chunk):
             weights = jnp.exp(score_ref[:, pl.ds(c * chunk, chunk)] - peak).astype(bf16)
-            block = v_ref[pl.ds(c * chunk, chunk), cols]
+            block = part(c, 1)
             block = jnp.where(half_mask(block.shape, parity), block, jnp.ones_like(block))
             acc = acc + jnp.dot(weights, block, preferred_element_type=f32)
         other = pltpu.roll(acc, HD, 1)
@@ -259,17 +280,17 @@
                 jnp.where(lane == HD + 1, second, jnp.where(lane == HD + 2, third, 0.0)),
             ),
         )
-        groups = packed.reshape(2, ROWS, 8, 128)
+        groups = packed.reshape(2, AGENTS // 16, 8, 128)
         groups = jnp.concatenate([groups[0], groups[1]], 1).reshape(AGENTS, 128)
-        out_ref[pl.ds(head * AGENTS, AGENTS), :] = groups.astype(bf16)
+        out_ref[pl.ds(parity * AGENTS, AGENTS), :] = groups.astype(bf16)
 
 
 def merge_kernel(parts_ref, out_ref):
     source = lax.broadcasted_iota(jnp.int32, (128, 128), 0)
     picker = jnp.where((source >= HD) & (source < HD + 3), 1.0, 0.0).astype(bf16)
     parts = parts_ref[...]
-    logs = jnp.dot(parts, picker, preferred_element_type=f32).reshape(TILES, ROWS, 128)
-    values = parts.astype(f32).reshape(TILES, ROWS, 128)
+    logs = jnp.dot(parts, picker, preferred_element_type=f32).reshape(PEERS, 16, 128)
+    values = parts.astype(f32).reshape(PEERS, 16, 128)
     peak = jnp.max(logs, 0)
     weights = jnp.exp(logs - peak[None])
     merged = jnp.sum(weights * values, 0) / jnp.sum(weights, 0)
@@ -435,10 +456,11 @@
         )
         copies[c].start()
     eye = lax.broadcasted_iota(jnp.int32, (128, 128), 0) == lanes((128, 128))
+    av = av_ref[...].astype(f32).reshape(2, AGENTS // 16, 2, 8, 128)
     for pair in range(2):
         pieces = []
         for parity in range(2):
-            part = av_ref[pl.ds((2 * pair + parity) * 128, 128), :].astype(f32)
+            part = av[parity, :, pair].reshape(128, 128)
             other = pltpu.roll(part, HD, 1)
             own = half_mask(part.shape, parity)
             for piece in (part, other) if parity == 0 else (other, part):
@@ -497,9 +519,13 @@
         copy.wait()
 
 
-def spread(x):
-    slot = x.reshape(TILES, x.shape[0] // TILES, 128)
-    return lax.all_to_all(slot, ("row", "col"), 0, 0).reshape(x.shape)
+TILE_AXES = ("row", "z", "core")
+
+
+def spread(x, axes=TILE_AXES):
+    count = lax.axis_size(axes)
+    slot = x.reshape(count, x.shape[0] // count, 128)
+    return lax.all_to_all(slot, axes, 0, 0).reshape(x.shape)
 
 
 def swap(x, axis, pairs):
@@ -534,26 +560,29 @@
     )(jnp.swapaxes(positions, 1, 2), q)
     agents = spread(packed)
     held_table = pltpu.VMEM((2, TR + TC, 128), f32)
-    tk, inner, outer = call(
+    tk, *sends, inner, outer = call(
         key_kernel,
-        (near((N, CH), bf16),) + (far((TR, CH), bf16),) * 2,
+        (near((N, 128), bf16),)
+        + (near((2 * N // PIECES, 128), bf16),) * PIECES
+        + (far((TR, CH), bf16),) * 2,
         "h h",
         scratch=[held_table, pltpu.VMEM((N, CH), bf16), pltpu.SemaphoreType.DMA((AGR + 1,))],
         nbytes=4 * mb,
         name="turn_keys",
     )(table, values, k)
+    got = [swap(send, "core", chain("core", 0)) for send in sends]
+    inner = swap(inner, "core", chain("core", 0))
+    outer = swap(outer, ("z", "core"), chain(("z", "core"), 1))
     parts = call(
         partial_kernel,
-        far((TILES * ROWS, 128), bf16),
-        " v ",
-        scratch=[pltpu.VMEM((AGENTS, N), f32), wide],
+        far((2 * AGENTS, 128), bf16),
+        " v " + " " * PIECES,
+        scratch=[pltpu.VMEM((AGENTS, 2 * N), f32), wide],
         nbytes=10 * mb,
         name="partials",
-    )(agents, tk, v)
-    inner = swap(inner, "col", chain("col", 0))
-    outer = swap(outer, "col", chain("col", 1))
+    )(agents, tk, v, *got)
     parts, inner, outer = lax.optimization_barrier((parts, inner, outer))
-    received = spread(parts)
+    received = spread(parts, ("row", "z"))
     mate, rest = call(
         line_kernel,
         (near((TC + 16, CH), bf16),) * 2,
@@ -617,14 +646,15 @@
 
 
 def solution(mesh):
-    in_specs = (
-        P("row", "col", "head"),
-        P("row", "col", "head"),
-        P("row", "col", "head"),
-        P(None, "row", "col"),
+    rows, cols, heads = mesh.devices.shape
+    cores = jax.sharding.Mesh(
+        mesh.devices.reshape(rows, cols // 2, 2, heads), ("row", "z", "core", "head")
+    )
+    tile = P("row", ("z", "core"), "head")
+    in_specs = (tile,) * 3 + (
+        P(None, "row", ("z", "core")),
         P(None, "head"),
         P("head"),
         P("head"),
     )
-    out_specs = P("row", "col", "head")
-    return jax.shard_map(shards, mesh=mesh, in_specs=in_specs, out_specs=out_specs, check_vma=False)
+    return jax.shard_map(shards, mesh=cores, in_specs=in_specs, out_specs=tile, check_vma=False)

time: 76 us -> 75.3 us (level)
  starting transfers between devices: 34.9 us -> 38.3 us
  waiting for transfers between devices: 19.7 us -> 16.5 us
    all_to_all x3, waiting for transfers between devices: 15.9 us -> 12.2 us  [spread(): return lax.all_to_all(slot, axes, 0, 0).reshape(x.shape)]
    all_to_all x3, starting transfers between devices: 25 us -> 27.5 us  [spread(): return lax.all_to_all(slot, axes, 0, 0).reshape(x.shape)]
    ppermute x4 -> x8, starting transfers between devices: 5.7 us -> 6.56 us  [swap(): lax.ppermute(x, axis, [p for i, j in pairs for p in ((i, j), (j, i))])]
    pallas_call x8, Pallas kernels: 19.9 us -> 19.2 us  [run(): fn(*[pltpu.with_memory_space_constraint(x, spaces[c]) if c in spaces else...]
  transfers between devices with their start and end apart: 10 -> 14, of which waited for: 5 -> 7; matrix products, arithmetic and copies ran while one was open for 0% -> 0% of each run, Pallas kernels for 18% -> 18%
where the time goes in v11:
time: 75.3 us; the launch traced here: 74.3 us
  starting transfers between devices  38.3 us (51%)
  Pallas kernels  19.2 us (25%)
  waiting for transfers between devices  16.5 us (22%)
    all_to_all x3, starting transfers between devices, spread(): return lax.all_to_all(slot, axes, 0, 0).reshape(x.shape)  27.5 us
    pallas_call x8, Pallas kernels, run(): fn(*[pltpu.with_memory_space_constraint(x, spaces[c]) if c in spaces else...  19.2 us
    all_to_all x3, waiting for transfers between devices, spread(): return lax.all_to_all(slot, axes, 0, 0).reshape(x.shape)  12.2 us
    ppermute x8, starting transfers between devices, swap(): lax.ppermute(x, axis, [p for i, j in pairs for p in ((i, j), (j, i))])  6.56 us
    ppermute x3, starting transfers between devices, shards(): lax.ppermute(stats, 'head', [(i, i ^ d) for i in range(heads)])  4.18 us
    ppermute x3, waiting for transfers between devices, shards(): lax.ppermute(stats, 'head', [(i, i ^ d) for i in range(heads)])  3.87 us
  transfers between devices with their start and end apart: 14, of which 7 were waited for; matrix products, arithmetic and copies ran while one was open for 0% of the time, Pallas kernels for 18%

profile of v11, /device:TPU:8, one launch (start us, length us, event | category | flops | bytes accessed | tf_op | source)
XLA Modules:
  0.0 74.3 jit_solution(4659235879101266686)
XLA Ops:
  0.0 0.0 copy-start
  0.0 2.9 %pool_queries.1 = (bf16[512,128]{1,0:T(8,128)(2,1)}, f32[2,80,128]{2,1,0:T(8,128)}) custom-call(s32[2,32,48]{2,1,0:T(8,128)} %bitcast.26, bf16[1536,256]{1,0:T(8,128)(2,1)} %bitcast.20), custom_call_target="tpu_custom_call" | custom-call | bytes 8388608 | tf_op jit(solution)/shard_map/pool_queries/pallas_call | solution.py:50
  2.9 12.1 %all-to-all-start = ((bf16[64,8,128]{2,1,0:T(8,128)(2,1)}), bf16[64,8,128]{2,1,0:T(8,128)(2,1)S(1)}, u32[]{:S(2)}, u32[]{:S(2)}) async-start(bf16[64,8,128]{2,1,0:T(8,128)(2,1)} %bitcast.25), calls=%async_computation | async-start | bytes 262144 | tf_op jit(solution)/shard_map/all_to_all | solution.py:528
  15.0 0.0 copy-done
  15.0 2.4 %turn_keys.1 = (bf16[1536,128]{1,0:T(8,128)(2,1)S(1)}, bf16[768,128]{1,0:T(8,128)(2,1)S(1)}, bf16[768,128]{1,0:T(8,128)(2,1)S(1)}, bf16[768,128]{1,0:T(8,128)(2,...) custom-call(f32[2,80,128]{2,1,0:T(8,128)} %get-tuple-element.27.tab_hbm_ref, ...), custom_call_target="tpu_custom_call" | custom-call | bytes 4194304 | tf_op jit(solution)/shard_map/turn_keys/pallas_call | solution.py:50
  17.4 0.2 collective-permute-start
  17.7 0.4 collective-permute-start.1
  18.0 0.1 collective-permute-start.2
  18.2 0.4 collective-permute-start.3
  18.5 0.1 collective-permute-start.4
  18.7 0.3 collective-permute-done.refs_0_
  18.9 0.7 collective-permute-start.5
  19.6 0.0 collective-permute-done.1.refs_1_
  19.6 0.0 collective-permute-done.2.refs_2_
  19.6 0.2 collective-permute-done.3.refs_3_
  19.8 4.6 %all-to-all-done = bf16[64,8,128]{2,1,0:T(8,128)(2,1)S(1)} async-done(((bf16[64,8,128]{2,1,0:T(8,128)(2,1)}), bf16[64,8,128]{2,1,0:T(8,128)(2,1)S(1)}, u32[]{:S(2)}, u32[]{:S(2)}) %all-to-all-start) | async-done | bytes 131104 | tf_op jit(solution)/shard_map/all_to_all | solution.py:528
  24.4 0.0 copy-start.1
  24.4 3.4 %partials.1 = bf16[512,128]{1,0:T(8,128)(2,1)} custom-call(bf16[512,128]{1,0:T(8,128)(2,1)S(1)} %bitcast.14, bf16[1536,128]{1,0:T(8,128)(2,1)S(1)} %get-tuple-element.28.tk_ref, bf16[1536,256]{1,0:T(8,128)(2,1)S(1)} %bitcast.13, bf16[768,128]{1,0:T(8,128)(2,1)S(1)} %collective-permute-done.refs_0_, bf16[768,128]{1,0:T(8,128)(2,1)S(1)} %collective-permute-done.1.refs_1_, ...), custom_call_target="tpu_custom_call" | custom-call | bytes 10485760 | tf_op jit(solution)/shard_map/partials/pallas_call | solution.py:50
  27.8 0.0 collective-permute-done.4.near_ref
  27.8 0.0 collective-permute-done.5.far_ref
  27.8 7.6 %all-to-all-start.1 = ((bf16[32,16,128]{2,1,0:T(8,128)(2,1)}), bf16[32,16,128]{2,1,0:T(8,128)(2,1)S(1)}, u32[]{:S(2)}, u32[]{:S(2)}) async-start(bf16[32,16,128]{2,1,0:T(8,128)(2,1)} %bitcast.23), calls=%async_computation.1 | async-start | bytes 262144 | tf_op jit(solution)/shard_map/all_to_all | solution.py:528
  35.4 0.8 %lines.1 = (bf16[48,256]{1,0:T(8,128)(2,1)S(1)}, bf16[48,256]{1,0:T(8,128)(2,1)S(1)}) custom-call(bf16[48,32,256]{2,1,0:T(8,128)(2,1)} %v_hbm_ref.1, bf16[48,256]{1,0:T(8,128)(2,1)S(1)} %collective-permute-done.4.near_ref, bf16[48,256]{1,0:T(8,128)(2,1)S(1)} %collective-permute-done.5.far_ref), custom_call_target="tpu_custom_call" | custom-call | bytes 262144 | tf_op jit(solution)/shard_map/lines/pallas_call | solution.py:50
  36.2 0.3 collective-permute-start.6
  36.5 4.3 %collective-permute-start.7 = (bf16[48,256]{1,0:T(8,128)(2,1)S(1)}, bf16[48,256]{1,0:T(8,128)(2,1)S(1)}, u32[]{:S(2)}, u32[]{:S(2)}) collective-permute-start(bf16[48,256]{1,0:T(8,128)(2,1)S(1)} %get-tuple-element.39), channel_id=1, source_target_pairs={{64,128},{128,64},{65,129},{129,65},{66,130},{130,66},{67,131},{13... | collective-permute-start | bytes 73736 | tf_op jit(solution)/shard_map/ppermute | solution.py:532
  40.9 3.7 %all-to-all-done.1 = bf16[32,16,128]{2,1,0:T(8,128)(2,1)S(1)} async-done(((bf16[32,16,128]{2,1,0:T(8,128)(2,1)}), bf16[32,16,128]{2,1,0:T(8,128)(2,1)S(1)}, u32[]{:S(2)}, u32[]{:S(2)}) %all-to-all-start.1) | async-done | bytes 131104 | tf_op jit(solution)/shard_map/all_to_all | solution.py:528
  44.6 1.0 %merge.1 = bf16[512,128]{1,0:T(8,128)(2,1)} custom-call(bf16[512,128]{1,0:T(8,128)(2,1)S(1)} %bitcast.17), custom_call_target="tpu_custom_call" | custom-call | bytes 2097152 | tf_op jit(solution)/shard_map/merge/pallas_call | solution.py:50
  45.6 0.0 collective-permute-done.6.mate_ref
  45.6 0.0 collective-permute-done.7.rest_ref
  45.6 7.8 %all-to-all-start.2 = ((bf16[64,8,128]{2,1,0:T(8,128)(2,1)}), bf16[64,8,128]{2,1,0:T(8,128)(2,1)S(1)}, u32[]{:S(2)}, u32[]{:S(2)}) async-start(bf16[64,8,128]{2,1,0:T(8,128)(2,1)} %bitcast.24), calls=%async_computation.2 | async-start | bytes 262144 | tf_op jit(solution)/shard_map/all_to_all | solution.py:528
  53.4 0.0 copy-done.1
  53.4 5.6 %conv_and_probabilities.1 = (bf16[1536,1024]{1,0:T(8,128)(2,1)S(1)}, f32[1536,256]{1,0:T(8,128)}) custom-call(bf16[512,128]{1,0:T(8,128)(2,1)S(1)} %bitcast.15, f32[2,80,128]{2,1,0:T(8,128)} %get-tuple-element.27.tab_hbm_ref, bf16[1536,256]{1,0:T(8,128)(2,1)} %bitcast.21, bf16[48,32,256]{2,1,0:T(8,128)(2,1)} %v_hbm_ref.1, ...), custom_call_target="tpu_custom_call" | custom-call | bytes 20971520 | tf_op jit(solution)/shard_map/conv_and_probabilities/pallas_call | solution.py:50
  59.0 3.8 %all-to-all-done.2 = bf16[64,8,128]{2,1,0:T(8,128)(2,1)S(1)} async-done(((bf16[64,8,128]{2,1,0:T(8,128)(2,1)}), bf16[64,8,128]{2,1,0:T(8,128)(2,1)S(1)}, u32[]{:S(2)}, u32[]{:S(2)}) %all-to-all-start.2) | async-done | bytes 131104 | tf_op jit(solution)/shard_map/all_to_all | solution.py:528
  62.8 0.0 copy-start.2
  62.8 0.0 copy-start.3
  62.8 2.0 %attend.1 = (f32[1536,256]{1,0:T(8,128)S(1)}, f32[24,128]{1,0:T(8,128)S(1)}) custom-call(bf16[512,128]{1,0:T(8,128)(2,1)S(1)} %bitcast.16, bf16[1536,1024]{1,0:T(8,128)(2,1)S(1)} %get-tuple-element.43.prob_ref, f32[1536,256]{1,0:T(8,128)} %get-tuple-element.44.conv_hbm_ref), custom_call_target="tpu_custom_call" | custom-call | bytes 4194304 | tf_op jit(solution)/shard_map/attend/pallas_call | solution.py:50
  64.8 2.8 %collective-permute-start.10 = (f32[24,128]{1,0:T(8,128)S(1)}, f32[24,128]{1,0:T(8,128)S(1)}, u32[]{:S(2)}, u32[]{:S(2)}) collective-permute-start(f32[24,128]{1,0:T(8,128)S(1)} %get-tuple-element.45.s0_ref), channel_id=1, source_target_pairs={{0,3},{1,2},{2,1},{3,0},{4,7},{5,6},{6,5},{7,4},{8,11},{9,10},{10,... | collective-permute-start | bytes 36872 | tf_op jit(solution)/shard_map/ppermute | solution.py:632
  67.7 0.8 %collective-permute-start.9 = (f32[24,128]{1,0:T(8,128)S(1)}, f32[24,128]{1,0:T(8,128)S(1)}, u32[]{:S(2)}, u32[]{:S(2)}) collective-permute-start(f32[24,128]{1,0:T(8,128)S(1)} %get-tuple-element.45.s0_ref), channel_id=1, source_target_pairs={{0,2},{1,3},{2,0},{3,1},{4,6},{5,7},{6,4},{7,5},{8,10},{9,11},{10,... | collective-permute-start | bytes 36872 | tf_op jit(solution)/shard_map/ppermute | solution.py:632
  68.5 0.5 collective-permute-start.8
  69.0 0.8 %collective-permute-done.10.s3_ref = f32[24,128]{1,0:T(8,128)S(1)} collective-permute-done((f32[24,128]{1,0:T(8,128)S(1)}, f32[24,128]{1,0:T(8,128)S(1)}, u32[]{:S(2)}, u32[]{:S(2)}) %collective-permute-start.10) | collective-permute-done | bytes 12320 | tf_op jit(solution)/shard_map/ppermute | solution.py:632
  69.8 3.1 %collective-permute-done.9.s2_ref = f32[24,128]{1,0:T(8,128)S(1)} collective-permute-done((f32[24,128]{1,0:T(8,128)S(1)}, f32[24,128]{1,0:T(8,128)S(1)}, u32[]{:S(2)}, u32[]{:S(2)}) %collective-permute-start.9) | collective-permute-done | bytes 12320 | tf_op jit(solution)/shard_map/ppermute | solution.py:632
  72.9 0.0 collective-permute-done.8.s1_ref
  72.9 0.0 copy-done.2
  72.9 0.0 copy-done.3
  72.9 1.2 %norm.1 = bf16[1536,256]{1,0:T(8,128)(2,1)} custom-call(f32[24,128]{1,0:T(8,128)S(1)} %get-tuple-element.45.s0_ref, f32[24,128]{1,0:T(8,128)S(1)} %collective-permute-done.8.s1_ref, f32[24,128]{1,0:T(8,128)S(1)} %collective-permute-done.9.s2_ref, f32[24,128]{1,0:T(8,128)S(1)} %collective-permute-done.10.s3_ref, f32[1536,256]{1,0:T(8,128)S(1)} %get-tuple-element.46.sum_ref, ...), custom_call_target="tpu_custom_call" | custom-call | bytes 4194304 | tf_op jit(solution)/shard_map/norm/pallas_call | solution.py:50
Async XLA Ops:
  0.0 15.0 %copy-start = (bf16[48,32,256]{2,1,0:T(8,128)(2,1)S(1)}, bf16[48,32,256]{2,1,0:T(8,128)(2,1)}, u32[]{:S(2)}) copy-start(bf16[48,32,256]{2,1,0:T(8,128)(2,1)} %v_hbm_ref.1) | copy-start | bytes 2359300
  2.9 21.5 %all-to-all-start = ((bf16[64,8,128]{2,1,0:T(8,128)(2,1)}), bf16[64,8,128]{2,1,0:T(8,128)(2,1)S(1)}, u32[]{:S(2)}, u32[]{:S(2)}) async-start(bf16[64,8,128]{2,1,0:T(8,128)(2,1)} %bitcast.25), calls=%async_computation | async-start | bytes 262144 | tf_op jit(solution)/shard_map/all_to_all | solution.py:528
  17.4 1.5 %collective-permute-start = (bf16[768,128]{1,0:T(8,128)(2,1)S(1)}, bf16[768,128]{1,0:T(8,128)(2,1)S(1)}, u32[]{:S(2)}, u32[]{:S(2)}) collective-permute-start(bf16[768,128]{1,0:T(8,128)(2,1)S(1)} %get-tuple-element.29), channel_id=1, source_target_pairs={{0,4},{4,0},{1,5},{5,1},{2,6},{6,2},{3,7},{7,3},{8,12},{12,8},{9,1... | collective-permute-start | bytes 589832 | tf_op jit(solution)/shard_map/ppermute | solution.py:532
  17.7 2.0 %collective-permute-start.1 = (bf16[768,128]{1,0:T(8,128)(2,1)S(1)}, bf16[768,128]{1,0:T(8,128)(2,1)S(1)}, u32[]{:S(2)}, u32[]{:S(2)}) collective-permute-start(bf16[768,128]{1,0:T(8,128)(2,1)S(1)} %get-tuple-element.30), channel_id=1, source_target_pairs={{0,4},{4,0},{1,5},{5,1},{2,6},{6,2},{3,7},{7,3},{8,12},{12,8},{9,1... | collective-permute-start | bytes 589832 | tf_op jit(solution)/shard_map/ppermute | solution.py:532
  18.0 1.6 %collective-permute-start.2 = (bf16[768,128]{1,0:T(8,128)(2,1)S(1)}, bf16[768,128]{1,0:T(8,128)(2,1)S(1)}, u32[]{:S(2)}, u32[]{:S(2)}) collective-permute-start(bf16[768,128]{1,0:T(8,128)(2,1)S(1)} %get-tuple-element.31), channel_id=1, source_target_pairs={{0,4},{4,0},{1,5},{5,1},{2,6},{6,2},{3,7},{7,3},{8,12},{12,8},{9,1... | collective-permute-start | bytes 589832 | tf_op jit(solution)/shard_map/ppermute | solution.py:532
  18.2 1.6 %collective-permute-start.3 = (bf16[768,128]{1,0:T(8,128)(2,1)S(1)}, bf16[768,128]{1,0:T(8,128)(2,1)S(1)}, u32[]{:S(2)}, u32[]{:S(2)}) collective-permute-start(bf16[768,128]{1,0:T(8,128)(2,1)S(1)} %get-tuple-element.32), channel_id=1, source_target_pairs={{0,4},{4,0},{1,5},{5,1},{2,6},{6,2},{3,7},{7,3},{8,12},{12,8},{9,1... | collective-permute-start | bytes 589832 | tf_op jit(solution)/shard_map/ppermute | solution.py:532
  18.5 9.3 %collective-permute-start.4 = (bf16[48,256]{1,0:T(8,128)(2,1)}, bf16[48,256]{1,0:T(8,128)(2,1)S(1)}, u32[]{:S(2)}, u32[]{:S(2)}) collective-permute-start(bf16[48,256]{1,0:T(8,128)(2,1)} %get-tuple-element.33), channel_id=1, source_target_pairs={{0,4},{4,0},{1,5},{5,1},{2,6},{6,2},{3,7},{7,3},{8,12},{12,8},{9,1... | collective-permute-start | bytes 73736 | tf_op jit(solution)/shard_map/ppermute | solution.py:532
  18.9 8.9 %collective-permute-start.5 = (bf16[48,256]{1,0:T(8,128)(2,1)}, bf16[48,256]{1,0:T(8,128)(2,1)S(1)}, u32[]{:S(2)}, u32[]{:S(2)}) collective-permute-start(bf16[48,256]{1,0:T(8,128)(2,1)} %get-tuple-element.34), channel_id=1, source_target_pairs={{4,8},{8,4},{12,16},{16,12},{20,24},{24,20},{28,32},{32,28},{36,40... | collective-permute-start | bytes 73736 | tf_op jit(solution)/shard_map/ppermute | solution.py:532
  24.4 29.0 %copy-start.1 = (f32[9,256]{1,0:T(8,128)S(1)}, f32[9,256]{1,0:T(8,128)}, u32[]{:S(2)}) copy-start(f32[9,256]{1,0:T(8,128)} %w_ref.1) | copy-start | bytes 27652
  27.8 16.8 %all-to-all-start.1 = ((bf16[32,16,128]{2,1,0:T(8,128)(2,1)}), bf16[32,16,128]{2,1,0:T(8,128)(2,1)S(1)}, u32[]{:S(2)}, u32[]{:S(2)}) async-start(bf16[32,16,128]{2,1,0:T(8,128)(2,1)} %bitcast.23), calls=%async_computation.1 | async-start | bytes 262144 | tf_op jit(solution)/shard_map/all_to_all | solution.py:528
  36.2 9.4 %collective-permute-start.6 = (bf16[48,256]{1,0:T(8,128)(2,1)S(1)}, bf16[48,256]{1,0:T(8,128)(2,1)S(1)}, u32[]{:S(2)}, u32[]{:S(2)}) collective-permute-start(bf16[48,256]{1,0:T(8,128)(2,1)S(1)} %get-tuple-element.38), channel_id=1, source_target_pairs={{0,64},{64,0},{128,192},{192,128},{1,65},{65,1},{129,193},{193,129... | collective-permute-start | bytes 73736 | tf_op jit(solution)/shard_map/ppermute | solution.py:532
  36.5 9.1 %collective-permute-start.7 = (bf16[48,256]{1,0:T(8,128)(2,1)S(1)}, bf16[48,256]{1,0:T(8,128)(2,1)S(1)}, u32[]{:S(2)}, u32[]{:S(2)}) collective-permute-start(bf16[48,256]{1,0:T(8,128)(2,1)S(1)} %get-tuple-element.39), channel_id=1, source_target_pairs={{64,128},{128,64},{65,129},{129,65},{66,130},{130,66},{67,131},{13... | collective-permute-start | bytes 73736 | tf_op jit(solution)/shard_map/ppermute | solution.py:532
  45.6 17.2 %all-to-all-start.2 = ((bf16[64,8,128]{2,1,0:T(8,128)(2,1)}), bf16[64,8,128]{2,1,0:T(8,128)(2,1)S(1)}, u32[]{:S(2)}, u32[]{:S(2)}) async-start(bf16[64,8,128]{2,1,0:T(8,128)(2,1)} %bitcast.24), calls=%async_computation.2 | async-start | bytes 262144 | tf_op jit(solution)/shard_map/all_to_all | solution.py:528
  62.8 10.1 %copy-start.2 = (f32[256]{0:T(256)S(1)}, f32[256]{0:T(256)}, u32[]{:S(2)}) copy-start(f32[256]{0:T(256)} %param.12) | copy-start | bytes 3076
  62.8 10.1 %copy-start.3 = (f32[256]{0:T(256)S(1)}, f32[256]{0:T(256)}, u32[]{:S(2)}) copy-start(f32[256]{0:T(256)} %param.13) | copy-start | bytes 3076
  64.8 5.0 %collective-permute-start.10 = (f32[24,128]{1,0:T(8,128)S(1)}, f32[24,128]{1,0:T(8,128)S(1)}, u32[]{:S(2)}, u32[]{:S(2)}) collective-permute-start(f32[24,128]{1,0:T(8,128)S(1)} %get-tuple-element.45.s0_ref), channel_id=1, source_target_pairs={{0,3},{1,2},{2,1},{3,0},{4,7},{5,6},{6,5},{7,4},{8,11},{9,10},{10,... | collective-permute-start | bytes 36872 | tf_op jit(solution)/shard_map/ppermute | solution.py:632
  67.7 5.2 %collective-permute-start.9 = (f32[24,128]{1,0:T(8,128)S(1)}, f32[24,128]{1,0:T(8,128)S(1)}, u32[]{:S(2)}, u32[]{:S(2)}) collective-permute-start(f32[24,128]{1,0:T(8,128)S(1)} %get-tuple-element.45.s0_ref), channel_id=1, source_target_pairs={{0,2},{1,3},{2,0},{3,1},{4,6},{5,7},{6,4},{7,5},{8,10},{9,11},{10,... | collective-permute-start | bytes 36872 | tf_op jit(solution)/shard_map/ppermute | solution.py:632
  68.5 4.4 %collective-permute-start.8 = (f32[24,128]{1,0:T(8,128)S(1)}, f32[24,128]{1,0:T(8,128)S(1)}, u32[]{:S(2)}, u32[]{:S(2)}) collective-permute-start(f32[24,128]{1,0:T(8,128)S(1)} %get-tuple-element.45.s0_ref), channel_id=1, source_target_pairs={{0,1},{1,0},{2,3},{3,2},{4,5},{5,4},{6,7},{7,6},{8,9},{9,8},{10,11... | collective-permute-start | bytes 36872 | tf_op jit(solution)/shard_map/ppermute | solution.py:632

commit v12 on v11

--- a/solution.py
+++ b/solution.py
@@ -348,105 +348,88 @@
     rest_ref[...] = jnp.where(even_row(), lines[0], lines[1]).astype(bf16)
 
 
-def local_kernel(
-    agents_ref,
-    tab_hbm_ref,
-    q_ref,
-    v_hbm_ref,
-    near_ref,
-    far_ref,
-    mate_ref,
-    rest_ref,
-    w_ref,
-    prob_ref,
-    out_hbm_ref,
-    wide_ref,
-    tab_ref,
-    held_ref,
-    v_ref,
-    above_ref,
-    below_ref,
-    l_ref,
-    r_ref,
-    out_ref,
-    sems,
+def probability_kernel(
+    agents_ref, tab_hbm_ref, q_ref, prob_ref, wide_ref, tab_ref, held_ref, sems
 ):
-    v_fetches = []
+    table = pltpu.make_async_copy(tab_hbm_ref, tab_ref, sems.at[3])
+    table.start()
+    fetches = []
+    for c in range(3):
+        part = pl.ds(c * (N // 3), N // 3)
+        fetches.append(pltpu.make_async_copy(q_ref.at[part, :], held_ref.at[part, :], sems.at[c]))
+        fetches[c].start()
+    pairs = agent_pairs(agents_ref, wide_ref, 1.0 / math.sqrt(HD))
+    probabilities(pairs, tab_ref, table, held_ref, fetches, prob_ref)
+
+
+def shifted(row, left, right):
+    column = lax.broadcasted_iota(jnp.int32, row.shape, 0)
+    before = jnp.where(column == 0, left, pltpu.roll(row, 1, 0))
+    behind = jnp.where(column == TC - 1, right, pltpu.roll(row, TC - 1, 0))
+    return before, row, behind
+
+
+def conv_kernel(
+    v_hbm_ref, near_ref, far_ref, w_ref, out_hbm_ref, v_ref, l_ref, r_ref, out_ref, sems
+):
+    fetches, outs = [], []
     for half in range(2):
         cols = pl.ds(half * 128, 128)
-        v_fetches.append(
+        fetches.append(
             pltpu.make_async_copy(v_hbm_ref.at[:, :, cols], v_ref.at[:, :, cols], sems.at[half])
         )
-    table = pltpu.make_async_copy(tab_hbm_ref, tab_ref, sems.at[2])
-    q_fetches = []
-    for c in range(3):
-        part = pl.ds(c * (N // 3), N // 3)
-        q_fetches.append(
-            pltpu.make_async_copy(q_ref.at[part, :], held_ref.at[part, :], sems.at[3 + c])
-        )
-    for copy in v_fetches + [table] + q_fetches:
-        copy.start()
-    pairs = agent_pairs(agents_ref, wide_ref, 1.0 / math.sqrt(HD))
-    outs = []
-    for half in range(2):
-        cols = pl.ds(half * 128, 128)
+        fetches[half].start()
         outs.append(
             pltpu.make_async_copy(
-                out_ref.at[:, cols], out_hbm_ref.at[:, cols], sems.at[6 + half]
+                out_ref.at[:, cols], out_hbm_ref.at[:, cols], sems.at[2 + half]
             )
         )
-    mate, rest = mate_ref[...].astype(f32), rest_ref[...].astype(f32)
-    above_ref[...] = jnp.where(even_row(), rest, mate)
-    below_ref[...] = jnp.where(even_row(), mate, rest)
     mate, rest = near_ref[...].astype(f32), far_ref[...].astype(f32)
     l_ref[...] = jnp.where(even_core(), rest, mate)
     r_ref[...] = jnp.where(even_core(), mate, rest)
     for half in range(2):
         cols = pl.ds(half * 128, 128)
-        v_fetches[half].wait()
-
-        def put(at, total):
-            out_ref[pl.ds(at, TC), cols] = total
-
         w = [jnp.broadcast_to(w_ref[t : t + 1, cols], (TC, 128)) for t in range(9)]
-        column = lax.broadcasted_iota(jnp.int32, (TC, 128), 0)
-
-        def taps(row, left, right):
-            row = row.astype(f32)
-            before = jnp.where(column == 0, left, pltpu.roll(row, 1, 0))
-            after = jnp.where(column == TC - 1, right, pltpu.roll(row, TC - 1, 0))
-            return [before * w[3 * d] + row * w[3 * d + 1] + after * w[3 * d + 2] for d in range(3)]
-
-        tail = above_ref[pl.ds(TC, 8), cols]
-        t0 = taps(above_ref[pl.ds(0, TC), cols], tail[0:1], tail[1:2])
 
         def group(start, carry):
             a, b = carry
             lefts, rights = l_ref[pl.ds(start, 8), cols], r_ref[pl.ds(start, 8), cols]
             for k in range(8):
-                t = taps(v_ref[start + k, :, cols], lefts[k : k + 1], rights[k : k + 1])
+                row = v_ref[start + k, :, cols].astype(f32)
+                x = shifted(row, lefts[k : k + 1], rights[k : k + 1])
+                t = [sum(x[e] * w[3 * d + e] for e in range(3)) for d in range(3)]
                 if a is not None:
                     at = (start + k - 1) * TC
                     if not isinstance(at, int):
                         at = pl.multiple_of(at, TC)
-                    put(at, a + t[2])
-                a, b = b + t[1], t[0]
+                    out_ref[pl.ds(at, TC), cols] = a + t[2]
+                    b = b + t[1]
+                else:
+                    b = t[1]
+                a, b = b, t[0]
             return a, b
 
-        carry = group(0, (None, t0[0]))
-        a, b = lax.fori_loop(
-            1, TR // 8, lambda g, c: group(pl.multiple_of(g * 8, 8), c), carry
-        )
-        tail = below_ref[pl.ds(TC, 8), cols]
-        t = taps(below_ref[pl.ds(0, TC), cols], tail[0:1], tail[1:2])
-        put((TR - 1) * TC, a + t[2])
+        fetches[half].wait()
+        carry = group(0, (None, None))
+        a, b = lax.fori_loop(1, TR // 8, lambda g, c: group(pl.multiple_of(g * 8, 8), c), carry)
+        out_ref[pl.ds((TR - 1) * TC, TC), cols] = a
         outs[half].start()
-    probabilities(pairs, tab_ref, table, held_ref, q_fetches, prob_ref)
     for copy in outs:
         copy.wait()
 
 
-def attend_kernel(av_ref, prob_ref, conv_hbm_ref, sum_ref, stat_ref, conv_ref, sems):
+def attend_kernel(
+    av_ref,
+    prob_ref,
+    conv_hbm_ref,
+    mate_ref,
+    rest_ref,
+    w_ref,
+    sum_ref,
+    stat_ref,
+    conv_ref,
+    sems,
+):
     step = N // AGR
     copies = []
     for c in range(AGR):
@@ -473,6 +456,13 @@
                 agent_values,
                 preferred_element_type=f32,
             )
+    mate, rest = mate_ref[...].astype(f32), rest_ref[...].astype(f32)
+    above = jnp.where(even_row(), rest, mate)
+    below = jnp.where(even_row(), mate, rest)
+    for line, tap, at in ((above, 0, 0), (below, 6, N - TC)):
+        x = shifted(line[:TC], line[TC : TC + 1], line[TC + 1 : TC + 2])
+        total = sum(x[e] * w_ref[tap + e : tap + e + 1, :] for e in range(3))
+        sum_ref[pl.ds(at, TC), :] = sum_ref[pl.ds(at, TC), :] + total
     for b in range(BLOCKS):
         if b * 128 % step == 0:
             copies[b * 128 // step].wait()
@@ -591,42 +581,52 @@
         nbytes=mb // 4,
         name="lines",
     )(values, inner, outer)
-    received = after(received, mate, rest)
-    mate = swap(mate, "row", chain("row", 0))
-    rest = swap(rest, "row", chain("row", 1))
-    merged = call(merge_kernel, far((TILES * 8, 128), bf16), " ", nbytes=2 * mb, name="merge")(
-        received
-    )
-    merged = after(merged, mate, rest)
-    agent_values = spread(merged)
-    prob, convolved = call(
-        local_kernel,
-        (near((N, LOCAL_HEADS * AGENTS), bf16), far((N, CH), f32)),
-        " hhhvvvv ",
+    prob = call(
+        probability_kernel,
+        near((N, LOCAL_HEADS * AGENTS), bf16),
+        " hh",
         scratch=[
             wide,
             held_table,
             pltpu.VMEM((N, CH), bf16),
+            pltpu.SemaphoreType.DMA((4,)),
+        ],
+        nbytes=20 * mb,
+        name="probabilities",
+    )(agents, table, q)
+    received = after(received, mate, rest, prob)
+    merged = call(merge_kernel, far((TILES * 8, 128), bf16), " ", nbytes=2 * mb, name="merge")(
+        received
+    )
+    mate, rest, inner, outer, merged = lax.optimization_barrier(
+        (mate, rest, inner, outer, merged)
+    )
+    mate = swap(mate, "row", chain("row", 0))
+    rest = swap(rest, "row", chain("row", 1))
+    agent_values = spread(merged)
+    convolved = call(
+        conv_kernel,
+        (far((N, CH), f32),),
+        "hvv ",
+        scratch=[
             pltpu.VMEM((TR, TC, CH), bf16),
-            pltpu.VMEM((TC + 16, CH), f32),
-            pltpu.VMEM((TC + 16, CH), f32),
             pltpu.VMEM((TR, CH), f32),
             pltpu.VMEM((TR, CH), f32),
             pltpu.VMEM((N, CH), f32),
-            pltpu.SemaphoreType.DMA((8,)),
+            pltpu.SemaphoreType.DMA((4,)),
         ],
-        nbytes=20 * mb,
-        out_spaces=" h",
-        name="conv_and_probabilities",
-    )(after(agents, merged), table, q, values, inner, outer, mate, rest, conv_weight)
+        nbytes=8 * mb,
+        out_spaces="h",
+        name="conv",
+    )(values, inner, outer, conv_weight)[0]
     summed, stats = call(
         attend_kernel,
         (near((N, CH), f32), near((2 * BLOCKS, 128), f32)),
-        " vh",
+        " vh   ",
         scratch=[pltpu.VMEM((N, CH), f32), pltpu.SemaphoreType.DMA((AGR,))],
         nbytes=4 * mb,
         name="attend",
-    )(agent_values, prob, convolved)
+    )(agent_values, prob, convolved, mate, rest, conv_weight)
     heads = lax.axis_size("head")
     others = [
         lax.ppermute(stats, "head", [(i, i ^ d) for i in range(heads)]) for d in range(1, heads)

time: 75.3 us -> 73.5 us (0.976)
  waiting for transfers between devices: 16.5 us -> 14.5 us
  Pallas kernels: 19.2 us -> 21 us
  starting transfers between devices: 38.3 us -> 36.6 us
    all_to_all x3, waiting for transfers between devices: 12.2 us -> 10.2 us  [spread(): return lax.all_to_all(slot, axes, 0, 0).reshape(x.shape)]
    all_to_all x3, starting transfers between devices: 27.5 us -> 25.7 us  [spread(): return lax.all_to_all(slot, axes, 0, 0).reshape(x.shape)]
    pallas_call x8 -> x9, Pallas kernels: 19.2 us -> 21 us  [run(): fn(*[pltpu.with_memory_space_constraint(x, spaces[c]) if c in spaces else...]
  transfers between devices with their start and end apart: 14 -> 14, of which waited for: 7 -> 7; matrix products, arithmetic and copies ran while one was open for 0% -> 0% of each run, Pallas kernels for 18% -> 19%
where the time goes in v12:
time: 73.5 us; the launch traced here: 72.4 us
  starting transfers between devices  36.6 us (50%)
  Pallas kernels  21 us (29%)
  waiting for transfers between devices  14.5 us (20%)
    all_to_all x3, starting transfers between devices, spread(): return lax.all_to_all(slot, axes, 0, 0).reshape(x.shape)  25.7 us
    pallas_call x9, Pallas kernels, run(): fn(*[pltpu.with_memory_space_constraint(x, spaces[c]) if c in spaces else...  21 us
    all_to_all x3, waiting for transfers between devices, spread(): return lax.all_to_all(slot, axes, 0, 0).reshape(x.shape)  10.2 us
    ppermute x8, starting transfers between devices, swap(): lax.ppermute(x, axis, [p for i, j in pairs for p in ((i, j), (j, i))])  6.72 us
    ppermute x3, starting transfers between devices, shards(): lax.ppermute(stats, 'head', [(i, i ^ d) for i in range(heads)])  4.18 us
    ppermute x3, waiting for transfers between devices, shards(): lax.ppermute(stats, 'head', [(i, i ^ d) for i in range(heads)])  3.87 us
  transfers between devices with their start and end apart: 14, of which 7 were waited for; matrix products, arithmetic and copies ran while one was open for 0% of the time, Pallas kernels for 19%

profile of v12, /device:TPU:8, one launch (start us, length us, event | category | flops | bytes accessed | tf_op | source)
XLA Modules:
  0.0 72.4 jit_solution(14264937078438809187)
XLA Ops:
  0.0 0.0 copy-start
  0.0 2.9 %pool_queries.1 = (bf16[512,128]{1,0:T(8,128)(2,1)}, f32[2,80,128]{2,1,0:T(8,128)}) custom-call(s32[2,32,48]{2,1,0:T(8,128)} %bitcast.26, bf16[1536,256]{1,0:T(8,128)(2,1)} %bitcast.20), custom_call_target="tpu_custom_call" | custom-call | bytes 8388608 | tf_op jit(solution)/shard_map/pool_queries/pallas_call | solution.py:50
  2.9 12.1 %all-to-all-start = ((bf16[64,8,128]{2,1,0:T(8,128)(2,1)}), bf16[64,8,128]{2,1,0:T(8,128)(2,1)S(1)}, u32[]{:S(2)}, u32[]{:S(2)}) async-start(bf16[64,8,128]{2,1,0:T(8,128)(2,1)} %bitcast.25), calls=%async_computation | async-start | bytes 262144 | tf_op jit(solution)/shard_map/all_to_all | solution.py:518
  15.0 0.0 copy-done
  15.0 2.4 %turn_keys.1 = (bf16[1536,128]{1,0:T(8,128)(2,1)S(1)}, bf16[768,128]{1,0:T(8,128)(2,1)S(1)}, bf16[768,128]{1,0:T(8,128)(2,1)S(1)}, bf16[768,128]{1,0:T(8,128)(2,...) custom-call(f32[2,80,128]{2,1,0:T(8,128)} %get-tuple-element.28.tab_hbm_ref, ...), custom_call_target="tpu_custom_call" | custom-call | bytes 4194304 | tf_op jit(solution)/shard_map/turn_keys/pallas_call | solution.py:50
  17.4 0.2 collective-permute-start
  17.6 0.4 collective-permute-start.1
  18.0 0.1 collective-permute-start.2
  18.2 0.4 collective-permute-start.3
  18.5 0.1 collective-permute-start.4
  18.7 0.3 collective-permute-done.refs_0_
  18.9 0.7 collective-permute-start.5
  19.6 0.0 collective-permute-done.1.refs_1_
  19.6 0.0 collective-permute-done.2.refs_2_
  19.6 0.2 collective-permute-done.3.refs_3_
  19.8 4.6 %all-to-all-done = bf16[64,8,128]{2,1,0:T(8,128)(2,1)S(1)} async-done(((bf16[64,8,128]{2,1,0:T(8,128)(2,1)}), bf16[64,8,128]{2,1,0:T(8,128)(2,1)S(1)}, u32[]{:S(2)}, u32[]{:S(2)}) %all-to-all-start) | async-done | bytes 131104 | tf_op jit(solution)/shard_map/all_to_all | solution.py:518
  24.4 3.4 %partials.1 = bf16[512,128]{1,0:T(8,128)(2,1)} custom-call(bf16[512,128]{1,0:T(8,128)(2,1)S(1)} %bitcast.14, bf16[1536,128]{1,0:T(8,128)(2,1)S(1)} %get-tuple-element.29.tk_ref, bf16[1536,256]{1,0:T(8,128)(2,1)S(1)} %bitcast.13, bf16[768,128]{1,0:T(8,128)(2,1)S(1)} %collective-permute-done.refs_0_, bf16[768,128]{1,0:T(8,128)(2,1)S(1)} %collective-permute-done.1.refs_1_, ...), custom_call_target="tpu_custom_call" | custom-call | bytes 10485760 | tf_op jit(solution)/shard_map/partials/pallas_call | solution.py:50
  27.8 0.0 collective-permute-done.4.near_ref
  27.8 0.0 collective-permute-done.5.far_ref
  27.8 7.6 %all-to-all-start.1 = ((bf16[32,16,128]{2,1,0:T(8,128)(2,1)}), bf16[32,16,128]{2,1,0:T(8,128)(2,1)S(1)}, u32[]{:S(2)}, u32[]{:S(2)}) async-start(bf16[32,16,128]{2,1,0:T(8,128)(2,1)} %bitcast.23), calls=%async_computation.1 | async-start | bytes 262144 | tf_op jit(solution)/shard_map/all_to_all | solution.py:518
  35.4 0.0 copy-start.1
  35.4 4.1 %probabilities.1.prob_ref = bf16[1536,1024]{1,0:T(8,128)(2,1)S(1)} custom-call(bf16[512,128]{1,0:T(8,128)(2,1)S(1)} %bitcast.15, f32[2,80,128]{2,1,0:T(8,128)} %get-tuple-element.28.tab_hbm_ref, bf16[1536,256]{1,0:T(8,128)(2,1)} %bitcast.21), custom_call_target="tpu_custom_call" | custom-call | bytes 20971520 | tf_op jit(solution)/shard_map/probabilities/pallas_call | solution.py:50
  39.6 0.8 %lines.1 = (bf16[48,256]{1,0:T(8,128)(2,1)S(1)}, bf16[48,256]{1,0:T(8,128)(2,1)S(1)}) custom-call(bf16[48,32,256]{2,1,0:T(8,128)(2,1)} %v_hbm_ref.1, bf16[48,256]{1,0:T(8,128)(2,1)S(1)} %collective-permute-done.4.near_ref, bf16[48,256]{1,0:T(8,128)(2,1)S(1)} %collective-permute-done.5.far_ref), custom_call_target="tpu_custom_call" | custom-call | bytes 262144 | tf_op jit(solution)/shard_map/lines/pallas_call | solution.py:50
  40.4 4.2 %all-to-all-done.1 = bf16[32,16,128]{2,1,0:T(8,128)(2,1)S(1)} async-done(((bf16[32,16,128]{2,1,0:T(8,128)(2,1)}), bf16[32,16,128]{2,1,0:T(8,128)(2,1)S(1)}, u32[]{:S(2)}, u32[]{:S(2)}) %all-to-all-start.1) | async-done | bytes 131104 | tf_op jit(solution)/shard_map/all_to_all | solution.py:518
  44.6 1.0 %merge.1 = bf16[512,128]{1,0:T(8,128)(2,1)} custom-call(bf16[512,128]{1,0:T(8,128)(2,1)S(1)} %bitcast.17), custom_call_target="tpu_custom_call" | custom-call | bytes 2097152 | tf_op jit(solution)/shard_map/merge/pallas_call | solution.py:50
  45.6 6.0 %all-to-all-start.2 = ((bf16[64,8,128]{2,1,0:T(8,128)(2,1)}), bf16[64,8,128]{2,1,0:T(8,128)(2,1)S(1)}, u32[]{:S(2)}, u32[]{:S(2)}) async-start(bf16[64,8,128]{2,1,0:T(8,128)(2,1)} %bitcast.24), calls=%async_computation.2 | async-start | bytes 262144 | tf_op jit(solution)/shard_map/all_to_all | solution.py:518
  51.6 0.5 collective-permute-start.6
  52.1 4.3 %collective-permute-start.7 = (bf16[48,256]{1,0:T(8,128)(2,1)S(1)}, bf16[48,256]{1,0:T(8,128)(2,1)S(1)}, u32[]{:S(2)}, u32[]{:S(2)}) collective-permute-start(bf16[48,256]{1,0:T(8,128)(2,1)S(1)} %get-tuple-element.46), channel_id=1, source_target_pairs={{64,128},{128,64},{65,129},{129,65},{66,130},{130,66},{67,131},{13... | collective-permute-start | bytes 73736 | tf_op jit(solution)/shard_map/ppermute | solution.py:522
  56.4 0.0 copy-done.1
  56.4 3.2 %conv.1.conv_hbm_ref = f32[1536,256]{1,0:T(8,128)} custom-call(bf16[48,32,256]{2,1,0:T(8,128)(2,1)} %v_hbm_ref.1, bf16[48,256]{1,0:T(8,128)(2,1)S(1)} %collective-permute-done.4.near_ref, bf16[48,256]{1,0:T(8,128)(2,1)S(1)} %collective-permute-done.5.far_ref, f32[9,256]{1,0:T(8,128)S(1)} %copy-done.1), custom_call_target="tpu_custom_call" | custom-call | bytes 8388608 | tf_op jit(solution)/shard_map/conv/pallas_call | solution.py:50
  59.6 0.0 collective-permute-done.6.mate_ref
  59.6 0.0 collective-permute-done.7.rest_ref
  59.6 1.3 %all-to-all-done.2 = bf16[64,8,128]{2,1,0:T(8,128)(2,1)S(1)} async-done(((bf16[64,8,128]{2,1,0:T(8,128)(2,1)}), bf16[64,8,128]{2,1,0:T(8,128)(2,1)S(1)}, u32[]{:S(2)}, u32[]{:S(2)}) %all-to-all-start.2) | async-done | bytes 131104 | tf_op jit(solution)/shard_map/all_to_all | solution.py:518
  61.0 0.0 copy-start.2
  61.0 0.0 copy-start.3
  61.0 2.0 %attend.1 = (f32[1536,256]{1,0:T(8,128)S(1)}, f32[24,128]{1,0:T(8,128)S(1)}) custom-call(bf16[512,128]{1,0:T(8,128)(2,1)S(1)} %bitcast.16, bf16[1536,1024]{1,0:T(8,128)(2,1)S(1)} %probabilities.1.prob_ref, f32[1536,256]{1,0:T(8,128)} %conv.1.conv_hbm_ref, bf16[48,256]{1,0:T(8,128)(2,1)S(1)} %collective-permute-done.6.mate_ref, ...), custom_call_target="tpu_custom_call" | custom-call | bytes 4194304 | tf_op jit(solution)/shard_map/attend/pallas_call | solution.py:50
  63.0 2.8 %collective-permute-start.10 = (f32[24,128]{1,0:T(8,128)S(1)}, f32[24,128]{1,0:T(8,128)S(1)}, u32[]{:S(2)}, u32[]{:S(2)}) collective-permute-start(f32[24,128]{1,0:T(8,128)S(1)} %get-tuple-element.47.s0_ref), channel_id=1, source_target_pairs={{0,3},{1,2},{2,1},{3,0},{4,7},{5,6},{6,5},{7,4},{8,11},{9,10},{10,... | collective-permute-start | bytes 36872 | tf_op jit(solution)/shard_map/ppermute | solution.py:632
  65.8 0.8 %collective-permute-start.9 = (f32[24,128]{1,0:T(8,128)S(1)}, f32[24,128]{1,0:T(8,128)S(1)}, u32[]{:S(2)}, u32[]{:S(2)}) collective-permute-start(f32[24,128]{1,0:T(8,128)S(1)} %get-tuple-element.47.s0_ref), channel_id=1, source_target_pairs={{0,2},{1,3},{2,0},{3,1},{4,6},{5,7},{6,4},{7,5},{8,10},{9,11},{10,... | collective-permute-start | bytes 36872 | tf_op jit(solution)/shard_map/ppermute | solution.py:632
  66.6 0.5 collective-permute-start.8
  67.2 0.8 %collective-permute-done.10.s3_ref = f32[24,128]{1,0:T(8,128)S(1)} collective-permute-done((f32[24,128]{1,0:T(8,128)S(1)}, f32[24,128]{1,0:T(8,128)S(1)}, u32[]{:S(2)}, u32[]{:S(2)}) %collective-permute-start.10) | collective-permute-done | bytes 12320 | tf_op jit(solution)/shard_map/ppermute | solution.py:632
  68.0 3.1 %collective-permute-done.9.s2_ref = f32[24,128]{1,0:T(8,128)S(1)} collective-permute-done((f32[24,128]{1,0:T(8,128)S(1)}, f32[24,128]{1,0:T(8,128)S(1)}, u32[]{:S(2)}, u32[]{:S(2)}) %collective-permute-start.9) | collective-permute-done | bytes 12320 | tf_op jit(solution)/shard_map/ppermute | solution.py:632
  71.0 0.0 collective-permute-done.8.s1_ref
  71.0 0.0 copy-done.2
  71.0 0.0 copy-done.3
  71.0 1.2 %norm.1 = bf16[1536,256]{1,0:T(8,128)(2,1)} custom-call(f32[24,128]{1,0:T(8,128)S(1)} %get-tuple-element.47.s0_ref, f32[24,128]{1,0:T(8,128)S(1)} %collective-permute-done.8.s1_ref, f32[24,128]{1,0:T(8,128)S(1)} %collective-permute-done.9.s2_ref, f32[24,128]{1,0:T(8,128)S(1)} %collective-permute-done.10.s3_ref, f32[1536,256]{1,0:T(8,128)S(1)} %get-tuple-element.48.sum_ref, ...), custom_call_target="tpu_custom_call" | custom-call | bytes 4194304 | tf_op jit(solution)/shard_map/norm/pallas_call | solution.py:50
Async XLA Ops:
  0.0 15.0 %copy-start = (bf16[48,32,256]{2,1,0:T(8,128)(2,1)S(1)}, bf16[48,32,256]{2,1,0:T(8,128)(2,1)}, u32[]{:S(2)}) copy-start(bf16[48,32,256]{2,1,0:T(8,128)(2,1)} %v_hbm_ref.1) | copy-start | bytes 2359300
  2.9 21.5 %all-to-all-start = ((bf16[64,8,128]{2,1,0:T(8,128)(2,1)}), bf16[64,8,128]{2,1,0:T(8,128)(2,1)S(1)}, u32[]{:S(2)}, u32[]{:S(2)}) async-start(bf16[64,8,128]{2,1,0:T(8,128)(2,1)} %bitcast.25), calls=%async_computation | async-start | bytes 262144 | tf_op jit(solution)/shard_map/all_to_all | solution.py:518
  17.4 1.5 %collective-permute-start = (bf16[768,128]{1,0:T(8,128)(2,1)S(1)}, bf16[768,128]{1,0:T(8,128)(2,1)S(1)}, u32[]{:S(2)}, u32[]{:S(2)}) collective-permute-start(bf16[768,128]{1,0:T(8,128)(2,1)S(1)} %get-tuple-element.30), channel_id=1, source_target_pairs={{0,4},{4,0},{1,5},{5,1},{2,6},{6,2},{3,7},{7,3},{8,12},{12,8},{9,1... | collective-permute-start | bytes 589832 | tf_op jit(solution)/shard_map/ppermute | solution.py:522
  17.6 2.0 %collective-permute-start.1 = (bf16[768,128]{1,0:T(8,128)(2,1)S(1)}, bf16[768,128]{1,0:T(8,128)(2,1)S(1)}, u32[]{:S(2)}, u32[]{:S(2)}) collective-permute-start(bf16[768,128]{1,0:T(8,128)(2,1)S(1)} %get-tuple-element.31), channel_id=1, source_target_pairs={{0,4},{4,0},{1,5},{5,1},{2,6},{6,2},{3,7},{7,3},{8,12},{12,8},{9,1... | collective-permute-start | bytes 589832 | tf_op jit(solution)/shard_map/ppermute | solution.py:522
  18.0 1.6 %collective-permute-start.2 = (bf16[768,128]{1,0:T(8,128)(2,1)S(1)}, bf16[768,128]{1,0:T(8,128)(2,1)S(1)}, u32[]{:S(2)}, u32[]{:S(2)}) collective-permute-start(bf16[768,128]{1,0:T(8,128)(2,1)S(1)} %get-tuple-element.32), channel_id=1, source_target_pairs={{0,4},{4,0},{1,5},{5,1},{2,6},{6,2},{3,7},{7,3},{8,12},{12,8},{9,1... | collective-permute-start | bytes 589832 | tf_op jit(solution)/shard_map/ppermute | solution.py:522
  18.2 1.6 %collective-permute-start.3 = (bf16[768,128]{1,0:T(8,128)(2,1)S(1)}, bf16[768,128]{1,0:T(8,128)(2,1)S(1)}, u32[]{:S(2)}, u32[]{:S(2)}) collective-permute-start(bf16[768,128]{1,0:T(8,128)(2,1)S(1)} %get-tuple-element.33), channel_id=1, source_target_pairs={{0,4},{4,0},{1,5},{5,1},{2,6},{6,2},{3,7},{7,3},{8,12},{12,8},{9,1... | collective-permute-start | bytes 589832 | tf_op jit(solution)/shard_map/ppermute | solution.py:522
  18.5 9.3 %collective-permute-start.4 = (bf16[48,256]{1,0:T(8,128)(2,1)}, bf16[48,256]{1,0:T(8,128)(2,1)S(1)}, u32[]{:S(2)}, u32[]{:S(2)}) collective-permute-start(bf16[48,256]{1,0:T(8,128)(2,1)} %get-tuple-element.34), channel_id=1, source_target_pairs={{0,4},{4,0},{1,5},{5,1},{2,6},{6,2},{3,7},{7,3},{8,12},{12,8},{9,1... | collective-permute-start | bytes 73736 | tf_op jit(solution)/shard_map/ppermute | solution.py:522
  18.9 8.9 %collective-permute-start.5 = (bf16[48,256]{1,0:T(8,128)(2,1)}, bf16[48,256]{1,0:T(8,128)(2,1)S(1)}, u32[]{:S(2)}, u32[]{:S(2)}) collective-permute-start(bf16[48,256]{1,0:T(8,128)(2,1)} %get-tuple-element.35), channel_id=1, source_target_pairs={{4,8},{8,4},{12,16},{16,12},{20,24},{24,20},{28,32},{32,28},{36,40... | collective-permute-start | bytes 73736 | tf_op jit(solution)/shard_map/ppermute | solution.py:522
  27.8 16.8 %all-to-all-start.1 = ((bf16[32,16,128]{2,1,0:T(8,128)(2,1)}), bf16[32,16,128]{2,1,0:T(8,128)(2,1)S(1)}, u32[]{:S(2)}, u32[]{:S(2)}) async-start(bf16[32,16,128]{2,1,0:T(8,128)(2,1)} %bitcast.23), calls=%async_computation.1 | async-start | bytes 262144 | tf_op jit(solution)/shard_map/all_to_all | solution.py:518
  35.4 21.0 %copy-start.1 = (f32[9,256]{1,0:T(8,128)S(1)}, f32[9,256]{1,0:T(8,128)}, u32[]{:S(2)}) copy-start(f32[9,256]{1,0:T(8,128)} %w_ref.3) | copy-start | bytes 27652
  45.6 15.4 %all-to-all-start.2 = ((bf16[64,8,128]{2,1,0:T(8,128)(2,1)}), bf16[64,8,128]{2,1,0:T(8,128)(2,1)S(1)}, u32[]{:S(2)}, u32[]{:S(2)}) async-start(bf16[64,8,128]{2,1,0:T(8,128)(2,1)} %bitcast.24), calls=%async_computation.2 | async-start | bytes 262144 | tf_op jit(solution)/shard_map/all_to_all | solution.py:518
  51.6 8.1 %collective-permute-start.6 = (bf16[48,256]{1,0:T(8,128)(2,1)S(1)}, bf16[48,256]{1,0:T(8,128)(2,1)S(1)}, u32[]{:S(2)}, u32[]{:S(2)}) collective-permute-start(bf16[48,256]{1,0:T(8,128)(2,1)S(1)} %get-tuple-element.45), channel_id=1, source_target_pairs={{0,64},{64,0},{128,192},{192,128},{1,65},{65,1},{129,193},{193,129... | collective-permute-start | bytes 73736 | tf_op jit(solution)/shard_map/ppermute | solution.py:522
  52.1 7.5 %collective-permute-start.7 = (bf16[48,256]{1,0:T(8,128)(2,1)S(1)}, bf16[48,256]{1,0:T(8,128)(2,1)S(1)}, u32[]{:S(2)}, u32[]{:S(2)}) collective-permute-start(bf16[48,256]{1,0:T(8,128)(2,1)S(1)} %get-tuple-element.46), channel_id=1, source_target_pairs={{64,128},{128,64},{65,129},{129,65},{66,130},{130,66},{67,131},{13... | collective-permute-start | bytes 73736 | tf_op jit(solution)/shard_map/ppermute | solution.py:522
  61.0 10.1 %copy-start.2 = (f32[256]{0:T(256)S(1)}, f32[256]{0:T(256)}, u32[]{:S(2)}) copy-start(f32[256]{0:T(256)} %param.12) | copy-start | bytes 3076
  61.0 10.1 %copy-start.3 = (f32[256]{0:T(256)S(1)}, f32[256]{0:T(256)}, u32[]{:S(2)}) copy-start(f32[256]{0:T(256)} %param.13) | copy-start | bytes 3076
  63.0 5.0 %collective-permute-start.10 = (f32[24,128]{1,0:T(8,128)S(1)}, f32[24,128]{1,0:T(8,128)S(1)}, u32[]{:S(2)}, u32[]{:S(2)}) collective-permute-start(f32[24,128]{1,0:T(8,128)S(1)} %get-tuple-element.47.s0_ref), channel_id=1, source_target_pairs={{0,3},{1,2},{2,1},{3,0},{4,7},{5,6},{6,5},{7,4},{8,11},{9,10},{10,... | collective-permute-start | bytes 36872 | tf_op jit(solution)/shard_map/ppermute | solution.py:632
  65.8 5.2 %collective-permute-start.9 = (f32[24,128]{1,0:T(8,128)S(1)}, f32[24,128]{1,0:T(8,128)S(1)}, u32[]{:S(2)}, u32[]{:S(2)}) collective-permute-start(f32[24,128]{1,0:T(8,128)S(1)} %get-tuple-element.47.s0_ref), channel_id=1, source_target_pairs={{0,2},{1,3},{2,0},{3,1},{4,6},{5,7},{6,4},{7,5},{8,10},{9,11},{10,... | collective-permute-start | bytes 36872 | tf_op jit(solution)/shard_map/ppermute | solution.py:632
  66.6 4.4 %collective-permute-start.8 = (f32[24,128]{1,0:T(8,128)S(1)}, f32[24,128]{1,0:T(8,128)S(1)}, u32[]{:S(2)}, u32[]{:S(2)}) collective-permute-start(f32[24,128]{1,0:T(8,128)S(1)} %get-tuple-element.47.s0_ref), channel_id=1, source_target_pairs={{0,1},{1,0},{2,3},{3,2},{4,5},{5,4},{6,7},{7,6},{8,9},{9,8},{10,11... | collective-permute-start | bytes 36872 | tf_op jit(solution)/shard_map/ppermute | solution.py:632

commit v13 on v12

--- a/solution.py
+++ b/solution.py
@@ -131,7 +131,6 @@
         copy = pltpu.make_async_copy(q_ref.at[part, :], held_ref.at[part, :], sems.at[cell])
         copy.start()
         copies.append(copy)
-    matrix = turn_matrix()
     lane = lanes((1, 128)) % HD
     power = jnp.exp((lane % 16).astype(f32) * f32(-math.log(100.0) / 16))
     freq_r = jnp.where(lane < 32, power, 0.0)
@@ -147,13 +146,29 @@
     sines, cosines = sin_cos(angles)
     tab_ref[0] = cosines
     tab_ref[1] = sines
-    tables = split_tables(cosines, sines)
+    cos_r, sin_r, cos_c, sin_c = split_tables(cosines, sines)
+    place_in = lanes((1, CH)) % (HD // 2)
+    by_row = lanes((1, CH)) % HD < HD // 2
     means = []
     for cell in range(AGR):
-        cosine, sine = cell_tables(tables, cell * (TR // AGR), TR // AGR)
         copies[cell].wait()
-        rotated = turned(held_ref[pl.ds(cell * step, step), :], matrix, cosine, sine)
-        mean = jnp.sum(rotated.astype(f32), 0, keepdims=True) / step
+        columns = jnp.zeros((TC, CH), f32)
+        row_cos = jnp.zeros((8, CH), f32)
+        row_sin = jnp.zeros((8, CH), f32)
+        for i in range(cell * (TR // AGR), (cell + 1) * (TR // AGR)):
+            x = held_ref[pl.ds(i * TC, TC), :].astype(f32)
+            columns = columns + x
+            x = x[:8] + x[8:16] + x[16:24] + x[24:]
+            row_cos = row_cos + x * cos_r[i : i + 1]
+            row_sin = row_sin + x * sin_r[i : i + 1]
+        col_cos = jnp.sum(columns * cos_c, 0, keepdims=True)
+        col_sin = jnp.sum(columns * sin_c, 0, keepdims=True)
+        straight = jnp.where(by_row, jnp.sum(row_cos, 0, keepdims=True), col_cos)
+        crossed = jnp.where(by_row, jnp.sum(row_sin, 0, keepdims=True), col_sin)
+        crossed = jnp.where(
+            place_in < HD // 4, -pltpu.roll(crossed, CH - HD // 4, 1), pltpu.roll(crossed, HD // 4, 1)
+        )
+        mean = (straight + crossed) / step
         means.append(mean.astype(bf16).astype(f32))
     packed = jnp.concatenate([m[:, :128] for m in means] + [m[:, 128:] for m in means], axis=0)
     agents_ref[...] = slots(packed)
@@ -327,14 +342,39 @@
             prob_ref[rows, pl.ds(head * AGENTS, AGENTS)] = (weights * scale).astype(bf16)
 
 
-def line_kernel(v_ref, near_ref, far_ref, mate_ref, rest_ref, top_ref, bottom_ref, sems):
-    copies = [
-        pltpu.make_async_copy(v_ref.at[0], top_ref, sems.at[0]),
-        pltpu.make_async_copy(v_ref.at[TR - 1], bottom_ref, sems.at[1]),
+def probability_kernel(
+    agents_ref,
+    tab_hbm_ref,
+    q_ref,
+    v_ref,
+    near_ref,
+    far_ref,
+    prob_ref,
+    mate_ref,
+    rest_ref,
+    wide_ref,
+    tab_ref,
+    held_ref,
+    top_ref,
+    bottom_ref,
+    sems,
+):
+    table = pltpu.make_async_copy(tab_hbm_ref, tab_ref, sems.at[3])
+    table.start()
+    fetches = []
+    for c in range(3):
+        part = pl.ds(c * (N // 3), N // 3)
+        fetches.append(pltpu.make_async_copy(q_ref.at[part, :], held_ref.at[part, :], sems.at[c]))
+        fetches[c].start()
+    edges = [
+        pltpu.make_async_copy(v_ref.at[0], top_ref, sems.at[4]),
+        pltpu.make_async_copy(v_ref.at[TR - 1], bottom_ref, sems.at[5]),
     ]
-    for copy in copies:
+    for copy in edges:
         copy.start()
-    for copy in copies:
+    pairs = agent_pairs(agents_ref, wide_ref, 1.0 / math.sqrt(HD))
+    probabilities(pairs, tab_ref, table, held_ref, fetches, prob_ref)
+    for copy in edges:
         copy.wait()
     lines = []
     for row, line_ref in ((0, top_ref), (TR - 1, bottom_ref)):
@@ -346,20 +386,6 @@
         lines.append(jnp.concatenate([line_ref[...].astype(f32), tail], axis=0))
     mate_ref[...] = jnp.where(even_row(), lines[1], lines[0]).astype(bf16)
     rest_ref[...] = jnp.where(even_row(), lines[0], lines[1]).astype(bf16)
-
-
-def probability_kernel(
-    agents_ref, tab_hbm_ref, q_ref, prob_ref, wide_ref, tab_ref, held_ref, sems
-):
-    table = pltpu.make_async_copy(tab_hbm_ref, tab_ref, sems.at[3])
-    table.start()
-    fetches = []
-    for c in range(3):
-        part = pl.ds(c * (N // 3), N // 3)
-        fetches.append(pltpu.make_async_copy(q_ref.at[part, :], held_ref.at[part, :], sems.at[c]))
-        fetches[c].start()
-    pairs = agent_pairs(agents_ref, wide_ref, 1.0 / math.sqrt(HD))
-    probabilities(pairs, tab_ref, table, held_ref, fetches, prob_ref)
 
 
 def shifted(row, left, right):
@@ -573,27 +599,16 @@
     )(agents, tk, v, *got)
     parts, inner, outer = lax.optimization_barrier((parts, inner, outer))
     received = spread(parts, ("row", "z"))
-    mate, rest = call(
-        line_kernel,
-        (near((TC + 16, CH), bf16),) * 2,
-        "hvv",
-        scratch=[pltpu.VMEM((TC, CH), bf16)] * 2 + [pltpu.SemaphoreType.DMA((2,))],
-        nbytes=mb // 4,
-        name="lines",
-    )(values, inner, outer)
-    prob = call(
+    prob, mate, rest = call(
         probability_kernel,
-        near((N, LOCAL_HEADS * AGENTS), bf16),
-        " hh",
-        scratch=[
-            wide,
-            held_table,
-            pltpu.VMEM((N, CH), bf16),
-            pltpu.SemaphoreType.DMA((4,)),
-        ],
+        (near((N, LOCAL_HEADS * AGENTS), bf16),) + (near((TC + 16, CH), bf16),) * 2,
+        " hhhvv",
+        scratch=[wide, held_table, pltpu.VMEM((N, CH), bf16)]
+        + [pltpu.VMEM((TC, CH), bf16)] * 2
+        + [pltpu.SemaphoreType.DMA((6,))],
         nbytes=20 * mb,
         name="probabilities",
-    )(agents, table, q)
+    )(agents, table, q, values, inner, outer)
     received = after(received, mate, rest, prob)
     merged = call(merge_kernel, far((TILES * 8, 128), bf16), " ", nbytes=2 * mb, name="merge")(
         received

time: 73.5 us -> 72.7 us (0.989)
  Pallas kernels: 21 us -> 19.7 us
  waiting for transfers between devices: 14.5 us -> 15.3 us
    pallas_call x9 -> x8, Pallas kernels: 21 us -> 19.7 us  [run(): fn(*[pltpu.with_memory_space_constraint(x, spaces[c]) if c in spaces else...]
    all_to_all x3, waiting for transfers between devices: 10.2 us -> 10.9 us  [spread(): return lax.all_to_all(slot, axes, 0, 0).reshape(x.shape)]
  transfers between devices with their start and end apart: 14 -> 14, of which waited for: 7 -> 7; matrix products, arithmetic and copies ran while one was open for 0% -> 0% of each run, Pallas kernels for 19% -> 18%
where the time goes in v13:
time: 72.7 us; the launch traced here: 71.7 us
  starting transfers between devices  36.4 us (50%)
  Pallas kernels  19.7 us (27%)
  waiting for transfers between devices  15.3 us (21%)
    all_to_all x3, starting transfers between devices, spread(): return lax.all_to_all(slot, axes, 0, 0).reshape(x.shape)  25.5 us
    pallas_call x8, Pallas kernels, run(): fn(*[pltpu.with_memory_space_constraint(x, spaces[c]) if c in spaces else...  19.7 us
    all_to_all x3, waiting for transfers between devices, spread(): return lax.all_to_all(slot, axes, 0, 0).reshape(x.shape)  10.9 us
    ppermute x8, starting transfers between devices, swap(): lax.ppermute(x, axis, [p for i, j in pairs for p in ((i, j), (j, i))])  6.74 us
    ppermute x3, starting transfers between devices, shards(): lax.ppermute(stats, 'head', [(i, i ^ d) for i in range(heads)])  4.18 us
    ppermute x3, waiting for transfers between devices, shards(): lax.ppermute(stats, 'head', [(i, i ^ d) for i in range(heads)])  3.87 us
  transfers between devices with their start and end apart: 14, of which 7 were waited for; matrix products, arithmetic and copies ran while one was open for 0% of the time, Pallas kernels for 18%

profile of v13, /device:TPU:8, one launch (start us, length us, event | category | flops | bytes accessed | tf_op | source)
XLA Modules:
  0.0 71.7 jit_solution(18154927065577554681)
XLA Ops:
  0.0 0.0 copy-start
  0.0 2.3 %pool_queries.1 = (bf16[512,128]{1,0:T(8,128)(2,1)}, f32[2,80,128]{2,1,0:T(8,128)}) custom-call(s32[2,32,48]{2,1,0:T(8,128)} %bitcast.26, bf16[1536,256]{1,0:T(8,128)(2,1)} %bitcast.20), custom_call_target="tpu_custom_call" | custom-call | bytes 8388608 | tf_op jit(solution)/shard_map/pool_queries/pallas_call | solution.py:50
  2.3 12.1 %all-to-all-start = ((bf16[64,8,128]{2,1,0:T(8,128)(2,1)}), bf16[64,8,128]{2,1,0:T(8,128)(2,1)S(1)}, u32[]{:S(2)}, u32[]{:S(2)}) async-start(bf16[64,8,128]{2,1,0:T(8,128)(2,1)} %bitcast.25), calls=%async_computation | async-start | bytes 262144 | tf_op jit(solution)/shard_map/all_to_all | solution.py:544
  14.5 0.0 copy-done
  14.5 2.4 %turn_keys.1 = (bf16[1536,128]{1,0:T(8,128)(2,1)S(1)}, bf16[768,128]{1,0:T(8,128)(2,1)S(1)}, bf16[768,128]{1,0:T(8,128)(2,1)S(1)}, bf16[768,128]{1,0:T(8,128)(2,...) custom-call(f32[2,80,128]{2,1,0:T(8,128)} %get-tuple-element.29.tab_hbm_ref, ...), custom_call_target="tpu_custom_call" | custom-call | bytes 4194304 | tf_op jit(solution)/shard_map/turn_keys/pallas_call | solution.py:50
  16.9 0.2 collective-permute-start
  17.1 0.4 collective-permute-start.1
  17.5 0.1 collective-permute-start.2
  17.6 0.4 collective-permute-start.3
  18.0 0.1 collective-permute-start.4
  18.1 0.3 collective-permute-done.refs_0_
  18.4 0.7 collective-permute-start.5
  19.1 0.0 collective-permute-done.1.refs_1_
  19.1 0.0 collective-permute-done.2.refs_2_
  19.1 0.2 collective-permute-done.3.refs_3_
  19.3 4.6 %all-to-all-done = bf16[64,8,128]{2,1,0:T(8,128)(2,1)S(1)} async-done(((bf16[64,8,128]{2,1,0:T(8,128)(2,1)}), bf16[64,8,128]{2,1,0:T(8,128)(2,1)S(1)}, u32[]{:S(2)}, u32[]{:S(2)}) %all-to-all-start) | async-done | bytes 131104 | tf_op jit(solution)/shard_map/all_to_all | solution.py:544
  23.9 3.4 %partials.1 = bf16[512,128]{1,0:T(8,128)(2,1)} custom-call(bf16[512,128]{1,0:T(8,128)(2,1)S(1)} %bitcast.14, bf16[1536,128]{1,0:T(8,128)(2,1)S(1)} %get-tuple-element.30.tk_ref, bf16[1536,256]{1,0:T(8,128)(2,1)S(1)} %bitcast.13, bf16[768,128]{1,0:T(8,128)(2,1)S(1)} %collective-permute-done.refs_0_, bf16[768,128]{1,0:T(8,128)(2,1)S(1)} %collective-permute-done.1.refs_1_, ...), custom_call_target="tpu_custom_call" | custom-call | bytes 10485760 | tf_op jit(solution)/shard_map/partials/pallas_call | solution.py:50
  27.3 0.0 copy-start.1
  27.3 0.0 collective-permute-done.4.near_ref
  27.3 0.0 collective-permute-done.5.far_ref
  27.3 7.6 %all-to-all-start.1 = ((bf16[32,16,128]{2,1,0:T(8,128)(2,1)}), bf16[32,16,128]{2,1,0:T(8,128)(2,1)S(1)}, u32[]{:S(2)}, u32[]{:S(2)}) async-start(bf16[32,16,128]{2,1,0:T(8,128)(2,1)} %bitcast.23), calls=%async_computation.1 | async-start | bytes 262144 | tf_op jit(solution)/shard_map/all_to_all | solution.py:544
  34.9 4.2 %probabilities.1 = (bf16[1536,1024]{1,0:T(8,128)(2,1)S(1)}, bf16[48,256]{1,0:T(8,128)(2,1)S(1)}, bf16[48,256]{1,0:T(8,128)(2,1)S(1)}) custom-call(bf16[512,128]{1,0:T(8,128)(2,1)S(1)} %bitcast.15, f32[2,80,128]{2,1,0:T(8,128)} %get-tuple-element.29.tab_hbm_ref, bf16[1536,256]{1,0:T(8,128)(2,1)} %bitcast.21, bf16[48,32,256]{2,1,0:T(8,128)(2,1)} %v_hbm_ref.1, ...), custom_call_target="tpu_custom_call" | custom-call | bytes 20971520 | tf_op jit(solution)/shard_map/probabilities/pallas_call | solution.py:50
  39.1 5.0 %all-to-all-done.1 = bf16[32,16,128]{2,1,0:T(8,128)(2,1)S(1)} async-done(((bf16[32,16,128]{2,1,0:T(8,128)(2,1)}), bf16[32,16,128]{2,1,0:T(8,128)(2,1)S(1)}, u32[]{:S(2)}, u32[]{:S(2)}) %all-to-all-start.1) | async-done | bytes 131104 | tf_op jit(solution)/shard_map/all_to_all | solution.py:544
  44.1 1.0 %merge.1 = bf16[512,128]{1,0:T(8,128)(2,1)} custom-call(bf16[512,128]{1,0:T(8,128)(2,1)S(1)} %bitcast.17), custom_call_target="tpu_custom_call" | custom-call | bytes 2097152 | tf_op jit(solution)/shard_map/merge/pallas_call | solution.py:50
  45.1 5.7 %all-to-all-start.2 = ((bf16[64,8,128]{2,1,0:T(8,128)(2,1)}), bf16[64,8,128]{2,1,0:T(8,128)(2,1)S(1)}, u32[]{:S(2)}, u32[]{:S(2)}) async-start(bf16[64,8,128]{2,1,0:T(8,128)(2,1)} %bitcast.24), calls=%async_computation.2 | async-start | bytes 262144 | tf_op jit(solution)/shard_map/all_to_all | solution.py:544
  50.8 0.6 collective-permute-start.6
  51.4 4.3 %collective-permute-start.7 = (bf16[48,256]{1,0:T(8,128)(2,1)S(1)}, bf16[48,256]{1,0:T(8,128)(2,1)S(1)}, u32[]{:S(2)}, u32[]{:S(2)}) collective-permute-start(bf16[48,256]{1,0:T(8,128)(2,1)S(1)} %get-tuple-element.48), channel_id=1, source_target_pairs={{64,128},{128,64},{65,129},{129,65},{66,130},{130,66},{67,131},{13... | collective-permute-start | bytes 73736 | tf_op jit(solution)/shard_map/ppermute | solution.py:548
  55.7 0.0 copy-done.1
  55.7 3.2 %conv.1.conv_hbm_ref = f32[1536,256]{1,0:T(8,128)} custom-call(bf16[48,32,256]{2,1,0:T(8,128)(2,1)} %v_hbm_ref.1, bf16[48,256]{1,0:T(8,128)(2,1)S(1)} %collective-permute-done.4.near_ref, bf16[48,256]{1,0:T(8,128)(2,1)S(1)} %collective-permute-done.5.far_ref, f32[9,256]{1,0:T(8,128)S(1)} %copy-done.1), custom_call_target="tpu_custom_call" | custom-call | bytes 8388608 | tf_op jit(solution)/shard_map/conv/pallas_call | solution.py:50
  58.9 0.0 collective-permute-done.6.mate_ref
  58.9 0.0 collective-permute-done.7.rest_ref
  58.9 1.3 %all-to-all-done.2 = bf16[64,8,128]{2,1,0:T(8,128)(2,1)S(1)} async-done(((bf16[64,8,128]{2,1,0:T(8,128)(2,1)}), bf16[64,8,128]{2,1,0:T(8,128)(2,1)S(1)}, u32[]{:S(2)}, u32[]{:S(2)}) %all-to-all-start.2) | async-done | bytes 131104 | tf_op jit(solution)/shard_map/all_to_all | solution.py:544
  60.2 0.0 copy-start.2
  60.2 0.0 copy-start.3
  60.2 2.0 %attend.1 = (f32[1536,256]{1,0:T(8,128)S(1)}, f32[24,128]{1,0:T(8,128)S(1)}) custom-call(bf16[512,128]{1,0:T(8,128)(2,1)S(1)} %bitcast.16, bf16[1536,1024]{1,0:T(8,128)(2,1)S(1)} %get-tuple-element.42.prob_ref, f32[1536,256]{1,0:T(8,128)} %conv.1.conv_hbm_ref, bf16[48,256]{1,0:T(8,128)(2,1)S(1)} %collective-permute-done.6.mate_ref, ...), custom_call_target="tpu_custom_call" | custom-call | bytes 4194304 | tf_op jit(solution)/shard_map/attend/pallas_call | solution.py:50
  62.2 2.8 %collective-permute-start.10 = (f32[24,128]{1,0:T(8,128)S(1)}, f32[24,128]{1,0:T(8,128)S(1)}, u32[]{:S(2)}, u32[]{:S(2)}) collective-permute-start(f32[24,128]{1,0:T(8,128)S(1)} %get-tuple-element.49.s0_ref), channel_id=1, source_target_pairs={{0,3},{1,2},{2,1},{3,0},{4,7},{5,6},{6,5},{7,4},{8,11},{9,10},{10,... | collective-permute-start | bytes 36872 | tf_op jit(solution)/shard_map/ppermute | solution.py:647
  65.1 0.8 %collective-permute-start.9 = (f32[24,128]{1,0:T(8,128)S(1)}, f32[24,128]{1,0:T(8,128)S(1)}, u32[]{:S(2)}, u32[]{:S(2)}) collective-permute-start(f32[24,128]{1,0:T(8,128)S(1)} %get-tuple-element.49.s0_ref), channel_id=1, source_target_pairs={{0,2},{1,3},{2,0},{3,1},{4,6},{5,7},{6,4},{7,5},{8,10},{9,11},{10,... | collective-permute-start | bytes 36872 | tf_op jit(solution)/shard_map/ppermute | solution.py:647
  65.9 0.5 collective-permute-start.8
  66.4 0.8 %collective-permute-done.10.s3_ref = f32[24,128]{1,0:T(8,128)S(1)} collective-permute-done((f32[24,128]{1,0:T(8,128)S(1)}, f32[24,128]{1,0:T(8,128)S(1)}, u32[]{:S(2)}, u32[]{:S(2)}) %collective-permute-start.10) | collective-permute-done | bytes 12320 | tf_op jit(solution)/shard_map/ppermute | solution.py:647
  67.2 3.1 %collective-permute-done.9.s2_ref = f32[24,128]{1,0:T(8,128)S(1)} collective-permute-done((f32[24,128]{1,0:T(8,128)S(1)}, f32[24,128]{1,0:T(8,128)S(1)}, u32[]{:S(2)}, u32[]{:S(2)}) %collective-permute-start.9) | collective-permute-done | bytes 12320 | tf_op jit(solution)/shard_map/ppermute | solution.py:647
  70.3 0.0 collective-permute-done.8.s1_ref
  70.3 0.0 copy-done.2
  70.3 0.0 copy-done.3
  70.3 1.2 %norm.1 = bf16[1536,256]{1,0:T(8,128)(2,1)} custom-call(f32[24,128]{1,0:T(8,128)S(1)} %get-tuple-element.49.s0_ref, f32[24,128]{1,0:T(8,128)S(1)} %collective-permute-done.8.s1_ref, f32[24,128]{1,0:T(8,128)S(1)} %collective-permute-done.9.s2_ref, f32[24,128]{1,0:T(8,128)S(1)} %collective-permute-done.10.s3_ref, f32[1536,256]{1,0:T(8,128)S(1)} %get-tuple-element.50.sum_ref, ...), custom_call_target="tpu_custom_call" | custom-call | bytes 4194304 | tf_op jit(solution)/shard_map/norm/pallas_call | solution.py:50
Async XLA Ops:
  0.0 14.5 %copy-start = (bf16[48,32,256]{2,1,0:T(8,128)(2,1)S(1)}, bf16[48,32,256]{2,1,0:T(8,128)(2,1)}, u32[]{:S(2)}) copy-start(bf16[48,32,256]{2,1,0:T(8,128)(2,1)} %v_hbm_ref.1) | copy-start | bytes 2359300
  2.3 21.5 %all-to-all-start = ((bf16[64,8,128]{2,1,0:T(8,128)(2,1)}), bf16[64,8,128]{2,1,0:T(8,128)(2,1)S(1)}, u32[]{:S(2)}, u32[]{:S(2)}) async-start(bf16[64,8,128]{2,1,0:T(8,128)(2,1)} %bitcast.25), calls=%async_computation | async-start | bytes 262144 | tf_op jit(solution)/shard_map/all_to_all | solution.py:544
  16.9 1.5 %collective-permute-start = (bf16[768,128]{1,0:T(8,128)(2,1)S(1)}, bf16[768,128]{1,0:T(8,128)(2,1)S(1)}, u32[]{:S(2)}, u32[]{:S(2)}) collective-permute-start(bf16[768,128]{1,0:T(8,128)(2,1)S(1)} %get-tuple-element.31), channel_id=1, source_target_pairs={{0,4},{4,0},{1,5},{5,1},{2,6},{6,2},{3,7},{7,3},{8,12},{12,8},{9,1... | collective-permute-start | bytes 589832 | tf_op jit(solution)/shard_map/ppermute | solution.py:548
  17.1 2.0 %collective-permute-start.1 = (bf16[768,128]{1,0:T(8,128)(2,1)S(1)}, bf16[768,128]{1,0:T(8,128)(2,1)S(1)}, u32[]{:S(2)}, u32[]{:S(2)}) collective-permute-start(bf16[768,128]{1,0:T(8,128)(2,1)S(1)} %get-tuple-element.32), channel_id=1, source_target_pairs={{0,4},{4,0},{1,5},{5,1},{2,6},{6,2},{3,7},{7,3},{8,12},{12,8},{9,1... | collective-permute-start | bytes 589832 | tf_op jit(solution)/shard_map/ppermute | solution.py:548
  17.5 1.6 %collective-permute-start.2 = (bf16[768,128]{1,0:T(8,128)(2,1)S(1)}, bf16[768,128]{1,0:T(8,128)(2,1)S(1)}, u32[]{:S(2)}, u32[]{:S(2)}) collective-permute-start(bf16[768,128]{1,0:T(8,128)(2,1)S(1)} %get-tuple-element.33), channel_id=1, source_target_pairs={{0,4},{4,0},{1,5},{5,1},{2,6},{6,2},{3,7},{7,3},{8,12},{12,8},{9,1... | collective-permute-start | bytes 589832 | tf_op jit(solution)/shard_map/ppermute | solution.py:548
  17.6 1.6 %collective-permute-start.3 = (bf16[768,128]{1,0:T(8,128)(2,1)S(1)}, bf16[768,128]{1,0:T(8,128)(2,1)S(1)}, u32[]{:S(2)}, u32[]{:S(2)}) collective-permute-start(bf16[768,128]{1,0:T(8,128)(2,1)S(1)} %get-tuple-element.34), channel_id=1, source_target_pairs={{0,4},{4,0},{1,5},{5,1},{2,6},{6,2},{3,7},{7,3},{8,12},{12,8},{9,1... | collective-permute-start | bytes 589832 | tf_op jit(solution)/shard_map/ppermute | solution.py:548
  18.0 9.3 %collective-permute-start.4 = (bf16[48,256]{1,0:T(8,128)(2,1)}, bf16[48,256]{1,0:T(8,128)(2,1)S(1)}, u32[]{:S(2)}, u32[]{:S(2)}) collective-permute-start(bf16[48,256]{1,0:T(8,128)(2,1)} %get-tuple-element.35), channel_id=1, source_target_pairs={{0,4},{4,0},{1,5},{5,1},{2,6},{6,2},{3,7},{7,3},{8,12},{12,8},{9,1... | collective-permute-start | bytes 73736 | tf_op jit(solution)/shard_map/ppermute | solution.py:548
  18.4 8.9 %collective-permute-start.5 = (bf16[48,256]{1,0:T(8,128)(2,1)}, bf16[48,256]{1,0:T(8,128)(2,1)S(1)}, u32[]{:S(2)}, u32[]{:S(2)}) collective-permute-start(bf16[48,256]{1,0:T(8,128)(2,1)} %get-tuple-element.36), channel_id=1, source_target_pairs={{4,8},{8,4},{12,16},{16,12},{20,24},{24,20},{28,32},{32,28},{36,40... | collective-permute-start | bytes 73736 | tf_op jit(solution)/shard_map/ppermute | solution.py:548
  27.3 28.4 %copy-start.1 = (f32[9,256]{1,0:T(8,128)S(1)}, f32[9,256]{1,0:T(8,128)}, u32[]{:S(2)}) copy-start(f32[9,256]{1,0:T(8,128)} %w_ref.3) | copy-start | bytes 27652
  27.3 16.8 %all-to-all-start.1 = ((bf16[32,16,128]{2,1,0:T(8,128)(2,1)}), bf16[32,16,128]{2,1,0:T(8,128)(2,1)S(1)}, u32[]{:S(2)}, u32[]{:S(2)}) async-start(bf16[32,16,128]{2,1,0:T(8,128)(2,1)} %bitcast.23), calls=%async_computation.1 | async-start | bytes 262144 | tf_op jit(solution)/shard_map/all_to_all | solution.py:544
  45.1 15.2 %all-to-all-start.2 = ((bf16[64,8,128]{2,1,0:T(8,128)(2,1)}), bf16[64,8,128]{2,1,0:T(8,128)(2,1)S(1)}, u32[]{:S(2)}, u32[]{:S(2)}) async-start(bf16[64,8,128]{2,1,0:T(8,128)(2,1)} %bitcast.24), calls=%async_computation.2 | async-start | bytes 262144 | tf_op jit(solution)/shard_map/all_to_all | solution.py:544
  50.8 8.1 %collective-permute-start.6 = (bf16[48,256]{1,0:T(8,128)(2,1)S(1)}, bf16[48,256]{1,0:T(8,128)(2,1)S(1)}, u32[]{:S(2)}, u32[]{:S(2)}) collective-permute-start(bf16[48,256]{1,0:T(8,128)(2,1)S(1)} %get-tuple-element.47), channel_id=1, source_target_pairs={{0,64},{64,0},{128,192},{192,128},{1,65},{65,1},{129,193},{193,129... | collective-permute-start | bytes 73736 | tf_op jit(solution)/shard_map/ppermute | solution.py:548
  51.4 7.5 %collective-permute-start.7 = (bf16[48,256]{1,0:T(8,128)(2,1)S(1)}, bf16[48,256]{1,0:T(8,128)(2,1)S(1)}, u32[]{:S(2)}, u32[]{:S(2)}) collective-permute-start(bf16[48,256]{1,0:T(8,128)(2,1)S(1)} %get-tuple-element.48), channel_id=1, source_target_pairs={{64,128},{128,64},{65,129},{129,65},{66,130},{130,66},{67,131},{13... | collective-permute-start | bytes 73736 | tf_op jit(solution)/shard_map/ppermute | solution.py:548
  60.2 10.1 %copy-start.2 = (f32[256]{0:T(256)S(1)}, f32[256]{0:T(256)}, u32[]{:S(2)}) copy-start(f32[256]{0:T(256)} %param.12) | copy-start | bytes 3076
  60.2 10.1 %copy-start.3 = (f32[256]{0:T(256)S(1)}, f32[256]{0:T(256)}, u32[]{:S(2)}) copy-start(f32[256]{0:T(256)} %param.13) | copy-start | bytes 3076
  62.2 5.0 %collective-permute-start.10 = (f32[24,128]{1,0:T(8,128)S(1)}, f32[24,128]{1,0:T(8,128)S(1)}, u32[]{:S(2)}, u32[]{:S(2)}) collective-permute-start(f32[24,128]{1,0:T(8,128)S(1)} %get-tuple-element.49.s0_ref), channel_id=1, source_target_pairs={{0,3},{1,2},{2,1},{3,0},{4,7},{5,6},{6,5},{7,4},{8,11},{9,10},{10,... | collective-permute-start | bytes 36872 | tf_op jit(solution)/shard_map/ppermute | solution.py:647
  65.1 5.2 %collective-permute-start.9 = (f32[24,128]{1,0:T(8,128)S(1)}, f32[24,128]{1,0:T(8,128)S(1)}, u32[]{:S(2)}, u32[]{:S(2)}) collective-permute-start(f32[24,128]{1,0:T(8,128)S(1)} %get-tuple-element.49.s0_ref), channel_id=1, source_target_pairs={{0,2},{1,3},{2,0},{3,1},{4,6},{5,7},{6,4},{7,5},{8,10},{9,11},{10,... | collective-permute-start | bytes 36872 | tf_op jit(solution)/shard_map/ppermute | solution.py:647
  65.9 4.4 %collective-permute-start.8 = (f32[24,128]{1,0:T(8,128)S(1)}, f32[24,128]{1,0:T(8,128)S(1)}, u32[]{:S(2)}, u32[]{:S(2)}) collective-permute-start(f32[24,128]{1,0:T(8,128)S(1)} %get-tuple-element.49.s0_ref), channel_id=1, source_target_pairs={{0,1},{1,0},{2,3},{3,2},{4,5},{5,4},{6,7},{7,6},{8,9},{9,8},{10,11... | collective-permute-start | bytes 36872 | tf_op jit(solution)/shard_map/ppermute | solution.py:647

commit v14 on v13

--- a/solution.py
+++ b/solution.py
@@ -185,44 +185,45 @@
 def key_kernel(
     tab_hbm_ref,
     v_ref,
+    flat_ref,
     k_ref,
     tk_ref,
     *refs,
 ):
     sends, (near_ref, far_ref, tab_ref, held_ref, sems) = refs[:PIECES], refs[PIECES:]
     step = N // AGR
-    table = pltpu.make_async_copy(tab_hbm_ref, tab_ref, sems.at[AGR])
+    size = 2 * N // PIECES
+    half = PIECES // 2
+    offset = pl.multiple_of((1 - lax.axis_index("core")) * 128, 128)
+    table = pltpu.make_async_copy(tab_hbm_ref, tab_ref, sems.at[0])
     table.start()
+    whole = pltpu.make_async_copy(v_ref, held_ref, sems.at[1])
+    whole.start()
     copies = []
-    for cell in range(AGR):
-        part = pl.ds(cell * step, step)
-        copies.append(
-            pltpu.make_async_copy(k_ref.at[part, :], held_ref.at[part, :], sems.at[cell])
-        )
-        copies[cell].start()
-    first, last = v_ref[:, 0, :], v_ref[:, TC - 1, :]
+    for i in range(half):
+        source = flat_ref.at[pl.ds(i * size, size), pl.ds(offset, 128)]
+        copies.append(pltpu.make_async_copy(source, sends[half + i], sems.at[2 + i]))
+        copies[i].start()
     even = even_core()
-    near_ref[...] = jnp.where(even, last, first)
-    far_ref[...] = jnp.where(even, first, last)
-    other = jnp.where(even, v_ref[:, :, 128:], v_ref[:, :, :128])
-    other = other.reshape(N, 128)
-    size = 2 * N // PIECES
-    for i in range(PIECES // 2):
-        sends[PIECES // 2 + i][...] = other[i * size : (i + 1) * size]
     matrix = turn_matrix()
     table.wait()
     tables = split_tables(tab_ref[0], tab_ref[1])
     for cell in range(AGR):
         part = pl.ds(cell * step, step)
         cosine, sine = cell_tables(tables, cell * (TR // AGR), TR // AGR)
-        copies[cell].wait()
-        keys = turned(held_ref[part, :], matrix, cosine, sine)
+        keys = turned(k_ref[part, :], matrix, cosine, sine)
         tk_ref[part, :] = jnp.where(even, keys[:, :128], keys[:, 128:])
         keys = jnp.where(even, keys[:, 128:], keys[:, :128])
         span = math.gcd(size, step)
         for at in range(0, step, span):
             to = cell * step + at
             sends[to // size][pl.ds(to % size, span), :] = keys[at : at + span]
+    whole.wait()
+    first, last = held_ref[:, 0, :], held_ref[:, TC - 1, :]
+    near_ref[...] = jnp.where(even, last, first)
+    far_ref[...] = jnp.where(even, first, last)
+    for copy in copies:
+        copy.wait()
 
 
 def agent_pairs(agents_ref, wide_ref, scale):
@@ -580,12 +581,16 @@
         key_kernel,
         (near((N, 128), bf16),)
         + (near((2 * N // PIECES, 128), bf16),) * PIECES
-        + (far((TR, CH), bf16),) * 2,
-        "h h",
-        scratch=[held_table, pltpu.VMEM((N, CH), bf16), pltpu.SemaphoreType.DMA((AGR + 1,))],
+        + (near((TR, CH), bf16),) * 2,
+        "hhh ",
+        scratch=[
+            held_table,
+            pltpu.VMEM((TR, TC, CH), bf16),
+            pltpu.SemaphoreType.DMA((2 + PIECES // 2,)),
+        ],
         nbytes=4 * mb,
         name="turn_keys",
-    )(table, values, k)
+    )(table, values, v, k)
     got = [swap(send, "core", chain("core", 0)) for send in sends]
     inner = swap(inner, "core", chain("core", 0))
     outer = swap(outer, ("z", "core"), chain(("z", "core"), 1))

time: 72.7 us -> 71.6 us (0.985)
  starting transfers between devices: 36.4 us -> 35.4 us
  Pallas kernels: 19.7 us -> 18.9 us
    all_to_all x3, starting transfers between devices: 25.5 us -> 24.4 us  [spread(): return lax.all_to_all(slot, axes, 0, 0).reshape(x.shape)]
    pallas_call x8, Pallas kernels: 19.7 us -> 18.9 us  [run(): fn(*[pltpu.with_memory_space_constraint(x, spaces[c]) if c in spaces else...]
    all_to_all x3, waiting for transfers between devices: 10.9 us -> 11.7 us  [spread(): return lax.all_to_all(slot, axes, 0, 0).reshape(x.shape)]
  transfers between devices with their start and end apart: 14 -> 14, of which waited for: 7 -> 7; matrix products, arithmetic and copies ran while one was open for 0% -> 0% of each run, Pallas kernels for 18% -> 17%
where the time goes in v14:
time: 71.6 us; the launch traced here: 70.6 us
  starting transfers between devices  35.4 us (49%)
  Pallas kernels  18.9 us (26%)
  waiting for transfers between devices  16 us (22%)
    all_to_all x3, starting transfers between devices, spread(): return lax.all_to_all(slot, axes, 0, 0).reshape(x.shape)  24.4 us
    pallas_call x8, Pallas kernels, run(): fn(*[pltpu.with_memory_space_constraint(x, spaces[c]) if c in spaces else...  18.9 us
    all_to_all x3, waiting for transfers between devices, spread(): return lax.all_to_all(slot, axes, 0, 0).reshape(x.shape)  11.7 us
    ppermute x8, starting transfers between devices, swap(): lax.ppermute(x, axis, [p for i, j in pairs for p in ((i, j), (j, i))])  6.74 us
    ppermute x3, starting transfers between devices, shards(): lax.ppermute(stats, 'head', [(i, i ^ d) for i in range(heads)])  4.18 us
    ppermute x3, waiting for transfers between devices, shards(): lax.ppermute(stats, 'head', [(i, i ^ d) for i in range(heads)])  3.86 us
  transfers between devices with their start and end apart: 14, of which 7 were waited for; matrix products, arithmetic and copies ran while one was open for 0% of the time, Pallas kernels for 17%

profile of v14, /device:TPU:8, one launch (start us, length us, event | category | flops | bytes accessed | tf_op | source)
XLA Modules:
  0.0 70.6 jit_solution(9137486494952418270)
XLA Ops:
  0.0 0.0 copy-start.1
  0.0 0.0 copy-start
  0.0 2.4 %pool_queries.1 = (bf16[512,128]{1,0:T(8,128)(2,1)}, f32[2,80,128]{2,1,0:T(8,128)}) custom-call(s32[2,32,48]{2,1,0:T(8,128)} %bitcast.27, bf16[1536,256]{1,0:T(8,128)(2,1)} %bitcast.22), custom_call_target="tpu_custom_call" | custom-call | bytes 8388608 | tf_op jit(solution)/shard_map/pool_queries/pallas_call | solution.py:50
  2.4 12.1 %all-to-all-start = ((bf16[64,8,128]{2,1,0:T(8,128)(2,1)}), bf16[64,8,128]{2,1,0:T(8,128)(2,1)S(1)}, u32[]{:S(2)}, u32[]{:S(2)}) async-start(bf16[64,8,128]{2,1,0:T(8,128)(2,1)} %bitcast.26), calls=%async_computation | async-start | bytes 262144 | tf_op jit(solution)/shard_map/all_to_all | solution.py:545
  14.5 0.0 copy-done.1
  14.5 1.6 %turn_keys.1 = (bf16[1536,128]{1,0:T(8,128)(2,1)S(1)}, bf16[768,128]{1,0:T(8,128)(2,1)S(1)}, bf16[768,128]{1,0:T(8,128)(2,1)S(1)}, bf16[768,128]{1,0:T(8,128)(2,...) custom-call(f32[2,80,128]{2,1,0:T(8,128)} %get-tuple-element.29.tab_hbm_ref, ...), custom_call_target="tpu_custom_call" | custom-call | bytes 4194304 | tf_op jit(solution)/shard_map/turn_keys/pallas_call | solution.py:50
  16.1 0.2 collective-permute-start
  16.3 0.4 collective-permute-start.1
  16.7 0.1 collective-permute-start.2
  16.9 0.4 collective-permute-start.3
  17.2 0.1 collective-permute-start.4
  17.4 0.3 collective-permute-done.refs_0_
  17.6 0.7 collective-permute-start.5
  18.3 0.0 collective-permute-done.1.refs_1_
  18.3 0.0 collective-permute-done.2.refs_2_
  18.3 0.2 collective-permute-done.3.refs_3_
  18.5 5.4 %all-to-all-done = bf16[64,8,128]{2,1,0:T(8,128)(2,1)S(1)} async-done(((bf16[64,8,128]{2,1,0:T(8,128)(2,1)}), bf16[64,8,128]{2,1,0:T(8,128)(2,1)S(1)}, u32[]{:S(2)}, u32[]{:S(2)}) %all-to-all-start) | async-done | bytes 131104 | tf_op jit(solution)/shard_map/all_to_all | solution.py:545
  23.9 0.0 copy-done
  23.9 3.4 %partials.1 = bf16[512,128]{1,0:T(8,128)(2,1)} custom-call(bf16[512,128]{1,0:T(8,128)(2,1)S(1)} %bitcast.15, bf16[1536,128]{1,0:T(8,128)(2,1)S(1)} %get-tuple-element.30.tk_ref, bf16[1536,256]{1,0:T(8,128)(2,1)S(1)} %bitcast.14, bf16[768,128]{1,0:T(8,128)(2,1)S(1)} %collective-permute-done.refs_0_, bf16[768,128]{1,0:T(8,128)(2,1)S(1)} %collective-permute-done.1.refs_1_, ...), custom_call_target="tpu_custom_call" | custom-call | bytes 10485760 | tf_op jit(solution)/shard_map/partials/pallas_call | solution.py:50
  27.3 0.0 copy-start.2
  27.3 0.0 collective-permute-done.4.near_ref
  27.3 0.0 collective-permute-done.5.far_ref
  27.3 6.6 %all-to-all-start.1 = ((bf16[32,16,128]{2,1,0:T(8,128)(2,1)}), bf16[32,16,128]{2,1,0:T(8,128)(2,1)S(1)}, u32[]{:S(2)}, u32[]{:S(2)}) async-start(bf16[32,16,128]{2,1,0:T(8,128)(2,1)} %bitcast.24), calls=%async_computation.1 | async-start | bytes 262144 | tf_op jit(solution)/shard_map/all_to_all | solution.py:545
  33.9 4.2 %probabilities.1 = (bf16[1536,1024]{1,0:T(8,128)(2,1)S(1)}, bf16[48,256]{1,0:T(8,128)(2,1)S(1)}, bf16[48,256]{1,0:T(8,128)(2,1)S(1)}) custom-call(bf16[512,128]{1,0:T(8,128)(2,1)S(1)} %bitcast.16, f32[2,80,128]{2,1,0:T(8,128)} %get-tuple-element.29.tab_hbm_ref, bf16[1536,256]{1,0:T(8,128)(2,1)} %bitcast.23, bf16[48,32,256]{2,1,0:T(8,128)(2,1)} %v_hbm_ref.1, ...), custom_call_target="tpu_custom_call" | custom-call | bytes 20971520 | tf_op jit(solution)/shard_map/probabilities/pallas_call | solution.py:50
  38.1 4.9 %all-to-all-done.1 = bf16[32,16,128]{2,1,0:T(8,128)(2,1)S(1)} async-done(((bf16[32,16,128]{2,1,0:T(8,128)(2,1)}), bf16[32,16,128]{2,1,0:T(8,128)(2,1)S(1)}, u32[]{:S(2)}, u32[]{:S(2)}) %all-to-all-start.1) | async-done | bytes 131104 | tf_op jit(solution)/shard_map/all_to_all | solution.py:545
  43.0 1.0 %merge.1 = bf16[512,128]{1,0:T(8,128)(2,1)} custom-call(bf16[512,128]{1,0:T(8,128)(2,1)S(1)} %bitcast.19), custom_call_target="tpu_custom_call" | custom-call | bytes 2097152 | tf_op jit(solution)/shard_map/merge/pallas_call | solution.py:50
  44.0 5.7 %all-to-all-start.2 = ((bf16[64,8,128]{2,1,0:T(8,128)(2,1)}), bf16[64,8,128]{2,1,0:T(8,128)(2,1)S(1)}, u32[]{:S(2)}, u32[]{:S(2)}) async-start(bf16[64,8,128]{2,1,0:T(8,128)(2,1)} %bitcast.25), calls=%async_computation.2 | async-start | bytes 262144 | tf_op jit(solution)/shard_map/all_to_all | solution.py:545
  49.7 0.6 collective-permute-start.6
  50.3 4.3 %collective-permute-start.7 = (bf16[48,256]{1,0:T(8,128)(2,1)S(1)}, bf16[48,256]{1,0:T(8,128)(2,1)S(1)}, u32[]{:S(2)}, u32[]{:S(2)}) collective-permute-start(bf16[48,256]{1,0:T(8,128)(2,1)S(1)} %get-tuple-element.48), channel_id=1, source_target_pairs={{64,128},{128,64},{65,129},{129,65},{66,130},{130,66},{67,131},{13... | collective-permute-start | bytes 73736 | tf_op jit(solution)/shard_map/ppermute | solution.py:549
  54.6 0.0 copy-done.2
  54.6 3.2 %conv.1.conv_hbm_ref = f32[1536,256]{1,0:T(8,128)} custom-call(bf16[48,32,256]{2,1,0:T(8,128)(2,1)} %v_hbm_ref.1, bf16[48,256]{1,0:T(8,128)(2,1)S(1)} %collective-permute-done.4.near_ref, bf16[48,256]{1,0:T(8,128)(2,1)S(1)} %collective-permute-done.5.far_ref, f32[9,256]{1,0:T(8,128)S(1)} %copy-done.2), custom_call_target="tpu_custom_call" | custom-call | bytes 8388608 | tf_op jit(solution)/shard_map/conv/pallas_call | solution.py:50
  57.8 0.0 collective-permute-done.6.mate_ref
  57.8 0.0 collective-permute-done.7.rest_ref
  57.8 1.3 %all-to-all-done.2 = bf16[64,8,128]{2,1,0:T(8,128)(2,1)S(1)} async-done(((bf16[64,8,128]{2,1,0:T(8,128)(2,1)}), bf16[64,8,128]{2,1,0:T(8,128)(2,1)S(1)}, u32[]{:S(2)}, u32[]{:S(2)}) %all-to-all-start.2) | async-done | bytes 131104 | tf_op jit(solution)/shard_map/all_to_all | solution.py:545
  59.2 0.0 copy-start.3
  59.2 0.0 copy-start.4
  59.2 2.0 %attend.1 = (f32[1536,256]{1,0:T(8,128)S(1)}, f32[24,128]{1,0:T(8,128)S(1)}) custom-call(bf16[512,128]{1,0:T(8,128)(2,1)S(1)} %bitcast.18, bf16[1536,1024]{1,0:T(8,128)(2,1)S(1)} %get-tuple-element.42.prob_ref, f32[1536,256]{1,0:T(8,128)} %conv.1.conv_hbm_ref, bf16[48,256]{1,0:T(8,128)(2,1)S(1)} %collective-permute-done.6.mate_ref, ...), custom_call_target="tpu_custom_call" | custom-call | bytes 4194304 | tf_op jit(solution)/shard_map/attend/pallas_call | solution.py:50
  61.2 2.8 %collective-permute-start.10 = (f32[24,128]{1,0:T(8,128)S(1)}, f32[24,128]{1,0:T(8,128)S(1)}, u32[]{:S(2)}, u32[]{:S(2)}) collective-permute-start(f32[24,128]{1,0:T(8,128)S(1)} %get-tuple-element.49.s0_ref), channel_id=1, source_target_pairs={{0,3},{1,2},{2,1},{3,0},{4,7},{5,6},{6,5},{7,4},{8,11},{9,10},{10,... | collective-permute-start | bytes 36872 | tf_op jit(solution)/shard_map/ppermute | solution.py:652
  64.0 0.8 %collective-permute-start.9 = (f32[24,128]{1,0:T(8,128)S(1)}, f32[24,128]{1,0:T(8,128)S(1)}, u32[]{:S(2)}, u32[]{:S(2)}) collective-permute-start(f32[24,128]{1,0:T(8,128)S(1)} %get-tuple-element.49.s0_ref), channel_id=1, source_target_pairs={{0,2},{1,3},{2,0},{3,1},{4,6},{5,7},{6,4},{7,5},{8,10},{9,11},{10,... | collective-permute-start | bytes 36872 | tf_op jit(solution)/shard_map/ppermute | solution.py:652
  64.8 0.5 collective-permute-start.8
  65.4 0.8 %collective-permute-done.10.s3_ref = f32[24,128]{1,0:T(8,128)S(1)} collective-permute-done((f32[24,128]{1,0:T(8,128)S(1)}, f32[24,128]{1,0:T(8,128)S(1)}, u32[]{:S(2)}, u32[]{:S(2)}) %collective-permute-start.10) | collective-permute-done | bytes 12320 | tf_op jit(solution)/shard_map/ppermute | solution.py:652
  66.2 3.1 %collective-permute-done.9.s2_ref = f32[24,128]{1,0:T(8,128)S(1)} collective-permute-done((f32[24,128]{1,0:T(8,128)S(1)}, f32[24,128]{1,0:T(8,128)S(1)}, u32[]{:S(2)}, u32[]{:S(2)}) %collective-permute-start.9) | collective-permute-done | bytes 12320 | tf_op jit(solution)/shard_map/ppermute | solution.py:652
  69.2 0.0 collective-permute-done.8.s1_ref
  69.2 0.0 copy-done.3
  69.2 0.0 copy-done.4
  69.2 1.2 %norm.1 = bf16[1536,256]{1,0:T(8,128)(2,1)} custom-call(f32[24,128]{1,0:T(8,128)S(1)} %get-tuple-element.49.s0_ref, f32[24,128]{1,0:T(8,128)S(1)} %collective-permute-done.8.s1_ref, f32[24,128]{1,0:T(8,128)S(1)} %collective-permute-done.9.s2_ref, f32[24,128]{1,0:T(8,128)S(1)} %collective-permute-done.10.s3_ref, f32[1536,256]{1,0:T(8,128)S(1)} %get-tuple-element.50.sum_ref, ...), custom_call_target="tpu_custom_call" | custom-call | bytes 4194304 | tf_op jit(solution)/shard_map/norm/pallas_call | solution.py:50
Async XLA Ops:
  0.0 14.5 %copy-start.1 = (bf16[48,32,256]{2,1,0:T(8,128)(2,1)S(1)}, bf16[48,32,256]{2,1,0:T(8,128)(2,1)}, u32[]{:S(2)}) copy-start(bf16[48,32,256]{2,1,0:T(8,128)(2,1)} %param.8) | copy-start | bytes 2359300
  0.0 23.9 %copy-start = (bf16[48,32,256]{2,1,0:T(8,128)(2,1)S(1)}, bf16[48,32,256]{2,1,0:T(8,128)(2,1)}, u32[]{:S(2)}) copy-start(bf16[48,32,256]{2,1,0:T(8,128)(2,1)} %v_hbm_ref.1) | copy-start | bytes 2359300
  2.4 21.5 %all-to-all-start = ((bf16[64,8,128]{2,1,0:T(8,128)(2,1)}), bf16[64,8,128]{2,1,0:T(8,128)(2,1)S(1)}, u32[]{:S(2)}, u32[]{:S(2)}) async-start(bf16[64,8,128]{2,1,0:T(8,128)(2,1)} %bitcast.26), calls=%async_computation | async-start | bytes 262144 | tf_op jit(solution)/shard_map/all_to_all | solution.py:545
  16.1 1.5 %collective-permute-start = (bf16[768,128]{1,0:T(8,128)(2,1)S(1)}, bf16[768,128]{1,0:T(8,128)(2,1)S(1)}, u32[]{:S(2)}, u32[]{:S(2)}) collective-permute-start(bf16[768,128]{1,0:T(8,128)(2,1)S(1)} %get-tuple-element.31), channel_id=1, source_target_pairs={{0,4},{4,0},{1,5},{5,1},{2,6},{6,2},{3,7},{7,3},{8,12},{12,8},{9,1... | collective-permute-start | bytes 589832 | tf_op jit(solution)/shard_map/ppermute | solution.py:549
  16.3 2.0 %collective-permute-start.1 = (bf16[768,128]{1,0:T(8,128)(2,1)S(1)}, bf16[768,128]{1,0:T(8,128)(2,1)S(1)}, u32[]{:S(2)}, u32[]{:S(2)}) collective-permute-start(bf16[768,128]{1,0:T(8,128)(2,1)S(1)} %get-tuple-element.32), channel_id=1, source_target_pairs={{0,4},{4,0},{1,5},{5,1},{2,6},{6,2},{3,7},{7,3},{8,12},{12,8},{9,1... | collective-permute-start | bytes 589832 | tf_op jit(solution)/shard_map/ppermute | solution.py:549
  16.7 1.6 %collective-permute-start.2 = (bf16[768,128]{1,0:T(8,128)(2,1)S(1)}, bf16[768,128]{1,0:T(8,128)(2,1)S(1)}, u32[]{:S(2)}, u32[]{:S(2)}) collective-permute-start(bf16[768,128]{1,0:T(8,128)(2,1)S(1)} %get-tuple-element.33), channel_id=1, source_target_pairs={{0,4},{4,0},{1,5},{5,1},{2,6},{6,2},{3,7},{7,3},{8,12},{12,8},{9,1... | collective-permute-start | bytes 589832 | tf_op jit(solution)/shard_map/ppermute | solution.py:549
  16.9 1.6 %collective-permute-start.3 = (bf16[768,128]{1,0:T(8,128)(2,1)S(1)}, bf16[768,128]{1,0:T(8,128)(2,1)S(1)}, u32[]{:S(2)}, u32[]{:S(2)}) collective-permute-start(bf16[768,128]{1,0:T(8,128)(2,1)S(1)} %get-tuple-element.34), channel_id=1, source_target_pairs={{0,4},{4,0},{1,5},{5,1},{2,6},{6,2},{3,7},{7,3},{8,12},{12,8},{9,1... | collective-permute-start | bytes 589832 | tf_op jit(solution)/shard_map/ppermute | solution.py:549
  17.2 10.1 %collective-permute-start.4 = (bf16[48,256]{1,0:T(8,128)(2,1)S(1)}, bf16[48,256]{1,0:T(8,128)(2,1)S(1)}, u32[]{:S(2)}, u32[]{:S(2)}) collective-permute-start(bf16[48,256]{1,0:T(8,128)(2,1)S(1)} %get-tuple-element.35), channel_id=1, source_target_pairs={{0,4},{4,0},{1,5},{5,1},{2,6},{6,2},{3,7},{7,3},{8,12},{12,8},{9,1... | collective-permute-start | bytes 73736 | tf_op jit(solution)/shard_map/ppermute | solution.py:549
  17.6 9.7 %collective-permute-start.5 = (bf16[48,256]{1,0:T(8,128)(2,1)S(1)}, bf16[48,256]{1,0:T(8,128)(2,1)S(1)}, u32[]{:S(2)}, u32[]{:S(2)}) collective-permute-start(bf16[48,256]{1,0:T(8,128)(2,1)S(1)} %get-tuple-element.36), channel_id=1, source_target_pairs={{4,8},{8,4},{12,16},{16,12},{20,24},{24,20},{28,32},{32,28},{36,40... | collective-permute-start | bytes 73736 | tf_op jit(solution)/shard_map/ppermute | solution.py:549
  27.3 27.3 %copy-start.2 = (f32[9,256]{1,0:T(8,128)S(1)}, f32[9,256]{1,0:T(8,128)}, u32[]{:S(2)}) copy-start(f32[9,256]{1,0:T(8,128)} %w_ref.3) | copy-start | bytes 27652
  27.3 15.7 %all-to-all-start.1 = ((bf16[32,16,128]{2,1,0:T(8,128)(2,1)}), bf16[32,16,128]{2,1,0:T(8,128)(2,1)S(1)}, u32[]{:S(2)}, u32[]{:S(2)}) async-start(bf16[32,16,128]{2,1,0:T(8,128)(2,1)} %bitcast.24), calls=%async_computation.1 | async-start | bytes 262144 | tf_op jit(solution)/shard_map/all_to_all | solution.py:545
  44.0 15.2 %all-to-all-start.2 = ((bf16[64,8,128]{2,1,0:T(8,128)(2,1)}), bf16[64,8,128]{2,1,0:T(8,128)(2,1)S(1)}, u32[]{:S(2)}, u32[]{:S(2)}) async-start(bf16[64,8,128]{2,1,0:T(8,128)(2,1)} %bitcast.25), calls=%async_computation.2 | async-start | bytes 262144 | tf_op jit(solution)/shard_map/all_to_all | solution.py:545
  49.7 8.1 %collective-permute-start.6 = (bf16[48,256]{1,0:T(8,128)(2,1)S(1)}, bf16[48,256]{1,0:T(8,128)(2,1)S(1)}, u32[]{:S(2)}, u32[]{:S(2)}) collective-permute-start(bf16[48,256]{1,0:T(8,128)(2,1)S(1)} %get-tuple-element.47), channel_id=1, source_target_pairs={{0,64},{64,0},{128,192},{192,128},{1,65},{65,1},{129,193},{193,129... | collective-permute-start | bytes 73736 | tf_op jit(solution)/shard_map/ppermute | solution.py:549
  50.3 7.5 %collective-permute-start.7 = (bf16[48,256]{1,0:T(8,128)(2,1)S(1)}, bf16[48,256]{1,0:T(8,128)(2,1)S(1)}, u32[]{:S(2)}, u32[]{:S(2)}) collective-permute-start(bf16[48,256]{1,0:T(8,128)(2,1)S(1)} %get-tuple-element.48), channel_id=1, source_target_pairs={{64,128},{128,64},{65,129},{129,65},{66,130},{130,66},{67,131},{13... | collective-permute-start | bytes 73736 | tf_op jit(solution)/shard_map/ppermute | solution.py:549
  59.2 10.1 %copy-start.3 = (f32[256]{0:T(256)S(1)}, f32[256]{0:T(256)}, u32[]{:S(2)}) copy-start(f32[256]{0:T(256)} %param.12) | copy-start | bytes 3076
  59.2 10.1 %copy-start.4 = (f32[256]{0:T(256)S(1)}, f32[256]{0:T(256)}, u32[]{:S(2)}) copy-start(f32[256]{0:T(256)} %param.13) | copy-start | bytes 3076
  61.2 5.0 %collective-permute-start.10 = (f32[24,128]{1,0:T(8,128)S(1)}, f32[24,128]{1,0:T(8,128)S(1)}, u32[]{:S(2)}, u32[]{:S(2)}) collective-permute-start(f32[24,128]{1,0:T(8,128)S(1)} %get-tuple-element.49.s0_ref), channel_id=1, source_target_pairs={{0,3},{1,2},{2,1},{3,0},{4,7},{5,6},{6,5},{7,4},{8,11},{9,10},{10,... | collective-permute-start | bytes 36872 | tf_op jit(solution)/shard_map/ppermute | solution.py:652
  64.0 5.2 %collective-permute-start.9 = (f32[24,128]{1,0:T(8,128)S(1)}, f32[24,128]{1,0:T(8,128)S(1)}, u32[]{:S(2)}, u32[]{:S(2)}) collective-permute-start(f32[24,128]{1,0:T(8,128)S(1)} %get-tuple-element.49.s0_ref), channel_id=1, source_target_pairs={{0,2},{1,3},{2,0},{3,1},{4,6},{5,7},{6,4},{7,5},{8,10},{9,11},{10,... | collective-permute-start | bytes 36872 | tf_op jit(solution)/shard_map/ppermute | solution.py:652
  64.8 4.4 %collective-permute-start.8 = (f32[24,128]{1,0:T(8,128)S(1)}, f32[24,128]{1,0:T(8,128)S(1)}, u32[]{:S(2)}, u32[]{:S(2)}) collective-permute-start(f32[24,128]{1,0:T(8,128)S(1)} %get-tuple-element.49.s0_ref), channel_id=1, source_target_pairs={{0,1},{1,0},{2,3},{3,2},{4,5},{5,4},{6,7},{7,6},{8,9},{9,8},{10,11... | collective-permute-start | bytes 36872 | tf_op jit(solution)/shard_map/ppermute | solution.py:652

commit v15 on v14

--- a/solution.py
+++ b/solution.py
@@ -256,9 +256,9 @@
             return tk_ref[pl.ds(at, chunk), :]
         return v_ref[pl.ds(at, chunk), pl.ds(offset, 128)]
 
+    peaks = []
     for parity in range(2):
-        own = mine
-        own = jnp.where(half_mask(own.shape, parity), own, jnp.zeros_like(own))
+        own = jnp.where(half_mask(mine.shape, parity), mine, jnp.zeros_like(mine))
         peak = None
         for c in range(2 * N // chunk):
             scores = lax.dot_general(
@@ -267,14 +267,16 @@
                 (((1,), (1,)), ((), ())),
                 preferred_element_type=f32,
             )
-            score_ref[:, pl.ds(c * chunk, chunk)] = scores
+            score_ref[parity, :, pl.ds(c * chunk, chunk)] = scores
             for s in range(chunk // 128):
                 piece = scores[:, s * 128 : (s + 1) * 128]
                 peak = piece if peak is None else jnp.maximum(peak, piece)
-        peak = jnp.max(peak, 1, keepdims=True)
+        peaks.append(jnp.max(peak, 1, keepdims=True))
+    for parity in range(2):
+        peak = peaks[parity]
         acc = jnp.zeros((AGENTS, 128), f32)
         for c in range(2 * N // chunk):
-            weights = jnp.exp(score_ref[:, pl.ds(c * chunk, chunk)] - peak).astype(bf16)
+            weights = jnp.exp(score_ref[parity, :, pl.ds(c * chunk, chunk)] - peak).astype(bf16)
             block = part(c, 1)
             block = jnp.where(half_mask(block.shape, parity), block, jnp.ones_like(block))
             acc = acc + jnp.dot(weights, block, preferred_element_type=f32)
@@ -598,7 +600,7 @@
         partial_kernel,
         far((2 * AGENTS, 128), bf16),
         " v " + " " * PIECES,
-        scratch=[pltpu.VMEM((AGENTS, 2 * N), f32), wide],
+        scratch=[pltpu.VMEM((2, AGENTS, 2 * N), f32), wide],
         nbytes=10 * mb,
         name="partials",
     )(agents, tk, v, *got)

time: 71.6 us -> 71.7 us (level)
  no operation moved by 1% of the time
where the time goes in v15:
time: 71.7 us; the launch traced here: 70.7 us
  starting transfers between devices  35.6 us (50%)
  Pallas kernels  18.7 us (26%)
  waiting for transfers between devices  16 us (22%)
    all_to_all x3, starting transfers between devices, spread(): return lax.all_to_all(slot, axes, 0, 0).reshape(x.shape)  24.7 us
    pallas_call x8, Pallas kernels, run(): fn(*[pltpu.with_memory_space_constraint(x, spaces[c]) if c in spaces else...  18.7 us
    all_to_all x3, waiting for transfers between devices, spread(): return lax.all_to_all(slot, axes, 0, 0).reshape(x.shape)  11.7 us
    ppermute x8, starting transfers between devices, swap(): lax.ppermute(x, axis, [p for i, j in pairs for p in ((i, j), (j, i))])  6.74 us
    ppermute x3, starting transfers between devices, shards(): lax.ppermute(stats, 'head', [(i, i ^ d) for i in range(heads)])  4.18 us
    ppermute x3, waiting for transfers between devices, shards(): lax.ppermute(stats, 'head', [(i, i ^ d) for i in range(heads)])  3.87 us
  transfers between devices with their start and end apart: 14, of which 7 were waited for; matrix products, arithmetic and copies ran while one was open for 0% of the time, Pallas kernels for 17%

profile of v15, /device:TPU:8, one launch (start us, length us, event | category | flops | bytes accessed | tf_op | source)
XLA Modules:
  0.0 70.7 jit_solution(16495948657031422083)
XLA Ops:
  0.0 0.0 copy-start.1
  0.0 0.0 copy-start
  0.0 2.4 %pool_queries.1 = (bf16[512,128]{1,0:T(8,128)(2,1)}, f32[2,80,128]{2,1,0:T(8,128)}) custom-call(s32[2,32,48]{2,1,0:T(8,128)} %bitcast.27, bf16[1536,256]{1,0:T(8,128)(2,1)} %bitcast.22), custom_call_target="tpu_custom_call" | custom-call | bytes 8388608 | tf_op jit(solution)/shard_map/pool_queries/pallas_call | solution.py:50
  2.4 12.1 %all-to-all-start = ((bf16[64,8,128]{2,1,0:T(8,128)(2,1)}), bf16[64,8,128]{2,1,0:T(8,128)(2,1)S(1)}, u32[]{:S(2)}, u32[]{:S(2)}) async-start(bf16[64,8,128]{2,1,0:T(8,128)(2,1)} %bitcast.26), calls=%async_computation | async-start | bytes 262144 | tf_op jit(solution)/shard_map/all_to_all | solution.py:547
  14.5 0.0 copy-done.1
  14.5 1.6 %turn_keys.1 = (bf16[1536,128]{1,0:T(8,128)(2,1)S(1)}, bf16[768,128]{1,0:T(8,128)(2,1)S(1)}, bf16[768,128]{1,0:T(8,128)(2,1)S(1)}, bf16[768,128]{1,0:T(8,128)(2,...) custom-call(f32[2,80,128]{2,1,0:T(8,128)} %get-tuple-element.29.tab_hbm_ref, ...), custom_call_target="tpu_custom_call" | custom-call | bytes 4194304 | tf_op jit(solution)/shard_map/turn_keys/pallas_call | solution.py:50
  16.1 0.2 collective-permute-start
  16.3 0.4 collective-permute-start.1
  16.7 0.1 collective-permute-start.2
  16.9 0.4 collective-permute-start.3
  17.2 0.1 collective-permute-start.4
  17.4 0.3 collective-permute-done.refs_0_
  17.6 0.7 collective-permute-start.5
  18.3 0.0 collective-permute-done.1.refs_1_
  18.3 0.0 collective-permute-done.2.refs_2_
  18.3 0.2 collective-permute-done.3.refs_3_
  18.5 5.4 %all-to-all-done = bf16[64,8,128]{2,1,0:T(8,128)(2,1)S(1)} async-done(((bf16[64,8,128]{2,1,0:T(8,128)(2,1)}), bf16[64,8,128]{2,1,0:T(8,128)(2,1)S(1)}, u32[]{:S(2)}, u32[]{:S(2)}) %all-to-all-start) | async-done | bytes 131104 | tf_op jit(solution)/shard_map/all_to_all | solution.py:547
  23.9 0.0 copy-done
  23.9 3.2 %partials.1 = bf16[512,128]{1,0:T(8,128)(2,1)} custom-call(bf16[512,128]{1,0:T(8,128)(2,1)S(1)} %bitcast.15, bf16[1536,128]{1,0:T(8,128)(2,1)S(1)} %get-tuple-element.30.tk_ref, bf16[1536,256]{1,0:T(8,128)(2,1)S(1)} %bitcast.14, bf16[768,128]{1,0:T(8,128)(2,1)S(1)} %collective-permute-done.refs_0_, bf16[768,128]{1,0:T(8,128)(2,1)S(1)} %collective-permute-done.1.refs_1_, ...), custom_call_target="tpu_custom_call" | custom-call | bytes 10485760 | tf_op jit(solution)/shard_map/partials/pallas_call | solution.py:50
  27.1 0.0 copy-start.2
  27.1 0.0 collective-permute-done.4.near_ref
  27.1 0.0 collective-permute-done.5.far_ref
  27.1 6.8 %all-to-all-start.1 = ((bf16[32,16,128]{2,1,0:T(8,128)(2,1)}), bf16[32,16,128]{2,1,0:T(8,128)(2,1)S(1)}, u32[]{:S(2)}, u32[]{:S(2)}) async-start(bf16[32,16,128]{2,1,0:T(8,128)(2,1)} %bitcast.24), calls=%async_computation.1 | async-start | bytes 262144 | tf_op jit(solution)/shard_map/all_to_all | solution.py:547
  33.9 4.2 %probabilities.1 = (bf16[1536,1024]{1,0:T(8,128)(2,1)S(1)}, bf16[48,256]{1,0:T(8,128)(2,1)S(1)}, bf16[48,256]{1,0:T(8,128)(2,1)S(1)}) custom-call(bf16[512,128]{1,0:T(8,128)(2,1)S(1)} %bitcast.16, f32[2,80,128]{2,1,0:T(8,128)} %get-tuple-element.29.tab_hbm_ref, bf16[1536,256]{1,0:T(8,128)(2,1)} %bitcast.23, bf16[48,32,256]{2,1,0:T(8,128)(2,1)} %v_hbm_ref.1, ...), custom_call_target="tpu_custom_call" | custom-call | bytes 20971520 | tf_op jit(solution)/shard_map/probabilities/pallas_call | solution.py:50
  38.1 4.9 %all-to-all-done.1 = bf16[32,16,128]{2,1,0:T(8,128)(2,1)S(1)} async-done(((bf16[32,16,128]{2,1,0:T(8,128)(2,1)}), bf16[32,16,128]{2,1,0:T(8,128)(2,1)S(1)}, u32[]{:S(2)}, u32[]{:S(2)}) %all-to-all-start.1) | async-done | bytes 131104 | tf_op jit(solution)/shard_map/all_to_all | solution.py:547
  43.0 1.0 %merge.1 = bf16[512,128]{1,0:T(8,128)(2,1)} custom-call(bf16[512,128]{1,0:T(8,128)(2,1)S(1)} %bitcast.19), custom_call_target="tpu_custom_call" | custom-call | bytes 2097152 | tf_op jit(solution)/shard_map/merge/pallas_call | solution.py:50
  44.0 5.8 %all-to-all-start.2 = ((bf16[64,8,128]{2,1,0:T(8,128)(2,1)}), bf16[64,8,128]{2,1,0:T(8,128)(2,1)S(1)}, u32[]{:S(2)}, u32[]{:S(2)}) async-start(bf16[64,8,128]{2,1,0:T(8,128)(2,1)} %bitcast.25), calls=%async_computation.2 | async-start | bytes 262144 | tf_op jit(solution)/shard_map/all_to_all | solution.py:547
  49.8 0.6 collective-permute-start.6
  50.4 4.3 %collective-permute-start.7 = (bf16[48,256]{1,0:T(8,128)(2,1)S(1)}, bf16[48,256]{1,0:T(8,128)(2,1)S(1)}, u32[]{:S(2)}, u32[]{:S(2)}) collective-permute-start(bf16[48,256]{1,0:T(8,128)(2,1)S(1)} %get-tuple-element.48), channel_id=1, source_target_pairs={{64,128},{128,64},{65,129},{129,65},{66,130},{130,66},{67,131},{13... | collective-permute-start | bytes 73736 | tf_op jit(solution)/shard_map/ppermute | solution.py:551
  54.7 0.0 copy-done.2
  54.7 3.2 %conv.1.conv_hbm_ref = f32[1536,256]{1,0:T(8,128)} custom-call(bf16[48,32,256]{2,1,0:T(8,128)(2,1)} %v_hbm_ref.1, bf16[48,256]{1,0:T(8,128)(2,1)S(1)} %collective-permute-done.4.near_ref, bf16[48,256]{1,0:T(8,128)(2,1)S(1)} %collective-permute-done.5.far_ref, f32[9,256]{1,0:T(8,128)S(1)} %copy-done.2), custom_call_target="tpu_custom_call" | custom-call | bytes 8388608 | tf_op jit(solution)/shard_map/conv/pallas_call | solution.py:50
  57.9 0.0 collective-permute-done.6.mate_ref
  57.9 0.0 collective-permute-done.7.rest_ref
  57.9 1.3 %all-to-all-done.2 = bf16[64,8,128]{2,1,0:T(8,128)(2,1)S(1)} async-done(((bf16[64,8,128]{2,1,0:T(8,128)(2,1)}), bf16[64,8,128]{2,1,0:T(8,128)(2,1)S(1)}, u32[]{:S(2)}, u32[]{:S(2)}) %all-to-all-start.2) | async-done | bytes 131104 | tf_op jit(solution)/shard_map/all_to_all | solution.py:547
  59.2 0.0 copy-start.3
  59.2 0.0 copy-start.4
  59.2 2.0 %attend.1 = (f32[1536,256]{1,0:T(8,128)S(1)}, f32[24,128]{1,0:T(8,128)S(1)}) custom-call(bf16[512,128]{1,0:T(8,128)(2,1)S(1)} %bitcast.18, bf16[1536,1024]{1,0:T(8,128)(2,1)S(1)} %get-tuple-element.42.prob_ref, f32[1536,256]{1,0:T(8,128)} %conv.1.conv_hbm_ref, bf16[48,256]{1,0:T(8,128)(2,1)S(1)} %collective-permute-done.6.mate_ref, ...), custom_call_target="tpu_custom_call" | custom-call | bytes 4194304 | tf_op jit(solution)/shard_map/attend/pallas_call | solution.py:50
  61.3 2.8 %collective-permute-start.10 = (f32[24,128]{1,0:T(8,128)S(1)}, f32[24,128]{1,0:T(8,128)S(1)}, u32[]{:S(2)}, u32[]{:S(2)}) collective-permute-start(f32[24,128]{1,0:T(8,128)S(1)} %get-tuple-element.49.s0_ref), channel_id=1, source_target_pairs={{0,3},{1,2},{2,1},{3,0},{4,7},{5,6},{6,5},{7,4},{8,11},{9,10},{10,... | collective-permute-start | bytes 36872 | tf_op jit(solution)/shard_map/ppermute | solution.py:654
  64.1 0.8 %collective-permute-start.9 = (f32[24,128]{1,0:T(8,128)S(1)}, f32[24,128]{1,0:T(8,128)S(1)}, u32[]{:S(2)}, u32[]{:S(2)}) collective-permute-start(f32[24,128]{1,0:T(8,128)S(1)} %get-tuple-element.49.s0_ref), channel_id=1, source_target_pairs={{0,2},{1,3},{2,0},{3,1},{4,6},{5,7},{6,4},{7,5},{8,10},{9,11},{10,... | collective-permute-start | bytes 36872 | tf_op jit(solution)/shard_map/ppermute | solution.py:654
  64.9 0.5 collective-permute-start.8
  65.4 0.8 %collective-permute-done.10.s3_ref = f32[24,128]{1,0:T(8,128)S(1)} collective-permute-done((f32[24,128]{1,0:T(8,128)S(1)}, f32[24,128]{1,0:T(8,128)S(1)}, u32[]{:S(2)}, u32[]{:S(2)}) %collective-permute-start.10) | collective-permute-done | bytes 12320 | tf_op jit(solution)/shard_map/ppermute | solution.py:654
  66.2 3.1 %collective-permute-done.9.s2_ref = f32[24,128]{1,0:T(8,128)S(1)} collective-permute-done((f32[24,128]{1,0:T(8,128)S(1)}, f32[24,128]{1,0:T(8,128)S(1)}, u32[]{:S(2)}, u32[]{:S(2)}) %collective-permute-start.9) | collective-permute-done | bytes 12320 | tf_op jit(solution)/shard_map/ppermute | solution.py:654
  69.3 0.0 collective-permute-done.8.s1_ref
  69.3 0.0 copy-done.3
  69.3 0.0 copy-done.4
  69.3 1.2 %norm.1 = bf16[1536,256]{1,0:T(8,128)(2,1)} custom-call(f32[24,128]{1,0:T(8,128)S(1)} %get-tuple-element.49.s0_ref, f32[24,128]{1,0:T(8,128)S(1)} %collective-permute-done.8.s1_ref, f32[24,128]{1,0:T(8,128)S(1)} %collective-permute-done.9.s2_ref, f32[24,128]{1,0:T(8,128)S(1)} %collective-permute-done.10.s3_ref, f32[1536,256]{1,0:T(8,128)S(1)} %get-tuple-element.50.sum_ref, ...), custom_call_target="tpu_custom_call" | custom-call | bytes 4194304 | tf_op jit(solution)/shard_map/norm/pallas_call | solution.py:50
Async XLA Ops:
  0.0 14.5 %copy-start.1 = (bf16[48,32,256]{2,1,0:T(8,128)(2,1)S(1)}, bf16[48,32,256]{2,1,0:T(8,128)(2,1)}, u32[]{:S(2)}) copy-start(bf16[48,32,256]{2,1,0:T(8,128)(2,1)} %param.8) | copy-start | bytes 2359300
  0.0 23.9 %copy-start = (bf16[48,32,256]{2,1,0:T(8,128)(2,1)S(1)}, bf16[48,32,256]{2,1,0:T(8,128)(2,1)}, u32[]{:S(2)}) copy-start(bf16[48,32,256]{2,1,0:T(8,128)(2,1)} %v_hbm_ref.1) | copy-start | bytes 2359300
  2.4 21.5 %all-to-all-start = ((bf16[64,8,128]{2,1,0:T(8,128)(2,1)}), bf16[64,8,128]{2,1,0:T(8,128)(2,1)S(1)}, u32[]{:S(2)}, u32[]{:S(2)}) async-start(bf16[64,8,128]{2,1,0:T(8,128)(2,1)} %bitcast.26), calls=%async_computation | async-start | bytes 262144 | tf_op jit(solution)/shard_map/all_to_all | solution.py:547
  16.1 1.5 %collective-permute-start = (bf16[768,128]{1,0:T(8,128)(2,1)S(1)}, bf16[768,128]{1,0:T(8,128)(2,1)S(1)}, u32[]{:S(2)}, u32[]{:S(2)}) collective-permute-start(bf16[768,128]{1,0:T(8,128)(2,1)S(1)} %get-tuple-element.31), channel_id=1, source_target_pairs={{0,4},{4,0},{1,5},{5,1},{2,6},{6,2},{3,7},{7,3},{8,12},{12,8},{9,1... | collective-permute-start | bytes 589832 | tf_op jit(solution)/shard_map/ppermute | solution.py:551
  16.3 2.0 %collective-permute-start.1 = (bf16[768,128]{1,0:T(8,128)(2,1)S(1)}, bf16[768,128]{1,0:T(8,128)(2,1)S(1)}, u32[]{:S(2)}, u32[]{:S(2)}) collective-permute-start(bf16[768,128]{1,0:T(8,128)(2,1)S(1)} %get-tuple-element.32), channel_id=1, source_target_pairs={{0,4},{4,0},{1,5},{5,1},{2,6},{6,2},{3,7},{7,3},{8,12},{12,8},{9,1... | collective-permute-start | bytes 589832 | tf_op jit(solution)/shard_map/ppermute | solution.py:551
  16.7 1.6 %collective-permute-start.2 = (bf16[768,128]{1,0:T(8,128)(2,1)S(1)}, bf16[768,128]{1,0:T(8,128)(2,1)S(1)}, u32[]{:S(2)}, u32[]{:S(2)}) collective-permute-start(bf16[768,128]{1,0:T(8,128)(2,1)S(1)} %get-tuple-element.33), channel_id=1, source_target_pairs={{0,4},{4,0},{1,5},{5,1},{2,6},{6,2},{3,7},{7,3},{8,12},{12,8},{9,1... | collective-permute-start | bytes 589832 | tf_op jit(solution)/shard_map/ppermute | solution.py:551
  16.9 1.6 %collective-permute-start.3 = (bf16[768,128]{1,0:T(8,128)(2,1)S(1)}, bf16[768,128]{1,0:T(8,128)(2,1)S(1)}, u32[]{:S(2)}, u32[]{:S(2)}) collective-permute-start(bf16[768,128]{1,0:T(8,128)(2,1)S(1)} %get-tuple-element.34), channel_id=1, source_target_pairs={{0,4},{4,0},{1,5},{5,1},{2,6},{6,2},{3,7},{7,3},{8,12},{12,8},{9,1... | collective-permute-start | bytes 589832 | tf_op jit(solution)/shard_map/ppermute | solution.py:551
  17.2 9.9 %collective-permute-start.4 = (bf16[48,256]{1,0:T(8,128)(2,1)S(1)}, bf16[48,256]{1,0:T(8,128)(2,1)S(1)}, u32[]{:S(2)}, u32[]{:S(2)}) collective-permute-start(bf16[48,256]{1,0:T(8,128)(2,1)S(1)} %get-tuple-element.35), channel_id=1, source_target_pairs={{0,4},{4,0},{1,5},{5,1},{2,6},{6,2},{3,7},{7,3},{8,12},{12,8},{9,1... | collective-permute-start | bytes 73736 | tf_op jit(solution)/shard_map/ppermute | solution.py:551
  17.6 9.5 %collective-permute-start.5 = (bf16[48,256]{1,0:T(8,128)(2,1)S(1)}, bf16[48,256]{1,0:T(8,128)(2,1)S(1)}, u32[]{:S(2)}, u32[]{:S(2)}) collective-permute-start(bf16[48,256]{1,0:T(8,128)(2,1)S(1)} %get-tuple-element.36), channel_id=1, source_target_pairs={{4,8},{8,4},{12,16},{16,12},{20,24},{24,20},{28,32},{32,28},{36,40... | collective-permute-start | bytes 73736 | tf_op jit(solution)/shard_map/ppermute | solution.py:551
  27.1 27.6 %copy-start.2 = (f32[9,256]{1,0:T(8,128)S(1)}, f32[9,256]{1,0:T(8,128)}, u32[]{:S(2)}) copy-start(f32[9,256]{1,0:T(8,128)} %w_ref.3) | copy-start | bytes 27652
  27.1 15.9 %all-to-all-start.1 = ((bf16[32,16,128]{2,1,0:T(8,128)(2,1)}), bf16[32,16,128]{2,1,0:T(8,128)(2,1)S(1)}, u32[]{:S(2)}, u32[]{:S(2)}) async-start(bf16[32,16,128]{2,1,0:T(8,128)(2,1)} %bitcast.24), calls=%async_computation.1 | async-start | bytes 262144 | tf_op jit(solution)/shard_map/all_to_all | solution.py:547
  44.0 15.3 %all-to-all-start.2 = ((bf16[64,8,128]{2,1,0:T(8,128)(2,1)}), bf16[64,8,128]{2,1,0:T(8,128)(2,1)S(1)}, u32[]{:S(2)}, u32[]{:S(2)}) async-start(bf16[64,8,128]{2,1,0:T(8,128)(2,1)} %bitcast.25), calls=%async_computation.2 | async-start | bytes 262144 | tf_op jit(solution)/shard_map/all_to_all | solution.py:547
  49.8 8.1 %collective-permute-start.6 = (bf16[48,256]{1,0:T(8,128)(2,1)S(1)}, bf16[48,256]{1,0:T(8,128)(2,1)S(1)}, u32[]{:S(2)}, u32[]{:S(2)}) collective-permute-start(bf16[48,256]{1,0:T(8,128)(2,1)S(1)} %get-tuple-element.47), channel_id=1, source_target_pairs={{0,64},{64,0},{128,192},{192,128},{1,65},{65,1},{129,193},{193,129... | collective-permute-start | bytes 73736 | tf_op jit(solution)/shard_map/ppermute | solution.py:551
  50.4 7.5 %collective-permute-start.7 = (bf16[48,256]{1,0:T(8,128)(2,1)S(1)}, bf16[48,256]{1,0:T(8,128)(2,1)S(1)}, u32[]{:S(2)}, u32[]{:S(2)}) collective-permute-start(bf16[48,256]{1,0:T(8,128)(2,1)S(1)} %get-tuple-element.48), channel_id=1, source_target_pairs={{64,128},{128,64},{65,129},{129,65},{66,130},{130,66},{67,131},{13... | collective-permute-start | bytes 73736 | tf_op jit(solution)/shard_map/ppermute | solution.py:551
  59.2 10.1 %copy-start.3 = (f32[256]{0:T(256)S(1)}, f32[256]{0:T(256)}, u32[]{:S(2)}) copy-start(f32[256]{0:T(256)} %param.12) | copy-start | bytes 3076
  59.2 10.1 %copy-start.4 = (f32[256]{0:T(256)S(1)}, f32[256]{0:T(256)}, u32[]{:S(2)}) copy-start(f32[256]{0:T(256)} %param.13) | copy-start | bytes 3076
  61.3 5.0 %collective-permute-start.10 = (f32[24,128]{1,0:T(8,128)S(1)}, f32[24,128]{1,0:T(8,128)S(1)}, u32[]{:S(2)}, u32[]{:S(2)}) collective-permute-start(f32[24,128]{1,0:T(8,128)S(1)} %get-tuple-element.49.s0_ref), channel_id=1, source_target_pairs={{0,3},{1,2},{2,1},{3,0},{4,7},{5,6},{6,5},{7,4},{8,11},{9,10},{10,... | collective-permute-start | bytes 36872 | tf_op jit(solution)/shard_map/ppermute | solution.py:654
  64.1 5.2 %collective-permute-start.9 = (f32[24,128]{1,0:T(8,128)S(1)}, f32[24,128]{1,0:T(8,128)S(1)}, u32[]{:S(2)}, u32[]{:S(2)}) collective-permute-start(f32[24,128]{1,0:T(8,128)S(1)} %get-tuple-element.49.s0_ref), channel_id=1, source_target_pairs={{0,2},{1,3},{2,0},{3,1},{4,6},{5,7},{6,4},{7,5},{8,10},{9,11},{10,... | collective-permute-start | bytes 36872 | tf_op jit(solution)/shard_map/ppermute | solution.py:654
  64.9 4.4 %collective-permute-start.8 = (f32[24,128]{1,0:T(8,128)S(1)}, f32[24,128]{1,0:T(8,128)S(1)}, u32[]{:S(2)}, u32[]{:S(2)}) collective-permute-start(f32[24,128]{1,0:T(8,128)S(1)} %get-tuple-element.49.s0_ref), channel_id=1, source_target_pairs={{0,1},{1,0},{2,3},{3,2},{4,5},{5,4},{6,7},{7,6},{8,9},{9,8},{10,11... | collective-permute-start | bytes 36872 | tf_op jit(solution)/shard_map/ppermute | solution.py:654

commit v16 on v15

--- a/solution.py
+++ b/solution.py
@@ -240,7 +240,8 @@
 
 
 def partial_kernel(agents_ref, tk_ref, v_ref, *refs):
-    got, (out_ref, score_ref, wide_ref) = refs[:PIECES], refs[PIECES:]
+    got, (out_ref, score_ref, wide_ref, done_ref, sems) = refs[:PIECES], refs[PIECES:]
+    outs = []
     size = 2 * N // PIECES
     pairs = agent_pairs(agents_ref, wide_ref, 1.0 / math.sqrt(HD))
     mine = jnp.where(even_core(), pairs[0], pairs[1])
@@ -300,7 +301,14 @@
         )
         groups = packed.reshape(2, AGENTS // 16, 8, 128)
         groups = jnp.concatenate([groups[0], groups[1]], 1).reshape(AGENTS, 128)
-        out_ref[pl.ds(parity * AGENTS, AGENTS), :] = groups.astype(bf16)
+        rows = pl.ds(parity * AGENTS, AGENTS)
+        done_ref[rows, :] = groups.astype(bf16)
+        outs.append(
+            pltpu.make_async_copy(done_ref.at[rows, :], out_ref.at[rows, :], sems.at[parity])
+        )
+        outs[parity].start()
+    for copy in outs:
+        copy.wait()
 
 
 def merge_kernel(parts_ref, out_ref):
@@ -598,12 +606,18 @@
     outer = swap(outer, ("z", "core"), chain(("z", "core"), 1))
     parts = call(
         partial_kernel,
-        far((2 * AGENTS, 128), bf16),
+        (far((2 * AGENTS, 128), bf16),),
         " v " + " " * PIECES,
-        scratch=[pltpu.VMEM((2, AGENTS, 2 * N), f32), wide],
+        scratch=[
+            pltpu.VMEM((2, AGENTS, 2 * N), f32),
+            wide,
+            pltpu.VMEM((2 * AGENTS, 128), bf16),
+            pltpu.SemaphoreType.DMA((2,)),
+        ],
+        out_spaces="h",
         nbytes=10 * mb,
         name="partials",
-    )(agents, tk, v, *got)
+    )(agents, tk, v, *got)[0]
     parts, inner, outer = lax.optimization_barrier((parts, inner, outer))
     received = spread(parts, ("row", "z"))
     prob, mate, rest = call(

time: 71.7 us -> 71.7 us (level)
  no operation moved by 1% of the time
where the time goes in v16:
time: 71.7 us; the launch traced here: 70.7 us
  starting transfers between devices  35.6 us (50%)
  Pallas kernels  18.7 us (26%)
  waiting for transfers between devices  16.1 us (22%)
    all_to_all x3, starting transfers between devices, spread(): return lax.all_to_all(slot, axes, 0, 0).reshape(x.shape)  24.6 us
    pallas_call x8, Pallas kernels, run(): fn(*[pltpu.with_memory_space_constraint(x, spaces[c]) if c in spaces else...  18.7 us
    all_to_all x3, waiting for transfers between devices, spread(): return lax.all_to_all(slot, axes, 0, 0).reshape(x.shape)  11.8 us
    ppermute x8, starting transfers between devices, swap(): lax.ppermute(x, axis, [p for i, j in pairs for p in ((i, j), (j, i))])  6.74 us
    ppermute x3, starting transfers between devices, shards(): lax.ppermute(stats, 'head', [(i, i ^ d) for i in range(heads)])  4.18 us
    ppermute x3, waiting for transfers between devices, shards(): lax.ppermute(stats, 'head', [(i, i ^ d) for i in range(heads)])  3.87 us
  transfers between devices with their start and end apart: 14, of which 7 were waited for; matrix products, arithmetic and copies ran while one was open for 0% of the time, Pallas kernels for 17%

profile of v16, /device:TPU:8, one launch (start us, length us, event | category | flops | bytes accessed | tf_op | source)
XLA Modules:
  0.0 70.7 jit_solution(18226739543527845267)
XLA Ops:
  0.0 0.0 copy-start.1
  0.0 0.0 copy-start
  0.0 2.4 %pool_queries.1 = (bf16[512,128]{1,0:T(8,128)(2,1)}, f32[2,80,128]{2,1,0:T(8,128)}) custom-call(s32[2,32,48]{2,1,0:T(8,128)} %bitcast.27, bf16[1536,256]{1,0:T(8,128)(2,1)} %bitcast.22), custom_call_target="tpu_custom_call" | custom-call | bytes 8388608 | tf_op jit(solution)/shard_map/pool_queries/pallas_call | solution.py:50
  2.4 12.1 %all-to-all-start = ((bf16[64,8,128]{2,1,0:T(8,128)(2,1)}), bf16[64,8,128]{2,1,0:T(8,128)(2,1)S(1)}, u32[]{:S(2)}, u32[]{:S(2)}) async-start(bf16[64,8,128]{2,1,0:T(8,128)(2,1)} %bitcast.26), calls=%async_computation | async-start | bytes 262144 | tf_op jit(solution)/shard_map/all_to_all | solution.py:555
  14.5 0.0 copy-done.1
  14.5 1.6 %turn_keys.1 = (bf16[1536,128]{1,0:T(8,128)(2,1)S(1)}, bf16[768,128]{1,0:T(8,128)(2,1)S(1)}, bf16[768,128]{1,0:T(8,128)(2,1)S(1)}, bf16[768,128]{1,0:T(8,128)(2,...) custom-call(f32[2,80,128]{2,1,0:T(8,128)} %get-tuple-element.29.tab_hbm_ref, ...), custom_call_target="tpu_custom_call" | custom-call | bytes 4194304 | tf_op jit(solution)/shard_map/turn_keys/pallas_call | solution.py:50
  16.1 0.2 collective-permute-start
  16.3 0.4 collective-permute-start.1
  16.7 0.1 collective-permute-start.2
  16.9 0.4 collective-permute-start.3
  17.2 0.1 collective-permute-start.4
  17.4 0.3 collective-permute-done.refs_0_
  17.6 0.7 collective-permute-start.5
  18.3 0.0 collective-permute-done.1.refs_1_
  18.3 0.0 collective-permute-done.2.refs_2_
  18.3 0.2 collective-permute-done.3.refs_3_
  18.5 5.4 %all-to-all-done = bf16[64,8,128]{2,1,0:T(8,128)(2,1)S(1)} async-done(((bf16[64,8,128]{2,1,0:T(8,128)(2,1)}), bf16[64,8,128]{2,1,0:T(8,128)(2,1)S(1)}, u32[]{:S(2)}, u32[]{:S(2)}) %all-to-all-start) | async-done | bytes 131104 | tf_op jit(solution)/shard_map/all_to_all | solution.py:555
  23.9 0.0 copy-done
  23.9 3.2 %partials.1 = bf16[512,128]{1,0:T(8,128)(2,1)} custom-call(bf16[512,128]{1,0:T(8,128)(2,1)S(1)} %bitcast.15, bf16[1536,128]{1,0:T(8,128)(2,1)S(1)} %get-tuple-element.30.tk_ref, bf16[1536,256]{1,0:T(8,128)(2,1)S(1)} %bitcast.14, bf16[768,128]{1,0:T(8,128)(2,1)S(1)} %collective-permute-done.refs_0_, bf16[768,128]{1,0:T(8,128)(2,1)S(1)} %collective-permute-done.1.refs_1_, ...), custom_call_target="tpu_custom_call" | custom-call | bytes 10485760 | tf_op jit(solution)/shard_map/partials/pallas_call | solution.py:50
  27.1 0.0 copy-start.2
  27.1 0.0 collective-permute-done.4.near_ref
  27.1 0.0 collective-permute-done.5.far_ref
  27.1 6.8 %all-to-all-start.1 = ((bf16[32,16,128]{2,1,0:T(8,128)(2,1)}), bf16[32,16,128]{2,1,0:T(8,128)(2,1)S(1)}, u32[]{:S(2)}, u32[]{:S(2)}) async-start(bf16[32,16,128]{2,1,0:T(8,128)(2,1)} %bitcast.24), calls=%async_computation.1 | async-start | bytes 262144 | tf_op jit(solution)/shard_map/all_to_all | solution.py:555
  33.9 4.2 %probabilities.1 = (bf16[1536,1024]{1,0:T(8,128)(2,1)S(1)}, bf16[48,256]{1,0:T(8,128)(2,1)S(1)}, bf16[48,256]{1,0:T(8,128)(2,1)S(1)}) custom-call(bf16[512,128]{1,0:T(8,128)(2,1)S(1)} %bitcast.16, f32[2,80,128]{2,1,0:T(8,128)} %get-tuple-element.29.tab_hbm_ref, bf16[1536,256]{1,0:T(8,128)(2,1)} %bitcast.23, bf16[48,32,256]{2,1,0:T(8,128)(2,1)} %v_hbm_ref.1, ...), custom_call_target="tpu_custom_call" | custom-call | bytes 20971520 | tf_op jit(solution)/shard_map/probabilities/pallas_call | solution.py:50
  38.1 5.0 %all-to-all-done.1 = bf16[32,16,128]{2,1,0:T(8,128)(2,1)S(1)} async-done(((bf16[32,16,128]{2,1,0:T(8,128)(2,1)}), bf16[32,16,128]{2,1,0:T(8,128)(2,1)S(1)}, u32[]{:S(2)}, u32[]{:S(2)}) %all-to-all-start.1) | async-done | bytes 131104 | tf_op jit(solution)/shard_map/all_to_all | solution.py:555
  43.1 1.0 %merge.1 = bf16[512,128]{1,0:T(8,128)(2,1)} custom-call(bf16[512,128]{1,0:T(8,128)(2,1)S(1)} %bitcast.19), custom_call_target="tpu_custom_call" | custom-call | bytes 2097152 | tf_op jit(solution)/shard_map/merge/pallas_call | solution.py:50
  44.1 5.7 %all-to-all-start.2 = ((bf16[64,8,128]{2,1,0:T(8,128)(2,1)}), bf16[64,8,128]{2,1,0:T(8,128)(2,1)S(1)}, u32[]{:S(2)}, u32[]{:S(2)}) async-start(bf16[64,8,128]{2,1,0:T(8,128)(2,1)} %bitcast.25), calls=%async_computation.2 | async-start | bytes 262144 | tf_op jit(solution)/shard_map/all_to_all | solution.py:555
  49.8 0.6 collective-permute-start.6
  50.4 4.3 %collective-permute-start.7 = (bf16[48,256]{1,0:T(8,128)(2,1)S(1)}, bf16[48,256]{1,0:T(8,128)(2,1)S(1)}, u32[]{:S(2)}, u32[]{:S(2)}) collective-permute-start(bf16[48,256]{1,0:T(8,128)(2,1)S(1)} %get-tuple-element.48), channel_id=1, source_target_pairs={{64,128},{128,64},{65,129},{129,65},{66,130},{130,66},{67,131},{13... | collective-permute-start | bytes 73736 | tf_op jit(solution)/shard_map/ppermute | solution.py:559
  54.7 0.0 copy-done.2
  54.7 3.2 %conv.1.conv_hbm_ref = f32[1536,256]{1,0:T(8,128)} custom-call(bf16[48,32,256]{2,1,0:T(8,128)(2,1)} %v_hbm_ref.1, bf16[48,256]{1,0:T(8,128)(2,1)S(1)} %collective-permute-done.4.near_ref, bf16[48,256]{1,0:T(8,128)(2,1)S(1)} %collective-permute-done.5.far_ref, f32[9,256]{1,0:T(8,128)S(1)} %copy-done.2), custom_call_target="tpu_custom_call" | custom-call | bytes 8388608 | tf_op jit(solution)/shard_map/conv/pallas_call | solution.py:50
  57.9 0.0 collective-permute-done.6.mate_ref
  57.9 0.0 collective-permute-done.7.rest_ref
  57.9 1.3 %all-to-all-done.2 = bf16[64,8,128]{2,1,0:T(8,128)(2,1)S(1)} async-done(((bf16[64,8,128]{2,1,0:T(8,128)(2,1)}), bf16[64,8,128]{2,1,0:T(8,128)(2,1)S(1)}, u32[]{:S(2)}, u32[]{:S(2)}) %all-to-all-start.2) | async-done | bytes 131104 | tf_op jit(solution)/shard_map/all_to_all | solution.py:555
  59.2 0.0 copy-start.3
  59.2 0.0 copy-start.4
  59.2 2.0 %attend.1 = (f32[1536,256]{1,0:T(8,128)S(1)}, f32[24,128]{1,0:T(8,128)S(1)}) custom-call(bf16[512,128]{1,0:T(8,128)(2,1)S(1)} %bitcast.18, bf16[1536,1024]{1,0:T(8,128)(2,1)S(1)} %get-tuple-element.42.prob_ref, f32[1536,256]{1,0:T(8,128)} %conv.1.conv_hbm_ref, bf16[48,256]{1,0:T(8,128)(2,1)S(1)} %collective-permute-done.6.mate_ref, ...), custom_call_target="tpu_custom_call" | custom-call | bytes 4194304 | tf_op jit(solution)/shard_map/attend/pallas_call | solution.py:50
  61.3 2.8 %collective-permute-start.10 = (f32[24,128]{1,0:T(8,128)S(1)}, f32[24,128]{1,0:T(8,128)S(1)}, u32[]{:S(2)}, u32[]{:S(2)}) collective-permute-start(f32[24,128]{1,0:T(8,128)S(1)} %get-tuple-element.49.s0_ref), channel_id=1, source_target_pairs={{0,3},{1,2},{2,1},{3,0},{4,7},{5,6},{6,5},{7,4},{8,11},{9,10},{10,... | collective-permute-start | bytes 36872 | tf_op jit(solution)/shard_map/ppermute | solution.py:668
  64.1 0.8 %collective-permute-start.9 = (f32[24,128]{1,0:T(8,128)S(1)}, f32[24,128]{1,0:T(8,128)S(1)}, u32[]{:S(2)}, u32[]{:S(2)}) collective-permute-start(f32[24,128]{1,0:T(8,128)S(1)} %get-tuple-element.49.s0_ref), channel_id=1, source_target_pairs={{0,2},{1,3},{2,0},{3,1},{4,6},{5,7},{6,4},{7,5},{8,10},{9,11},{10,... | collective-permute-start | bytes 36872 | tf_op jit(solution)/shard_map/ppermute | solution.py:668
  64.9 0.5 collective-permute-start.8
  65.4 0.8 %collective-permute-done.10.s3_ref = f32[24,128]{1,0:T(8,128)S(1)} collective-permute-done((f32[24,128]{1,0:T(8,128)S(1)}, f32[24,128]{1,0:T(8,128)S(1)}, u32[]{:S(2)}, u32[]{:S(2)}) %collective-permute-start.10) | collective-permute-done | bytes 12320 | tf_op jit(solution)/shard_map/ppermute | solution.py:668
  66.2 3.1 %collective-permute-done.9.s2_ref = f32[24,128]{1,0:T(8,128)S(1)} collective-permute-done((f32[24,128]{1,0:T(8,128)S(1)}, f32[24,128]{1,0:T(8,128)S(1)}, u32[]{:S(2)}, u32[]{:S(2)}) %collective-permute-start.9) | collective-permute-done | bytes 12320 | tf_op jit(solution)/shard_map/ppermute | solution.py:668
  69.3 0.0 collective-permute-done.8.s1_ref
  69.3 0.0 copy-done.3
  69.3 0.0 copy-done.4
  69.3 1.2 %norm.1 = bf16[1536,256]{1,0:T(8,128)(2,1)} custom-call(f32[24,128]{1,0:T(8,128)S(1)} %get-tuple-element.49.s0_ref, f32[24,128]{1,0:T(8,128)S(1)} %collective-permute-done.8.s1_ref, f32[24,128]{1,0:T(8,128)S(1)} %collective-permute-done.9.s2_ref, f32[24,128]{1,0:T(8,128)S(1)} %collective-permute-done.10.s3_ref, f32[1536,256]{1,0:T(8,128)S(1)} %get-tuple-element.50.sum_ref, ...), custom_call_target="tpu_custom_call" | custom-call | bytes 4194304 | tf_op jit(solution)/shard_map/norm/pallas_call | solution.py:50
Async XLA Ops:
  0.0 14.5 %copy-start.1 = (bf16[48,32,256]{2,1,0:T(8,128)(2,1)S(1)}, bf16[48,32,256]{2,1,0:T(8,128)(2,1)}, u32[]{:S(2)}) copy-start(bf16[48,32,256]{2,1,0:T(8,128)(2,1)} %param.8) | copy-start | bytes 2359300
  0.0 23.9 %copy-start = (bf16[48,32,256]{2,1,0:T(8,128)(2,1)S(1)}, bf16[48,32,256]{2,1,0:T(8,128)(2,1)}, u32[]{:S(2)}) copy-start(bf16[48,32,256]{2,1,0:T(8,128)(2,1)} %v_hbm_ref.1) | copy-start | bytes 2359300
  2.4 21.5 %all-to-all-start = ((bf16[64,8,128]{2,1,0:T(8,128)(2,1)}), bf16[64,8,128]{2,1,0:T(8,128)(2,1)S(1)}, u32[]{:S(2)}, u32[]{:S(2)}) async-start(bf16[64,8,128]{2,1,0:T(8,128)(2,1)} %bitcast.26), calls=%async_computation | async-start | bytes 262144 | tf_op jit(solution)/shard_map/all_to_all | solution.py:555
  16.1 1.5 %collective-permute-start = (bf16[768,128]{1,0:T(8,128)(2,1)S(1)}, bf16[768,128]{1,0:T(8,128)(2,1)S(1)}, u32[]{:S(2)}, u32[]{:S(2)}) collective-permute-start(bf16[768,128]{1,0:T(8,128)(2,1)S(1)} %get-tuple-element.31), channel_id=1, source_target_pairs={{0,4},{4,0},{1,5},{5,1},{2,6},{6,2},{3,7},{7,3},{8,12},{12,8},{9,1... | collective-permute-start | bytes 589832 | tf_op jit(solution)/shard_map/ppermute | solution.py:559
  16.3 2.0 %collective-permute-start.1 = (bf16[768,128]{1,0:T(8,128)(2,1)S(1)}, bf16[768,128]{1,0:T(8,128)(2,1)S(1)}, u32[]{:S(2)}, u32[]{:S(2)}) collective-permute-start(bf16[768,128]{1,0:T(8,128)(2,1)S(1)} %get-tuple-element.32), channel_id=1, source_target_pairs={{0,4},{4,0},{1,5},{5,1},{2,6},{6,2},{3,7},{7,3},{8,12},{12,8},{9,1... | collective-permute-start | bytes 589832 | tf_op jit(solution)/shard_map/ppermute | solution.py:559
  16.7 1.6 %collective-permute-start.2 = (bf16[768,128]{1,0:T(8,128)(2,1)S(1)}, bf16[768,128]{1,0:T(8,128)(2,1)S(1)}, u32[]{:S(2)}, u32[]{:S(2)}) collective-permute-start(bf16[768,128]{1,0:T(8,128)(2,1)S(1)} %get-tuple-element.33), channel_id=1, source_target_pairs={{0,4},{4,0},{1,5},{5,1},{2,6},{6,2},{3,7},{7,3},{8,12},{12,8},{9,1... | collective-permute-start | bytes 589832 | tf_op jit(solution)/shard_map/ppermute | solution.py:559
  16.9 1.6 %collective-permute-start.3 = (bf16[768,128]{1,0:T(8,128)(2,1)S(1)}, bf16[768,128]{1,0:T(8,128)(2,1)S(1)}, u32[]{:S(2)}, u32[]{:S(2)}) collective-permute-start(bf16[768,128]{1,0:T(8,128)(2,1)S(1)} %get-tuple-element.34), channel_id=1, source_target_pairs={{0,4},{4,0},{1,5},{5,1},{2,6},{6,2},{3,7},{7,3},{8,12},{12,8},{9,1... | collective-permute-start | bytes 589832 | tf_op jit(solution)/shard_map/ppermute | solution.py:559
  17.2 9.9 %collective-permute-start.4 = (bf16[48,256]{1,0:T(8,128)(2,1)S(1)}, bf16[48,256]{1,0:T(8,128)(2,1)S(1)}, u32[]{:S(2)}, u32[]{:S(2)}) collective-permute-start(bf16[48,256]{1,0:T(8,128)(2,1)S(1)} %get-tuple-element.35), channel_id=1, source_target_pairs={{0,4},{4,0},{1,5},{5,1},{2,6},{6,2},{3,7},{7,3},{8,12},{12,8},{9,1... | collective-permute-start | bytes 73736 | tf_op jit(solution)/shard_map/ppermute | solution.py:559
  17.6 9.5 %collective-permute-start.5 = (bf16[48,256]{1,0:T(8,128)(2,1)S(1)}, bf16[48,256]{1,0:T(8,128)(2,1)S(1)}, u32[]{:S(2)}, u32[]{:S(2)}) collective-permute-start(bf16[48,256]{1,0:T(8,128)(2,1)S(1)} %get-tuple-element.36), channel_id=1, source_target_pairs={{4,8},{8,4},{12,16},{16,12},{20,24},{24,20},{28,32},{32,28},{36,40... | collective-permute-start | bytes 73736 | tf_op jit(solution)/shard_map/ppermute | solution.py:559
  27.1 27.6 %copy-start.2 = (f32[9,256]{1,0:T(8,128)S(1)}, f32[9,256]{1,0:T(8,128)}, u32[]{:S(2)}) copy-start(f32[9,256]{1,0:T(8,128)} %w_ref.3) | copy-start | bytes 27652
  27.1 16.0 %all-to-all-start.1 = ((bf16[32,16,128]{2,1,0:T(8,128)(2,1)}), bf16[32,16,128]{2,1,0:T(8,128)(2,1)S(1)}, u32[]{:S(2)}, u32[]{:S(2)}) async-start(bf16[32,16,128]{2,1,0:T(8,128)(2,1)} %bitcast.24), calls=%async_computation.1 | async-start | bytes 262144 | tf_op jit(solution)/shard_map/all_to_all | solution.py:555
  44.1 15.2 %all-to-all-start.2 = ((bf16[64,8,128]{2,1,0:T(8,128)(2,1)}), bf16[64,8,128]{2,1,0:T(8,128)(2,1)S(1)}, u32[]{:S(2)}, u32[]{:S(2)}) async-start(bf16[64,8,128]{2,1,0:T(8,128)(2,1)} %bitcast.25), calls=%async_computation.2 | async-start | bytes 262144 | tf_op jit(solution)/shard_map/all_to_all | solution.py:555
  49.8 8.1 %collective-permute-start.6 = (bf16[48,256]{1,0:T(8,128)(2,1)S(1)}, bf16[48,256]{1,0:T(8,128)(2,1)S(1)}, u32[]{:S(2)}, u32[]{:S(2)}) collective-permute-start(bf16[48,256]{1,0:T(8,128)(2,1)S(1)} %get-tuple-element.47), channel_id=1, source_target_pairs={{0,64},{64,0},{128,192},{192,128},{1,65},{65,1},{129,193},{193,129... | collective-permute-start | bytes 73736 | tf_op jit(solution)/shard_map/ppermute | solution.py:559
  50.4 7.5 %collective-permute-start.7 = (bf16[48,256]{1,0:T(8,128)(2,1)S(1)}, bf16[48,256]{1,0:T(8,128)(2,1)S(1)}, u32[]{:S(2)}, u32[]{:S(2)}) collective-permute-start(bf16[48,256]{1,0:T(8,128)(2,1)S(1)} %get-tuple-element.48), channel_id=1, source_target_pairs={{64,128},{128,64},{65,129},{129,65},{66,130},{130,66},{67,131},{13... | collective-permute-start | bytes 73736 | tf_op jit(solution)/shard_map/ppermute | solution.py:559
  59.2 10.1 %copy-start.3 = (f32[256]{0:T(256)S(1)}, f32[256]{0:T(256)}, u32[]{:S(2)}) copy-start(f32[256]{0:T(256)} %param.12) | copy-start | bytes 3076
  59.2 10.1 %copy-start.4 = (f32[256]{0:T(256)S(1)}, f32[256]{0:T(256)}, u32[]{:S(2)}) copy-start(f32[256]{0:T(256)} %param.13) | copy-start | bytes 3076
  61.3 5.0 %collective-permute-start.10 = (f32[24,128]{1,0:T(8,128)S(1)}, f32[24,128]{1,0:T(8,128)S(1)}, u32[]{:S(2)}, u32[]{:S(2)}) collective-permute-start(f32[24,128]{1,0:T(8,128)S(1)} %get-tuple-element.49.s0_ref), channel_id=1, source_target_pairs={{0,3},{1,2},{2,1},{3,0},{4,7},{5,6},{6,5},{7,4},{8,11},{9,10},{10,... | collective-permute-start | bytes 36872 | tf_op jit(solution)/shard_map/ppermute | solution.py:668
  64.1 5.2 %collective-permute-start.9 = (f32[24,128]{1,0:T(8,128)S(1)}, f32[24,128]{1,0:T(8,128)S(1)}, u32[]{:S(2)}, u32[]{:S(2)}) collective-permute-start(f32[24,128]{1,0:T(8,128)S(1)} %get-tuple-element.49.s0_ref), channel_id=1, source_target_pairs={{0,2},{1,3},{2,0},{3,1},{4,6},{5,7},{6,4},{7,5},{8,10},{9,11},{10,... | collective-permute-start | bytes 36872 | tf_op jit(solution)/shard_map/ppermute | solution.py:668
  64.9 4.4 %collective-permute-start.8 = (f32[24,128]{1,0:T(8,128)S(1)}, f32[24,128]{1,0:T(8,128)S(1)}, u32[]{:S(2)}, u32[]{:S(2)}) collective-permute-start(f32[24,128]{1,0:T(8,128)S(1)} %get-tuple-element.49.s0_ref), channel_id=1, source_target_pairs={{0,1},{1,0},{2,3},{3,2},{4,5},{5,4},{6,7},{7,6},{8,9},{9,8},{10,11... | collective-permute-start | bytes 36872 | tf_op jit(solution)/shard_map/ppermute | solution.py:668
